TPU v7x, 512 devices: a whole 4x8x8 slice. The times are simulated.
512 devices in a mesh: lat: 16 (over z_lo, x, core), lon: 32 (over y, z_hi).
Axes of the slice: x: 4, y: 8, z: 8 (z_hi: 4, z_lo: 2; z = z_hi * 2 + z_lo), core: 2. Of those that a mesh axis runs over, the one named last changes fastest.
Arguments:
- field: bfloat16 [64, 2048, 512], P('lat', 'lon'), may hold values from -6 to 6
- w_qkv: bfloat16 [512, 1152], replicated, may hold values from -2 to 2
- w_out: bfloat16 [512, 512], replicated, may hold values from -0.25 to 0.25
- conv_w: float32 [7, 7, 512], replicated, may hold values from -0.875 to 0.875
- w_in: bfloat16 [512, 1024], replicated, may hold values from -0.25 to 0.25
- w_back: bfloat16 [1024, 512], replicated, may hold values from -0.1875 to 0.1875
Outputs:
- result: bfloat16 [64, 2048, 512], P('lat', 'lon')
All inputs are finite; a program needn't handle non-finite values.
Results may differ from a plain program's by a relative error of at most 0.012.
The roundings to bfloat16 on the way count: a program that leaves them out, or rounds other values in their place, can miss the bound.
Values may be sent and summed in bfloat16 or wider, within the bound.
No kernel may reach another device: no remote copies, remote signals or barrier semaphores. Data moves between devices by JAX's collectives and lax.ppermute only.
A program may use at most 64 MiB of HBM per device.

v0:
```python
import math

import jax
import jax.numpy as jnp
from jax import lax
from jax.sharding import PartitionSpec as P

C = 512
HD = 64
ZHEADS = 4
MHEADS = 4


def padded_2(array, sides, width, wrap):
    for axis, dim in sides:
        peers, length = (lax.axis_size(axis), array.shape[dim])
        up = [(i, (i + 1) % peers) for i in range(peers if wrap else peers - 1)]
        down = [(j, i) for i, j in up]
        last = lax.slice_in_dim(array, length - width, length, axis=dim)
        first = lax.slice_in_dim(array, 0, width, axis=dim)
        before = lax.ppermute(last, axis, up)
        after = lax.ppermute(first, axis, down)
        array = jnp.concatenate([before, array, after], axis=dim)
    return array


def layer_norm(values):
    center = values - jnp.mean(values, axis=-1, keepdims=True)
    spread = jnp.mean(center * center, axis=-1, keepdims=True)
    return center * lax.rsqrt(spread + 1e-06)


def split_heads(projected):
    zq_end = ZHEADS * HD
    mq_end = zq_end + MHEADS * HD
    kz_end = mq_end + HD
    vz_end = kz_end + HD
    km_end = vz_end + MHEADS * HD
    lead = projected.shape[:2]
    zonal_q = projected[..., :zq_end].reshape(lead + (ZHEADS, HD))
    merid_q = projected[..., zq_end:mq_end].reshape(lead + (MHEADS, HD))
    zonal_k = projected[..., mq_end:kz_end]
    zonal_v = projected[..., kz_end:vz_end]
    merid_k = projected[..., vz_end:km_end].reshape(lead + (MHEADS, HD))
    merid_v = projected[..., km_end:].reshape(lead + (MHEADS, HD))
    return (zonal_q, merid_q, zonal_k, zonal_v, merid_k, merid_v)


def merid_attend(queries, keys, values):
    scores = jnp.einsum("rchd,schd->chrs", queries, keys, preferred_element_type=jnp.float32) * (
        1.0 / math.sqrt(HD)
    )
    peak = jnp.max(scores, axis=-1, keepdims=True)
    weights = jnp.exp(scores - peak)
    mass = jnp.sum(weights, axis=-1)
    blended = jnp.einsum(
        "chrs,schd->rchd", weights.astype(jnp.bfloat16), values, preferred_element_type=jnp.float32
    )
    return blended / jnp.transpose(mass, (2, 0, 1))[..., None]


def per_device(field, w_qkv, w_out, conv_w, w_in, w_back):
    rows_dev, cols_dev = (field.shape[0], field.shape[1])
    field_wide = field.astype(jnp.float32)
    normed = layer_norm(field_wide).astype(jnp.bfloat16)
    projected = jnp.dot(normed.reshape(-1, C), w_qkv, preferred_element_type=jnp.float32).astype(
        jnp.bfloat16
    )
    projected = projected.reshape(rows_dev, cols_dev, -1)
    zonal_q, merid_q, zonal_k, zonal_v, merid_k, merid_v = split_heads(projected)
    scale_factor = 1.0 / math.sqrt(HD)
    start_state = (
        jnp.full((rows_dev, ZHEADS, cols_dev), -1e30, jnp.float32),
        jnp.zeros((rows_dev, ZHEADS, cols_dev), jnp.float32),
        jnp.zeros((rows_dev, ZHEADS, cols_dev, HD), jnp.float32),
    )
    keys = lax.all_gather(zonal_k, "lon", axis=1, tiled=True)
    values = lax.all_gather(zonal_v, "lon", axis=1, tiled=True)
    length = keys.shape[1]
    block = math.gcd(cols_dev, length)
    count = length // block
    key_blocks = keys.reshape(rows_dev, count, block, HD).transpose(1, 0, 2, 3)
    value_blocks = values.reshape(rows_dev, count, block, HD).transpose(1, 0, 2, 3)

    def key_block(state, pair):
        run_max, run_mass, run_acc = state
        block_keys, block_values = pair
        scores = (
            jnp.einsum("rqhd,rkd->rhqk", zonal_q, block_keys, preferred_element_type=jnp.float32)
            * scale_factor
        )
        new_max = jnp.maximum(run_max, jnp.max(scores, axis=-1))
        shrink = jnp.exp(run_max - new_max)
        weights = jnp.exp(scores - new_max[..., None])
        run_mass = run_mass * shrink + jnp.sum(weights, axis=-1)
        added = jnp.einsum(
            "rhqk,rkd->rhqd",
            weights.astype(jnp.bfloat16),
            block_values,
            preferred_element_type=jnp.float32,
        )
        run_acc = run_acc * shrink[..., None] + added
        return ((new_max, run_mass, run_acc), None)

    result_state, unused = lax.scan(key_block, start_state, (key_blocks, value_blocks))
    final_max, final_mass, final_acc = result_state
    zonal = (
        (final_acc / final_mass[..., None])
        .transpose(0, 2, 1, 3)
        .reshape(rows_dev, cols_dev, ZHEADS * HD)
    )
    all_keys, all_values = (
        lax.all_gather(merid_k, "lat", axis=0, tiled=True),
        lax.all_gather(merid_v, "lat", axis=0, tiled=True),
    )
    meridional = merid_attend(merid_q, all_keys, all_values)
    heads = jnp.concatenate(
        [
            zonal.astype(jnp.bfloat16),
            meridional.reshape(rows_dev, cols_dev, MHEADS * HD).astype(jnp.bfloat16),
        ],
        axis=-1,
    )
    attended = jnp.dot(
        heads.reshape(-1, heads.shape[-1]), w_out, preferred_element_type=jnp.float32
    )
    mixed = (field_wide + attended.reshape(rows_dev, cols_dev, C)).astype(jnp.bfloat16)
    widened = padded_2(mixed, (("lon", 1),), 3, True)
    padded = padded_2(widened, (("lat", 0),), 3, False)
    conv = jnp.zeros((rows_dev, cols_dev, C), jnp.float32)
    for row_off in range(7):
        for col_off in range(7):
            window = padded[row_off : row_off + rows_dev, col_off : col_off + cols_dev].astype(
                jnp.float32
            )
            conv = conv + window * conv_w[row_off, col_off]
    normed2 = layer_norm(conv).astype(jnp.bfloat16)
    expanded = jax.nn.gelu(
        jnp.dot(normed2.reshape(-1, C), w_in, preferred_element_type=jnp.float32), approximate=False
    ).astype(jnp.bfloat16)
    back = jnp.dot(expanded, w_back, preferred_element_type=jnp.float32).reshape(
        rows_dev, cols_dev, C
    )
    return (mixed.astype(jnp.float32) + back).astype(jnp.bfloat16)


def solution(mesh):
    return jax.shard_map(
        per_device,
        mesh=mesh,
        in_specs=(P("lat", "lon", None), P(), P(), P(), P(), P()),
        out_specs=P("lat", "lon", None),
        check_vma=False,
    )
```

profile of v0, /device:TPU:7, one launch (start us, length us, event | category | flops | bytes accessed | tf_op | source)
XLA Modules:
  0.0 342.5 jit_solution(17092721222973324507)
XLA Ops:
  14.5 85.9 %all-gather.5.cloned.1.call-done = bf16[4,2048,64]{2,1,0:T(8,128)(2,1)} async-done(((bf16[4,64,64]{2,1,0:T(8,128)(2,1)}), bf16[4,2048,64]{2,1,0:T(8,128)(2,1)}) %all-gather.5.cloned.1.call-update) | async-done | bytes 1048592 | tf_op jit(solution)/shard_map/all_gather | solution.py:77
  100.4 86.1 %all-gather.7.cloned.1.call-done = bf16[4,2048,64]{2,1,0:T(8,128)(2,1)} async-done(((bf16[4,64,64]{2,1,0:T(8,128)(2,1)}), bf16[4,2048,64]{2,1,0:T(8,128)(2,1)}) %all-gather.7.cloned.1.call-update) | async-done | bytes 1048592 | tf_op jit(solution)/shard_map/all_gather | solution.py:78
  186.5 87.2 %while.15 = (s32[]{:T(128)}, f32[4,4,64]{2,1,0:T(4,128)S(1)}, f32[4,4,64]{2,1,0:T(4,128)S(1)}, f32[4,4,64,64]{3,2,1,0:T(8,128)S(1)}, bf16[32,4,64,64]{3,2,0,1:T(...) while((s32[]{:T(128)}, f32[4,4,64]{2,1,0:T(4,128)S(1)}, ...), condition=%wide.region_5.6_spmd.clone, body=%wide.region_2.5_spmd.clone.sunk | while | flops 17372164 | bytes 1639529 | solution.py:105
  187.9 1.3 convolution_add_fusion.3
  190.7 1.3 convolution_add_fusion.3
  193.4 1.3 convolution_add_fusion.3
  196.1 1.3 convolution_add_fusion.3
  198.8 1.3 convolution_add_fusion.3
  201.5 1.3 convolution_add_fusion.3
  204.3 1.3 convolution_add_fusion.3
  207.0 1.3 convolution_add_fusion.3
  209.7 1.3 convolution_add_fusion.3
  212.4 1.3 convolution_add_fusion.3
  213.8 1.2 fusion.144
  215.2 1.3 convolution_add_fusion.3
  217.9 1.3 convolution_add_fusion.3
  220.6 1.3 convolution_add_fusion.3
  221.9 1.2 fusion.144
  223.3 1.3 convolution_add_fusion.3
  226.0 1.3 convolution_add_fusion.3
  228.7 1.3 convolution_add_fusion.3
  231.5 1.3 convolution_add_fusion.3
  234.2 1.3 convolution_add_fusion.3
  236.9 1.3 convolution_add_fusion.3
  239.6 1.3 convolution_add_fusion.3
  242.3 1.3 convolution_add_fusion.3
  245.1 1.3 convolution_add_fusion.3
  246.4 1.3 fusion.144
  247.8 1.3 convolution_add_fusion.3
  250.5 1.3 convolution_add_fusion.3
  253.3 1.3 convolution_add_fusion.3
  256.0 1.3 convolution_add_fusion.3
  257.3 1.2 fusion.144
  258.7 1.3 convolution_add_fusion.3
  261.4 1.3 convolution_add_fusion.3
  264.1 1.3 convolution_add_fusion.3
  266.9 1.3 convolution_add_fusion.3
  269.6 1.3 convolution_add_fusion.3
  272.3 1.3 convolution_add_fusion.3
  274.5 10.7 %fusion.126 = (f32[64,4,4]{2,1,0:T(4,128)S(1)}, f32[64,4,4,64]{3,2,1,0:T(4,128)S(1)}) fusion(bf16[64,64,4,64]{3,1,2,0:T(8,128)(2,1)} %all-gather.11.cloned.1.call-done, bf16[4,64,4,64]{3,2,1,0:T(4,128)(2,1)S(1)} %reshape.80), kind=kOutput, calls=%fused_computation.157 | convolution fusion | flops 8518656 | bytes 2494464 | tf_op jit(solution)/shard_map/rchd,schd->chrs/dot_general | solution.py:50
  286.0 11.0 %fusion.36 = bf16[4,64,4,64]{3,0,2,1:T(4,128)(2,1)S(1)} fusion(bf16[64,64,4,64]{3,1,2,0:T(8,128)(2,1)} %all-gather.9.cloned.1.call-done, f32[64,4,4,64]{3,2,1,0:T(4,128)S(1)} %get-tuple-element.165, f32[4,64,4]{0,2,1:T(4,128)S(1)} %bitcast.110, f32[64,4,4]{2,1,0:T(4,128)S(1)} %get-tuple-element.164), kind=kOutput, calls=%fused_computation.47 | convolution fusion | flops 8650752 | bytes 2498560 | tf_op jit(solution)/shard_map/chrs,schd->rchd/dot_general | solution.py:56
  297.6 3.7 %collective-permute-start = (bf16[4,3,512]{2,1,0:T(4,128)(2,1)S(1)}, bf16[4,3,512]{2,1,0:T(4,128)(2,1)S(1)}, u32[]{:S(2)}, u32[]{:S(2)}) collective-permute-start(bf16[4,3,512]{2,1,0:T(4,128)(2,1)S(1)} %get-tuple-element.113), channel_id=1, source_target_pairs={{0,1},{1,2},{2,3},{3,4},{4,5},{5,6},{6,7},{7,8},{8,9},{9,10},{10,1... | collective-permute-start | bytes 36872 | tf_op jit(solution)/shard_map/ppermute | solution.py:21
  301.3 5.8 %collective-permute-start.1 = (bf16[4,3,512]{2,1,0:T(4,128)(2,1)S(1)}, bf16[4,3,512]{2,1,0:T(4,128)(2,1)S(1)}, u32[]{:S(2)}, u32[]{:S(2)}) collective-permute-start(bf16[4,3,512]{2,1,0:T(4,128)(2,1)S(1)} %get-tuple-element.114), channel_id=1, source_target_pairs={{1,0},{2,1},{3,2},{4,3},{5,4},{6,5},{7,6},{8,7},{9,8},{10,9},{11,1... | collective-permute-start | bytes 36872 | tf_op jit(solution)/shard_map/ppermute | solution.py:22
  308.1 8.1 %collective-permute-start.2 = (bf16[3,70,512]{2,1,0:T(8,128)(2,1)S(1)}, bf16[3,70,512]{2,1,0:T(8,128)(2,1)S(1)}, u32[]{:S(2)}, u32[]{:S(2)}) collective-permute-start(bf16[3,70,512]{2,1,0:T(8,128)(2,1)S(1)} %get-tuple-element.111), channel_id=1, source_target_pairs={{0,32},{32,64},{64,96},{96,128},{128,160},{160,192},{192,224},{224... | collective-permute-start | bytes 645128 | tf_op jit(solution)/shard_map/ppermute | solution.py:21
  316.2 1.9 collective-permute-start.3
  319.1 6.5 %collective-permute-done.3 = bf16[3,70,512]{2,1,0:T(8,128)(2,1)S(1)} collective-permute-done((bf16[3,70,512]{2,1,0:T(8,128)(2,1)S(1)}, bf16[3,70,512]{2,1,0:T(8,128)(2,1)S(1)}, u32[]{:S(2)}, u32[]{:S(2)}) %collective-permute-start.3) | collective-permute-done | bytes 215072 | tf_op jit(solution)/shard_map/ppermute | solution.py:22
  325.7 4.9 %fusion.116 = (f32[4,64]{1,0:T(4,128)S(1)}, f32[4,64,512]{2,1,0:T(8,128)S(1)}) fusion(f32[512]{0:T(512)S(1)} %bitcast.160, bf16[7,70,512]{2,1,0:T(8,128)(2,1)S(1)} %get-tuple-element.110, f32[512]{0:T(512)S(1)} %bitcast.161, f32[512]{0:T(512)S(1)} %bitcast.114, f32[512]{0:T(512)S(1)} %bitcast.115, f32[512]{0:T(512)S(1)} %bitcast.116, f32[512]{0:T(512)S(1)} %bitcast.117, ...), kind=kLoop, calls=%fused_computation.148 | loop fusion | flops 21626624 | bytes 11922432 | tf_op jit(solution)/shard_map/reduce_sum | solution.py:28
  331.0 4.1 %fusion.70 = f32[256,512]{1,0:T(8,128)S(1)} fusion(bf16[1024,512]{1,0:T(8,128)(2,1)S(1)} %copy-done.3, bf16[256,512]{1,0:T(8,128)(2,1)S(1)} %bitcast.109, bf16[512,1024]{1,0:T(8,128)(2,1)} %param.12), kind=kOutput, calls=%fused_computation.87 | convolution fusion | flops 553910272 | bytes 2883584 | tf_op jit(solution)/shard_map/dot_general | solution.py:141
  (216 shorter events, 52.3 us)
Async XLA Ops:
  6.5 3.5 %copy-start = (bf16[512,1152]{1,0:T(8,128)(2,1)S(1)}, bf16[512,1152]{1,0:T(8,128)(2,1)}, u32[]{:S(2)}) copy-start(bf16[512,1152]{1,0:T(8,128)(2,1)} %param.9) | copy-start | bytes 3538948
  6.5 93.9 %all-gather.5.cloned.1.call-start = ((), (), s32[]{:S(2)}) async-start(), calls=%async_computation | async-start | bytes 2162688 | tf_op jit(solution)/shard_map/all_gather | solution.py:77
  11.3 175.3 %all-gather.7.cloned.1.call-start = ((), (), s32[]{:S(2)}) async-start(), calls=%async_computation.1 | async-start | bytes 2162688 | tf_op jit(solution)/shard_map/all_gather | solution.py:78
  12.0 262.4 %all-gather.11.cloned.1.call-start = ((), (), s32[]{:S(2)}) async-start(), calls=%async_computation.3 | async-start | bytes 4456448 | tf_op jit(solution)/shard_map/all_gather | solution.py:113
  12.1 2.4 copy-start.2
  13.1 272.9 %all-gather.9.cloned.1.call-start = ((), (), s32[]{:S(2)}) async-start(), calls=%async_computation.2 | async-start | bytes 4456448 | tf_op jit(solution)/shard_map/all_gather | solution.py:114
  285.9 11.3 %copy-start.1 = (bf16[4,64,512]{2,1,0:T(8,128)(2,1)S(1)}, bf16[4,64,512]{2,1,0:T(8,128)(2,1)}, u32[]{:S(2)}) copy-start(bf16[4,64,512]{2,1,0:T(8,128)(2,1)} %param.8) | copy-start | bytes 786436
  285.9 11.3 %copy-start.4 = (bf16[512,512]{1,0:T(8,128)(2,1)S(1)}, bf16[512,512]{1,0:T(8,128)(2,1)}, u32[]{:S(2)}) copy-start(bf16[512,512]{1,0:T(8,128)(2,1)} %param.10) | copy-start | bytes 1572868
  297.6 9.6 %collective-permute-start = (bf16[4,3,512]{2,1,0:T(4,128)(2,1)S(1)}, bf16[4,3,512]{2,1,0:T(4,128)(2,1)S(1)}, u32[]{:S(2)}, u32[]{:S(2)}) collective-permute-start(bf16[4,3,512]{2,1,0:T(4,128)(2,1)S(1)} %get-tuple-element.113), channel_id=1, source_target_pairs={{0,1},{1,2},{2,3},{3,4},{4,5},{5,6},{6,7},{7,8},{8,9},{9,10},{10,1... | collective-permute-start | bytes 36872 | tf_op jit(solution)/shard_map/ppermute | solution.py:21
  301.3 6.6 %collective-permute-start.1 = (bf16[4,3,512]{2,1,0:T(4,128)(2,1)S(1)}, bf16[4,3,512]{2,1,0:T(4,128)(2,1)S(1)}, u32[]{:S(2)}, u32[]{:S(2)}) collective-permute-start(bf16[4,3,512]{2,1,0:T(4,128)(2,1)S(1)} %get-tuple-element.114), channel_id=1, source_target_pairs={{1,0},{2,1},{3,2},{4,3},{5,4},{6,5},{7,6},{8,7},{9,8},{10,9},{11,1... | collective-permute-start | bytes 36872 | tf_op jit(solution)/shard_map/ppermute | solution.py:22
  308.1 11.0 %collective-permute-start.2 = (bf16[3,70,512]{2,1,0:T(8,128)(2,1)S(1)}, bf16[3,70,512]{2,1,0:T(8,128)(2,1)S(1)}, u32[]{:S(2)}, u32[]{:S(2)}) collective-permute-start(bf16[3,70,512]{2,1,0:T(8,128)(2,1)S(1)} %get-tuple-element.111), channel_id=1, source_target_pairs={{0,32},{32,64},{64,96},{96,128},{128,160},{160,192},{192,224},{224... | collective-permute-start | bytes 645128 | tf_op jit(solution)/shard_map/ppermute | solution.py:21
  316.2 9.4 %collective-permute-start.3 = (bf16[3,70,512]{2,1,0:T(8,128)(2,1)S(1)}, bf16[3,70,512]{2,1,0:T(8,128)(2,1)S(1)}, u32[]{:S(2)}, u32[]{:S(2)}) collective-permute-start(bf16[3,70,512]{2,1,0:T(8,128)(2,1)S(1)} %get-tuple-element.112), channel_id=1, source_target_pairs={{32,0},{64,32},{96,64},{128,96},{160,128},{192,160},{224,192},{256... | collective-permute-start | bytes 645128 | tf_op jit(solution)/shard_map/ppermute | solution.py:22
  325.7 5.3 %copy-start.3 = (bf16[1024,512]{1,0:T(8,128)(2,1)S(1)}, bf16[1024,512]{1,0:T(8,128)(2,1)}, u32[]{:S(2)}) copy-start(bf16[1024,512]{1,0:T(8,128)(2,1)} %param.13) | copy-start | bytes 3145732
Sparse Core Ops, SparseCore 0:
  11.4 88.9 all-gather.4
  103.6 82.9 all-gather.6
  188.7 41.1 all-gather.10
  231.9 42.8 all-gather.8
where the time goes:
time: 346 us; the launch traced here: 342 us
  waiting for transfers between devices  181 us (52%)
  matrix products  107 us (31%)
  starting transfers between devices  19.7 us (6%)
  other arithmetic  15.2 us (4%)
  between operations  13.5 us (4%)
  local copies, waits for them, and re-layouts  3.94 us (1%)
    all_gather x1, waiting for transfers between devices, per_device(): values = lax.all_gather(zonal_v, 'lon', axis=1, tiled=True)  86.1 us
    all_gather x1, waiting for transfers between devices, per_device(): keys = lax.all_gather(zonal_k, 'lon', axis=1, tiled=True)  85.9 us
    dot_general x32, matrix products, key_block(): jnp.einsum('rhqk,rkd->rhqd', weights.astype(jnp.bfloat16), block_values,...  41.1 us
    dot_general x32, matrix products, key_block(): jnp.einsum('rqhd,rkd->rhqk', zonal_q, block_keys, preferred_element_type=...  39.6 us
    ppermute x2, starting transfers between devices, padded_2(): before = lax.ppermute(last, axis, up)  11.9 us
    dot_general x1, matrix products, merid_attend(): jnp.einsum('chrs,schd->rchd', weights.astype(jnp.bfloat16), values, prefe...  11 us
    dot_general x1, matrix products, merid_attend(): jnp.einsum('rchd,schd->chrs', queries, keys, preferred_element_type=jnp.f...  10.7 us
    ppermute x2, starting transfers between devices, padded_2(): after = lax.ppermute(first, axis, down)  7.69 us
  transfers between devices with their start and end apart: 8, of which 5 were waited for; matrix products, arithmetic and copies ran while one was open for 29% of the time, Pallas kernels for 0%

commit v1 on v0

v1 whole, which is shorter than its diff:
```python
import math

import jax
import jax.numpy as jnp
from jax import lax
from jax.experimental import pallas as pl
from jax.experimental.pallas import tpu as pltpu
from jax.sharding import PartitionSpec as P

C = 512
HD = 64
LAT = 16
LON = 32
R = 4
W = 64
CELLS = R * W
G = 8
WIDE = W + 16
SLOT = W + 2 * G
BACK = 3 * G
F32 = jnp.float32
BF = jnp.bfloat16
VMEM = 48 * 1024 * 1024


def iota(shape, dim):
    return lax.broadcasted_iota(jnp.int32, shape, dim)


def one_hot(hit):
    return jnp.where(hit, 1.0, 0.0).astype(BF)


def mm(a, b):
    return jnp.dot(a, b, preferred_element_type=F32)


def mm_nt(a, b):
    return lax.dot_general(a, b, (((1,), (1,)), ((), ())), preferred_element_type=F32)


def layer_norm(values):
    center = values - jnp.mean(values, axis=-1, keepdims=True)
    spread = jnp.mean(center * center, axis=-1, keepdims=True)
    return center * lax.rsqrt(spread + 1e-06)


def call(kernel, out_shape, flops, **kw):
    return pl.pallas_call(
        kernel,
        out_shape=out_shape,
        compiler_params=pltpu.CompilerParams(vmem_limit_bytes=VMEM),
        cost_estimate=pl.CostEstimate(flops=flops, bytes_accessed=2_000_000, transcendentals=0),
        **kw,
    )


def project_kernel(field_ref, w_ref, zonal_ref, merid_ref):
    normed = layer_norm(field_ref[...].astype(F32)).astype(BF)
    t, s = iota((CELLS, CELLS), 0), iota((CELLS, CELLS), 1)
    j, r, g = t // 32, (t // 8) % 4, t % 8
    normed_q = mm(one_hot(s == r * W + g * 8 + j), normed).astype(BF)
    m, r, cc = t // 16, (t // 4) % 4, t % 4
    normed_m = mm(one_hot(s == r * W + m * 4 + cc), normed).astype(BF)
    kv = mm(normed, w_ref[:, 512:640]).astype(BF)
    q = mm(normed_q, w_ref[:, 0:256])
    q = jnp.concatenate(
        [q[:, 0:128].reshape(LON, G, 128), q[:, 128:256].reshape(LON, G, 128)], axis=1
    ).astype(BF)
    for row in range(R):
        piece = kv[row * W : (row + 1) * W]
        for chunk in range(LON // R):
            zonal_ref[chunk * R + row, 0:W, :] = piece
    zonal_ref[:, W:SLOT, :] = q
    merid_ref[:, :, 0:256] = mm(normed_m, w_ref[:, 256:512]).astype(BF).reshape(LAT, 16, 256)
    merid_ref[:, :, 256:768] = mm(normed_m, w_ref[:, 640:1152]).astype(BF).reshape(LAT, 16, 512)


def merid_kernel(in_ref, out_ref):
    x = in_ref[...].reshape(CELLS, 768)
    t, s = iota((CELLS, CELLS), 0), iota((CELLS, CELLS), 1)
    bias = jnp.where(t % 4 == s % 4, 0.0, -1e30)
    low = iota((CELLS, 128), 1) < HD
    scale = 1.0 / math.sqrt(HD)
    for pair in range(2):
        q = x[:, pair * 128 : (pair + 1) * 128]
        k = x[:, 256 + pair * 128 : 384 + pair * 128]
        v = x[:, 512 + pair * 128 : 640 + pair * 128]
        outs = []
        for side in (low, jnp.logical_not(low)):
            score = mm_nt(jnp.where(side, q, jnp.zeros_like(q)), k) * scale + bias
            weight = jnp.exp(score - jnp.max(score, axis=-1, keepdims=True))
            mass = jnp.sum(weight, axis=-1, keepdims=True)
            outs.append(mm(weight.astype(BF), v) / mass)
        both = jnp.where(low, outs[0], outs[1]).astype(BF)
        out_ref[:, :, pair * 128 : (pair + 1) * 128] = both.reshape(LAT, 16, 128)


def zonal_kernel(chunk_ref, in_ref, out_ref):
    kv = in_ref[:, 0:W, :].reshape(LON * W, 128)
    ones = iota((LON * W, 128), 1) < HD
    kv_one = jnp.where(ones, jnp.ones_like(kv), kv)
    low = iota((LON * G, 128), 1) < HD
    q_all = in_ref[:, W:SLOT, :].astype(F32) * (1.0 / math.sqrt(HD))
    pairs = []
    for pair in range(2):
        q = q_all[:, pair * G : (pair + 1) * G, :].reshape(LON * G, 128)
        outs = []
        for head in range(2):
            placed = q if head == 0 else pltpu.roll(q, HD, 1)
            placed = jnp.where(low, placed, 0.0).astype(BF)
            score = mm_nt(placed, kv)
            weight = jnp.exp(score - jnp.max(score, axis=-1, keepdims=True)).astype(BF)
            both = mm(weight, kv_one)
            outs.append(both)
        even, odd = outs
        even = pltpu.roll(even, HD, 1)
        blended = jnp.where(low, even, odd)
        mass = jnp.where(low, pltpu.roll(even, HD, 1), pltpu.roll(odd, HD, 1))
        pairs.append(blended / mass)
    chunk = chunk_ref[0]
    t, u = iota((LON * G, LON * G), 0), iota((LON * G, LON * G), 1)
    s = t // G
    ahead, behind = ((s + 1) % LON) * G, ((s + LON - 1) % LON) * G + G - 1
    source = jnp.where(chunk < 4, ahead, behind)
    halo = mm(one_hot((t % G == 0) & (u == source)), pairs[0].astype(BF))
    halo = halo + mm(one_hot((t % G == 1) & (u == source)), pairs[1].astype(BF))
    parts = [a.reshape(LON, G, 128) for a in (pairs[0], pairs[1], halo)]
    out_ref[...] = jnp.concatenate(parts, axis=1).astype(BF)


def mix_kernel(zonal_ref, merid_ref, ml_ref, mr_ref, field_ref, fl_ref, fr_ref, w_ref, mixed_ref, up_ref, down_ref):
    rows = R * WIDE
    x = zonal_ref[...].astype(F32)
    x0 = x[:, 0:G].reshape(CELLS, 128).astype(BF)
    x1 = x[:, G : 2 * G].reshape(CELLS, 128).astype(BF)
    xh = x[:, 2 * G :].reshape(CELLS, 128).astype(BF)
    u, t = iota((rows, CELLS), 0), iota((rows, CELLS), 1)
    r, c = u // WIDE, u % WIDE - 8
    inside = (c >= 0) & (c < W)
    own = one_hot(inside & (t == ((c % 8) * 4 + r) * 8 + c // 8))
    left, right = (c >= -3) & (c < 0), (c >= W) & (c < W + 3)
    slot = jnp.where(left, c + 8, c - W) * 4 + r
    halo0 = one_hot((left | right) & (t == slot * 8))
    halo1 = one_hot((left | right) & (t == slot * 8 + 1))
    z0 = mm(own, x0) + mm(halo0, xh)
    z1 = mm(own, x1) + mm(halo1, xh)
    own_m = one_hot(inside & (t == (c // 4) * 16 + r * 4 + c % 4))
    merid = mm(own_m, merid_ref[...].reshape(CELLS, 256))
    u, t = iota((rows, 16), 0), iota((rows, 16), 1)
    r, c = u // WIDE, u % WIDE - 8
    from_left = one_hot((c >= -3) & (c < 0) & (t == r * 4 + c + 4))
    from_right = one_hot((c >= W) & (c < W + 3) & (t == r * 4 + c - W))
    merid = merid + mm(from_left, ml_ref[...]) + mm(from_right, mr_ref[...])
    attended = mm(z0.astype(BF), w_ref[0:128]) + mm(z1.astype(BF), w_ref[128:256])
    attended = attended + mm(merid.astype(BF), w_ref[256:512])
    wide = jnp.concatenate(
        [fl_ref[...].astype(F32), field_ref[...].astype(F32), fr_ref[...].astype(F32)], axis=1
    )
    mixed = (wide + attended.reshape(R, WIDE, C)).astype(BF)
    mixed_ref[...] = mixed
    up_ref[...] = mixed[0:3]
    down_ref[...] = mixed[1:4]


def block_kernel(mixed_ref, before_ref, after_ref, conv_ref, w_in_ref, w_back_ref, out_ref, conv_out):
    for lane in range(0, C, 128):
        rows = [before_ref[i, :, lane : lane + 128].astype(F32) for i in range(3)]
        rows += [mixed_ref[i, :, lane : lane + 128].astype(F32) for i in range(R)]
        rows += [after_ref[i, :, lane : lane + 128].astype(F32) for i in range(3)]
        for r in range(R):
            total = None
            for b in range(7):
                part = None
                for a in range(7):
                    term = rows[r + a] * conv_ref[a * 7 + b, lane : lane + 128][None, :]
                    part = term if part is None else part + term
                moved = part[b + 5 : b + 5 + W]
                total = moved if total is None else total + moved
            conv_out[r * W : (r + 1) * W, lane : lane + 128] = total
    normed = layer_norm(conv_out[...]).astype(BF)
    hidden = mm(normed, w_in_ref[...])
    hidden = 0.5 * hidden * (1.0 + lax.erf(hidden * math.sqrt(0.5)))
    back = mm(hidden.astype(BF), w_back_ref[...])
    own = mixed_ref[...].astype(F32)[:, 8 : 8 + W].reshape(CELLS, C)
    out_ref[...] = (own + back).astype(BF).reshape(R, W, C)


def shape(*dims):
    return jax.ShapeDtypeStruct(dims, BF)


def per_device(field, w_qkv, w_out, conv_w, w_in, w_back):
    right = [(i, (i + 1) % LON) for i in range(LON)]
    left = [(j, i) for i, j in right]
    down = [(i, i + 1) for i in range(LAT - 1)]
    up = [(j, i) for i, j in down]
    zonal_in, merid_in = call(
        project_kernel, (shape(LON, SLOT, 128), shape(LAT, 16, 768)), 400_000_000
    )(field.reshape(CELLS, C), w_qkv)
    merid_in = lax.all_to_all(merid_in, "lat", 0, 0)
    zonal_in = lax.all_to_all(zonal_in, "lon", 0, 0)
    merid = call(merid_kernel, shape(LAT, 16, 256), 800_000_000)(merid_in)
    merid = lax.all_to_all(merid, "lat", 0, 0)
    chunk = (lax.axis_index("lon") // R).astype(jnp.int32).reshape(1)
    zonal = call(
        zonal_kernel,
        shape(LON, BACK, 128),
        4_000_000_000,
        in_specs=[pl.BlockSpec(memory_space=pltpu.SMEM), pl.BlockSpec(memory_space=pltpu.VMEM)],
    )(chunk, zonal_in)
    zonal = lax.all_to_all(zonal, "lon", 0, 0)
    merid_left = lax.ppermute(merid[LAT - 1], "lon", right)
    merid_right = lax.ppermute(merid[0], "lon", left)
    field_left = lax.ppermute(field[:, W - 8 :], "lon", right)
    field_right = lax.ppermute(field[:, :8], "lon", left)
    mixed, first, last = call(
        mix_kernel, (shape(R, WIDE, C), shape(3, WIDE, C), shape(3, WIDE, C)), 800_000_000
    )(zonal, merid, merid_left, merid_right, field, field_left, field_right, w_out)
    before = lax.ppermute(last, "lat", down)
    after = lax.ppermute(first, "lat", up)
    return call(
        block_kernel,
        shape(R, W, C),
        2_000_000_000,
        scratch_shapes=[pltpu.VMEM((CELLS, C), F32)],
    )(mixed, before, after, conv_w.reshape(49, C), w_in, w_back)


def solution(mesh):
    return jax.shard_map(
        per_device,
        mesh=mesh,
        in_specs=(P("lat", "lon", None), P(), P(), P(), P(), P()),
        out_specs=P("lat", "lon", None),
        check_vma=False,
    )
```

time: 346 us -> 114 us (0.33)
  waiting for transfers between devices: 181 us -> 27.7 us
  matrix products: 107 us -> 0 us
  starting transfers between devices: 19.7 us -> 52.1 us
  blocking collectives: 0 us -> 16.1 us
  other arithmetic: 15.2 us -> 0 us
  between operations: 13.5 us -> 0.19 us
  Pallas kernels: 0 us -> 12.3 us
    all_gather x4 -> x0, waiting for transfers between devices: 172 us -> none  [the longest x1 86.1 us: per_device(): values = lax.all_gather(zonal_v, 'lon', axis=1, tiled=True)]
    dot_general x69 -> x0, matrix products: 107 us -> none  [the longest x32 41.1 us: key_block(): jnp.einsum('rhqk,rkd->rhqd', weights.astype(jnp.bfloat16), block_values,...]
    all_to_all x0 -> x3, starting transfers between devices: none -> 25 us  [the longest x1 12.8 us: per_device(): zonal_in = lax.all_to_all(zonal_in, 'lon', 0, 0)]
    all_to_all x0 -> x3, waiting for transfers between devices: none -> 19.3 us  [the longest x1 18.7 us: per_device(): zonal_in = lax.all_to_all(zonal_in, 'lon', 0, 0)]
    all_to_all x0 -> x1, blocking collectives: none -> 16.1 us  [per_device(): merid_in = lax.all_to_all(merid_in, 'lat', 0, 0)]
    pallas_call x0 -> x5, Pallas kernels: none -> 12.3 us  [the longest x1 4.06 us: per_device(): call(zonal_kernel, shape(LON, BACK, 128), 4000000000, in_specs=[pl.BlockS...]
    reduce_sum x37 -> x0, other arithmetic: 12 us -> none  [the longest x2 6.09 us: layer_norm(): center = values - jnp.mean(values, axis=-1, keepdims=True)]
    ppermute x4 -> x6, starting transfers between devices: 19.6 us -> 27 us  [the longest x1 7.71 us: per_device(): merid_right = lax.ppermute(merid[0], 'lon', left)]
  transfers between devices with their start and end apart: 8 -> 9, of which waited for: 5 -> 5; matrix products, arithmetic and copies ran while one was open for 29% -> 0% of each run, Pallas kernels for 0% -> 5%
where the time goes in v1:
time: 114 us; the launch traced here: 113 us
  starting transfers between devices  52.1 us (46%)
  waiting for transfers between devices  27.7 us (24%)
  blocking collectives  16.1 us (14%)
  Pallas kernels  12.3 us (11%)
  local copies, waits for them, and re-layouts  5.01 us (4%)
    all_to_all x1, waiting for transfers between devices, per_device(): zonal_in = lax.all_to_all(zonal_in, 'lon', 0, 0)  18.7 us
    all_to_all x1, blocking collectives, per_device(): merid_in = lax.all_to_all(merid_in, 'lat', 0, 0)  16.1 us
    all_to_all x1, starting transfers between devices, per_device(): zonal_in = lax.all_to_all(zonal_in, 'lon', 0, 0)  12.8 us
    ppermute x1, starting transfers between devices, per_device(): merid_right = lax.ppermute(merid[0], 'lon', left)  7.71 us
    ppermute x1, waiting for transfers between devices, per_device(): after = lax.ppermute(first, 'lat', up)  6.51 us
    all_to_all x1, starting transfers between devices, per_device(): merid = lax.all_to_all(merid, 'lat', 0, 0)  6.31 us
    ppermute x1, starting transfers between devices, per_device(): before = lax.ppermute(last, 'lat', down)  5.99 us
    all_to_all x1, starting transfers between devices, per_device(): zonal = lax.all_to_all(zonal, 'lon', 0, 0)  5.87 us
  transfers between devices with their start and end apart: 9, of which 5 were waited for; matrix products, arithmetic and copies ran while one was open for 0% of the time, Pallas kernels for 5%

profile of v1, /device:TPU:7, one launch (start us, length us, event | category | flops | bytes accessed | tf_op | source)
XLA Modules:
  0.0 113.3 jit_solution(1642428469047248577)
XLA Ops:
  0.0 0.0 copy-start
  0.0 0.9 copy-done
  1.0 0.0 copy-start.2
  1.0 1.3 %copy-done.2 = bf16[512,1152]{1,0:T(8,128)(2,1)S(1)} copy-done((bf16[512,1152]{1,0:T(8,128)(2,1)S(1)}, bf16[512,1152]{1,0:T(8,128)(2,1)}, u32[]{:S(2)}) %copy-start.2) | copy-done | bytes 1179672
  2.2 1.6 %shard_map.64 = (bf16[32,80,128]{2,1,0:T(8,128)(2,1)}, bf16[16,16,768]{2,1,0:T(8,128)(2,1)S(1)}) custom-call(bf16[256,512]{1,0:T(8,128)(2,1)S(1)} %bitcast.6, bf16[512,1152]{1,0:T(8,128)(2,1)S(1)} %copy-done.2), custom_call_target="tpu_custom_call" | custom-call | flops 400000000 | bytes 2000000 | tf_op jit(solution)/shard_map/pallas_call | solution.py:198
  3.8 16.1 %all_to_all.20.in_ref = bf16[16,16,768]{2,1,0:T(8,128)(2,1)S(1)} all-to-all(bf16[16,16,768]{2,1,0:T(8,128)(2,1)S(1)} %get-tuple-element.11), channel_id=1, replica_groups=mesh['lat'=16,'lon'=32] {'lat'}, dimensions={0} | all-to-all | bytes 786432 | tf_op jit(solution)/shard_map/all_to_all | solution.py:201
  19.9 12.8 %all-to-all-start = ((bf16[32,80,128]{2,1,0:T(8,128)(2,1)}), bf16[32,80,128]{2,1,0:T(8,128)(2,1)S(1)}, u32[]{:S(2)}, u32[]{:S(2)}) async-start(bf16[32,80,128]{2,1,0:T(8,128)(2,1)} %get-tuple-element.10), calls=%async_computation | async-start | bytes 1310720 | tf_op jit(solution)/shard_map/all_to_all | solution.py:202
  32.8 1.5 %shard_map.66 = bf16[16,16,256]{2,1,0:T(8,128)(2,1)} custom-call(bf16[16,16,768]{2,1,0:T(8,128)(2,1)S(1)} %all_to_all.20.in_ref), custom_call_target="tpu_custom_call" | custom-call | flops 800000000 | bytes 2000000 | tf_op jit(solution)/shard_map/pallas_call | solution.py:203
  34.2 18.7 %all-to-all-done.in_ref = bf16[32,80,128]{2,1,0:T(8,128)(2,1)S(1)} async-done(((bf16[32,80,128]{2,1,0:T(8,128)(2,1)}), bf16[32,80,128]{2,1,0:T(8,128)(2,1)S(1)}, u32[]{:S(2)}, u32[]{:S(2)}) %all-to-all-start) | async-done | bytes 655392 | tf_op jit(solution)/shard_map/all_to_all | solution.py:202
  53.0 6.3 %all-to-all-start.3 = ((bf16[16,16,256]{2,1,0:T(8,128)(2,1)}), bf16[16,16,256]{2,1,0:T(8,128)(2,1)S(1)}, u32[]{:S(2)}, u32[]{:S(2)}) async-start(bf16[16,16,256]{2,1,0:T(8,128)(2,1)} %shard_map.66), calls=%async_computation.3 | async-start | bytes 262144 | tf_op jit(solution)/shard_map/all_to_all | solution.py:204
  59.3 0.0 copy-start.1
  59.3 4.1 %shard_map.65 = bf16[32,24,128]{2,1,0:T(8,128)(2,1)} custom-call(s32[1]{0:T(128)} %bitcast.chunk_ref, bf16[32,80,128]{2,1,0:T(8,128)(2,1)S(1)} %all-to-all-done.in_ref), custom_call_target="tpu_custom_call" | custom-call | flops 4000000000 | bytes 2000000 | tf_op jit(solution)/shard_map/pallas_call | solution.py:206
  63.3 0.6 all-to-all-done.3.merid_ref
  63.9 5.9 %all-to-all-start.1 = ((bf16[32,24,128]{2,1,0:T(8,128)(2,1)}), bf16[32,24,128]{2,1,0:T(8,128)(2,1)S(1)}, u32[]{:S(2)}, u32[]{:S(2)}) async-start(bf16[32,24,128]{2,1,0:T(8,128)(2,1)} %shard_map.65), calls=%async_computation.1 | async-start | bytes 393216 | tf_op jit(solution)/shard_map/all_to_all | solution.py:212
  69.8 0.0 copy-done.1
  69.8 4.0 %collective-permute-start.2 = (bf16[4,8,512]{2,1,0:T(8,128)(2,1)S(1)}, bf16[4,8,512]{2,1,0:T(8,128)(2,1)S(1)}, u32[]{:S(2)}, u32[]{:S(2)}) collective-permute-start(bf16[4,8,512]{2,1,0:T(8,128)(2,1)S(1)} %get-tuple-element.16), channel_id=1, source_target_pairs={{0,1},{1,2},{2,3},{3,4},{4,5},{5,6},{6,7},{7,8},{8,9},{9,10},{10,1... | collective-permute-start | bytes 98312 | tf_op jit(solution)/shard_map/ppermute | solution.py:215
  73.8 5.5 %collective-permute-start.3 = (bf16[4,8,512]{2,1,0:T(8,128)(2,1)S(1)}, bf16[4,8,512]{2,1,0:T(8,128)(2,1)S(1)}, u32[]{:S(2)}, u32[]{:S(2)}) collective-permute-start(bf16[4,8,512]{2,1,0:T(8,128)(2,1)S(1)} %get-tuple-element.15), channel_id=1, source_target_pairs={{1,0},{2,1},{3,2},{4,3},{5,4},{6,5},{7,6},{8,7},{9,8},{10,9},{11,1... | collective-permute-start | bytes 98312 | tf_op jit(solution)/shard_map/ppermute | solution.py:216
  79.3 1.9 %collective-permute-start = (bf16[16,256]{1,0:T(8,128)(2,1)S(1)}, bf16[16,256]{1,0:T(8,128)(2,1)S(1)}, u32[]{:S(2)}, u32[]{:S(2)}) collective-permute-start(bf16[16,256]{1,0:T(8,128)(2,1)S(1)} %get-tuple-element.18), channel_id=1, source_target_pairs={{0,1},{1,2},{2,3},{3,4},{4,5},{5,6},{6,7},{7,8},{8,9},{9,10},{10,1... | collective-permute-start | bytes 24584 | tf_op jit(solution)/shard_map/ppermute | solution.py:213
  81.3 0.0 copy-start.3
  81.3 0.0 copy-start.4
  81.3 7.7 %collective-permute-start.1 = (bf16[16,256]{1,0:T(8,128)(2,1)S(1)}, bf16[16,256]{1,0:T(8,128)(2,1)S(1)}, u32[]{:S(2)}, u32[]{:S(2)}) collective-permute-start(bf16[16,256]{1,0:T(8,128)(2,1)S(1)} %get-tuple-element.17), channel_id=1, source_target_pairs={{1,0},{2,1},{3,2},{4,3},{5,4},{6,5},{7,6},{8,7},{9,8},{10,9},{11,1... | collective-permute-start | bytes 24584 | tf_op jit(solution)/shard_map/ppermute | solution.py:214
  89.0 0.0 collective-permute-done.2.fl_ref
  89.0 0.0 collective-permute-done.3.fr_ref
  89.0 0.0 collective-permute-done.ml_ref
  89.0 0.7 collective-permute-done.1.mr_ref
  89.8 0.0 all-to-all-done.1.zonal_ref
  89.8 0.0 copy-start.5
  89.8 1.0 copy-done.5
  90.8 0.0 copy-start.8
  90.8 1.3 %shard_map.67 = (bf16[4,80,512]{2,1,0:T(8,128)(2,1)S(1)}, bf16[3,80,512]{2,1,0:T(8,128)(2,1)S(1)}, bf16[3,80,512]{2,1,0:T(8,128)(2,1)S(1)}) custom-call(bf16[32,24,128]{2,1,0:T(8,128)(2,1)S(1)} %all-to-all-done.1.zonal_ref, bf16[16,16,256]{2,1,0:T(8,128)(2,1)S(1)} %all-to-all-done.3.merid_ref, bf16[16,256]{1,0:T(8,128)(2,1)S(1)} %collective-permute-done.ml_ref, ...), custom_call_target="tpu_custom_call" | custom-call | flops 800000000 | bytes 2000000 | tf_op jit(solution)/shard_map/pallas_call | solution.py:217
  92.1 0.0 copy-start.6
  92.2 0.7 copy-done.6
  92.9 6.0 %collective-permute-start.4 = (bf16[3,80,512]{2,1,0:T(8,128)(2,1)S(1)}, bf16[3,80,512]{2,1,0:T(8,128)(2,1)S(1)}, u32[]{:S(2)}, u32[]{:S(2)}) collective-permute-start(bf16[3,80,512]{2,1,0:T(8,128)(2,1)S(1)} %get-tuple-element.13), channel_id=1, source_target_pairs={{0,32},{32,64},{64,96},{96,128},{128,160},{160,192},{192,224},{224... | collective-permute-start | bytes 737288 | tf_op jit(solution)/shard_map/ppermute | solution.py:220
  98.9 1.9 %collective-permute-start.5 = (bf16[3,80,512]{2,1,0:T(8,128)(2,1)S(1)}, bf16[3,80,512]{2,1,0:T(8,128)(2,1)S(1)}, u32[]{:S(2)}, u32[]{:S(2)}) collective-permute-start(bf16[3,80,512]{2,1,0:T(8,128)(2,1)S(1)} %get-tuple-element.14), channel_id=1, source_target_pairs={{32,0},{64,32},{96,64},{128,96},{160,128},{192,160},{224,192},{256... | collective-permute-start | bytes 737288 | tf_op jit(solution)/shard_map/ppermute | solution.py:221
  100.8 0.0 copy-done.8
  100.8 1.2 %collective-permute-done.4.before_ref = bf16[3,80,512]{2,1,0:T(8,128)(2,1)S(1)} collective-permute-done((bf16[3,80,512]{2,1,0:T(8,128)(2,1)S(1)}, bf16[3,80,512]{2,1,0:T(8,128)(2,1)S(1)}, u32[]{:S(2)}, u32[]{:S(2)}) %collective-permute-start.4) | collective-permute-done | bytes 245792 | tf_op jit(solution)/shard_map/ppermute | solution.py:220
  102.0 6.5 %collective-permute-done.5.after_ref = bf16[3,80,512]{2,1,0:T(8,128)(2,1)S(1)} collective-permute-done((bf16[3,80,512]{2,1,0:T(8,128)(2,1)S(1)}, bf16[3,80,512]{2,1,0:T(8,128)(2,1)S(1)}, u32[]{:S(2)}, u32[]{:S(2)}) %collective-permute-start.5) | collective-permute-done | bytes 245792 | tf_op jit(solution)/shard_map/ppermute | solution.py:221
  108.5 0.0 copy-done.3
  108.5 0.0 copy-done.4
  108.5 0.0 copy-start.7
  108.5 1.0 copy-done.7
  109.5 3.9 %shard_map.68 = bf16[4,64,512]{2,1,0:T(8,128)(2,1)} custom-call(bf16[4,80,512]{2,1,0:T(8,128)(2,1)S(1)} %copy-done.7, bf16[3,80,512]{2,1,0:T(8,128)(2,1)S(1)} %collective-permute-done.4.before_ref, bf16[3,80,512]{2,1,0:T(8,128)(2,1)S(1)} %collective-permute-done.5.after_ref, f32[49,512]{1,0:T(8,128)S(1)} %reshape.11.conv_ref, ...), custom_call_target="tpu_custom_call" | custom-call | flops 2000000000 | bytes 2000000 | tf_op jit(solution)/shard_map/pallas_call | solution.py:222
  (3 shorter events, 0.0 us)
Async XLA Ops:
  0.0 0.9 copy-start
  1.0 1.3 %copy-start.2 = (bf16[512,1152]{1,0:T(8,128)(2,1)S(1)}, bf16[512,1152]{1,0:T(8,128)(2,1)}, u32[]{:S(2)}) copy-start(bf16[512,1152]{1,0:T(8,128)(2,1)} %w_ref.2) | copy-start | bytes 3538948
  19.9 33.0 %all-to-all-start = ((bf16[32,80,128]{2,1,0:T(8,128)(2,1)}), bf16[32,80,128]{2,1,0:T(8,128)(2,1)S(1)}, u32[]{:S(2)}, u32[]{:S(2)}) async-start(bf16[32,80,128]{2,1,0:T(8,128)(2,1)} %get-tuple-element.10), calls=%async_computation | async-start | bytes 1310720 | tf_op jit(solution)/shard_map/all_to_all | solution.py:202
  53.0 10.9 %all-to-all-start.3 = ((bf16[16,16,256]{2,1,0:T(8,128)(2,1)}), bf16[16,16,256]{2,1,0:T(8,128)(2,1)S(1)}, u32[]{:S(2)}, u32[]{:S(2)}) async-start(bf16[16,16,256]{2,1,0:T(8,128)(2,1)} %shard_map.66), calls=%async_computation.3 | async-start | bytes 262144 | tf_op jit(solution)/shard_map/all_to_all | solution.py:204
  59.3 10.5 %copy-start.1 = (bf16[4,64,512]{2,1,0:T(8,128)(2,1)S(1)}, bf16[4,64,512]{2,1,0:T(8,128)(2,1)}, u32[]{:S(2)}) copy-start(bf16[4,64,512]{2,1,0:T(8,128)(2,1)} %field_ref.1) | copy-start | bytes 786436
  63.9 25.9 %all-to-all-start.1 = ((bf16[32,24,128]{2,1,0:T(8,128)(2,1)}), bf16[32,24,128]{2,1,0:T(8,128)(2,1)S(1)}, u32[]{:S(2)}, u32[]{:S(2)}) async-start(bf16[32,24,128]{2,1,0:T(8,128)(2,1)} %shard_map.65), calls=%async_computation.1 | async-start | bytes 393216 | tf_op jit(solution)/shard_map/all_to_all | solution.py:212
  69.8 19.2 %collective-permute-start.2 = (bf16[4,8,512]{2,1,0:T(8,128)(2,1)S(1)}, bf16[4,8,512]{2,1,0:T(8,128)(2,1)S(1)}, u32[]{:S(2)}, u32[]{:S(2)}) collective-permute-start(bf16[4,8,512]{2,1,0:T(8,128)(2,1)S(1)} %get-tuple-element.16), channel_id=1, source_target_pairs={{0,1},{1,2},{2,3},{3,4},{4,5},{5,6},{6,7},{7,8},{8,9},{9,10},{10,1... | collective-permute-start | bytes 98312 | tf_op jit(solution)/shard_map/ppermute | solution.py:215
  73.8 15.2 %collective-permute-start.3 = (bf16[4,8,512]{2,1,0:T(8,128)(2,1)S(1)}, bf16[4,8,512]{2,1,0:T(8,128)(2,1)S(1)}, u32[]{:S(2)}, u32[]{:S(2)}) collective-permute-start(bf16[4,8,512]{2,1,0:T(8,128)(2,1)S(1)} %get-tuple-element.15), channel_id=1, source_target_pairs={{1,0},{2,1},{3,2},{4,3},{5,4},{6,5},{7,6},{8,7},{9,8},{10,9},{11,1... | collective-permute-start | bytes 98312 | tf_op jit(solution)/shard_map/ppermute | solution.py:216
  79.3 9.7 %collective-permute-start = (bf16[16,256]{1,0:T(8,128)(2,1)S(1)}, bf16[16,256]{1,0:T(8,128)(2,1)S(1)}, u32[]{:S(2)}, u32[]{:S(2)}) collective-permute-start(bf16[16,256]{1,0:T(8,128)(2,1)S(1)} %get-tuple-element.18), channel_id=1, source_target_pairs={{0,1},{1,2},{2,3},{3,4},{4,5},{5,6},{6,7},{7,8},{8,9},{9,10},{10,1... | collective-permute-start | bytes 24584 | tf_op jit(solution)/shard_map/ppermute | solution.py:213
  81.3 27.2 %copy-start.3 = (bf16[512,1024]{1,0:T(8,128)(2,1)S(1)}, bf16[512,1024]{1,0:T(8,128)(2,1)}, u32[]{:S(2)}) copy-start(bf16[512,1024]{1,0:T(8,128)(2,1)} %w_in_ref.1) | copy-start | bytes 3145732
  81.3 27.2 %copy-start.4 = (bf16[1024,512]{1,0:T(8,128)(2,1)S(1)}, bf16[1024,512]{1,0:T(8,128)(2,1)}, u32[]{:S(2)}) copy-start(bf16[1024,512]{1,0:T(8,128)(2,1)} %w_back_ref.1) | copy-start | bytes 3145732
  81.3 8.5 %collective-permute-start.1 = (bf16[16,256]{1,0:T(8,128)(2,1)S(1)}, bf16[16,256]{1,0:T(8,128)(2,1)S(1)}, u32[]{:S(2)}, u32[]{:S(2)}) collective-permute-start(bf16[16,256]{1,0:T(8,128)(2,1)S(1)} %get-tuple-element.17), channel_id=1, source_target_pairs={{1,0},{2,1},{3,2},{4,3},{5,4},{6,5},{7,6},{8,7},{9,8},{10,9},{11,1... | collective-permute-start | bytes 24584 | tf_op jit(solution)/shard_map/ppermute | solution.py:214
  89.8 1.0 copy-start.5
  90.8 10.0 %copy-start.8 = (f32[7,7,512]{2,1,0:T(8,128)S(1)}, f32[7,7,512]{2,1,0:T(8,128)}, u32[]{:S(2)}) copy-start(f32[7,7,512]{2,1,0:T(8,128)} %param.9) | copy-start | bytes 301060
  92.1 0.7 copy-start.6
  92.9 9.1 %collective-permute-start.4 = (bf16[3,80,512]{2,1,0:T(8,128)(2,1)S(1)}, bf16[3,80,512]{2,1,0:T(8,128)(2,1)S(1)}, u32[]{:S(2)}, u32[]{:S(2)}) collective-permute-start(bf16[3,80,512]{2,1,0:T(8,128)(2,1)S(1)} %get-tuple-element.13), channel_id=1, source_target_pairs={{0,32},{32,64},{64,96},{96,128},{128,160},{160,192},{192,224},{224... | collective-permute-start | bytes 737288 | tf_op jit(solution)/shard_map/ppermute | solution.py:220
  98.9 9.6 %collective-permute-start.5 = (bf16[3,80,512]{2,1,0:T(8,128)(2,1)S(1)}, bf16[3,80,512]{2,1,0:T(8,128)(2,1)S(1)}, u32[]{:S(2)}, u32[]{:S(2)}) collective-permute-start(bf16[3,80,512]{2,1,0:T(8,128)(2,1)S(1)} %get-tuple-element.14), channel_id=1, source_target_pairs={{32,0},{64,32},{96,64},{128,96},{160,128},{192,160},{224,192},{256... | collective-permute-start | bytes 737288 | tf_op jit(solution)/shard_map/ppermute | solution.py:221
  108.5 1.0 copy-start.7

commit v2 on v1

v2 whole, which is shorter than its diff:
```python
import math

import jax
import jax.numpy as jnp
from jax import lax
from jax.experimental import pallas as pl
from jax.experimental.pallas import tpu as pltpu
from jax.sharding import PartitionSpec as P

C = 512
HD = 64
LAT = 16
LON = 32
R = 4
W = 64
CELLS = R * W
E = 8
YS = 8
ZS = 4
SPAN = ZS * W
GROUPS = 8
WIDE = W + 2 * E
KEYS = SPAN + 4 * E
F32 = jnp.float32
BF = jnp.bfloat16


def iota(shape, dim):
    return lax.broadcasted_iota(jnp.int32, shape, dim)


def mm(a, b):
    return jnp.dot(a, b, preferred_element_type=F32)


def mm_nt(a, b):
    return lax.dot_general(a, b, (((1,), (1,)), ((), ())), preferred_element_type=F32)


def layer_norm(values):
    center = values - jnp.mean(values, axis=-1, keepdims=True)
    spread = jnp.mean(center * center, axis=-1, keepdims=True)
    return center * lax.rsqrt(spread + 1e-06)


def call(kernel, out_shape, flops, vmem=16, **kw):
    return pl.pallas_call(
        kernel,
        out_shape=out_shape,
        compiler_params=pltpu.CompilerParams(vmem_limit_bytes=vmem * 1024 * 1024),
        cost_estimate=pl.CostEstimate(flops=flops, bytes_accessed=2_000_000, transcendentals=0),
        **kw,
    )


def by_group(values):
    split = values.reshape(R, GROUPS, E, values.shape[-1])
    return jnp.swapaxes(split, 0, 1).reshape(GROUPS, R * E, values.shape[-1])


def project_kernel(field_ref, w_hbm, zonal_ref, query_ref, kv_ref, w_ref, sem):
    load = pltpu.make_async_copy(w_hbm, w_ref, sem)
    load.start()
    normed = layer_norm(field_ref[...].astype(F32)).astype(BF)
    load.wait()
    kv_ref[...] = by_group(mm(normed, w_ref[:, 640:1152])).astype(BF)
    query_ref[...] = by_group(mm(normed, w_ref[:, 256:512])).astype(BF)
    zonal_ref[:, :, 0:256] = mm(normed, w_ref[:, 0:256]).astype(BF).reshape(R, W, 256)
    zonal_ref[:, :, 256:384] = mm(normed, w_ref[:, 512:640]).astype(BF).reshape(R, W, 128)


def spread_kernel(in_ref, out_ref):
    kv = in_ref[:, :, 256:384].reshape(SPAN, 128)
    first = in_ref[0, :, 0:256].astype(F32)[0:E]
    last = in_ref[ZS - 1, :, 0:256].astype(F32)[W - E : W]
    edges = [first[:, 0:128], first[:, 128:256], last[:, 0:128], last[:, 128:256]]
    edges = jnp.concatenate(edges, axis=0).astype(BF)
    for y in range(YS):
        out_ref[y, 0:SPAN, :] = kv
        out_ref[y, SPAN:KEYS, :] = edges


def zonal_kernel(y_ref, own_ref, all_ref, out_ref):
    y = y_ref[0]
    kv = all_ref[:, 0:SPAN, :].reshape(YS * SPAN, 128)
    ones = iota((YS * SPAN, 128), 1) < HD
    kv_one = jnp.where(ones, jnp.ones_like(kv), kv)
    behind = all_ref[lax.rem(y + YS - 1, YS), SPAN + 2 * E : KEYS, :].astype(F32)
    ahead = all_ref[lax.rem(y + 1, YS), SPAN : SPAN + 2 * E, :].astype(F32)
    count = SPAN + 2 * E
    low = iota((count, 128), 1) < HD
    for pair in range(2):
        lanes = slice(pair * 128, pair * 128 + 128)
        rows = slice(pair * E, pair * E + E)
        q = own_ref[:, :, lanes].astype(F32).reshape(SPAN, 128)
        q = jnp.concatenate([behind[rows], q, ahead[rows]], axis=0) * (1.0 / math.sqrt(HD))
        outs = []
        for head in range(2):
            placed = q if head == 0 else pltpu.roll(q, HD, 1)
            placed = jnp.where(low, placed, 0.0).astype(BF)
            score = mm_nt(placed, kv)
            weight = jnp.exp(score - jnp.max(score, axis=-1, keepdims=True)).astype(BF)
            outs.append(mm(weight, kv_one))
        even, odd = outs
        blended = jnp.where(low, pltpu.roll(even, HD, 1), odd)
        mass = jnp.where(low, even, pltpu.roll(odd, HD, 1))
        heads = blended / mass
        for z in range(ZS):
            out_ref[z, :, lanes] = heads[z * W : z * W + WIDE].astype(BF)


def merid_kernel(query_ref, kv_ref, field_ref, out_ref, edge_ref):
    step = pl.program_id(0)
    rows, keys = R * E, LAT * R * E
    t, s = iota((2 * rows, keys), 0), iota((2 * rows, keys), 1)
    bias = jnp.where(t % E == s % E, 0.0, -1e30)
    low = iota((rows, 128), 1) < HD
    scale = 1.0 / math.sqrt(HD)
    for group in range(2):
        for pair in range(2):
            lanes = slice(pair * 128, pair * 128 + 128)
            q = query_ref[group, :, lanes].astype(F32) * scale
            q = jnp.concatenate([jnp.where(low, q, 0.0), jnp.where(low, 0.0, q)], axis=0).astype(BF)
            k = kv_ref[:, group, :, pair * 128 : pair * 128 + 128].reshape(keys, 128)
            v = kv_ref[:, group, :, 256 + pair * 128 : 384 + pair * 128].reshape(keys, 128)
            score = mm_nt(q, k) + bias
            weight = jnp.exp(score - jnp.max(score, axis=-1, keepdims=True))
            mass = jnp.sum(weight, axis=-1, keepdims=True)
            both = mm(weight.astype(BF), v) / mass
            out_ref[group, :, lanes] = jnp.where(low, both[0:rows], both[rows:]).astype(BF)

    @pl.when(step == 0)
    def first():
        edge_ref[0, :, 0:256] = out_ref[0]
        edge_ref[0, :, 256:768] = field_ref[...].astype(F32)[:, 0:E].reshape(rows, C).astype(BF)

    @pl.when(step == GROUPS // 2 - 1)
    def last():
        edge_ref[1, :, 0:256] = out_ref[1]
        edge_ref[1, :, 256:768] = field_ref[...].astype(F32)[:, W - E :].reshape(rows, C).astype(BF)


def widened(left, own, right):
    left, right = (a.astype(F32).reshape(R, E, a.shape[-1]) for a in (left, right))
    return jnp.concatenate([left, own, right], axis=1)


def mix_kernel(zonal_ref, merid_ref, el_ref, er_ref, field_ref, w_ref, mixed_ref, up_ref, down_ref):
    own = merid_ref[...].astype(F32).reshape(GROUPS, R, E, 256)
    own = jnp.swapaxes(own, 0, 1).reshape(R, W, 256)
    merid = widened(el_ref[:, 0:256], own, er_ref[:, 0:256]).astype(BF)
    wide = widened(el_ref[:, 256:768], field_ref[...].astype(F32), er_ref[:, 256:768])
    attended = mm(zonal_ref[...].reshape(R * WIDE, 256), w_ref[0:256])
    attended = attended + mm(merid.reshape(R * WIDE, 256), w_ref[256:512])
    mixed = (wide + attended.reshape(R, WIDE, C)).astype(BF)
    mixed_ref[...] = mixed
    up_ref[...] = mixed[0:3]
    down_ref[...] = mixed[1:4]


def block_kernel(mixed_ref, before_ref, after_ref, conv_ref, w_in_ref, w_back_ref, out_ref, conv_out):
    for lane in range(0, C, 128):
        rows = [before_ref[i, :, lane : lane + 128].astype(F32) for i in range(3)]
        rows += [mixed_ref[i, :, lane : lane + 128].astype(F32) for i in range(R)]
        rows += [after_ref[i, :, lane : lane + 128].astype(F32) for i in range(3)]
        for r in range(R):
            total = None
            for b in range(7):
                part = None
                for a in range(7):
                    term = rows[r + a] * conv_ref[a * 7 + b, lane : lane + 128][None, :]
                    part = term if part is None else part + term
                moved = part[b + 5 : b + 5 + W]
                total = moved if total is None else total + moved
            conv_out[r * W : (r + 1) * W, lane : lane + 128] = total
    normed = layer_norm(conv_out[...]).astype(BF)
    hidden = mm(normed, w_in_ref[...])
    hidden = 0.5 * hidden * (1.0 + lax.erf(hidden * math.sqrt(0.5)))
    back = mm(hidden.astype(BF), w_back_ref[...])
    own = mixed_ref[...].astype(F32)[:, 8 : 8 + W].reshape(CELLS, C)
    out_ref[...] = (own + back).astype(BF).reshape(R, W, C)


def shape(*dims):
    return jax.ShapeDtypeStruct(dims, BF)


def per_device(field, w_qkv, w_out, conv_w, w_in, w_back):
    right = [(i, (i + 1) % LON) for i in range(LON)]
    left = [(j, i) for i, j in right]
    down = [(i, i + 1) for i in range(LAT - 1)]
    up = [(j, i) for i, j in down]
    along_y = [[y * ZS + z for y in range(YS)] for z in range(ZS)]
    along_z = [[y * ZS + z for z in range(ZS)] for y in range(YS)]
    vmem = pl.BlockSpec(memory_space=pltpu.VMEM)
    zonal_in, query, kv = call(
        project_kernel,
        (shape(R, W, 384), shape(GROUPS, R * E, 256), shape(GROUPS, R * E, 512)),
        400_000_000,
        in_specs=[vmem, pl.BlockSpec(memory_space=pl.ANY)],
        scratch_shapes=[pltpu.VMEM((C, 1152), BF), pltpu.SemaphoreType.DMA],
    )(field.reshape(CELLS, C), w_qkv)
    kv_all = lax.all_gather(kv, "lat")
    row = lax.all_to_all(zonal_in, "lon", 0, 0, axis_index_groups=along_z)
    slots = call(spread_kernel, shape(YS, KEYS, 128), 10_000_000)(row)
    slots = lax.all_to_all(slots, "lon", 0, 0, axis_index_groups=along_y)
    y = (lax.axis_index("lon") // ZS).astype(jnp.int32).reshape(1)
    zonal_out = call(
        zonal_kernel,
        shape(ZS, WIDE, 256),
        4_000_000_000,
        vmem=24,
        in_specs=[pl.BlockSpec(memory_space=pltpu.SMEM), vmem, vmem],
    )(y, row, slots)
    zonal = lax.all_to_all(zonal_out, "lon", 0, 0, axis_index_groups=along_z)
    kv_all = lax.optimization_barrier((kv_all, zonal_out))[0]
    merid, edges = call(
        merid_kernel,
        (shape(GROUPS, R * E, 256), shape(2, R * E, 768)),
        1_000_000_000,
        grid=(GROUPS // 2,),
        in_specs=[
            pl.BlockSpec((2, R * E, 256), lambda i: (i, 0, 0)),
            pl.BlockSpec((LAT, 2, R * E, 512), lambda i: (0, i, 0, 0)),
            pl.BlockSpec((R, W, C), lambda i: (0, 0, 0)),
        ],
        out_specs=[
            pl.BlockSpec((2, R * E, 256), lambda i: (i, 0, 0)),
            pl.BlockSpec((2, R * E, 768), lambda i: (0, 0, 0)),
        ],
    )(query, kv_all, field)
    edge_left = lax.ppermute(edges[1], "lon", right)
    edge_right = lax.ppermute(edges[0], "lon", left)
    mixed, first, last = call(
        mix_kernel, (shape(R, WIDE, C), shape(3, WIDE, C), shape(3, WIDE, C)), 400_000_000
    )(zonal, merid, edge_left, edge_right, field, w_out)
    before = lax.ppermute(last, "lat", down)
    after = lax.ppermute(first, "lat", up)
    return call(
        block_kernel,
        shape(R, W, C),
        2_000_000_000,
        scratch_shapes=[pltpu.VMEM((CELLS, C), F32)],
    )(mixed, before, after, conv_w.reshape(49, C), w_in, w_back)


def solution(mesh):
    return jax.shard_map(
        per_device,
        mesh=mesh,
        in_specs=(P("lat", "lon", None), P(), P(), P(), P(), P()),
        out_specs=P("lat", "lon", None),
        check_vma=False,
    )
```

time: 114 us -> 111 us (0.974)
  starting transfers between devices: 52.1 us -> 30.3 us
  between operations: 0.19 us -> 13.5 us
  Pallas kernels: 12.3 us -> 15.5 us
  local copies, waits for them, and re-layouts: 5.01 us -> 7.18 us
  waiting for transfers between devices: 27.7 us -> 25.7 us
  blocking collectives: 16.1 us -> 17.8 us
    all_to_all x3 -> x2, starting transfers between devices: 25 us -> 13 us  [the longest x1 6.82 us: per_device(): slots = lax.all_to_all(slots, 'lon', 0, 0, axis_index_groups=along_y)]
    ppermute x4 -> x2, starting transfers between devices: 19.1 us -> 9.5 us  [the longest x1 5.23 us: per_device(): edge_right = lax.ppermute(edges[0], 'lon', left)]
    pallas_call x3 -> x4, Pallas kernels: 7.14 us -> 11.3 us  [the longest x1 4.9 us: per_device(): call(merid_kernel, (shape(GROUPS, R * E, 256), shape(2, R * E, 768)), 100...]
    all_to_all x3 -> x2, waiting for transfers between devices: 19.3 us -> 16.3 us  [the longest x1 16.3 us: per_device(): slots = lax.all_to_all(slots, 'lon', 0, 0, axis_index_groups=along_y)]
    unnamed x18 -> x20, local copies, waits for them, and re-layouts: 4.98 us -> 7.16 us
    all_to_all x1, blocking collectives: 16.1 us -> 17.8 us  [per_device(): row = lax.all_to_all(zonal_in, 'lon', 0, 0, axis_index_groups=along_z)]
  transfers between devices with their start and end apart: 9 -> 7, of which waited for: 5 -> 4; matrix products, arithmetic and copies ran while one was open for 0% -> 0% of each run, Pallas kernels for 5% -> 9%
where the time goes in v2:
time: 111 us; the launch traced here: 110 us
  starting transfers between devices  30.3 us (27%)
  waiting for transfers between devices  25.7 us (23%)
  blocking collectives  17.8 us (16%)
  Pallas kernels  15.5 us (14%)
  between operations  13.5 us (12%)
  local copies, waits for them, and re-layouts  7.18 us (6%)
    all_to_all x1, blocking collectives, per_device(): row = lax.all_to_all(zonal_in, 'lon', 0, 0, axis_index_groups=along_z)  17.8 us
    all_to_all x1, waiting for transfers between devices, per_device(): slots = lax.all_to_all(slots, 'lon', 0, 0, axis_index_groups=along_y)  16.3 us
    unnamed x20, local copies, waits for them, and re-layouts  7.16 us
    all_to_all x1, starting transfers between devices, per_device(): slots = lax.all_to_all(slots, 'lon', 0, 0, axis_index_groups=along_y)  6.82 us
    ppermute x1, waiting for transfers between devices, per_device(): after = lax.ppermute(first, 'lat', up)  6.51 us
    all_to_all x1, starting transfers between devices, per_device(): zonal = lax.all_to_all(zonal_out, 'lon', 0, 0, axis_index_groups=along_z)  6.17 us
    ppermute x1, starting transfers between devices, per_device(): before = lax.ppermute(last, 'lat', down)  5.93 us
    ppermute x1, starting transfers between devices, per_device(): edge_right = lax.ppermute(edges[0], 'lon', left)  5.23 us
  transfers between devices with their start and end apart: 7, of which 4 were waited for; matrix products, arithmetic and copies ran while one was open for 0% of the time, Pallas kernels for 9%

profile of v2, /device:TPU:7, one launch (start us, length us, event | category | flops | bytes accessed | tf_op | source)
XLA Modules:
  0.0 110.0 jit_solution(17642253805630318686)
XLA Ops:
  6.5 0.0 all-gather.3.cloned.1.call-start
  6.5 0.0 copy-start.1
  6.5 0.9 copy-done.1
  7.5 0.0 copy-start.3
  7.5 1.3 %copy-done.3 = bf16[512,1152]{1,0:T(8,128)(2,1)S(1)} copy-done((bf16[512,1152]{1,0:T(8,128)(2,1)S(1)}, bf16[512,1152]{1,0:T(8,128)(2,1)}, u32[]{:S(2)}) %copy-start.3) | copy-done | bytes 1179672
  8.8 1.5 %shard_map.64 = (bf16[4,64,384]{2,1,0:T(8,128)(2,1)S(1)}, bf16[8,32,256]{2,1,0:T(8,128)(2,1)S(1)}, bf16[8,32,512]{2,1,0:T(8,128)(2,1)}) custom-call(bf16[256,512]{1,0:T(8,128)(2,1)S(1)} %bitcast.8, bf16[512,1152]{1,0:T(8,128)(2,1)S(1)} %copy-done.3), custom_call_target="tpu_custom_call" | custom-call | flops 400000000 | bytes 2000000 | tf_op jit(solution)/shard_map/pallas_call | solution.py:196
  10.3 0.0 all-gather.3.cloned.1.call-update
  10.3 17.8 %all_to_all.15.in_ref.own_ref = bf16[4,64,384]{2,1,0:T(8,128)(2,1)S(1)} all-to-all(bf16[4,64,384]{2,1,0:T(8,128)(2,1)S(1)} %get-tuple-element.14), channel_id=1, replica_groups={{0,1,2,3},{4,5,6,7},{8,9,10,11},{12,13,14,15},{16,17,18,19},{20,21,22,2..., dimensions={0} | all-to-all | bytes 393216 | tf_op jit(solution)/shard_map/all_to_all | solution.py:204
  28.1 0.9 shard_map.65
  29.0 6.8 %all-to-all-start.1 = ((bf16[8,288,128]{2,1,0:T(8,128)(2,1)}), bf16[8,288,128]{2,1,0:T(8,128)(2,1)S(1)}, u32[]{:S(2)}, u32[]{:S(2)}) async-start(bf16[8,288,128]{2,1,0:T(8,128)(2,1)} %shard_map.65), calls=%async_computation.1 | async-start | bytes 1179648 | tf_op jit(solution)/shard_map/all_to_all | solution.py:206
  35.8 16.3 %all-to-all-done.1.all_ref = bf16[8,288,128]{2,1,0:T(8,128)(2,1)S(1)} async-done(((bf16[8,288,128]{2,1,0:T(8,128)(2,1)}), bf16[8,288,128]{2,1,0:T(8,128)(2,1)S(1)}, u32[]{:S(2)}, u32[]{:S(2)}) %all-to-all-start.1) | async-done | bytes 589856 | tf_op jit(solution)/shard_map/all_to_all | solution.py:206
  52.1 0.0 copy-start.2
  52.1 0.0 copy-start.4
  52.1 0.0 copy-start.5
  52.1 4.0 %shard_map.66 = bf16[4,80,256]{2,1,0:T(8,128)(2,1)} custom-call(s32[1]{0:T(128)} %bitcast.y_ref, bf16[4,64,384]{2,1,0:T(8,128)(2,1)S(1)} %all_to_all.15.in_ref.own_ref, bf16[8,288,128]{2,1,0:T(8,128)(2,1)S(1)} %all-to-all-done.1.all_ref), custom_call_target="tpu_custom_call" | custom-call | flops 4000000000 | bytes 2000000 | tf_op jit(solution)/shard_map/pallas_call | solution.py:208
  56.1 0.0 copy-start.9
  56.1 6.2 %all-to-all-start.2 = ((bf16[4,80,256]{2,1,0:T(8,128)(2,1)}), bf16[4,80,256]{2,1,0:T(8,128)(2,1)S(1)}, u32[]{:S(2)}, u32[]{:S(2)}) async-start(bf16[4,80,256]{2,1,0:T(8,128)(2,1)} %shard_map.66), calls=%async_computation.2 | async-start | bytes 327680 | tf_op jit(solution)/shard_map/all_to_all | solution.py:215
  62.3 0.0 all-gather.3.cloned.1.call-done
  62.3 0.0 copy-done.2
  62.3 0.0 copy-start
  62.3 2.2 %copy-done = bf16[128,32,512]{2,1,0:T(8,128)(2,1)S(1)} copy-done((bf16[128,32,512]{2,1,0:T(8,128)(2,1)S(1)}, bf16[128,32,512]{2,1,0:T(8,128)(2,1)}, u32[]{:S(2)}) %copy-start) | copy-done | bytes 4194328
  64.5 4.9 %shard_map.67 = (bf16[8,32,256]{2,1,0:T(8,128)(2,1)S(1)}, bf16[2,32,768]{2,1,0:T(8,128)(2,1)S(1)}) custom-call(bf16[8,32,256]{2,1,0:T(8,128)(2,1)S(1)} %get-tuple-element.15.query_ref, bf16[16,8,32,512]{3,2,1,0:T(8,128)(2,1)S(1)} %bitcast.7, bf16[4,64,512]{2,1,0:T(8,128)(2,1)S(1)} %copy-done.2), custom_call_target="tpu_custom_call" | custom-call | flops 1000000000 | bytes 2000000 | tf_op jit(solution)/shard_map/pallas_call | solution.py:217
  69.4 4.3 %collective-permute-start = (bf16[32,768]{1,0:T(8,128)(2,1)S(1)}, bf16[32,768]{1,0:T(8,128)(2,1)S(1)}, u32[]{:S(2)}, u32[]{:S(2)}) collective-permute-start(bf16[32,768]{1,0:T(8,128)(2,1)S(1)} %get-tuple-element.24), channel_id=1, source_target_pairs={{0,1},{1,2},{2,3},{3,4},{4,5},{5,6},{6,7},{7,8},{8,9},{9,10},{10,1... | collective-permute-start | bytes 147464 | tf_op jit(solution)/shard_map/ppermute | solution.py:232
  73.7 5.2 %collective-permute-start.1 = (bf16[32,768]{1,0:T(8,128)(2,1)S(1)}, bf16[32,768]{1,0:T(8,128)(2,1)S(1)}, u32[]{:S(2)}, u32[]{:S(2)}) collective-permute-start(bf16[32,768]{1,0:T(8,128)(2,1)S(1)} %get-tuple-element.23), channel_id=1, source_target_pairs={{1,0},{2,1},{3,2},{4,3},{5,4},{6,5},{7,6},{8,7},{9,8},{10,9},{11,1... | collective-permute-start | bytes 147464 | tf_op jit(solution)/shard_map/ppermute | solution.py:233
  78.9 0.0 all-to-all-done.2.zonal_ref
  78.9 0.0 collective-permute-done.el_ref
  79.0 1.7 %collective-permute-done.1.er_ref = bf16[32,768]{1,0:T(8,128)(2,1)S(1)} collective-permute-done((bf16[32,768]{1,0:T(8,128)(2,1)S(1)}, bf16[32,768]{1,0:T(8,128)(2,1)S(1)}, u32[]{:S(2)}, u32[]{:S(2)}) %collective-permute-start.1) | collective-permute-done | bytes 49184 | tf_op jit(solution)/shard_map/ppermute | solution.py:233
  80.7 0.0 copy-start.6
  80.7 1.0 copy-done.6
  81.7 0.3 shard_map.68
  82.0 0.0 copy-start.7
  82.1 0.7 copy-done.7
  82.8 5.9 %collective-permute-start.2 = (bf16[3,80,512]{2,1,0:T(8,128)(2,1)S(1)}, bf16[3,80,512]{2,1,0:T(8,128)(2,1)S(1)}, u32[]{:S(2)}, u32[]{:S(2)}) collective-permute-start(bf16[3,80,512]{2,1,0:T(8,128)(2,1)S(1)} %get-tuple-element.21), channel_id=1, source_target_pairs={{0,32},{32,64},{64,96},{96,128},{128,160},{160,192},{192,224},{224... | collective-permute-start | bytes 737288 | tf_op jit(solution)/shard_map/ppermute | solution.py:237
  88.7 1.9 %collective-permute-start.3 = (bf16[3,80,512]{2,1,0:T(8,128)(2,1)S(1)}, bf16[3,80,512]{2,1,0:T(8,128)(2,1)S(1)}, u32[]{:S(2)}, u32[]{:S(2)}) collective-permute-start(bf16[3,80,512]{2,1,0:T(8,128)(2,1)S(1)} %get-tuple-element.22), channel_id=1, source_target_pairs={{32,0},{64,32},{96,64},{128,96},{160,128},{192,160},{224,192},{256... | collective-permute-start | bytes 737288 | tf_op jit(solution)/shard_map/ppermute | solution.py:238
  90.6 0.0 copy-done.9
  90.7 1.2 %collective-permute-done.2.before_ref = bf16[3,80,512]{2,1,0:T(8,128)(2,1)S(1)} collective-permute-done((bf16[3,80,512]{2,1,0:T(8,128)(2,1)S(1)}, bf16[3,80,512]{2,1,0:T(8,128)(2,1)S(1)}, u32[]{:S(2)}, u32[]{:S(2)}) %collective-permute-start.2) | collective-permute-done | bytes 245792 | tf_op jit(solution)/shard_map/ppermute | solution.py:237
  91.8 6.5 %collective-permute-done.3.after_ref = bf16[3,80,512]{2,1,0:T(8,128)(2,1)S(1)} collective-permute-done((bf16[3,80,512]{2,1,0:T(8,128)(2,1)S(1)}, bf16[3,80,512]{2,1,0:T(8,128)(2,1)S(1)}, u32[]{:S(2)}, u32[]{:S(2)}) %collective-permute-start.3) | collective-permute-done | bytes 245792 | tf_op jit(solution)/shard_map/ppermute | solution.py:238
  98.3 0.0 copy-done.4
  98.3 0.0 copy-done.5
  98.3 0.0 copy-start.8
  98.3 1.0 copy-done.8
  99.3 3.9 %shard_map.69 = bf16[4,64,512]{2,1,0:T(8,128)(2,1)} custom-call(bf16[4,80,512]{2,1,0:T(8,128)(2,1)S(1)} %copy-done.8, bf16[3,80,512]{2,1,0:T(8,128)(2,1)S(1)} %collective-permute-done.2.before_ref, bf16[3,80,512]{2,1,0:T(8,128)(2,1)S(1)} %collective-permute-done.3.after_ref, f32[49,512]{1,0:T(8,128)S(1)} %reshape.11.conv_ref, ...), custom_call_target="tpu_custom_call" | custom-call | flops 2000000000 | bytes 2000000 | tf_op jit(solution)/shard_map/pallas_call | solution.py:239
  (2 shorter events, 0.0 us)
Async XLA Ops:
  6.5 55.8 %all-gather.3.cloned.1.call-start = ((), (), s32[]{:S(2)}) async-start(), calls=%async_computation.3 | async-start | bytes 4456448 | tf_op jit(solution)/shard_map/all_gather | solution.py:203
  6.5 0.9 copy-start.1
  7.5 1.3 %copy-start.3 = (bf16[512,1152]{1,0:T(8,128)(2,1)S(1)}, bf16[512,1152]{1,0:T(8,128)(2,1)}, u32[]{:S(2)}) copy-start(bf16[512,1152]{1,0:T(8,128)(2,1)} %w_hbm.1) | copy-start | bytes 3538948
  29.0 23.1 %all-to-all-start.1 = ((bf16[8,288,128]{2,1,0:T(8,128)(2,1)}), bf16[8,288,128]{2,1,0:T(8,128)(2,1)S(1)}, u32[]{:S(2)}, u32[]{:S(2)}) async-start(bf16[8,288,128]{2,1,0:T(8,128)(2,1)} %shard_map.65), calls=%async_computation.1 | async-start | bytes 1179648 | tf_op jit(solution)/shard_map/all_to_all | solution.py:206
  52.1 10.2 %copy-start.2 = (bf16[4,64,512]{2,1,0:T(8,128)(2,1)S(1)}, bf16[4,64,512]{2,1,0:T(8,128)(2,1)}, u32[]{:S(2)}) copy-start(bf16[4,64,512]{2,1,0:T(8,128)(2,1)} %field_ref.3) | copy-start | bytes 786436
  52.1 46.3 %copy-start.4 = (bf16[512,1024]{1,0:T(8,128)(2,1)S(1)}, bf16[512,1024]{1,0:T(8,128)(2,1)}, u32[]{:S(2)}) copy-start(bf16[512,1024]{1,0:T(8,128)(2,1)} %w_in_ref.1) | copy-start | bytes 3145732
  52.1 46.3 %copy-start.5 = (bf16[1024,512]{1,0:T(8,128)(2,1)S(1)}, bf16[1024,512]{1,0:T(8,128)(2,1)}, u32[]{:S(2)}) copy-start(bf16[1024,512]{1,0:T(8,128)(2,1)} %w_back_ref.1) | copy-start | bytes 3145732
  56.1 34.5 %copy-start.9 = (f32[7,7,512]{2,1,0:T(8,128)S(1)}, f32[7,7,512]{2,1,0:T(8,128)}, u32[]{:S(2)}) copy-start(f32[7,7,512]{2,1,0:T(8,128)} %param.9) | copy-start | bytes 301060
  56.1 22.8 %all-to-all-start.2 = ((bf16[4,80,256]{2,1,0:T(8,128)(2,1)}), bf16[4,80,256]{2,1,0:T(8,128)(2,1)S(1)}, u32[]{:S(2)}, u32[]{:S(2)}) async-start(bf16[4,80,256]{2,1,0:T(8,128)(2,1)} %shard_map.66), calls=%async_computation.2 | async-start | bytes 327680 | tf_op jit(solution)/shard_map/all_to_all | solution.py:215
  62.3 2.2 %copy-start = (bf16[128,32,512]{2,1,0:T(8,128)(2,1)S(1)}, bf16[128,32,512]{2,1,0:T(8,128)(2,1)}, u32[]{:S(2)}) copy-start(bf16[128,32,512]{2,1,0:T(8,128)(2,1)} %all-gather.3.cloned.1.call-done) | copy-start | bytes 12582916
  69.4 9.5 %collective-permute-start = (bf16[32,768]{1,0:T(8,128)(2,1)S(1)}, bf16[32,768]{1,0:T(8,128)(2,1)S(1)}, u32[]{:S(2)}, u32[]{:S(2)}) collective-permute-start(bf16[32,768]{1,0:T(8,128)(2,1)S(1)} %get-tuple-element.24), channel_id=1, source_target_pairs={{0,1},{1,2},{2,3},{3,4},{4,5},{5,6},{6,7},{7,8},{8,9},{9,10},{10,1... | collective-permute-start | bytes 147464 | tf_op jit(solution)/shard_map/ppermute | solution.py:232
  73.7 7.0 %collective-permute-start.1 = (bf16[32,768]{1,0:T(8,128)(2,1)S(1)}, bf16[32,768]{1,0:T(8,128)(2,1)S(1)}, u32[]{:S(2)}, u32[]{:S(2)}) collective-permute-start(bf16[32,768]{1,0:T(8,128)(2,1)S(1)} %get-tuple-element.23), channel_id=1, source_target_pairs={{1,0},{2,1},{3,2},{4,3},{5,4},{6,5},{7,6},{8,7},{9,8},{10,9},{11,1... | collective-permute-start | bytes 147464 | tf_op jit(solution)/shard_map/ppermute | solution.py:233
  80.7 1.0 copy-start.6
  82.0 0.7 copy-start.7
  82.8 9.1 %collective-permute-start.2 = (bf16[3,80,512]{2,1,0:T(8,128)(2,1)S(1)}, bf16[3,80,512]{2,1,0:T(8,128)(2,1)S(1)}, u32[]{:S(2)}, u32[]{:S(2)}) collective-permute-start(bf16[3,80,512]{2,1,0:T(8,128)(2,1)S(1)} %get-tuple-element.21), channel_id=1, source_target_pairs={{0,32},{32,64},{64,96},{96,128},{128,160},{160,192},{192,224},{224... | collective-permute-start | bytes 737288 | tf_op jit(solution)/shard_map/ppermute | solution.py:237
  88.7 9.6 %collective-permute-start.3 = (bf16[3,80,512]{2,1,0:T(8,128)(2,1)S(1)}, bf16[3,80,512]{2,1,0:T(8,128)(2,1)S(1)}, u32[]{:S(2)}, u32[]{:S(2)}) collective-permute-start(bf16[3,80,512]{2,1,0:T(8,128)(2,1)S(1)} %get-tuple-element.22), channel_id=1, source_target_pairs={{32,0},{64,32},{96,64},{128,96},{160,128},{192,160},{224,192},{256... | collective-permute-start | bytes 737288 | tf_op jit(solution)/shard_map/ppermute | solution.py:238
  98.3 1.0 copy-start.8
Sparse Core Ops, SparseCore 0:
  10.4 47.1 all-gather.2

commit v3 on v2

v3 whole, which is shorter than its diff:
```python
import math

import jax
import jax.numpy as jnp
from jax import lax
from jax.experimental import pallas as pl
from jax.experimental.pallas import tpu as pltpu
from jax.sharding import PartitionSpec as P

C = 512
HD = 64
LAT = 16
LON = 32
R = 4
W = 64
CELLS = R * W
E = 8
WIDE = W + 2 * E
MC = WIDE // LAT
MROWS = 24
YS = 8
ZS = 4
SPAN = ZS * W
KEYS = SPAN + 2 * E
F32 = jnp.float32
BF = jnp.bfloat16


def iota(shape, dim):
    return lax.broadcasted_iota(jnp.int32, shape, dim)


def one_hot(hit):
    return jnp.where(hit, 1.0, 0.0).astype(BF)


def mm(a, b):
    return jnp.dot(a, b, preferred_element_type=F32)


def mm_nt(a, b):
    return lax.dot_general(a, b, (((1,), (1,)), ((), ())), preferred_element_type=F32)


def layer_norm(values):
    center = values - jnp.mean(values, axis=-1, keepdims=True)
    spread = jnp.mean(center * center, axis=-1, keepdims=True)
    return center * lax.rsqrt(spread + 1e-06)


def shape(*dims):
    return jax.ShapeDtypeStruct(dims, BF)


VMEM = pl.BlockSpec(memory_space=pltpu.VMEM)
ANY = pl.BlockSpec(memory_space=pl.ANY)
SMEM = pl.BlockSpec(memory_space=pltpu.SMEM)


def call(kernel, out_shape, flops, vmem=16, **kw):
    return pl.pallas_call(
        kernel,
        out_shape=out_shape,
        compiler_params=pltpu.CompilerParams(vmem_limit_bytes=vmem * 1024 * 1024),
        cost_estimate=pl.CostEstimate(flops=flops, bytes_accessed=2_000_000, transcendentals=0),
        **kw,
    )


def in_hbm(array):
    return pltpu.with_memory_space_constraint(array, pltpu.HBM)


def zonal_project_kernel(field_hbm, w_hbm, out_ref, first_ref, last_ref, field_ref, wq_ref, wkv_ref, sems):
    loads = [
        pltpu.make_async_copy(field_hbm, field_ref, sems.at[0]),
        pltpu.make_async_copy(w_hbm.at[:, 512:640], wkv_ref, sems.at[1]),
        pltpu.make_async_copy(w_hbm.at[:, 0:256], wq_ref, sems.at[2]),
    ]
    for load in loads:
        load.start()
    loads[0].wait()
    field = field_ref[...].astype(F32)
    first_ref[...] = field[:, 0:E].reshape(R * E, C).astype(BF)
    last_ref[...] = field[:, W - E : W].reshape(R * E, C).astype(BF)
    normed = layer_norm(field.reshape(CELLS, C)).astype(BF)
    loads[1].wait()
    out_ref[:, :, 256:384] = mm(normed, wkv_ref[...]).astype(BF).reshape(R, W, 128)
    loads[2].wait()
    out_ref[:, :, 0:256] = mm(normed, wq_ref[...]).astype(BF).reshape(R, W, 256)


def spread_kernel(in_ref, out_ref):
    kv = in_ref[:, :, 256:384].reshape(SPAN, 128)
    first = in_ref[0, :, 0:256].astype(F32)[0:E]
    last = in_ref[ZS - 1, :, 0:256].astype(F32)[W - E : W]
    edge = jnp.where(iota((E, 256), 0) < E // 2, first, last)
    edge = jnp.concatenate([edge[:, 0:128], edge[:, 128:256]], axis=0).astype(BF)
    for y in range(YS):
        out_ref[y, 0:SPAN, :] = kv
        out_ref[y, SPAN:KEYS, :] = edge


def zonal_kernel(y_ref, own_ref, all_ref, out_ref):
    y = y_ref[0]
    kv = all_ref[:, 0:SPAN, :].reshape(YS * SPAN, 128)
    ones = iota((YS * SPAN, 128), 1) < HD
    kv_one = jnp.where(ones, jnp.ones_like(kv), kv)
    behind = all_ref[lax.rem(y + YS - 1, YS), SPAN:KEYS, :].astype(F32)
    ahead = all_ref[lax.rem(y + 1, YS), SPAN:KEYS, :].astype(F32)
    count = SPAN + 2 * E
    low = iota((count, 128), 1) < HD
    for pair in range(2):
        lanes = slice(pair * 128, pair * 128 + 128)
        rows = slice(pair * E, pair * E + E)
        q = own_ref[:, :, lanes].astype(F32).reshape(SPAN, 128)
        q = jnp.concatenate([behind[rows], q, ahead[rows]], axis=0) * (1.0 / math.sqrt(HD))
        outs = []
        for head in range(2):
            placed = q if head == 0 else pltpu.roll(q, HD, 1)
            placed = jnp.where(low, placed, 0.0).astype(BF)
            score = mm_nt(placed, kv)
            weight = jnp.exp(score - jnp.max(score, axis=-1, keepdims=True)).astype(BF)
            outs.append(mm(weight, kv_one))
        even, odd = outs
        blended = jnp.where(low, pltpu.roll(even, HD, 1), odd)
        mass = jnp.where(low, even, pltpu.roll(odd, HD, 1))
        heads = blended / mass
        for z in range(ZS):
            out_ref[z, :, lanes] = heads[z * W : z * W + WIDE].astype(BF)


def widened(left, own, right):
    left, right = (a.astype(F32).reshape(R, E, a.shape[-1]) for a in (left, right))
    return jnp.concatenate([left, own.astype(F32), right], axis=1)


def merid_slots():
    dims = (LAT, MROWS, R * WIDE)
    m, i, u = iota(dims, 0), iota(dims, 1), iota(dims, 2)
    cell = (i & 3) * WIDE + m * MC + (i >> 2)
    return one_hot((cell == u) & (i < R * MC)).reshape(LAT * MROWS, R * WIDE)


def merid_select_kernel(field_ref, left_ref, right_ref, out_ref):
    wide = widened(left_ref[...], field_ref[...], right_ref[...]).reshape(R * WIDE, C)
    normed = mm(merid_slots(), layer_norm(wide).astype(BF))
    out_ref[...] = normed.reshape(LAT, MROWS, C).astype(BF)


def merid_kernel(in_ref, w_ref, out_ref):
    count = LAT * MROWS
    normed = in_ref[...].astype(F32).reshape(count, C).astype(BF)
    queries = mm(normed, w_ref[:, 256:512]).astype(BF)
    keys = mm(normed, w_ref[:, 640:896]).astype(BF)
    values = mm(normed, w_ref[:, 896:1152]).astype(BF)
    row = iota((LAT, MROWS, count), 1).reshape(count, count) >> 2
    key = iota((count, count), 1)
    key = (key - ((key * 2731) >> 16) * MROWS) >> 2
    bias = jnp.where(row == key, 0.0, -1e30)
    low = iota((count, 128), 1) < HD
    scale = 1.0 / math.sqrt(HD)
    for pair in range(2):
        lanes = slice(pair * 128, pair * 128 + 128)
        q, k, v = queries[:, lanes], keys[:, lanes], values[:, lanes]
        outs = []
        for side in (low, jnp.logical_not(low)):
            score = mm_nt(jnp.where(side, q, jnp.zeros_like(q)), k) * scale + bias
            weight = jnp.exp(score - jnp.max(score, axis=-1, keepdims=True))
            mass = jnp.sum(weight, axis=-1, keepdims=True)
            outs.append(mm(weight.astype(BF), v) / mass)
        both = jnp.where(low, outs[0], outs[1]).reshape(LAT, MROWS, 128)
        out_ref[:, :, lanes] = both.astype(BF)


def mix_kernel(zonal_ref, merid_ref, left_ref, right_ref, field_ref, w_ref, mixed_ref, up_ref, down_ref):
    rows = R * WIDE
    merid = merid_ref[...].astype(F32).reshape(LAT * MROWS, 256).astype(BF)
    dims = (R, WIDE, LAT * MROWS)
    r, w, t = iota(dims, 0), iota(dims, 1), iota(dims, 2)
    m = (t * 2731) >> 16
    i = t - m * MROWS
    cell = one_hot((m * MC + (i >> 2) == w) & ((i & 3) == r) & (i < R * MC))
    merid = mm(cell.reshape(rows, LAT * MROWS), merid).astype(BF)
    attended = mm(zonal_ref[...].reshape(rows, 256), w_ref[0:256]) + mm(merid, w_ref[256:512])
    wide = widened(left_ref[...], field_ref[...], right_ref[...])
    mixed = (wide + attended.reshape(R, WIDE, C)).astype(BF)
    mixed_ref[...] = mixed
    up_ref[...] = mixed[0:3]
    down_ref[...] = mixed[1:4]


def block_kernel(
    mixed_hbm, before_ref, after_ref, conv_ref, w_in_hbm, w_back_hbm, out_ref,
    mixed_ref, w_in_ref, w_back_ref, conv_out, sems,
):
    pairs = ((mixed_hbm, mixed_ref), (w_in_hbm, w_in_ref), (w_back_hbm, w_back_ref))
    loads = [pltpu.make_async_copy(a, b, sems.at[i]) for i, (a, b) in enumerate(pairs)]
    for load in loads:
        load.start()
    for part in range(2):
        if part == 1:
            loads[0].wait()
        for lane in range(0, C, 128):
            lanes = slice(lane, lane + 128)
            if part == 0:
                rows = {i: before_ref[i, :, lanes].astype(F32) for i in range(3)}
                rows.update({7 + i: after_ref[i, :, lanes].astype(F32) for i in range(3)})
            else:
                rows = {3 + i: mixed_ref[i, :, lanes].astype(F32) for i in range(R)}
            for r in range(R):
                total = None
                for b in range(7):
                    column = None
                    for a in range(7):
                        if r + a in rows:
                            term = rows[r + a] * conv_ref[a * 7 + b, lanes][None, :]
                            column = term if column is None else column + term
                    moved = column[b + 5 : b + 5 + W]
                    total = moved if total is None else total + moved
                here = (slice(r * W, (r + 1) * W), lanes)
                conv_out[here] = total if part == 0 else conv_out[here] + total
    normed = layer_norm(conv_out[...]).astype(BF)
    loads[1].wait()
    hidden = mm(normed, w_in_ref[...])
    hidden = 0.5 * hidden * (1.0 + lax.erf(hidden * math.sqrt(0.5)))
    loads[2].wait()
    back = mm(hidden.astype(BF), w_back_ref[...])
    own = mixed_ref[...].astype(F32)[:, E : E + W].reshape(CELLS, C)
    out_ref[...] = (own + back).astype(BF).reshape(R, W, C)


def per_device(field, w_qkv, w_out, conv_w, w_in, w_back):
    right = [(i, (i + 1) % LON) for i in range(LON)]
    left = [(j, i) for i, j in right]
    down = [(i, i + 1) for i in range(LAT - 1)]
    up = [(j, i) for i, j in down]
    along_y = [[y * ZS + z for y in range(YS)] for z in range(ZS)]
    along_z = [[y * ZS + z for z in range(ZS)] for y in range(YS)]
    row, first, last = call(
        zonal_project_kernel,
        (shape(R, W, 384), shape(R * E, C), shape(R * E, C)),
        200_000_000,
        in_specs=[ANY, ANY],
        scratch_shapes=[
            pltpu.VMEM((R, W, C), BF),
            pltpu.VMEM((C, 256), BF),
            pltpu.VMEM((C, 128), BF),
            pltpu.SemaphoreType.DMA((3,)),
        ],
    )(in_hbm(field), in_hbm(w_qkv))
    row = lax.all_to_all(row, "lon", 0, 0, axis_index_groups=along_z)
    slots = call(spread_kernel, shape(YS, KEYS, 128), 10_000_000)(row)
    slots = lax.all_to_all(slots, "lon", 0, 0, axis_index_groups=along_y)
    field_left = lax.ppermute(last, "lon", right)
    field_right = lax.ppermute(first, "lon", left)
    merid = call(merid_select_kernel, shape(LAT, MROWS, C), 300_000_000)(
        field, field_left, field_right
    )
    slots, merid = lax.optimization_barrier((slots, merid))
    merid = lax.all_to_all(merid, "lat", 0, 0)
    y = (lax.axis_index("lon") // ZS).astype(jnp.int32).reshape(1)
    zonal = call(
        zonal_kernel, shape(ZS, WIDE, 256), 4_000_000_000, vmem=24, in_specs=[SMEM, VMEM, VMEM]
    )(y, row, slots)
    zonal = lax.all_to_all(zonal, "lon", 0, 0, axis_index_groups=along_z)
    merid = call(merid_kernel, shape(LAT, MROWS, 256), 1_000_000_000)(merid, w_qkv)
    merid = lax.all_to_all(merid, "lat", 0, 0)
    mixed, first, last = call(
        mix_kernel, (shape(R, WIDE, C), shape(3, WIDE, C), shape(3, WIDE, C)), 800_000_000
    )(zonal, merid, field_left, field_right, field, w_out)
    before = lax.ppermute(last, "lat", down)
    after = lax.ppermute(first, "lat", up)
    return call(
        block_kernel,
        shape(R, W, C),
        2_000_000_000,
        in_specs=[ANY, VMEM, VMEM, VMEM, ANY, ANY],
        scratch_shapes=[
            pltpu.VMEM((R, WIDE, C), BF),
            pltpu.VMEM(w_in.shape, BF),
            pltpu.VMEM(w_back.shape, BF),
            pltpu.VMEM((CELLS, C), F32),
            pltpu.SemaphoreType.DMA((3,)),
        ],
    )(mixed, before, after, conv_w.reshape(49, C), in_hbm(w_in), in_hbm(w_back))


def solution(mesh):
    return jax.shard_map(
        per_device,
        mesh=mesh,
        in_specs=(P("lat", "lon", None), P(), P(), P(), P(), P()),
        out_specs=P("lat", "lon", None),
        check_vma=False,
    )
```

time: 111 us -> 103 us (0.928)
  between operations: 13.5 us -> 0.12 us
  blocking collectives: 17.8 us -> 29.6 us
  local copies, waits for them, and re-layouts: 7.18 us -> 0.04 us
  starting transfers between devices: 30.3 us -> 34.1 us
  waiting for transfers between devices: 25.7 us -> 22.6 us
    all_to_all x1, waiting for transfers between devices: 16.3 us -> 0.01 us  [per_device(): slots = lax.all_to_all(slots, 'lon', 0, 0, axis_index_groups=along_y)]
    all_to_all x1 -> x2, blocking collectives: 17.8 us -> 29.6 us  [the longest x1 17.9 us: per_device(): row = lax.all_to_all(row, 'lon', 0, 0, axis_index_groups=along_z)]
    all_to_all x1 -> x2, waiting for transfers between devices: 0.01 us -> 9.32 us  [the longest x1 5.92 us: per_device(): zonal = lax.all_to_all(zonal, 'lon', 0, 0, axis_index_groups=along_z)]
    unnamed x20 -> x8, local copies, waits for them, and re-layouts: 7.16 us -> 0.02 us
    all_to_all x1 -> x2, starting transfers between devices: 6.17 us -> 11.7 us  [the longest x1 8.4 us: per_device(): merid = lax.all_to_all(merid, 'lat', 0, 0)]
    ppermute x2, waiting for transfers between devices: 1.71 us -> 5.65 us  [the longest x1 5.65 us: per_device(): field_left = lax.ppermute(last, 'lon', right)]
    ppermute x1, starting transfers between devices: 5.93 us -> 4.1 us  [per_device(): before = lax.ppermute(last, 'lat', down)]
    pallas_call x4 -> x5, Pallas kernels: 14.3 us -> 13.3 us  [the longest x1 4.39 us: per_device(): call(block_kernel, shape(R, W, C), 2000000000, in_specs=[ANY, VMEM, VMEM,...]
  transfers between devices with their start and end apart: 7 -> 7, of which waited for: 4 -> 5; matrix products, arithmetic and copies ran while one was open for 0% -> 0% of each run, Pallas kernels for 9% -> 7%
where the time goes in v3:
time: 103 us; the launch traced here: 101 us
  starting transfers between devices  34.1 us (33%)
  blocking collectives  29.6 us (29%)
  waiting for transfers between devices  22.6 us (22%)
  Pallas kernels  14.8 us (14%)
    all_to_all x1, blocking collectives, per_device(): row = lax.all_to_all(row, 'lon', 0, 0, axis_index_groups=along_z)  17.9 us
    all_to_all x1, blocking collectives, per_device(): merid = lax.all_to_all(merid, 'lat', 0, 0)  11.7 us
    all_to_all x1, starting transfers between devices, per_device(): merid = lax.all_to_all(merid, 'lat', 0, 0)  8.4 us
    ppermute x1, starting transfers between devices, per_device(): field_right = lax.ppermute(first, 'lon', left)  7.58 us
    all_to_all x1, starting transfers between devices, per_device(): slots = lax.all_to_all(slots, 'lon', 0, 0, axis_index_groups=along_y)  6.81 us
    ppermute x1, waiting for transfers between devices, per_device(): after = lax.ppermute(first, 'lat', up)  6.51 us
    all_to_all x1, waiting for transfers between devices, per_device(): zonal = lax.all_to_all(zonal, 'lon', 0, 0, axis_index_groups=along_z)  5.92 us
    ppermute x1, waiting for transfers between devices, per_device(): field_left = lax.ppermute(last, 'lon', right)  5.65 us
  transfers between devices with their start and end apart: 7, of which 5 were waited for; matrix products, arithmetic and copies ran while one was open for 0% of the time, Pallas kernels for 7%

profile of v3, /device:TPU:7, one launch (start us, length us, event | category | flops | bytes accessed | tf_op | source)
XLA Modules:
  0.0 101.3 jit_solution(12662912421310645163)
XLA Ops:
  0.0 1.7 %shard_map.64 = (bf16[4,64,384]{2,1,0:T(8,128)(2,1)S(1)}, bf16[32,512]{1,0:T(8,128)(2,1)S(1)}, bf16[32,512]{1,0:T(8,128)(2,1)S(1)}) custom-call(bf16[4,64,512]{2,1,0:T(8,128)(2,1)} %field_ref.3, bf16[512,1152]{1,0:T(8,128)(2,1)} %w_ref.2), custom_call_target="tpu_custom_call" | custom-call | flops 200000000 | bytes 2000000 | tf_op jit(solution)/shard_map/pallas_call | solution.py:240
  1.7 0.0 copy-start.1
  1.7 17.9 %all_to_all.25.in_ref.own_ref = bf16[4,64,384]{2,1,0:T(8,128)(2,1)S(1)} all-to-all(bf16[4,64,384]{2,1,0:T(8,128)(2,1)S(1)} %get-tuple-element.13), channel_id=1, replica_groups={{0,1,2,3},{4,5,6,7},{8,9,10,11},{12,13,14,15},{16,17,18,19},{20,21,22,2..., dimensions={0} | all-to-all | bytes 393216 | tf_op jit(solution)/shard_map/all_to_all | solution.py:252
  19.6 0.9 shard_map.65
  20.5 6.8 %all-to-all-start.1 = ((bf16[8,272,128]{2,1,0:T(8,128)(2,1)}), bf16[8,272,128]{2,1,0:T(8,128)(2,1)S(1)}, u32[]{:S(2)}, u32[]{:S(2)}) async-start(bf16[8,272,128]{2,1,0:T(8,128)(2,1)} %shard_map.65), calls=%async_computation.1 | async-start | bytes 1114112 | tf_op jit(solution)/shard_map/all_to_all | solution.py:254
  27.3 1.9 %collective-permute-start = (bf16[32,512]{1,0:T(8,128)(2,1)S(1)}, bf16[32,512]{1,0:T(8,128)(2,1)S(1)}, u32[]{:S(2)}, u32[]{:S(2)}) collective-permute-start(bf16[32,512]{1,0:T(8,128)(2,1)S(1)} %get-tuple-element.14), channel_id=1, source_target_pairs={{0,1},{1,2},{2,3},{3,4},{4,5},{5,6},{6,7},{7,8},{8,9},{9,10},{10,1... | collective-permute-start | bytes 98312 | tf_op jit(solution)/shard_map/ppermute | solution.py:255
  29.2 7.6 %collective-permute-start.1 = (bf16[32,512]{1,0:T(8,128)(2,1)S(1)}, bf16[32,512]{1,0:T(8,128)(2,1)S(1)}, u32[]{:S(2)}, u32[]{:S(2)}) collective-permute-start(bf16[32,512]{1,0:T(8,128)(2,1)S(1)} %get-tuple-element.15), channel_id=1, source_target_pairs={{1,0},{2,1},{3,2},{4,3},{5,4},{6,5},{7,6},{8,7},{9,8},{10,9},{11,1... | collective-permute-start | bytes 98312 | tf_op jit(solution)/shard_map/ppermute | solution.py:256
  36.8 5.6 %collective-permute-done.left_ref = bf16[32,512]{1,0:T(8,128)(2,1)S(1)} collective-permute-done((bf16[32,512]{1,0:T(8,128)(2,1)S(1)}, bf16[32,512]{1,0:T(8,128)(2,1)S(1)}, u32[]{:S(2)}, u32[]{:S(2)}) %collective-permute-start) | collective-permute-done | bytes 32800 | tf_op jit(solution)/shard_map/ppermute | solution.py:255
  42.4 0.0 collective-permute-done.1.right_ref
  42.4 0.0 copy-done.1
  42.4 1.3 %shard_map.66 = bf16[16,24,512]{2,1,0:T(8,128)(2,1)} custom-call(bf16[4,64,512]{2,1,0:T(8,128)(2,1)S(1)} %copy-done.1, bf16[32,512]{1,0:T(8,128)(2,1)S(1)} %collective-permute-done.left_ref, bf16[32,512]{1,0:T(8,128)(2,1)S(1)} %collective-permute-done.1.right_ref), custom_call_target="tpu_custom_call" | custom-call | flops 300000000 | bytes 2000000 | tf_op jit(solution)/shard_map/pallas_call | solution.py:257
  43.8 0.0 all-to-all-done.1.all_ref
  43.8 8.4 %all-to-all-start.3 = ((bf16[16,24,512]{2,1,0:T(8,128)(2,1)}), bf16[16,24,512]{2,1,0:T(8,128)(2,1)S(1)}, u32[]{:S(2)}, u32[]{:S(2)}) async-start(bf16[16,24,512]{2,1,0:T(8,128)(2,1)} %shard_map.66), calls=%async_computation.3 | async-start | bytes 786432 | tf_op jit(solution)/shard_map/all_to_all | solution.py:261
  52.2 0.0 copy-start
  52.2 4.0 %shard_map.67 = bf16[4,80,256]{2,1,0:T(8,128)(2,1)} custom-call(s32[1]{0:T(128)} %bitcast.y_ref, bf16[4,64,384]{2,1,0:T(8,128)(2,1)S(1)} %all_to_all.25.in_ref.own_ref, bf16[8,272,128]{2,1,0:T(8,128)(2,1)S(1)} %all-to-all-done.1.all_ref), custom_call_target="tpu_custom_call" | custom-call | flops 4000000000 | bytes 2000000 | tf_op jit(solution)/shard_map/pallas_call | solution.py:263
  56.2 3.4 %all-to-all-done.3.in_ref = bf16[16,24,512]{2,1,0:T(8,128)(2,1)S(1)} async-done(((bf16[16,24,512]{2,1,0:T(8,128)(2,1)}), bf16[16,24,512]{2,1,0:T(8,128)(2,1)S(1)}, u32[]{:S(2)}, u32[]{:S(2)}) %all-to-all-start.3) | async-done | bytes 393248 | tf_op jit(solution)/shard_map/all_to_all | solution.py:261
  59.6 3.3 %all-to-all-start.2 = ((bf16[4,80,256]{2,1,0:T(8,128)(2,1)}), bf16[4,80,256]{2,1,0:T(8,128)(2,1)S(1)}, u32[]{:S(2)}, u32[]{:S(2)}) async-start(bf16[4,80,256]{2,1,0:T(8,128)(2,1)} %shard_map.67), calls=%async_computation.2 | async-start | bytes 327680 | tf_op jit(solution)/shard_map/all_to_all | solution.py:266
  63.0 0.0 copy-done
  63.0 0.0 copy-start.2
  63.0 1.9 %shard_map.68 = bf16[16,24,256]{2,1,0:T(8,128)(2,1)S(1)} custom-call(bf16[16,24,512]{2,1,0:T(8,128)(2,1)S(1)} %all-to-all-done.3.in_ref, bf16[512,1152]{1,0:T(8,128)(2,1)S(1)} %copy-done), custom_call_target="tpu_custom_call" | custom-call | flops 1000000000 | bytes 2000000 | tf_op jit(solution)/shard_map/pallas_call | solution.py:267
  64.9 5.9 %all-to-all-done.2.zonal_ref = bf16[4,80,256]{2,1,0:T(8,128)(2,1)S(1)} async-done(((bf16[4,80,256]{2,1,0:T(8,128)(2,1)}), bf16[4,80,256]{2,1,0:T(8,128)(2,1)S(1)}, u32[]{:S(2)}, u32[]{:S(2)}) %all-to-all-start.2) | async-done | bytes 163872 | tf_op jit(solution)/shard_map/all_to_all | solution.py:266
  70.8 11.7 %all_to_all.26.merid_ref = bf16[16,24,256]{2,1,0:T(8,128)(2,1)S(1)} all-to-all(bf16[16,24,256]{2,1,0:T(8,128)(2,1)S(1)} %shard_map.68), channel_id=1, replica_groups=mesh['lat'=16,'lon'=32] {'lat'}, dimensions={0} | all-to-all | bytes 393216 | tf_op jit(solution)/shard_map/all_to_all | solution.py:268
  82.5 0.0 copy-done.2
  82.5 0.0 copy-start.3
  82.5 0.6 shard_map.69
  83.1 4.1 %collective-permute-start.2 = (bf16[3,80,512]{2,1,0:T(8,128)(2,1)S(1)}, bf16[3,80,512]{2,1,0:T(8,128)(2,1)S(1)}, u32[]{:S(2)}, u32[]{:S(2)}) collective-permute-start(bf16[3,80,512]{2,1,0:T(8,128)(2,1)S(1)} %get-tuple-element.19), channel_id=1, source_target_pairs={{0,32},{32,64},{64,96},{96,128},{128,160},{160,192},{192,224},{224... | collective-permute-start | bytes 737288 | tf_op jit(solution)/shard_map/ppermute | solution.py:272
  87.2 1.9 %collective-permute-start.3 = (bf16[3,80,512]{2,1,0:T(8,128)(2,1)S(1)}, bf16[3,80,512]{2,1,0:T(8,128)(2,1)S(1)}, u32[]{:S(2)}, u32[]{:S(2)}) collective-permute-start(bf16[3,80,512]{2,1,0:T(8,128)(2,1)S(1)} %get-tuple-element.20), channel_id=1, source_target_pairs={{32,0},{64,32},{96,64},{128,96},{160,128},{192,160},{224,192},{256... | collective-permute-start | bytes 737288 | tf_op jit(solution)/shard_map/ppermute | solution.py:273
  89.2 0.0 copy-done.3
  89.2 1.2 %collective-permute-done.2.before_ref = bf16[3,80,512]{2,1,0:T(8,128)(2,1)S(1)} collective-permute-done((bf16[3,80,512]{2,1,0:T(8,128)(2,1)S(1)}, bf16[3,80,512]{2,1,0:T(8,128)(2,1)S(1)}, u32[]{:S(2)}, u32[]{:S(2)}) %collective-permute-start.2) | collective-permute-done | bytes 245792 | tf_op jit(solution)/shard_map/ppermute | solution.py:272
  90.4 6.5 %collective-permute-done.3.after_ref = bf16[3,80,512]{2,1,0:T(8,128)(2,1)S(1)} collective-permute-done((bf16[3,80,512]{2,1,0:T(8,128)(2,1)S(1)}, bf16[3,80,512]{2,1,0:T(8,128)(2,1)S(1)}, u32[]{:S(2)}, u32[]{:S(2)}) %collective-permute-start.3) | collective-permute-done | bytes 245792 | tf_op jit(solution)/shard_map/ppermute | solution.py:273
  96.9 4.4 %shard_map.70 = bf16[4,64,512]{2,1,0:T(8,128)(2,1)} custom-call(bf16[4,80,512]{2,1,0:T(8,128)(2,1)S(1)} %get-tuple-element.18.mixed_hbm, bf16[3,80,512]{2,1,0:T(8,128)(2,1)S(1)} %collective-permute-done.2.before_ref, bf16[3,80,512]{2,1,0:T(8,128)(2,1)S(1)} %collective-permute-done.3.after_ref, f32[49,512]{1,0:T(8,128)S(1)} %reshape.7.conv_ref, ...), custom_call_target="tpu_custom_call" | custom-call | flops 2000000000 | bytes 2000000 | tf_op jit(solution)/shard_map/pallas_call | solution.py:274
  (1 shorter events, 0.0 us)
Async XLA Ops:
  1.7 40.8 %copy-start.1 = (bf16[4,64,512]{2,1,0:T(8,128)(2,1)S(1)}, bf16[4,64,512]{2,1,0:T(8,128)(2,1)}, u32[]{:S(2)}) copy-start(bf16[4,64,512]{2,1,0:T(8,128)(2,1)} %field_ref.3) | copy-start | bytes 786436
  20.5 23.3 %all-to-all-start.1 = ((bf16[8,272,128]{2,1,0:T(8,128)(2,1)}), bf16[8,272,128]{2,1,0:T(8,128)(2,1)S(1)}, u32[]{:S(2)}, u32[]{:S(2)}) async-start(bf16[8,272,128]{2,1,0:T(8,128)(2,1)} %shard_map.65), calls=%async_computation.1 | async-start | bytes 1114112 | tf_op jit(solution)/shard_map/all_to_all | solution.py:254
  27.3 15.2 %collective-permute-start = (bf16[32,512]{1,0:T(8,128)(2,1)S(1)}, bf16[32,512]{1,0:T(8,128)(2,1)S(1)}, u32[]{:S(2)}, u32[]{:S(2)}) collective-permute-start(bf16[32,512]{1,0:T(8,128)(2,1)S(1)} %get-tuple-element.14), channel_id=1, source_target_pairs={{0,1},{1,2},{2,3},{3,4},{4,5},{5,6},{6,7},{7,8},{8,9},{9,10},{10,1... | collective-permute-start | bytes 98312 | tf_op jit(solution)/shard_map/ppermute | solution.py:255
  29.2 13.2 %collective-permute-start.1 = (bf16[32,512]{1,0:T(8,128)(2,1)S(1)}, bf16[32,512]{1,0:T(8,128)(2,1)S(1)}, u32[]{:S(2)}, u32[]{:S(2)}) collective-permute-start(bf16[32,512]{1,0:T(8,128)(2,1)S(1)} %get-tuple-element.15), channel_id=1, source_target_pairs={{1,0},{2,1},{3,2},{4,3},{5,4},{6,5},{7,6},{8,7},{9,8},{10,9},{11,1... | collective-permute-start | bytes 98312 | tf_op jit(solution)/shard_map/ppermute | solution.py:256
  43.8 15.9 %all-to-all-start.3 = ((bf16[16,24,512]{2,1,0:T(8,128)(2,1)}), bf16[16,24,512]{2,1,0:T(8,128)(2,1)S(1)}, u32[]{:S(2)}, u32[]{:S(2)}) async-start(bf16[16,24,512]{2,1,0:T(8,128)(2,1)} %shard_map.66), calls=%async_computation.3 | async-start | bytes 786432 | tf_op jit(solution)/shard_map/all_to_all | solution.py:261
  52.2 10.8 %copy-start = (bf16[512,1152]{1,0:T(8,128)(2,1)S(1)}, bf16[512,1152]{1,0:T(8,128)(2,1)}, u32[]{:S(2)}) copy-start(bf16[512,1152]{1,0:T(8,128)(2,1)} %w_ref.2) | copy-start | bytes 3538948
  59.6 11.2 %all-to-all-start.2 = ((bf16[4,80,256]{2,1,0:T(8,128)(2,1)}), bf16[4,80,256]{2,1,0:T(8,128)(2,1)S(1)}, u32[]{:S(2)}, u32[]{:S(2)}) async-start(bf16[4,80,256]{2,1,0:T(8,128)(2,1)} %shard_map.67), calls=%async_computation.2 | async-start | bytes 327680 | tf_op jit(solution)/shard_map/all_to_all | solution.py:266
  63.0 19.5 %copy-start.2 = (bf16[512,512]{1,0:T(8,128)(2,1)S(1)}, bf16[512,512]{1,0:T(8,128)(2,1)}, u32[]{:S(2)}) copy-start(bf16[512,512]{1,0:T(8,128)(2,1)} %w_ref.3) | copy-start | bytes 1572868
  82.5 6.7 %copy-start.3 = (f32[7,7,512]{2,1,0:T(8,128)S(1)}, f32[7,7,512]{2,1,0:T(8,128)}, u32[]{:S(2)}) copy-start(f32[7,7,512]{2,1,0:T(8,128)} %param.9) | copy-start | bytes 301060
  83.1 7.2 %collective-permute-start.2 = (bf16[3,80,512]{2,1,0:T(8,128)(2,1)S(1)}, bf16[3,80,512]{2,1,0:T(8,128)(2,1)S(1)}, u32[]{:S(2)}, u32[]{:S(2)}) collective-permute-start(bf16[3,80,512]{2,1,0:T(8,128)(2,1)S(1)} %get-tuple-element.19), channel_id=1, source_target_pairs={{0,32},{32,64},{64,96},{96,128},{128,160},{160,192},{192,224},{224... | collective-permute-start | bytes 737288 | tf_op jit(solution)/shard_map/ppermute | solution.py:272
  87.2 9.6 %collective-permute-start.3 = (bf16[3,80,512]{2,1,0:T(8,128)(2,1)S(1)}, bf16[3,80,512]{2,1,0:T(8,128)(2,1)S(1)}, u32[]{:S(2)}, u32[]{:S(2)}) collective-permute-start(bf16[3,80,512]{2,1,0:T(8,128)(2,1)S(1)} %get-tuple-element.20), channel_id=1, source_target_pairs={{32,0},{64,32},{96,64},{128,96},{160,128},{192,160},{224,192},{256... | collective-permute-start | bytes 737288 | tf_op jit(solution)/shard_map/ppermute | solution.py:273

commit v4 on v3

--- a/solution.py
+++ b/solution.py
@@ -16,8 +16,7 @@
 CELLS = R * W
 E = 8
 WIDE = W + 2 * E
-MC = WIDE // LAT
-MROWS = 24
+MCELLS = 16
 YS = 8
 ZS = 4
 SPAN = ZS * W
@@ -71,7 +70,9 @@
     return pltpu.with_memory_space_constraint(array, pltpu.HBM)
 
 
-def zonal_project_kernel(field_hbm, w_hbm, out_ref, first_ref, last_ref, field_ref, wq_ref, wkv_ref, sems):
+def project_kernel(
+    field_hbm, w_hbm, row_ref, merid_ref, first_ref, last_ref, field_ref, wq_ref, wkv_ref, sems
+):
     loads = [
         pltpu.make_async_copy(field_hbm, field_ref, sems.at[0]),
         pltpu.make_async_copy(w_hbm.at[:, 512:640], wkv_ref, sems.at[1]),
@@ -79,15 +80,19 @@
     ]
     for load in loads:
         load.start()
+    t, s = iota((CELLS, CELLS), 0), iota((CELLS, CELLS), 1)
+    select = one_hot(s == ((t >> 2) & 3) * W + (t >> 4) * 4 + (t & 3))
     loads[0].wait()
-    field = field_ref[...].astype(F32)
-    first_ref[...] = field[:, 0:E].reshape(R * E, C).astype(BF)
-    last_ref[...] = field[:, W - E : W].reshape(R * E, C).astype(BF)
-    normed = layer_norm(field.reshape(CELLS, C)).astype(BF)
+    field = field_ref[...].astype(F32).reshape(CELLS, C)
+    normed = layer_norm(field).astype(BF)
+    merid_ref[...] = mm(select, normed).astype(BF).reshape(LAT, MCELLS, C)
+    edges = mm(jnp.concatenate([select[0:MCELLS], select[CELLS - MCELLS :]], axis=0), field.astype(BF))
+    first_ref[...] = edges[0:MCELLS].astype(BF)
+    last_ref[...] = edges[MCELLS:].astype(BF)
     loads[1].wait()
-    out_ref[:, :, 256:384] = mm(normed, wkv_ref[...]).astype(BF).reshape(R, W, 128)
+    row_ref[:, :, 256:384] = mm(normed, wkv_ref[...]).astype(BF).reshape(R, W, 128)
     loads[2].wait()
-    out_ref[:, :, 0:256] = mm(normed, wq_ref[...]).astype(BF).reshape(R, W, 256)
+    row_ref[:, :, 0:256] = mm(normed, wq_ref[...]).astype(BF).reshape(R, W, 256)
 
 
 def spread_kernel(in_ref, out_ref):
@@ -130,35 +135,14 @@
             out_ref[z, :, lanes] = heads[z * W : z * W + WIDE].astype(BF)
 
 
-def widened(left, own, right):
-    left, right = (a.astype(F32).reshape(R, E, a.shape[-1]) for a in (left, right))
-    return jnp.concatenate([left, own.astype(F32), right], axis=1)
-
-
-def merid_slots():
-    dims = (LAT, MROWS, R * WIDE)
-    m, i, u = iota(dims, 0), iota(dims, 1), iota(dims, 2)
-    cell = (i & 3) * WIDE + m * MC + (i >> 2)
-    return one_hot((cell == u) & (i < R * MC)).reshape(LAT * MROWS, R * WIDE)
-
-
-def merid_select_kernel(field_ref, left_ref, right_ref, out_ref):
-    wide = widened(left_ref[...], field_ref[...], right_ref[...]).reshape(R * WIDE, C)
-    normed = mm(merid_slots(), layer_norm(wide).astype(BF))
-    out_ref[...] = normed.reshape(LAT, MROWS, C).astype(BF)
-
-
 def merid_kernel(in_ref, w_ref, out_ref):
-    count = LAT * MROWS
-    normed = in_ref[...].astype(F32).reshape(count, C).astype(BF)
+    normed = in_ref[...].reshape(CELLS, C)
     queries = mm(normed, w_ref[:, 256:512]).astype(BF)
     keys = mm(normed, w_ref[:, 640:896]).astype(BF)
     values = mm(normed, w_ref[:, 896:1152]).astype(BF)
-    row = iota((LAT, MROWS, count), 1).reshape(count, count) >> 2
-    key = iota((count, count), 1)
-    key = (key - ((key * 2731) >> 16) * MROWS) >> 2
-    bias = jnp.where(row == key, 0.0, -1e30)
-    low = iota((count, 128), 1) < HD
+    t, s = iota((CELLS, CELLS), 0), iota((CELLS, CELLS), 1)
+    bias = jnp.where((t & 3) == (s & 3), 0.0, -1e30)
+    low = iota((CELLS, 128), 1) < HD
     scale = 1.0 / math.sqrt(HD)
     for pair in range(2):
         lanes = slice(pair * 128, pair * 128 + 128)
@@ -169,21 +153,28 @@
             weight = jnp.exp(score - jnp.max(score, axis=-1, keepdims=True))
             mass = jnp.sum(weight, axis=-1, keepdims=True)
             outs.append(mm(weight.astype(BF), v) / mass)
-        both = jnp.where(low, outs[0], outs[1]).reshape(LAT, MROWS, 128)
+        both = jnp.where(low, outs[0], outs[1]).reshape(LAT, MCELLS, 128)
         out_ref[:, :, lanes] = both.astype(BF)
 
 
 def mix_kernel(zonal_ref, merid_ref, left_ref, right_ref, field_ref, w_ref, mixed_ref, up_ref, down_ref):
     rows = R * WIDE
-    merid = merid_ref[...].astype(F32).reshape(LAT * MROWS, 256).astype(BF)
-    dims = (R, WIDE, LAT * MROWS)
-    r, w, t = iota(dims, 0), iota(dims, 1), iota(dims, 2)
-    m = (t * 2731) >> 16
-    i = t - m * MROWS
-    cell = one_hot((m * MC + (i >> 2) == w) & ((i & 3) == r) & (i < R * MC))
-    merid = mm(cell.reshape(rows, LAT * MROWS), merid).astype(BF)
-    attended = mm(zonal_ref[...].reshape(rows, 256), w_ref[0:256]) + mm(merid, w_ref[256:512])
-    wide = widened(left_ref[...], field_ref[...], right_ref[...])
+    dims = (R, WIDE, CELLS)
+    r, c, t = iota(dims, 0), iota(dims, 1) - E, iota(dims, 2)
+    own = ((c >> 2) << 4) + (r << 2) + (c & 3)
+    own = one_hot((c >= 0) & (c < W) & (t == own)).reshape(rows, CELLS)
+    dims = (R, WIDE, MCELLS)
+    r, c, t = iota(dims, 0), iota(dims, 1) - E, iota(dims, 2)
+    edge = t == (r << 2) + (c & 3)
+    left = one_hot(edge & (c >= -4) & (c < 0)).reshape(rows, MCELLS)
+    right = one_hot(edge & (c >= W) & (c < W + 4)).reshape(rows, MCELLS)
+    edges = mm(left, left_ref[...]) + mm(right, right_ref[...])
+    merid = mm(own, merid_ref[...].reshape(CELLS, 256)) + edges[:, 0:256]
+    attended = mm(zonal_ref[...].reshape(rows, 256), w_ref[0:256])
+    attended = attended + mm(merid.astype(BF), w_ref[256:512])
+    blank = jnp.zeros((R, E, C), F32)
+    wide = jnp.concatenate([blank, field_ref[...].astype(F32), blank], axis=1)
+    wide = wide + edges[:, 256:].reshape(R, WIDE, C)
     mixed = (wide + attended.reshape(R, WIDE, C)).astype(BF)
     mixed_ref[...] = mixed
     up_ref[...] = mixed[0:3]
@@ -237,9 +228,9 @@
     up = [(j, i) for i, j in down]
     along_y = [[y * ZS + z for y in range(YS)] for z in range(ZS)]
     along_z = [[y * ZS + z for z in range(ZS)] for y in range(YS)]
-    row, first, last = call(
-        zonal_project_kernel,
-        (shape(R, W, 384), shape(R * E, C), shape(R * E, C)),
+    row, merid, first, last = call(
+        project_kernel,
+        (shape(R, W, 384), shape(LAT, MCELLS, C), shape(MCELLS, C), shape(MCELLS, C)),
         200_000_000,
         in_specs=[ANY, ANY],
         scratch_shapes=[
@@ -249,26 +240,25 @@
             pltpu.SemaphoreType.DMA((3,)),
         ],
     )(in_hbm(field), in_hbm(w_qkv))
+    merid = lax.all_to_all(merid, "lat", 0, 0)
+    row, merid = lax.optimization_barrier((row, merid))
     row = lax.all_to_all(row, "lon", 0, 0, axis_index_groups=along_z)
-    slots = call(spread_kernel, shape(YS, KEYS, 128), 10_000_000)(row)
+    merid = call(merid_kernel, shape(LAT, MCELLS, 256), 1_000_000_000)(merid, w_qkv)
+    merid = lax.all_to_all(merid, "lat", 0, 0)
+    slots = call(spread_kernel, shape(YS, KEYS, 128), 300_000_000)(row)
+    slots, merid = lax.optimization_barrier((slots, merid))
     slots = lax.all_to_all(slots, "lon", 0, 0, axis_index_groups=along_y)
-    field_left = lax.ppermute(last, "lon", right)
-    field_right = lax.ppermute(first, "lon", left)
-    merid = call(merid_select_kernel, shape(LAT, MROWS, C), 300_000_000)(
-        field, field_left, field_right
-    )
-    slots, merid = lax.optimization_barrier((slots, merid))
-    merid = lax.all_to_all(merid, "lat", 0, 0)
+    edge_left = lax.ppermute(jnp.concatenate([merid[LAT - 1], last], axis=1), "lon", right)
+    edge_right = lax.ppermute(jnp.concatenate([merid[0], first], axis=1), "lon", left)
+    slots, edge_left, edge_right = lax.optimization_barrier((slots, edge_left, edge_right))
     y = (lax.axis_index("lon") // ZS).astype(jnp.int32).reshape(1)
     zonal = call(
         zonal_kernel, shape(ZS, WIDE, 256), 4_000_000_000, vmem=24, in_specs=[SMEM, VMEM, VMEM]
     )(y, row, slots)
     zonal = lax.all_to_all(zonal, "lon", 0, 0, axis_index_groups=along_z)
-    merid = call(merid_kernel, shape(LAT, MROWS, 256), 1_000_000_000)(merid, w_qkv)
-    merid = lax.all_to_all(merid, "lat", 0, 0)
     mixed, first, last = call(
         mix_kernel, (shape(R, WIDE, C), shape(3, WIDE, C), shape(3, WIDE, C)), 800_000_000
-    )(zonal, merid, field_left, field_right, field, w_out)
+    )(zonal, merid, edge_left, edge_right, field, w_out)
     before = lax.ppermute(last, "lat", down)
     after = lax.ppermute(first, "lat", up)
     return call(

time: 103 us -> 105 us (1.019); the launches traced: 101 us -> 105 us
  starting transfers between devices: 34.1 us -> 39.1 us
  blocking collectives: 29.6 us -> 24.8 us
  waiting for transfers between devices: 22.6 us -> 27.1 us
  Pallas kernels: 14.8 us -> 13.6 us
    all_to_all x1, blocking collectives: 17.9 us -> 10.2 us  [per_device(): zonal = lax.all_to_all(zonal, 'lon', 0, 0, axis_index_groups=along_z)]
    all_to_all x1, waiting for transfers between devices: 0.01 us -> 6.3 us  [per_device(): slots = lax.all_to_all(slots, 'lon', 0, 0, axis_index_groups=along_y)]
    all_to_all x1, starting transfers between devices: 3.35 us -> 7.18 us  [per_device(): row = lax.all_to_all(row, 'lon', 0, 0, axis_index_groups=along_z)]
    all_to_all x1, blocking collectives: 11.7 us -> 14.7 us  [per_device(): merid = lax.all_to_all(merid, 'lat', 0, 0)]
    ppermute x2, waiting for transfers between devices: 5.65 us -> 2.8 us  [the longest x1 2.79 us: per_device(): lax.ppermute(jnp.concatenate([merid[LAT - 1], last], axis=1), 'lon', right)]
    ppermute x1, starting transfers between devices: 4.1 us -> 6.23 us  [per_device(): before = lax.ppermute(last, 'lat', down)]
    pallas_call x4 -> x3, Pallas kernels: 5.71 us -> 5.17 us  [the longest x1 2.73 us: per_device(): call(project_kernel, (shape(R, W, 384), shape(LAT, MCELLS, C), shape(MCEL...]
  transfers between devices with their start and end apart: 7 -> 7, of which waited for: 5 -> 6; matrix products, arithmetic and copies ran while one was open for 0% -> 0% of each run, Pallas kernels for 7% -> 2%
where the time goes in v4:
time: 105 us
  starting transfers between devices  39.1 us (37%)
  waiting for transfers between devices  27.1 us (26%)
  blocking collectives  24.8 us (24%)
  Pallas kernels  13.6 us (13%)
    all_to_all x1, blocking collectives, per_device(): merid = lax.all_to_all(merid, 'lat', 0, 0)  14.7 us
    all_to_all x1, blocking collectives, per_device(): zonal = lax.all_to_all(zonal, 'lon', 0, 0, axis_index_groups=along_z)  10.2 us
    all_to_all x1, starting transfers between devices, per_device(): merid = lax.all_to_all(merid, 'lat', 0, 0)  7.42 us
    all_to_all x1, starting transfers between devices, per_device(): row = lax.all_to_all(row, 'lon', 0, 0, axis_index_groups=along_z)  7.18 us
    ppermute x1, starting transfers between devices, per_device(): lax.ppermute(jnp.concatenate([merid[0], first], axis=1), 'lon', left)  6.9 us
    all_to_all x1, starting transfers between devices, per_device(): slots = lax.all_to_all(slots, 'lon', 0, 0, axis_index_groups=along_y)  6.83 us
    all_to_all x1, waiting for transfers between devices, per_device(): row = lax.all_to_all(row, 'lon', 0, 0, axis_index_groups=along_z)  6.56 us
    ppermute x1, waiting for transfers between devices, per_device(): after = lax.ppermute(first, 'lat', up)  6.51 us
  transfers between devices with their start and end apart: 7, of which 6 were waited for; matrix products, arithmetic and copies ran while one was open for 0% of the time, Pallas kernels for 2%

profile of v4, /device:TPU:7, one launch (start us, length us, event | category | flops | bytes accessed | tf_op | source)
XLA Modules:
  0.0 104.8 jit_solution(631942999244198219)
XLA Ops:
  0.0 0.0 copy-start
  0.0 2.7 %shard_map.64 = (bf16[4,64,384]{2,1,0:T(8,128)(2,1)}, bf16[16,16,512]{2,1,0:T(8,128)(2,1)S(1)}, bf16[16,512]{1,0:T(8,128)(2,1)S(1)}, bf16[16,512]{1,0:T(8,128)(2,1)S(1)}) custom-call(bf16[4,64,512]{2,1,0:T(8,128)(2,1)} %field_ref.1, bf16[512,1152]{1,0:T(8,128)(2,1)} %w_ref.2), custom_call_target="tpu_custom_call" | custom-call | flops 200000000 | bytes 2000000 | tf_op jit(solution)/shard_map/pallas_call | solution.py:231
  2.7 14.7 %all_to_all.25.in_ref = bf16[16,16,512]{2,1,0:T(8,128)(2,1)S(1)} all-to-all(bf16[16,16,512]{2,1,0:T(8,128)(2,1)S(1)} %get-tuple-element.20), channel_id=1, replica_groups=mesh['lat'=16,'lon'=32] {'lat'}, dimensions={0} | all-to-all | bytes 524288 | tf_op jit(solution)/shard_map/all_to_all | solution.py:243
  17.4 7.2 %all-to-all-start.1 = ((bf16[4,64,384]{2,1,0:T(8,128)(2,1)}), bf16[4,64,384]{2,1,0:T(8,128)(2,1)S(1)}, u32[]{:S(2)}, u32[]{:S(2)}) async-start(bf16[4,64,384]{2,1,0:T(8,128)(2,1)} %get-tuple-element.21), calls=%async_computation.1 | async-start | bytes 393216 | tf_op jit(solution)/shard_map/all_to_all | solution.py:245
  24.6 0.0 copy-done
  24.6 1.6 %shard_map.66 = bf16[16,16,256]{2,1,0:T(8,128)(2,1)} custom-call(bf16[16,16,512]{2,1,0:T(8,128)(2,1)S(1)} %all_to_all.25.in_ref, bf16[512,1152]{1,0:T(8,128)(2,1)S(1)} %copy-done), custom_call_target="tpu_custom_call" | custom-call | flops 1000000000 | bytes 2000000 | tf_op jit(solution)/shard_map/pallas_call | solution.py:246
  26.2 6.6 %all-to-all-done.1.in_ref.own_ref = bf16[4,64,384]{2,1,0:T(8,128)(2,1)S(1)} async-done(((bf16[4,64,384]{2,1,0:T(8,128)(2,1)}), bf16[4,64,384]{2,1,0:T(8,128)(2,1)S(1)}, u32[]{:S(2)}, u32[]{:S(2)}) %all-to-all-start.1) | async-done | bytes 196640 | tf_op jit(solution)/shard_map/all_to_all | solution.py:245
  32.7 7.4 %all-to-all-start.2 = ((bf16[16,16,256]{2,1,0:T(8,128)(2,1)}), bf16[16,16,256]{2,1,0:T(8,128)(2,1)S(1)}, u32[]{:S(2)}, u32[]{:S(2)}) async-start(bf16[16,16,256]{2,1,0:T(8,128)(2,1)} %shard_map.66), calls=%async_computation.2 | async-start | bytes 262144 | tf_op jit(solution)/shard_map/all_to_all | solution.py:247
  40.2 0.9 shard_map.65
  41.0 3.8 %all-to-all-done.2.merid_ref = bf16[16,16,256]{2,1,0:T(8,128)(2,1)S(1)} async-done(((bf16[16,16,256]{2,1,0:T(8,128)(2,1)}), bf16[16,16,256]{2,1,0:T(8,128)(2,1)S(1)}, u32[]{:S(2)}, u32[]{:S(2)}) %all-to-all-start.2) | async-done | bytes 131104 | tf_op jit(solution)/shard_map/all_to_all | solution.py:247
  44.8 6.8 %all-to-all-start.3 = ((bf16[8,272,128]{2,1,0:T(8,128)(2,1)}), bf16[8,272,128]{2,1,0:T(8,128)(2,1)S(1)}, u32[]{:S(2)}, u32[]{:S(2)}) async-start(bf16[8,272,128]{2,1,0:T(8,128)(2,1)} %shard_map.65), calls=%async_computation.3 | async-start | bytes 1114112 | tf_op jit(solution)/shard_map/all_to_all | solution.py:250
  51.7 2.6 %collective-permute-start = (bf16[16,768]{1,0:T(8,128)(2,1)S(1)}, bf16[16,768]{1,0:T(8,128)(2,1)S(1)}, u32[]{:S(2)}, u32[]{:S(2)}) collective-permute-start(bf16[16,768]{1,0:T(8,128)(2,1)S(1)} %pad_maximum_fusion), channel_id=1, source_target_pairs={{0,1},{1,2},{2,3},{3,4},{4,5},{5,6},{6,7},{7,8},{8,9},{9,10},{10,1... | collective-permute-start | bytes 73736 | tf_op jit(solution)/shard_map/ppermute | solution.py:251
  54.3 6.9 %collective-permute-start.1 = (bf16[16,768]{1,0:T(8,128)(2,1)S(1)}, bf16[16,768]{1,0:T(8,128)(2,1)S(1)}, u32[]{:S(2)}, u32[]{:S(2)}) collective-permute-start(bf16[16,768]{1,0:T(8,128)(2,1)S(1)} %pad_maximum_fusion.1), channel_id=1, source_target_pairs={{1,0},{2,1},{3,2},{4,3},{5,4},{6,5},{7,6},{8,7},{9,8},{10,9},{11,1... | collective-permute-start | bytes 73736 | tf_op jit(solution)/shard_map/ppermute | solution.py:252
  61.2 2.8 %collective-permute-done.left_ref = bf16[16,768]{1,0:T(8,128)(2,1)S(1)} collective-permute-done((bf16[16,768]{1,0:T(8,128)(2,1)S(1)}, bf16[16,768]{1,0:T(8,128)(2,1)S(1)}, u32[]{:S(2)}, u32[]{:S(2)}) %collective-permute-start) | collective-permute-done | bytes 24608 | tf_op jit(solution)/shard_map/ppermute | solution.py:251
  64.0 0.0 collective-permute-done.1.right_ref
  64.0 6.3 %all-to-all-done.3.all_ref = bf16[8,272,128]{2,1,0:T(8,128)(2,1)S(1)} async-done(((bf16[8,272,128]{2,1,0:T(8,128)(2,1)}), bf16[8,272,128]{2,1,0:T(8,128)(2,1)S(1)}, u32[]{:S(2)}, u32[]{:S(2)}) %all-to-all-start.3) | async-done | bytes 557088 | tf_op jit(solution)/shard_map/all_to_all | solution.py:250
  70.3 0.0 copy-start.1
  70.3 0.0 copy-start.2
  70.3 3.4 %shard_map.67 = bf16[4,80,256]{2,1,0:T(8,128)(2,1)S(1)} custom-call(s32[1]{0:T(128)} %bitcast.y_ref, bf16[4,64,384]{2,1,0:T(8,128)(2,1)S(1)} %all-to-all-done.1.in_ref.own_ref, bf16[8,272,128]{2,1,0:T(8,128)(2,1)S(1)} %all-to-all-done.3.all_ref), custom_call_target="tpu_custom_call" | custom-call | flops 4000000000 | bytes 2000000 | tf_op jit(solution)/shard_map/pallas_call | solution.py:255
  73.7 10.2 %all_to_all.26.zonal_ref = bf16[4,80,256]{2,1,0:T(8,128)(2,1)S(1)} all-to-all(bf16[4,80,256]{2,1,0:T(8,128)(2,1)S(1)} %shard_map.67), channel_id=1, replica_groups={{0,1,2,3},{4,5,6,7},{8,9,10,11},{12,13,14,15},{16,17,18,19},{20,21,22,2..., dimensions={0} | all-to-all | bytes 327680 | tf_op jit(solution)/shard_map/all_to_all | solution.py:258
  83.8 0.0 copy-done.1
  83.8 0.0 copy-done.2
  83.8 0.0 copy-start.3
  83.8 0.7 shard_map.68
  84.5 6.2 %collective-permute-start.2 = (bf16[3,80,512]{2,1,0:T(8,128)(2,1)S(1)}, bf16[3,80,512]{2,1,0:T(8,128)(2,1)S(1)}, u32[]{:S(2)}, u32[]{:S(2)}) collective-permute-start(bf16[3,80,512]{2,1,0:T(8,128)(2,1)S(1)} %get-tuple-element.31), channel_id=1, source_target_pairs={{0,32},{32,64},{64,96},{96,128},{128,160},{160,192},{192,224},{224... | collective-permute-start | bytes 737288 | tf_op jit(solution)/shard_map/ppermute | solution.py:262
  90.8 1.9 %collective-permute-start.3 = (bf16[3,80,512]{2,1,0:T(8,128)(2,1)S(1)}, bf16[3,80,512]{2,1,0:T(8,128)(2,1)S(1)}, u32[]{:S(2)}, u32[]{:S(2)}) collective-permute-start(bf16[3,80,512]{2,1,0:T(8,128)(2,1)S(1)} %get-tuple-element.32), channel_id=1, source_target_pairs={{32,0},{64,32},{96,64},{128,96},{160,128},{192,160},{224,192},{256... | collective-permute-start | bytes 737288 | tf_op jit(solution)/shard_map/ppermute | solution.py:263
  92.7 0.0 copy-done.3
  92.7 1.2 %collective-permute-done.2.before_ref = bf16[3,80,512]{2,1,0:T(8,128)(2,1)S(1)} collective-permute-done((bf16[3,80,512]{2,1,0:T(8,128)(2,1)S(1)}, bf16[3,80,512]{2,1,0:T(8,128)(2,1)S(1)}, u32[]{:S(2)}, u32[]{:S(2)}) %collective-permute-start.2) | collective-permute-done | bytes 245792 | tf_op jit(solution)/shard_map/ppermute | solution.py:262
  93.9 6.5 %collective-permute-done.3.after_ref = bf16[3,80,512]{2,1,0:T(8,128)(2,1)S(1)} collective-permute-done((bf16[3,80,512]{2,1,0:T(8,128)(2,1)S(1)}, bf16[3,80,512]{2,1,0:T(8,128)(2,1)S(1)}, u32[]{:S(2)}, u32[]{:S(2)}) %collective-permute-start.3) | collective-permute-done | bytes 245792 | tf_op jit(solution)/shard_map/ppermute | solution.py:263
  100.4 4.4 %shard_map.69 = bf16[4,64,512]{2,1,0:T(8,128)(2,1)} custom-call(bf16[4,80,512]{2,1,0:T(8,128)(2,1)S(1)} %get-tuple-element.30.mixed_hbm, bf16[3,80,512]{2,1,0:T(8,128)(2,1)S(1)} %collective-permute-done.2.before_ref, bf16[3,80,512]{2,1,0:T(8,128)(2,1)S(1)} %collective-permute-done.3.after_ref, f32[49,512]{1,0:T(8,128)S(1)} %reshape.7.conv_ref, ...), custom_call_target="tpu_custom_call" | custom-call | flops 2000000000 | bytes 2000000 | tf_op jit(solution)/shard_map/pallas_call | solution.py:264
  (4 shorter events, 0.0 us)
Async XLA Ops:
  0.0 24.6 %copy-start = (bf16[512,1152]{1,0:T(8,128)(2,1)S(1)}, bf16[512,1152]{1,0:T(8,128)(2,1)}, u32[]{:S(2)}) copy-start(bf16[512,1152]{1,0:T(8,128)(2,1)} %w_ref.2) | copy-start | bytes 3538948
  17.4 15.3 %all-to-all-start.1 = ((bf16[4,64,384]{2,1,0:T(8,128)(2,1)}), bf16[4,64,384]{2,1,0:T(8,128)(2,1)S(1)}, u32[]{:S(2)}, u32[]{:S(2)}) async-start(bf16[4,64,384]{2,1,0:T(8,128)(2,1)} %get-tuple-element.21), calls=%async_computation.1 | async-start | bytes 393216 | tf_op jit(solution)/shard_map/all_to_all | solution.py:245
  32.7 12.1 %all-to-all-start.2 = ((bf16[16,16,256]{2,1,0:T(8,128)(2,1)}), bf16[16,16,256]{2,1,0:T(8,128)(2,1)S(1)}, u32[]{:S(2)}, u32[]{:S(2)}) async-start(bf16[16,16,256]{2,1,0:T(8,128)(2,1)} %shard_map.66), calls=%async_computation.2 | async-start | bytes 262144 | tf_op jit(solution)/shard_map/all_to_all | solution.py:247
  44.8 25.5 %all-to-all-start.3 = ((bf16[8,272,128]{2,1,0:T(8,128)(2,1)}), bf16[8,272,128]{2,1,0:T(8,128)(2,1)S(1)}, u32[]{:S(2)}, u32[]{:S(2)}) async-start(bf16[8,272,128]{2,1,0:T(8,128)(2,1)} %shard_map.65), calls=%async_computation.3 | async-start | bytes 1114112 | tf_op jit(solution)/shard_map/all_to_all | solution.py:250
  51.7 12.3 %collective-permute-start = (bf16[16,768]{1,0:T(8,128)(2,1)S(1)}, bf16[16,768]{1,0:T(8,128)(2,1)S(1)}, u32[]{:S(2)}, u32[]{:S(2)}) collective-permute-start(bf16[16,768]{1,0:T(8,128)(2,1)S(1)} %pad_maximum_fusion), channel_id=1, source_target_pairs={{0,1},{1,2},{2,3},{3,4},{4,5},{5,6},{6,7},{7,8},{8,9},{9,10},{10,1... | collective-permute-start | bytes 73736 | tf_op jit(solution)/shard_map/ppermute | solution.py:251
  54.3 9.7 %collective-permute-start.1 = (bf16[16,768]{1,0:T(8,128)(2,1)S(1)}, bf16[16,768]{1,0:T(8,128)(2,1)S(1)}, u32[]{:S(2)}, u32[]{:S(2)}) collective-permute-start(bf16[16,768]{1,0:T(8,128)(2,1)S(1)} %pad_maximum_fusion.1), channel_id=1, source_target_pairs={{1,0},{2,1},{3,2},{4,3},{5,4},{6,5},{7,6},{8,7},{9,8},{10,9},{11,1... | collective-permute-start | bytes 73736 | tf_op jit(solution)/shard_map/ppermute | solution.py:252
  70.3 13.5 %copy-start.1 = (bf16[4,64,512]{2,1,0:T(8,128)(2,1)S(1)}, bf16[4,64,512]{2,1,0:T(8,128)(2,1)}, u32[]{:S(2)}) copy-start(bf16[4,64,512]{2,1,0:T(8,128)(2,1)} %field_ref.1) | copy-start | bytes 786436
  70.3 13.5 %copy-start.2 = (bf16[512,512]{1,0:T(8,128)(2,1)S(1)}, bf16[512,512]{1,0:T(8,128)(2,1)}, u32[]{:S(2)}) copy-start(bf16[512,512]{1,0:T(8,128)(2,1)} %w_ref.3) | copy-start | bytes 1572868
  83.8 8.9 %copy-start.3 = (f32[7,7,512]{2,1,0:T(8,128)S(1)}, f32[7,7,512]{2,1,0:T(8,128)}, u32[]{:S(2)}) copy-start(f32[7,7,512]{2,1,0:T(8,128)} %param.9) | copy-start | bytes 301060
  84.5 9.4 %collective-permute-start.2 = (bf16[3,80,512]{2,1,0:T(8,128)(2,1)S(1)}, bf16[3,80,512]{2,1,0:T(8,128)(2,1)S(1)}, u32[]{:S(2)}, u32[]{:S(2)}) collective-permute-start(bf16[3,80,512]{2,1,0:T(8,128)(2,1)S(1)} %get-tuple-element.31), channel_id=1, source_target_pairs={{0,32},{32,64},{64,96},{96,128},{128,160},{160,192},{192,224},{224... | collective-permute-start | bytes 737288 | tf_op jit(solution)/shard_map/ppermute | solution.py:262
  90.8 9.6 %collective-permute-start.3 = (bf16[3,80,512]{2,1,0:T(8,128)(2,1)S(1)}, bf16[3,80,512]{2,1,0:T(8,128)(2,1)S(1)}, u32[]{:S(2)}, u32[]{:S(2)}) collective-permute-start(bf16[3,80,512]{2,1,0:T(8,128)(2,1)S(1)} %get-tuple-element.32), channel_id=1, source_target_pairs={{32,0},{64,32},{96,64},{128,96},{160,128},{192,160},{224,192},{256... | collective-permute-start | bytes 737288 | tf_op jit(solution)/shard_map/ppermute | solution.py:263

commit v5 on v3

--- a/solution.py
+++ b/solution.py
@@ -173,7 +173,7 @@
         out_ref[:, :, lanes] = both.astype(BF)
 
 
-def mix_kernel(zonal_ref, merid_ref, left_ref, right_ref, field_ref, w_ref, mixed_ref, up_ref, down_ref):
+def mix_kernel(odd_ref, zonal_ref, merid_ref, left_ref, right_ref, field_ref, w_ref, mixed_ref, far_ref, near_ref):
     rows = R * WIDE
     merid = merid_ref[...].astype(F32).reshape(LAT * MROWS, 256).astype(BF)
     dims = (R, WIDE, LAT * MROWS)
@@ -186,46 +186,66 @@
     wide = widened(left_ref[...], field_ref[...], right_ref[...])
     mixed = (wide + attended.reshape(R, WIDE, C)).astype(BF)
     mixed_ref[...] = mixed
-    up_ref[...] = mixed[0:3]
-    down_ref[...] = mixed[1:4]
+    odd = odd_ref[0] == 1
+
+    @pl.when(odd)
+    def after_is_far():
+        far_ref[...] = mixed[1:4]
+        near_ref[...] = mixed[0:3]
+
+    @pl.when(jnp.logical_not(odd))
+    def before_is_far():
+        far_ref[...] = mixed[0:3]
+        near_ref[...] = mixed[1:4]
+
+
+def conv_part(rows, conv_ref, lanes, r):
+    total = None
+    for b in range(7):
+        column = None
+        for a in range(7):
+            if r + a in rows:
+                term = rows[r + a] * conv_ref[a * 7 + b, lanes][None, :]
+                column = term if column is None else column + term
+        moved = column[b + 5 : b + 5 + W]
+        total = moved if total is None else total + moved
+    return total
+
+
+def own_conv_kernel(mixed_ref, conv_ref, out_ref):
+    for lane in range(0, C, 128):
+        lanes = slice(lane, lane + 128)
+        rows = {3 + i: mixed_ref[i, :, lanes].astype(F32) for i in range(R)}
+        for r in range(R):
+            out_ref[r * W : (r + 1) * W, lanes] = conv_part(rows, conv_ref, lanes, r)
 
 
 def block_kernel(
-    mixed_hbm, before_ref, after_ref, conv_ref, w_in_hbm, w_back_hbm, out_ref,
+    odd_ref, mixed_hbm, own_ref, far_ref, near_ref, conv_ref, w_in_hbm, w_back_hbm, out_ref,
     mixed_ref, w_in_ref, w_back_ref, conv_out, sems,
 ):
-    pairs = ((mixed_hbm, mixed_ref), (w_in_hbm, w_in_ref), (w_back_hbm, w_back_ref))
+    pairs = ((w_in_hbm, w_in_ref), (w_back_hbm, w_back_ref), (mixed_hbm, mixed_ref))
     loads = [pltpu.make_async_copy(a, b, sems.at[i]) for i, (a, b) in enumerate(pairs)]
     for load in loads:
         load.start()
-    for part in range(2):
-        if part == 1:
-            loads[0].wait()
-        for lane in range(0, C, 128):
-            lanes = slice(lane, lane + 128)
-            if part == 0:
-                rows = {i: before_ref[i, :, lanes].astype(F32) for i in range(3)}
-                rows.update({7 + i: after_ref[i, :, lanes].astype(F32) for i in range(3)})
-            else:
-                rows = {3 + i: mixed_ref[i, :, lanes].astype(F32) for i in range(R)}
-            for r in range(R):
-                total = None
-                for b in range(7):
-                    column = None
-                    for a in range(7):
-                        if r + a in rows:
-                            term = rows[r + a] * conv_ref[a * 7 + b, lanes][None, :]
-                            column = term if column is None else column + term
-                    moved = column[b + 5 : b + 5 + W]
-                    total = moved if total is None else total + moved
-                here = (slice(r * W, (r + 1) * W), lanes)
-                conv_out[here] = total if part == 0 else conv_out[here] + total
+    odd = odd_ref[0] == 1
+    for lane in range(0, C, 128):
+        lanes = slice(lane, lane + 128)
+        rows = {}
+        for i in range(3):
+            far, near = far_ref[i, :, lanes].astype(F32), near_ref[i, :, lanes].astype(F32)
+            rows[i] = jnp.where(odd, near, far)
+            rows[7 + i] = jnp.where(odd, far, near)
+        for r in range(R):
+            here = (slice(r * W, (r + 1) * W), lanes)
+            conv_out[here] = own_ref[here] + conv_part(rows, conv_ref, lanes, r)
     normed = layer_norm(conv_out[...]).astype(BF)
-    loads[1].wait()
+    loads[0].wait()
     hidden = mm(normed, w_in_ref[...])
     hidden = 0.5 * hidden * (1.0 + lax.erf(hidden * math.sqrt(0.5)))
+    loads[1].wait()
+    back = mm(hidden.astype(BF), w_back_ref[...])
     loads[2].wait()
-    back = mm(hidden.astype(BF), w_back_ref[...])
     own = mixed_ref[...].astype(F32)[:, E : E + W].reshape(CELLS, C)
     out_ref[...] = (own + back).astype(BF).reshape(R, W, C)
 
@@ -233,10 +253,14 @@
 def per_device(field, w_qkv, w_out, conv_w, w_in, w_back):
     right = [(i, (i + 1) % LON) for i in range(LON)]
     left = [(j, i) for i, j in right]
-    down = [(i, i + 1) for i in range(LAT - 1)]
-    up = [(j, i) for i, j in down]
+    near_pairs = [(i, i + 1) for i in range(0, LAT, 2)]
+    far_pairs = [(i, i + 1) for i in range(1, LAT - 1, 2)]
+    near_pairs, far_pairs = (pairs + [(j, i) for i, j in pairs] for pairs in (near_pairs, far_pairs))
     along_y = [[y * ZS + z for y in range(YS)] for z in range(ZS)]
     along_z = [[y * ZS + z for z in range(ZS)] for y in range(YS)]
+    y = (lax.axis_index("lon").astype(jnp.int32) >> 2).reshape(1)
+    odd = (lax.axis_index("lat").astype(jnp.int32) & 1).reshape(1)
+    field, y, odd = lax.optimization_barrier((field, y, odd))
     row, first, last = call(
         zonal_project_kernel,
         (shape(R, W, 384), shape(R * E, C), shape(R * E, C)),
@@ -259,23 +283,27 @@
     )
     slots, merid = lax.optimization_barrier((slots, merid))
     merid = lax.all_to_all(merid, "lat", 0, 0)
-    y = (lax.axis_index("lon") // ZS).astype(jnp.int32).reshape(1)
     zonal = call(
         zonal_kernel, shape(ZS, WIDE, 256), 4_000_000_000, vmem=24, in_specs=[SMEM, VMEM, VMEM]
     )(y, row, slots)
     zonal = lax.all_to_all(zonal, "lon", 0, 0, axis_index_groups=along_z)
     merid = call(merid_kernel, shape(LAT, MROWS, 256), 1_000_000_000)(merid, w_qkv)
     merid = lax.all_to_all(merid, "lat", 0, 0)
-    mixed, first, last = call(
-        mix_kernel, (shape(R, WIDE, C), shape(3, WIDE, C), shape(3, WIDE, C)), 800_000_000
-    )(zonal, merid, field_left, field_right, field, w_out)
-    before = lax.ppermute(last, "lat", down)
-    after = lax.ppermute(first, "lat", up)
+    mixed, far, near = call(
+        mix_kernel,
+        (shape(R, WIDE, C), shape(3, WIDE, C), shape(3, WIDE, C)),
+        800_000_000,
+        in_specs=[SMEM] + [VMEM] * 6,
+    )(odd, zonal, merid, field_left, field_right, field, w_out)
+    near = lax.ppermute(near, "lat", near_pairs)
+    far = lax.ppermute(far, "lat", far_pairs)
+    conv_w = conv_w.reshape(49, C)
+    own = call(own_conv_kernel, jax.ShapeDtypeStruct((CELLS, C), F32), 1_000_000_000)(mixed, conv_w)
     return call(
         block_kernel,
         shape(R, W, C),
         2_000_000_000,
-        in_specs=[ANY, VMEM, VMEM, VMEM, ANY, ANY],
+        in_specs=[SMEM, ANY, VMEM, VMEM, VMEM, VMEM, ANY, ANY],
         scratch_shapes=[
             pltpu.VMEM((R, WIDE, C), BF),
             pltpu.VMEM(w_in.shape, BF),
@@ -283,7 +311,7 @@
             pltpu.VMEM((CELLS, C), F32),
             pltpu.SemaphoreType.DMA((3,)),
         ],
-    )(mixed, before, after, conv_w.reshape(49, C), in_hbm(w_in), in_hbm(w_back))
+    )(odd, mixed, own, far, near, conv_w, in_hbm(w_in), in_hbm(w_back))
 
 
 def solution(mesh):

time: 103 us -> 97.4 us (0.946)
  waiting for transfers between devices: 22.6 us -> 17.1 us
    ppermute x2, waiting for transfers between devices: 7.66 us -> 2.15 us  [the longest x1 2.15 us: per_device(): far = lax.ppermute(far, 'lat', far_pairs)]
    pallas_call x1 -> x2, Pallas kernels: 4.39 us -> 4.54 us  [the longest x1 3.17 us: per_device(): call(block_kernel, shape(R, W, C), 2000000000, in_specs=[SMEM, ANY, VMEM,...]
  transfers between devices with their start and end apart: 7 -> 7, of which waited for: 5 -> 4; matrix products, arithmetic and copies ran while one was open for 0% -> 0% of each run, Pallas kernels for 7% -> 9%
where the time goes in v5:
time: 97.4 us; the launch traced here: 95.9 us
  starting transfers between devices  34.1 us (35%)
  blocking collectives  29.6 us (30%)
  waiting for transfers between devices  17.1 us (18%)
  Pallas kernels  14.9 us (15%)
    all_to_all x1, blocking collectives, per_device(): row = lax.all_to_all(row, 'lon', 0, 0, axis_index_groups=along_z)  17.9 us
    all_to_all x1, blocking collectives, per_device(): merid = lax.all_to_all(merid, 'lat', 0, 0)  11.7 us
    all_to_all x1, starting transfers between devices, per_device(): merid = lax.all_to_all(merid, 'lat', 0, 0)  8.4 us
    ppermute x1, starting transfers between devices, per_device(): field_right = lax.ppermute(first, 'lon', left)  7.58 us
    all_to_all x1, starting transfers between devices, per_device(): slots = lax.all_to_all(slots, 'lon', 0, 0, axis_index_groups=along_y)  6.81 us
    all_to_all x1, waiting for transfers between devices, per_device(): zonal = lax.all_to_all(zonal, 'lon', 0, 0, axis_index_groups=along_z)  5.92 us
    ppermute x1, waiting for transfers between devices, per_device(): field_left = lax.ppermute(last, 'lon', right)  5.65 us
    ppermute x1, starting transfers between devices, per_device(): far = lax.ppermute(far, 'lat', far_pairs)  4.13 us
  transfers between devices with their start and end apart: 7, of which 4 were waited for; matrix products, arithmetic and copies ran while one was open for 0% of the time, Pallas kernels for 9%

profile of v5, /device:TPU:7, one launch (start us, length us, event | category | flops | bytes accessed | tf_op | source)
XLA Modules:
  0.0 95.9 jit_solution(6991206488555814193)
XLA Ops:
  0.0 1.7 %shard_map.64 = (bf16[4,64,384]{2,1,0:T(8,128)(2,1)S(1)}, bf16[32,512]{1,0:T(8,128)(2,1)S(1)}, bf16[32,512]{1,0:T(8,128)(2,1)S(1)}) custom-call(bf16[4,64,512]{2,1,0:T(8,128)(2,1)} %field_ref.1, bf16[512,1152]{1,0:T(8,128)(2,1)} %w_ref.2), custom_call_target="tpu_custom_call" | custom-call | flops 200000000 | bytes 2000000 | tf_op jit(solution)/shard_map/pallas_call | solution.py:264
  1.7 0.0 copy-start.1
  1.7 17.9 %all_to_all.25.in_ref.own_ref = bf16[4,64,384]{2,1,0:T(8,128)(2,1)S(1)} all-to-all(bf16[4,64,384]{2,1,0:T(8,128)(2,1)S(1)} %get-tuple-element.19), channel_id=1, replica_groups={{0,1,2,3},{4,5,6,7},{8,9,10,11},{12,13,14,15},{16,17,18,19},{20,21,22,2..., dimensions={0} | all-to-all | bytes 393216 | tf_op jit(solution)/shard_map/all_to_all | solution.py:276
  19.6 0.9 shard_map.65
  20.5 6.8 %all-to-all-start.1 = ((bf16[8,272,128]{2,1,0:T(8,128)(2,1)}), bf16[8,272,128]{2,1,0:T(8,128)(2,1)S(1)}, u32[]{:S(2)}, u32[]{:S(2)}) async-start(bf16[8,272,128]{2,1,0:T(8,128)(2,1)} %shard_map.65), calls=%async_computation.1 | async-start | bytes 1114112 | tf_op jit(solution)/shard_map/all_to_all | solution.py:278
  27.3 1.9 %collective-permute-start = (bf16[32,512]{1,0:T(8,128)(2,1)S(1)}, bf16[32,512]{1,0:T(8,128)(2,1)S(1)}, u32[]{:S(2)}, u32[]{:S(2)}) collective-permute-start(bf16[32,512]{1,0:T(8,128)(2,1)S(1)} %get-tuple-element.20), channel_id=1, source_target_pairs={{0,1},{1,2},{2,3},{3,4},{4,5},{5,6},{6,7},{7,8},{8,9},{9,10},{10,1... | collective-permute-start | bytes 98312 | tf_op jit(solution)/shard_map/ppermute | solution.py:279
  29.2 7.6 %collective-permute-start.1 = (bf16[32,512]{1,0:T(8,128)(2,1)S(1)}, bf16[32,512]{1,0:T(8,128)(2,1)S(1)}, u32[]{:S(2)}, u32[]{:S(2)}) collective-permute-start(bf16[32,512]{1,0:T(8,128)(2,1)S(1)} %get-tuple-element.21), channel_id=1, source_target_pairs={{1,0},{2,1},{3,2},{4,3},{5,4},{6,5},{7,6},{8,7},{9,8},{10,9},{11,1... | collective-permute-start | bytes 98312 | tf_op jit(solution)/shard_map/ppermute | solution.py:280
  36.8 5.6 %collective-permute-done.left_ref = bf16[32,512]{1,0:T(8,128)(2,1)S(1)} collective-permute-done((bf16[32,512]{1,0:T(8,128)(2,1)S(1)}, bf16[32,512]{1,0:T(8,128)(2,1)S(1)}, u32[]{:S(2)}, u32[]{:S(2)}) %collective-permute-start) | collective-permute-done | bytes 32800 | tf_op jit(solution)/shard_map/ppermute | solution.py:279
  42.4 0.0 collective-permute-done.1.right_ref
  42.4 0.0 copy-done.1
  42.4 1.3 %shard_map.66 = bf16[16,24,512]{2,1,0:T(8,128)(2,1)} custom-call(bf16[4,64,512]{2,1,0:T(8,128)(2,1)S(1)} %copy-done.1, bf16[32,512]{1,0:T(8,128)(2,1)S(1)} %collective-permute-done.left_ref, bf16[32,512]{1,0:T(8,128)(2,1)S(1)} %collective-permute-done.1.right_ref), custom_call_target="tpu_custom_call" | custom-call | flops 300000000 | bytes 2000000 | tf_op jit(solution)/shard_map/pallas_call | solution.py:281
  43.8 0.0 all-to-all-done.1.all_ref
  43.8 8.4 %all-to-all-start.3 = ((bf16[16,24,512]{2,1,0:T(8,128)(2,1)}), bf16[16,24,512]{2,1,0:T(8,128)(2,1)S(1)}, u32[]{:S(2)}, u32[]{:S(2)}) async-start(bf16[16,24,512]{2,1,0:T(8,128)(2,1)} %shard_map.66), calls=%async_computation.3 | async-start | bytes 786432 | tf_op jit(solution)/shard_map/all_to_all | solution.py:285
  52.2 0.0 copy-start
  52.2 4.0 %shard_map.67 = bf16[4,80,256]{2,1,0:T(8,128)(2,1)} custom-call(s32[1]{0:T(128)} %bitcast.y_ref, bf16[4,64,384]{2,1,0:T(8,128)(2,1)S(1)} %all_to_all.25.in_ref.own_ref, bf16[8,272,128]{2,1,0:T(8,128)(2,1)S(1)} %all-to-all-done.1.all_ref), custom_call_target="tpu_custom_call" | custom-call | flops 4000000000 | bytes 2000000 | tf_op jit(solution)/shard_map/pallas_call | solution.py:286
  56.2 3.4 %all-to-all-done.3.in_ref = bf16[16,24,512]{2,1,0:T(8,128)(2,1)S(1)} async-done(((bf16[16,24,512]{2,1,0:T(8,128)(2,1)}), bf16[16,24,512]{2,1,0:T(8,128)(2,1)S(1)}, u32[]{:S(2)}, u32[]{:S(2)}) %all-to-all-start.3) | async-done | bytes 393248 | tf_op jit(solution)/shard_map/all_to_all | solution.py:285
  59.6 3.3 %all-to-all-start.2 = ((bf16[4,80,256]{2,1,0:T(8,128)(2,1)}), bf16[4,80,256]{2,1,0:T(8,128)(2,1)S(1)}, u32[]{:S(2)}, u32[]{:S(2)}) async-start(bf16[4,80,256]{2,1,0:T(8,128)(2,1)} %shard_map.67), calls=%async_computation.2 | async-start | bytes 327680 | tf_op jit(solution)/shard_map/all_to_all | solution.py:289
  63.0 0.0 copy-done
  63.0 0.0 copy-start.2
  63.0 1.9 %shard_map.68 = bf16[16,24,256]{2,1,0:T(8,128)(2,1)S(1)} custom-call(bf16[16,24,512]{2,1,0:T(8,128)(2,1)S(1)} %all-to-all-done.3.in_ref, bf16[512,1152]{1,0:T(8,128)(2,1)S(1)} %copy-done), custom_call_target="tpu_custom_call" | custom-call | flops 1000000000 | bytes 2000000 | tf_op jit(solution)/shard_map/pallas_call | solution.py:290
  64.9 5.9 %all-to-all-done.2.zonal_ref = bf16[4,80,256]{2,1,0:T(8,128)(2,1)S(1)} async-done(((bf16[4,80,256]{2,1,0:T(8,128)(2,1)}), bf16[4,80,256]{2,1,0:T(8,128)(2,1)S(1)}, u32[]{:S(2)}, u32[]{:S(2)}) %all-to-all-start.2) | async-done | bytes 163872 | tf_op jit(solution)/shard_map/all_to_all | solution.py:289
  70.8 11.7 %all_to_all.26.merid_ref = bf16[16,24,256]{2,1,0:T(8,128)(2,1)S(1)} all-to-all(bf16[16,24,256]{2,1,0:T(8,128)(2,1)S(1)} %shard_map.68), channel_id=1, replica_groups=mesh['lat'=16,'lon'=32] {'lat'}, dimensions={0} | all-to-all | bytes 393216 | tf_op jit(solution)/shard_map/all_to_all | solution.py:291
  82.5 0.0 copy-done.2
  82.5 0.0 copy-start.3
  82.5 0.6 shard_map.69
  83.1 4.1 %collective-permute-start.2 = (bf16[3,80,512]{2,1,0:T(8,128)(2,1)S(1)}, bf16[3,80,512]{2,1,0:T(8,128)(2,1)S(1)}, u32[]{:S(2)}, u32[]{:S(2)}) collective-permute-start(bf16[3,80,512]{2,1,0:T(8,128)(2,1)S(1)} %get-tuple-element.25), channel_id=1, source_target_pairs={{32,64},{96,128},{160,192},{224,256},{288,320},{352,384},{416,448}... | collective-permute-start | bytes 737288 | tf_op jit(solution)/shard_map/ppermute | solution.py:299
  87.3 1.9 %collective-permute-start.3 = (bf16[3,80,512]{2,1,0:T(8,128)(2,1)S(1)}, bf16[3,80,512]{2,1,0:T(8,128)(2,1)S(1)}, u32[]{:S(2)}, u32[]{:S(2)}) collective-permute-start(bf16[3,80,512]{2,1,0:T(8,128)(2,1)S(1)} %get-tuple-element.26), channel_id=1, source_target_pairs={{0,32},{64,96},{128,160},{192,224},{256,288},{320,352},{384,416},{... | collective-permute-start | bytes 737288 | tf_op jit(solution)/shard_map/ppermute | solution.py:298
  89.2 0.0 copy-done.3
  89.2 1.4 %shard_map.70.own_ref = f32[256,512]{1,0:T(8,128)S(1)} custom-call(bf16[4,80,512]{2,1,0:T(8,128)(2,1)S(1)} %get-tuple-element.24.mixed_ref.mixed_hbm, f32[49,512]{1,0:T(8,128)S(1)} %reshape.11.conv_ref), custom_call_target="tpu_custom_call" | custom-call | flops 1000000000 | bytes 2000000 | tf_op jit(solution)/shard_map/pallas_call | solution.py:301
  90.6 2.2 %collective-permute-done.2.far_ref = bf16[3,80,512]{2,1,0:T(8,128)(2,1)S(1)} collective-permute-done((bf16[3,80,512]{2,1,0:T(8,128)(2,1)S(1)}, bf16[3,80,512]{2,1,0:T(8,128)(2,1)S(1)}, u32[]{:S(2)}, u32[]{:S(2)}) %collective-permute-start.2) | collective-permute-done | bytes 245792 | tf_op jit(solution)/shard_map/ppermute | solution.py:299
  92.8 0.0 collective-permute-done.3.near_ref
  92.8 3.2 %shard_map.71 = bf16[4,64,512]{2,1,0:T(8,128)(2,1)} custom-call(s32[1]{0:T(128)} %bitcast.1.odd_ref, bf16[4,80,512]{2,1,0:T(8,128)(2,1)S(1)} %get-tuple-element.24.mixed_ref.mixed_hbm, f32[256,512]{1,0:T(8,128)S(1)} %shard_map.70.own_ref, bf16[3,80,512]{2,1,0:T(8,128)(2,1)S(1)} %collective-permute-done.2.far_ref, ...), custom_call_target="tpu_custom_call" | custom-call | flops 2000000000 | bytes 2000000 | tf_op jit(solution)/shard_map/pallas_call | solution.py:302
  (1 shorter events, 0.0 us)
Async XLA Ops:
  1.7 40.8 %copy-start.1 = (bf16[4,64,512]{2,1,0:T(8,128)(2,1)S(1)}, bf16[4,64,512]{2,1,0:T(8,128)(2,1)}, u32[]{:S(2)}) copy-start(bf16[4,64,512]{2,1,0:T(8,128)(2,1)} %field_ref.1) | copy-start | bytes 786436
  20.5 23.3 %all-to-all-start.1 = ((bf16[8,272,128]{2,1,0:T(8,128)(2,1)}), bf16[8,272,128]{2,1,0:T(8,128)(2,1)S(1)}, u32[]{:S(2)}, u32[]{:S(2)}) async-start(bf16[8,272,128]{2,1,0:T(8,128)(2,1)} %shard_map.65), calls=%async_computation.1 | async-start | bytes 1114112 | tf_op jit(solution)/shard_map/all_to_all | solution.py:278
  27.3 15.2 %collective-permute-start = (bf16[32,512]{1,0:T(8,128)(2,1)S(1)}, bf16[32,512]{1,0:T(8,128)(2,1)S(1)}, u32[]{:S(2)}, u32[]{:S(2)}) collective-permute-start(bf16[32,512]{1,0:T(8,128)(2,1)S(1)} %get-tuple-element.20), channel_id=1, source_target_pairs={{0,1},{1,2},{2,3},{3,4},{4,5},{5,6},{6,7},{7,8},{8,9},{9,10},{10,1... | collective-permute-start | bytes 98312 | tf_op jit(solution)/shard_map/ppermute | solution.py:279
  29.2 13.2 %collective-permute-start.1 = (bf16[32,512]{1,0:T(8,128)(2,1)S(1)}, bf16[32,512]{1,0:T(8,128)(2,1)S(1)}, u32[]{:S(2)}, u32[]{:S(2)}) collective-permute-start(bf16[32,512]{1,0:T(8,128)(2,1)S(1)} %get-tuple-element.21), channel_id=1, source_target_pairs={{1,0},{2,1},{3,2},{4,3},{5,4},{6,5},{7,6},{8,7},{9,8},{10,9},{11,1... | collective-permute-start | bytes 98312 | tf_op jit(solution)/shard_map/ppermute | solution.py:280
  43.8 15.9 %all-to-all-start.3 = ((bf16[16,24,512]{2,1,0:T(8,128)(2,1)}), bf16[16,24,512]{2,1,0:T(8,128)(2,1)S(1)}, u32[]{:S(2)}, u32[]{:S(2)}) async-start(bf16[16,24,512]{2,1,0:T(8,128)(2,1)} %shard_map.66), calls=%async_computation.3 | async-start | bytes 786432 | tf_op jit(solution)/shard_map/all_to_all | solution.py:285
  52.2 10.8 %copy-start = (bf16[512,1152]{1,0:T(8,128)(2,1)S(1)}, bf16[512,1152]{1,0:T(8,128)(2,1)}, u32[]{:S(2)}) copy-start(bf16[512,1152]{1,0:T(8,128)(2,1)} %w_ref.2) | copy-start | bytes 3538948
  59.6 11.2 %all-to-all-start.2 = ((bf16[4,80,256]{2,1,0:T(8,128)(2,1)}), bf16[4,80,256]{2,1,0:T(8,128)(2,1)S(1)}, u32[]{:S(2)}, u32[]{:S(2)}) async-start(bf16[4,80,256]{2,1,0:T(8,128)(2,1)} %shard_map.67), calls=%async_computation.2 | async-start | bytes 327680 | tf_op jit(solution)/shard_map/all_to_all | solution.py:289
  63.0 19.5 %copy-start.2 = (bf16[512,512]{1,0:T(8,128)(2,1)S(1)}, bf16[512,512]{1,0:T(8,128)(2,1)}, u32[]{:S(2)}) copy-start(bf16[512,512]{1,0:T(8,128)(2,1)} %w_ref.3) | copy-start | bytes 1572868
  82.5 6.7 %copy-start.3 = (f32[7,7,512]{2,1,0:T(8,128)S(1)}, f32[7,7,512]{2,1,0:T(8,128)}, u32[]{:S(2)}) copy-start(f32[7,7,512]{2,1,0:T(8,128)} %param.9) | copy-start | bytes 301060
  83.1 9.6 %collective-permute-start.2 = (bf16[3,80,512]{2,1,0:T(8,128)(2,1)S(1)}, bf16[3,80,512]{2,1,0:T(8,128)(2,1)S(1)}, u32[]{:S(2)}, u32[]{:S(2)}) collective-permute-start(bf16[3,80,512]{2,1,0:T(8,128)(2,1)S(1)} %get-tuple-element.25), channel_id=1, source_target_pairs={{32,64},{96,128},{160,192},{224,256},{288,320},{352,384},{416,448}... | collective-permute-start | bytes 737288 | tf_op jit(solution)/shard_map/ppermute | solution.py:299
  87.3 5.5 %collective-permute-start.3 = (bf16[3,80,512]{2,1,0:T(8,128)(2,1)S(1)}, bf16[3,80,512]{2,1,0:T(8,128)(2,1)S(1)}, u32[]{:S(2)}, u32[]{:S(2)}) collective-permute-start(bf16[3,80,512]{2,1,0:T(8,128)(2,1)S(1)} %get-tuple-element.26), channel_id=1, source_target_pairs={{0,32},{64,96},{128,160},{192,224},{256,288},{320,352},{384,416},{... | collective-permute-start | bytes 737288 | tf_op jit(solution)/shard_map/ppermute | solution.py:298

commit v6 on v5

--- a/solution.py
+++ b/solution.py
@@ -17,6 +17,7 @@
 E = 8
 WIDE = W + 2 * E
 MC = WIDE // LAT
+EDGES = (1, LAT - 2)
 MROWS = 24
 YS = 8
 ZS = 4
@@ -90,15 +91,17 @@
     out_ref[:, :, 0:256] = mm(normed, wq_ref[...]).astype(BF).reshape(R, W, 256)
 
 
-def spread_kernel(in_ref, out_ref):
-    kv = in_ref[:, :, 256:384].reshape(SPAN, 128)
+def spread_kernel(in_ref, out_hbm, slot_ref, sems):
+    slot_ref[0:SPAN, :] = in_ref[:, :, 256:384].reshape(SPAN, 128)
     first = in_ref[0, :, 0:256].astype(F32)[0:E]
     last = in_ref[ZS - 1, :, 0:256].astype(F32)[W - E : W]
     edge = jnp.where(iota((E, 256), 0) < E // 2, first, last)
-    edge = jnp.concatenate([edge[:, 0:128], edge[:, 128:256]], axis=0).astype(BF)
-    for y in range(YS):
-        out_ref[y, 0:SPAN, :] = kv
-        out_ref[y, SPAN:KEYS, :] = edge
+    slot_ref[SPAN:KEYS, :] = jnp.concatenate([edge[:, 0:128], edge[:, 128:256]], axis=0).astype(BF)
+    copies = [pltpu.make_async_copy(slot_ref, out_hbm.at[y], sems.at[y]) for y in range(YS)]
+    for copy in copies:
+        copy.start()
+    for copy in copies:
+        copy.wait()
 
 
 def zonal_kernel(y_ref, own_ref, all_ref, out_ref):
@@ -135,17 +138,30 @@
     return jnp.concatenate([left, own.astype(F32), right], axis=1)
 
 
-def merid_slots():
-    dims = (LAT, MROWS, R * WIDE)
+def merid_own_kernel(field_ref, out_ref, edge_ref):
+    normed = layer_norm(field_ref[...].astype(F32).reshape(CELLS, C)).astype(BF)
+    dims = (LAT, MROWS, CELLS)
     m, i, u = iota(dims, 0), iota(dims, 1), iota(dims, 2)
-    cell = (i & 3) * WIDE + m * MC + (i >> 2)
-    return one_hot((cell == u) & (i < R * MC)).reshape(LAT * MROWS, R * WIDE)
-
-
-def merid_select_kernel(field_ref, left_ref, right_ref, out_ref):
-    wide = widened(left_ref[...], field_ref[...], right_ref[...]).reshape(R * WIDE, C)
-    normed = mm(merid_slots(), layer_norm(wide).astype(BF))
-    out_ref[...] = normed.reshape(LAT, MROWS, C).astype(BF)
+    c = m * MC + (i >> 2) - E
+    hit = ((i & 3) * W + c == u) & (c >= 0) & (c < W) & (i < R * MC)
+    slots = mm(one_hot(hit).reshape(LAT * MROWS, CELLS), normed).reshape(LAT, MROWS, C).astype(BF)
+    out_ref[...] = slots
+    edge_ref[0] = slots[EDGES[0]]
+    edge_ref[1] = slots[EDGES[1]]
+
+
+def merid_edge_kernel(slots_hbm, edge_ref, left_ref, right_ref, out_hbm, done_ref, sems):
+    copies = []
+    for n, (m, ref) in enumerate(zip(EDGES, (left_ref, right_ref))):
+        normed = layer_norm(ref[...].astype(F32)).astype(BF)
+        i, u = iota((MROWS, R * E), 0), iota((MROWS, R * E), 1)
+        c = m * MC + (i >> 2) - n * (W + E)
+        hit = ((i & 3) * E + c == u) & (c >= 0) & (c < E) & (i < R * MC)
+        done_ref[n] = (edge_ref[n].astype(F32) + mm(one_hot(hit), normed)).astype(BF)
+        copies.append(pltpu.make_async_copy(done_ref.at[n], out_hbm.at[m], sems.at[n]))
+        copies[n].start()
+    for copy in copies:
+        copy.wait()
 
 
 def merid_kernel(in_ref, w_ref, out_ref):
@@ -212,22 +228,25 @@
     return total
 
 
-def own_conv_kernel(mixed_ref, conv_ref, out_ref):
+def own_conv_kernel(
+    mixed_ref, conv_ref, w_in_hbm, w_back_hbm, out_ref, w_in_ref, w_back_ref, sems
+):
+    pairs = ((w_in_hbm, w_in_ref), (w_back_hbm, w_back_ref))
+    loads = [pltpu.make_async_copy(a, b, sems.at[i]) for i, (a, b) in enumerate(pairs)]
+    for load in loads:
+        load.start()
     for lane in range(0, C, 128):
         lanes = slice(lane, lane + 128)
         rows = {3 + i: mixed_ref[i, :, lanes].astype(F32) for i in range(R)}
         for r in range(R):
             out_ref[r * W : (r + 1) * W, lanes] = conv_part(rows, conv_ref, lanes, r)
+    for load in loads:
+        load.wait()
 
 
 def block_kernel(
-    odd_ref, mixed_hbm, own_ref, far_ref, near_ref, conv_ref, w_in_hbm, w_back_hbm, out_ref,
-    mixed_ref, w_in_ref, w_back_ref, conv_out, sems,
+    odd_ref, mixed_ref, own_ref, far_ref, near_ref, conv_ref, w_in_ref, w_back_ref, out_ref, conv_out
 ):
-    pairs = ((w_in_hbm, w_in_ref), (w_back_hbm, w_back_ref), (mixed_hbm, mixed_ref))
-    loads = [pltpu.make_async_copy(a, b, sems.at[i]) for i, (a, b) in enumerate(pairs)]
-    for load in loads:
-        load.start()
     odd = odd_ref[0] == 1
     for lane in range(0, C, 128):
         lanes = slice(lane, lane + 128)
@@ -240,12 +259,9 @@
             here = (slice(r * W, (r + 1) * W), lanes)
             conv_out[here] = own_ref[here] + conv_part(rows, conv_ref, lanes, r)
     normed = layer_norm(conv_out[...]).astype(BF)
-    loads[0].wait()
     hidden = mm(normed, w_in_ref[...])
     hidden = 0.5 * hidden * (1.0 + lax.erf(hidden * math.sqrt(0.5)))
-    loads[1].wait()
     back = mm(hidden.astype(BF), w_back_ref[...])
-    loads[2].wait()
     own = mixed_ref[...].astype(F32)[:, E : E + W].reshape(CELLS, C)
     out_ref[...] = (own + back).astype(BF).reshape(R, W, C)
 
@@ -274,13 +290,28 @@
         ],
     )(in_hbm(field), in_hbm(w_qkv))
     row = lax.all_to_all(row, "lon", 0, 0, axis_index_groups=along_z)
-    slots = call(spread_kernel, shape(YS, KEYS, 128), 10_000_000)(row)
+    slots = call(
+        spread_kernel,
+        shape(YS, KEYS, 128),
+        10_000_000,
+        out_specs=ANY,
+        scratch_shapes=[pltpu.VMEM((KEYS, 128), BF), pltpu.SemaphoreType.DMA((YS,))],
+    )(row)
     slots = lax.all_to_all(slots, "lon", 0, 0, axis_index_groups=along_y)
     field_left = lax.ppermute(last, "lon", right)
     field_right = lax.ppermute(first, "lon", left)
-    merid = call(merid_select_kernel, shape(LAT, MROWS, C), 300_000_000)(
-        field, field_left, field_right
-    )
+    merid, merid_edges = call(
+        merid_own_kernel, (shape(LAT, MROWS, C), shape(2, MROWS, C)), 300_000_000
+    )(field)
+    merid = call(
+        merid_edge_kernel,
+        shape(LAT, MROWS, C),
+        10_000_000,
+        in_specs=[ANY, VMEM, VMEM, VMEM],
+        out_specs=ANY,
+        input_output_aliases={0: 0},
+        scratch_shapes=[pltpu.VMEM((2, MROWS, C), BF), pltpu.SemaphoreType.DMA((2,))],
+    )(merid, merid_edges, field_left, field_right)
     slots, merid = lax.optimization_barrier((slots, merid))
     merid = lax.all_to_all(merid, "lat", 0, 0)
     zonal = call(
@@ -298,20 +329,20 @@
     near = lax.ppermute(near, "lat", near_pairs)
     far = lax.ppermute(far, "lat", far_pairs)
     conv_w = conv_w.reshape(49, C)
-    own = call(own_conv_kernel, jax.ShapeDtypeStruct((CELLS, C), F32), 1_000_000_000)(mixed, conv_w)
+    own, w_in, w_back = call(
+        own_conv_kernel,
+        (jax.ShapeDtypeStruct((CELLS, C), F32), shape(*w_in.shape), shape(*w_back.shape)),
+        1_000_000_000,
+        in_specs=[VMEM, VMEM, ANY, ANY],
+        scratch_shapes=[pltpu.SemaphoreType.DMA((2,))],
+    )(mixed, conv_w, in_hbm(w_in), in_hbm(w_back))
     return call(
         block_kernel,
         shape(R, W, C),
         2_000_000_000,
-        in_specs=[SMEM, ANY, VMEM, VMEM, VMEM, VMEM, ANY, ANY],
-        scratch_shapes=[
-            pltpu.VMEM((R, WIDE, C), BF),
-            pltpu.VMEM(w_in.shape, BF),
-            pltpu.VMEM(w_back.shape, BF),
-            pltpu.VMEM((CELLS, C), F32),
-            pltpu.SemaphoreType.DMA((3,)),
-        ],
-    )(odd, mixed, own, far, near, conv_w, in_hbm(w_in), in_hbm(w_back))
+        in_specs=[SMEM] + [VMEM] * 7,
+        scratch_shapes=[pltpu.VMEM((CELLS, C), F32)],
+    )(odd, mixed, own, far, near, conv_w, w_in, w_back)
 
 
 def solution(mesh):

time: 97.4 us -> 96.8 us (level)
  waiting for transfers between devices: 17.1 us -> 15.7 us
    ppermute x1, waiting for transfers between devices: 5.65 us -> 4.41 us  [per_device(): field_left = lax.ppermute(last, 'lon', right)]
    pallas_call x4 -> x5, Pallas kernels: 6.74 us -> 7.49 us  [the longest x1 2.87 us: per_device(): call(block_kernel, shape(R, W, C), 2000000000, in_specs=[SMEM] + [VMEM] *...]
  transfers between devices with their start and end apart: 7 -> 7, of which waited for: 4 -> 4; matrix products, arithmetic and copies ran while one was open for 0% -> 0% of each run, Pallas kernels for 9% -> 10%
where the time goes in v6:
time: 96.8 us; the launch traced here: 95.7 us
  starting transfers between devices  34.5 us (36%)
  blocking collectives  29.6 us (31%)
  Pallas kernels  15.7 us (16%)
  waiting for transfers between devices  15.7 us (16%)
    all_to_all x1, blocking collectives, per_device(): row = lax.all_to_all(row, 'lon', 0, 0, axis_index_groups=along_z)  17.9 us
    all_to_all x1, blocking collectives, per_device(): merid = lax.all_to_all(merid, 'lat', 0, 0)  11.7 us
    all_to_all x1, starting transfers between devices, per_device(): merid = lax.all_to_all(merid, 'lat', 0, 0)  8.79 us
    ppermute x1, starting transfers between devices, per_device(): field_right = lax.ppermute(first, 'lon', left)  7.58 us
    all_to_all x1, starting transfers between devices, per_device(): slots = lax.all_to_all(slots, 'lon', 0, 0, axis_index_groups=along_y)  6.83 us
    all_to_all x1, waiting for transfers between devices, per_device(): zonal = lax.all_to_all(zonal, 'lon', 0, 0, axis_index_groups=along_z)  5.92 us
    ppermute x1, waiting for transfers between devices, per_device(): field_left = lax.ppermute(last, 'lon', right)  4.41 us
    ppermute x1, starting transfers between devices, per_device(): far = lax.ppermute(far, 'lat', far_pairs)  4.12 us
  transfers between devices with their start and end apart: 7, of which 4 were waited for; matrix products, arithmetic and copies ran while one was open for 0% of the time, Pallas kernels for 10%

profile of v6, /device:TPU:7, one launch (start us, length us, event | category | flops | bytes accessed | tf_op | source)
XLA Modules:
  0.0 95.7 jit_solution(2225228604462037454)
XLA Ops:
  0.0 1.7 %shard_map.64 = (bf16[4,64,384]{2,1,0:T(8,128)(2,1)S(1)}, bf16[32,512]{1,0:T(8,128)(2,1)S(1)}, bf16[32,512]{1,0:T(8,128)(2,1)S(1)}) custom-call(bf16[4,64,512]{2,1,0:T(8,128)(2,1)} %field_ref.1, bf16[512,1152]{1,0:T(8,128)(2,1)} %w_ref.2), custom_call_target="tpu_custom_call" | custom-call | flops 200000000 | bytes 2000000 | tf_op jit(solution)/shard_map/pallas_call | solution.py:280
  1.7 0.0 copy-start.1
  1.7 17.9 %all_to_all.25.in_ref.own_ref = bf16[4,64,384]{2,1,0:T(8,128)(2,1)S(1)} all-to-all(bf16[4,64,384]{2,1,0:T(8,128)(2,1)S(1)} %get-tuple-element.24), channel_id=1, replica_groups={{0,1,2,3},{4,5,6,7},{8,9,10,11},{12,13,14,15},{16,17,18,19},{20,21,22,2..., dimensions={0} | all-to-all | bytes 393216 | tf_op jit(solution)/shard_map/all_to_all | solution.py:292
  19.6 0.9 shard_map.65
  20.5 6.8 %all-to-all-start.1 = ((bf16[8,272,128]{2,1,0:T(8,128)(2,1)}), bf16[8,272,128]{2,1,0:T(8,128)(2,1)S(1)}, u32[]{:S(2)}, u32[]{:S(2)}) async-start(bf16[8,272,128]{2,1,0:T(8,128)(2,1)} %shard_map.65), calls=%async_computation.1 | async-start | bytes 1114112 | tf_op jit(solution)/shard_map/all_to_all | solution.py:300
  27.3 1.9 %collective-permute-start = (bf16[32,512]{1,0:T(8,128)(2,1)S(1)}, bf16[32,512]{1,0:T(8,128)(2,1)S(1)}, u32[]{:S(2)}, u32[]{:S(2)}) collective-permute-start(bf16[32,512]{1,0:T(8,128)(2,1)S(1)} %get-tuple-element.27), channel_id=1, source_target_pairs={{0,1},{1,2},{2,3},{3,4},{4,5},{5,6},{6,7},{7,8},{8,9},{9,10},{10,1... | collective-permute-start | bytes 98312 | tf_op jit(solution)/shard_map/ppermute | solution.py:301
  29.2 7.6 %collective-permute-start.1 = (bf16[32,512]{1,0:T(8,128)(2,1)S(1)}, bf16[32,512]{1,0:T(8,128)(2,1)S(1)}, u32[]{:S(2)}, u32[]{:S(2)}) collective-permute-start(bf16[32,512]{1,0:T(8,128)(2,1)S(1)} %get-tuple-element.28), channel_id=1, source_target_pairs={{1,0},{2,1},{3,2},{4,3},{5,4},{6,5},{7,6},{8,7},{9,8},{10,9},{11,1... | collective-permute-start | bytes 98312 | tf_op jit(solution)/shard_map/ppermute | solution.py:302
  36.8 0.0 copy-done.1
  36.8 1.2 %shard_map.66 = (bf16[16,24,512]{2,1,0:T(8,128)(2,1)}, bf16[2,24,512]{2,1,0:T(8,128)(2,1)S(1)}) custom-call(bf16[4,64,512]{2,1,0:T(8,128)(2,1)S(1)} %copy-done.1), custom_call_target="tpu_custom_call" | custom-call | flops 300000000 | bytes 2000000 | tf_op jit(solution)/shard_map/pallas_call | solution.py:303
  38.1 4.4 %collective-permute-done.left_ref = bf16[32,512]{1,0:T(8,128)(2,1)S(1)} collective-permute-done((bf16[32,512]{1,0:T(8,128)(2,1)S(1)}, bf16[32,512]{1,0:T(8,128)(2,1)S(1)}, u32[]{:S(2)}, u32[]{:S(2)}) %collective-permute-start) | collective-permute-done | bytes 32800 | tf_op jit(solution)/shard_map/ppermute | solution.py:301
  42.5 0.0 collective-permute-done.1.right_ref
  42.5 0.9 shard_map.67
  43.4 0.0 all-to-all-done.1.all_ref
  43.4 8.8 %all-to-all-start.3 = ((bf16[16,24,512]{2,1,0:T(8,128)(2,1)}), bf16[16,24,512]{2,1,0:T(8,128)(2,1)S(1)}, u32[]{:S(2)}, u32[]{:S(2)}) async-start(bf16[16,24,512]{2,1,0:T(8,128)(2,1)} %shard_map.67), calls=%async_computation.3 | async-start | bytes 786432 | tf_op jit(solution)/shard_map/all_to_all | solution.py:316
  52.2 0.0 copy-start
  52.2 4.0 %shard_map.68 = bf16[4,80,256]{2,1,0:T(8,128)(2,1)} custom-call(s32[1]{0:T(128)} %bitcast.y_ref, bf16[4,64,384]{2,1,0:T(8,128)(2,1)S(1)} %all_to_all.25.in_ref.own_ref, bf16[8,272,128]{2,1,0:T(8,128)(2,1)S(1)} %all-to-all-done.1.all_ref), custom_call_target="tpu_custom_call" | custom-call | flops 4000000000 | bytes 2000000 | tf_op jit(solution)/shard_map/pallas_call | solution.py:317
  56.3 3.4 %all-to-all-done.3.in_ref = bf16[16,24,512]{2,1,0:T(8,128)(2,1)S(1)} async-done(((bf16[16,24,512]{2,1,0:T(8,128)(2,1)}), bf16[16,24,512]{2,1,0:T(8,128)(2,1)S(1)}, u32[]{:S(2)}, u32[]{:S(2)}) %all-to-all-start.3) | async-done | bytes 393248 | tf_op jit(solution)/shard_map/all_to_all | solution.py:316
  59.7 3.3 %all-to-all-start.2 = ((bf16[4,80,256]{2,1,0:T(8,128)(2,1)}), bf16[4,80,256]{2,1,0:T(8,128)(2,1)S(1)}, u32[]{:S(2)}, u32[]{:S(2)}) async-start(bf16[4,80,256]{2,1,0:T(8,128)(2,1)} %shard_map.68), calls=%async_computation.2 | async-start | bytes 327680 | tf_op jit(solution)/shard_map/all_to_all | solution.py:320
  63.0 0.0 copy-done
  63.0 0.0 copy-start.2
  63.0 1.9 %shard_map.69 = bf16[16,24,256]{2,1,0:T(8,128)(2,1)S(1)} custom-call(bf16[16,24,512]{2,1,0:T(8,128)(2,1)S(1)} %all-to-all-done.3.in_ref, bf16[512,1152]{1,0:T(8,128)(2,1)S(1)} %copy-done), custom_call_target="tpu_custom_call" | custom-call | flops 1000000000 | bytes 2000000 | tf_op jit(solution)/shard_map/pallas_call | solution.py:321
  64.9 5.9 %all-to-all-done.2.zonal_ref = bf16[4,80,256]{2,1,0:T(8,128)(2,1)S(1)} async-done(((bf16[4,80,256]{2,1,0:T(8,128)(2,1)}), bf16[4,80,256]{2,1,0:T(8,128)(2,1)S(1)}, u32[]{:S(2)}, u32[]{:S(2)}) %all-to-all-start.2) | async-done | bytes 163872 | tf_op jit(solution)/shard_map/all_to_all | solution.py:320
  70.8 11.7 %all_to_all.26.merid_ref = bf16[16,24,256]{2,1,0:T(8,128)(2,1)S(1)} all-to-all(bf16[16,24,256]{2,1,0:T(8,128)(2,1)S(1)} %shard_map.69), channel_id=1, replica_groups=mesh['lat'=16,'lon'=32] {'lat'}, dimensions={0} | all-to-all | bytes 393216 | tf_op jit(solution)/shard_map/all_to_all | solution.py:322
  82.5 0.0 copy-done.2
  82.5 0.0 copy-start.3
  82.5 0.6 shard_map.70
  83.2 4.1 %collective-permute-start.2 = (bf16[3,80,512]{2,1,0:T(8,128)(2,1)S(1)}, bf16[3,80,512]{2,1,0:T(8,128)(2,1)S(1)}, u32[]{:S(2)}, u32[]{:S(2)}) collective-permute-start(bf16[3,80,512]{2,1,0:T(8,128)(2,1)S(1)} %get-tuple-element.33), channel_id=1, source_target_pairs={{32,64},{96,128},{160,192},{224,256},{288,320},{352,384},{416,448}... | collective-permute-start | bytes 737288 | tf_op jit(solution)/shard_map/ppermute | solution.py:330
  87.3 1.9 %collective-permute-start.3 = (bf16[3,80,512]{2,1,0:T(8,128)(2,1)S(1)}, bf16[3,80,512]{2,1,0:T(8,128)(2,1)S(1)}, u32[]{:S(2)}, u32[]{:S(2)}) collective-permute-start(bf16[3,80,512]{2,1,0:T(8,128)(2,1)S(1)} %get-tuple-element.34), channel_id=1, source_target_pairs={{0,32},{64,96},{128,160},{192,224},{256,288},{320,352},{384,416},{... | collective-permute-start | bytes 737288 | tf_op jit(solution)/shard_map/ppermute | solution.py:329
  89.2 0.0 copy-done.3
  89.3 1.6 %shard_map.71 = (f32[256,512]{1,0:T(8,128)S(1)}, bf16[512,1024]{1,0:T(8,128)(2,1)S(1)}, bf16[1024,512]{1,0:T(8,128)(2,1)S(1)}) custom-call(bf16[4,80,512]{2,1,0:T(8,128)(2,1)S(1)} %get-tuple-element.31.mixed_ref, f32[49,512]{1,0:T(8,128)S(1)} %reshape.11.conv_ref, bf16[512,1024]{1,0:T(8,128)(2,1)} %w_in_hbm.1, bf16[1024,512]{1,0:T(8,128)(2,1)} %w_back_hbm.1), custom_call_target="tpu_custom_call" | custom-call | flops 1000000000 | bytes 2000000 | tf_op jit(solution)/shard_map/pallas_call | solution.py:332
  90.9 2.0 %collective-permute-done.2.far_ref = bf16[3,80,512]{2,1,0:T(8,128)(2,1)S(1)} collective-permute-done((bf16[3,80,512]{2,1,0:T(8,128)(2,1)S(1)}, bf16[3,80,512]{2,1,0:T(8,128)(2,1)S(1)}, u32[]{:S(2)}, u32[]{:S(2)}) %collective-permute-start.2) | collective-permute-done | bytes 245792 | tf_op jit(solution)/shard_map/ppermute | solution.py:330
  92.8 0.0 collective-permute-done.3.near_ref
  92.8 2.9 %shard_map.72 = bf16[4,64,512]{2,1,0:T(8,128)(2,1)} custom-call(s32[1]{0:T(128)} %bitcast.1.odd_ref, bf16[4,80,512]{2,1,0:T(8,128)(2,1)S(1)} %get-tuple-element.31.mixed_ref, f32[256,512]{1,0:T(8,128)S(1)} %get-tuple-element.32.own_ref, bf16[3,80,512]{2,1,0:T(8,128)(2,1)S(1)} %collective-permute-done.2.far_ref, ...), custom_call_target="tpu_custom_call" | custom-call | flops 2000000000 | bytes 2000000 | tf_op jit(solution)/shard_map/pallas_call | solution.py:339
  (1 shorter events, 0.0 us)
Async XLA Ops:
  1.7 35.2 %copy-start.1 = (bf16[4,64,512]{2,1,0:T(8,128)(2,1)S(1)}, bf16[4,64,512]{2,1,0:T(8,128)(2,1)}, u32[]{:S(2)}) copy-start(bf16[4,64,512]{2,1,0:T(8,128)(2,1)} %field_ref.1) | copy-start | bytes 786436
  20.5 22.9 %all-to-all-start.1 = ((bf16[8,272,128]{2,1,0:T(8,128)(2,1)}), bf16[8,272,128]{2,1,0:T(8,128)(2,1)S(1)}, u32[]{:S(2)}, u32[]{:S(2)}) async-start(bf16[8,272,128]{2,1,0:T(8,128)(2,1)} %shard_map.65), calls=%async_computation.1 | async-start | bytes 1114112 | tf_op jit(solution)/shard_map/all_to_all | solution.py:300
  27.3 15.2 %collective-permute-start = (bf16[32,512]{1,0:T(8,128)(2,1)S(1)}, bf16[32,512]{1,0:T(8,128)(2,1)S(1)}, u32[]{:S(2)}, u32[]{:S(2)}) collective-permute-start(bf16[32,512]{1,0:T(8,128)(2,1)S(1)} %get-tuple-element.27), channel_id=1, source_target_pairs={{0,1},{1,2},{2,3},{3,4},{4,5},{5,6},{6,7},{7,8},{8,9},{9,10},{10,1... | collective-permute-start | bytes 98312 | tf_op jit(solution)/shard_map/ppermute | solution.py:301
  29.2 13.2 %collective-permute-start.1 = (bf16[32,512]{1,0:T(8,128)(2,1)S(1)}, bf16[32,512]{1,0:T(8,128)(2,1)S(1)}, u32[]{:S(2)}, u32[]{:S(2)}) collective-permute-start(bf16[32,512]{1,0:T(8,128)(2,1)S(1)} %get-tuple-element.28), channel_id=1, source_target_pairs={{1,0},{2,1},{3,2},{4,3},{5,4},{6,5},{7,6},{8,7},{9,8},{10,9},{11,1... | collective-permute-start | bytes 98312 | tf_op jit(solution)/shard_map/ppermute | solution.py:302
  43.4 16.2 %all-to-all-start.3 = ((bf16[16,24,512]{2,1,0:T(8,128)(2,1)}), bf16[16,24,512]{2,1,0:T(8,128)(2,1)S(1)}, u32[]{:S(2)}, u32[]{:S(2)}) async-start(bf16[16,24,512]{2,1,0:T(8,128)(2,1)} %shard_map.67), calls=%async_computation.3 | async-start | bytes 786432 | tf_op jit(solution)/shard_map/all_to_all | solution.py:316
  52.2 10.8 %copy-start = (bf16[512,1152]{1,0:T(8,128)(2,1)S(1)}, bf16[512,1152]{1,0:T(8,128)(2,1)}, u32[]{:S(2)}) copy-start(bf16[512,1152]{1,0:T(8,128)(2,1)} %w_ref.2) | copy-start | bytes 3538948
  59.7 11.2 %all-to-all-start.2 = ((bf16[4,80,256]{2,1,0:T(8,128)(2,1)}), bf16[4,80,256]{2,1,0:T(8,128)(2,1)S(1)}, u32[]{:S(2)}, u32[]{:S(2)}) async-start(bf16[4,80,256]{2,1,0:T(8,128)(2,1)} %shard_map.68), calls=%async_computation.2 | async-start | bytes 327680 | tf_op jit(solution)/shard_map/all_to_all | solution.py:320
  63.0 19.5 %copy-start.2 = (bf16[512,512]{1,0:T(8,128)(2,1)S(1)}, bf16[512,512]{1,0:T(8,128)(2,1)}, u32[]{:S(2)}) copy-start(bf16[512,512]{1,0:T(8,128)(2,1)} %w_ref.3) | copy-start | bytes 1572868
  82.5 6.7 %copy-start.3 = (f32[7,7,512]{2,1,0:T(8,128)S(1)}, f32[7,7,512]{2,1,0:T(8,128)}, u32[]{:S(2)}) copy-start(f32[7,7,512]{2,1,0:T(8,128)} %param.9) | copy-start | bytes 301060
  83.2 9.6 %collective-permute-start.2 = (bf16[3,80,512]{2,1,0:T(8,128)(2,1)S(1)}, bf16[3,80,512]{2,1,0:T(8,128)(2,1)S(1)}, u32[]{:S(2)}, u32[]{:S(2)}) collective-permute-start(bf16[3,80,512]{2,1,0:T(8,128)(2,1)S(1)} %get-tuple-element.33), channel_id=1, source_target_pairs={{32,64},{96,128},{160,192},{224,256},{288,320},{352,384},{416,448}... | collective-permute-start | bytes 737288 | tf_op jit(solution)/shard_map/ppermute | solution.py:330
  87.3 5.5 %collective-permute-start.3 = (bf16[3,80,512]{2,1,0:T(8,128)(2,1)S(1)}, bf16[3,80,512]{2,1,0:T(8,128)(2,1)S(1)}, u32[]{:S(2)}, u32[]{:S(2)}) collective-permute-start(bf16[3,80,512]{2,1,0:T(8,128)(2,1)S(1)} %get-tuple-element.34), channel_id=1, source_target_pairs={{0,32},{64,96},{128,160},{192,224},{256,288},{320,352},{384,416},{... | collective-permute-start | bytes 737288 | tf_op jit(solution)/shard_map/ppermute | solution.py:329

commit v7 on v6

--- a/solution.py
+++ b/solution.py
@@ -18,6 +18,7 @@
 WIDE = W + 2 * E
 MC = WIDE // LAT
 EDGES = (1, LAT - 2)
+ECELLS = 16
 MROWS = 24
 YS = 8
 ZS = 4
@@ -72,7 +73,17 @@
     return pltpu.with_memory_space_constraint(array, pltpu.HBM)
 
 
-def zonal_project_kernel(field_hbm, w_hbm, out_ref, first_ref, last_ref, field_ref, wq_ref, wkv_ref, sems):
+def packed(edge):
+    return jnp.concatenate([edge[:, lane : lane + 128] for lane in range(0, C, 128)], axis=0)
+
+
+def unpacked(rows):
+    return jnp.concatenate([rows[i : i + ECELLS] for i in range(0, W, ECELLS)], axis=1)
+
+
+def zonal_project_kernel(
+    z_ref, field_hbm, w_hbm, out_ref, border_ref, field_ref, wq_ref, wkv_ref, sems
+):
     loads = [
         pltpu.make_async_copy(field_hbm, field_ref, sems.at[0]),
         pltpu.make_async_copy(w_hbm.at[:, 512:640], wkv_ref, sems.at[1]),
@@ -80,11 +91,18 @@
     ]
     for load in loads:
         load.start()
+    z = z_ref[0]
+    i, u = iota((2 * ECELLS, CELLS), 0), iota((2 * ECELLS, CELLS), 1)
+    select = one_hot(u == ((i >> 2) & 3) * W + (i & 3) + jnp.where(i < ECELLS, 0, W - 4))
     loads[0].wait()
-    field = field_ref[...].astype(F32)
-    first_ref[...] = field[:, 0:E].reshape(R * E, C).astype(BF)
-    last_ref[...] = field[:, W - E : W].reshape(R * E, C).astype(BF)
-    normed = layer_norm(field.reshape(CELLS, C)).astype(BF)
+    field = field_ref[...].astype(F32).reshape(CELLS, C)
+    edges = mm(select, field.astype(BF)).astype(BF)
+    first, last = edges[0:ECELLS], edges[ECELLS:]
+    border_ref[...] = jnp.where(z == ZS - 1, last.astype(F32), first.astype(F32)).astype(BF)
+    out_ref[:, :, 384:512] = jnp.zeros((R, W, 128), BF)
+    out_ref[(z + 1) & 3, :, 384:512] = packed(last)
+    out_ref[(z + 3) & 3, :, 384:512] = packed(first)
+    normed = layer_norm(field).astype(BF)
     loads[1].wait()
     out_ref[:, :, 256:384] = mm(normed, wkv_ref[...]).astype(BF).reshape(R, W, 128)
     loads[2].wait()
@@ -133,11 +151,6 @@
             out_ref[z, :, lanes] = heads[z * W : z * W + WIDE].astype(BF)
 
 
-def widened(left, own, right):
-    left, right = (a.astype(F32).reshape(R, E, a.shape[-1]) for a in (left, right))
-    return jnp.concatenate([left, own.astype(F32), right], axis=1)
-
-
 def merid_own_kernel(field_ref, out_ref, edge_ref):
     normed = layer_norm(field_ref[...].astype(F32).reshape(CELLS, C)).astype(BF)
     dims = (LAT, MROWS, CELLS)
@@ -150,13 +163,21 @@
     edge_ref[1] = slots[EDGES[1]]
 
 
-def merid_edge_kernel(slots_hbm, edge_ref, left_ref, right_ref, out_hbm, done_ref, sems):
+def merid_edge_kernel(
+    z_ref, slots_hbm, edge_ref, row_ref, border_ref, out_hbm, left_ref, right_ref, done_ref, sems
+):
+    z = z_ref[0]
+    border = border_ref[...].astype(F32)
     copies = []
     for n, (m, ref) in enumerate(zip(EDGES, (left_ref, right_ref))):
-        normed = layer_norm(ref[...].astype(F32)).astype(BF)
-        i, u = iota((MROWS, R * E), 0), iota((MROWS, R * E), 1)
-        c = m * MC + (i >> 2) - n * (W + E)
-        hit = ((i & 3) * E + c == u) & (c >= 0) & (c < E) & (i < R * MC)
+        beside, outer = ((z + 3) & 3, 0) if n == 0 else ((z + 1) & 3, ZS - 1)
+        halo = unpacked(row_ref[beside, :, 384:512]).astype(F32)
+        halo = jnp.where(z == outer, border, halo)
+        ref[...] = halo.astype(BF)
+        normed = layer_norm(halo).astype(BF)
+        i, u = iota((MROWS, ECELLS), 0), iota((MROWS, ECELLS), 1)
+        c = m * MC + (i >> 2) - (E // 2 if n == 0 else W + E)
+        hit = ((i & 3) * 4 + c == u) & (c >= 0) & (c < 4) & (i < R * MC)
         done_ref[n] = (edge_ref[n].astype(F32) + mm(one_hot(hit), normed)).astype(BF)
         copies.append(pltpu.make_async_copy(done_ref.at[n], out_hbm.at[m], sems.at[n]))
         copies[n].start()
@@ -199,7 +220,15 @@
     cell = one_hot((m * MC + (i >> 2) == w) & ((i & 3) == r) & (i < R * MC))
     merid = mm(cell.reshape(rows, LAT * MROWS), merid).astype(BF)
     attended = mm(zonal_ref[...].reshape(rows, 256), w_ref[0:256]) + mm(merid, w_ref[256:512])
-    wide = widened(left_ref[...], field_ref[...], right_ref[...])
+    dims = (R, WIDE, ECELLS)
+    r, c, t = iota(dims, 0), iota(dims, 1) - E, iota(dims, 2)
+    edge = t == (r << 2) + (c & 3)
+    left = one_hot(edge & (c >= -4) & (c < 0)).reshape(rows, ECELLS)
+    right = one_hot(edge & (c >= W) & (c < W + 4)).reshape(rows, ECELLS)
+    halo = mm(left, left_ref[...]) + mm(right, right_ref[...])
+    blank = jnp.zeros((R, E, C), F32)
+    wide = jnp.concatenate([blank, field_ref[...].astype(F32), blank], axis=1)
+    wide = wide + halo.reshape(R, WIDE, C)
     mixed = (wide + attended.reshape(R, WIDE, C)).astype(BF)
     mixed_ref[...] = mixed
     odd = odd_ref[0] == 1
@@ -267,28 +296,29 @@
 
 
 def per_device(field, w_qkv, w_out, conv_w, w_in, w_back):
-    right = [(i, (i + 1) % LON) for i in range(LON)]
-    left = [(j, i) for i, j in right]
     near_pairs = [(i, i + 1) for i in range(0, LAT, 2)]
     far_pairs = [(i, i + 1) for i in range(1, LAT - 1, 2)]
     near_pairs, far_pairs = (pairs + [(j, i) for i, j in pairs] for pairs in (near_pairs, far_pairs))
+    borders = [(y * ZS + ZS - 1, (y + 1) % YS * ZS) for y in range(YS)]
+    borders = borders + [(j, i) for i, j in borders]
     along_y = [[y * ZS + z for y in range(YS)] for z in range(ZS)]
     along_z = [[y * ZS + z for z in range(ZS)] for y in range(YS)]
-    y = (lax.axis_index("lon").astype(jnp.int32) >> 2).reshape(1)
+    lon = lax.axis_index("lon").astype(jnp.int32)
+    y, z = (lon >> 2).reshape(1), (lon & 3).reshape(1)
     odd = (lax.axis_index("lat").astype(jnp.int32) & 1).reshape(1)
-    field, y, odd = lax.optimization_barrier((field, y, odd))
-    row, first, last = call(
+    field, y, z, odd = lax.optimization_barrier((field, y, z, odd))
+    row, border = call(
         zonal_project_kernel,
-        (shape(R, W, 384), shape(R * E, C), shape(R * E, C)),
+        (shape(R, W, 512), shape(ECELLS, C)),
         200_000_000,
-        in_specs=[ANY, ANY],
+        in_specs=[SMEM, ANY, ANY],
         scratch_shapes=[
             pltpu.VMEM((R, W, C), BF),
             pltpu.VMEM((C, 256), BF),
             pltpu.VMEM((C, 128), BF),
             pltpu.SemaphoreType.DMA((3,)),
         ],
-    )(in_hbm(field), in_hbm(w_qkv))
+    )(z, in_hbm(field), in_hbm(w_qkv))
     row = lax.all_to_all(row, "lon", 0, 0, axis_index_groups=along_z)
     slots = call(
         spread_kernel,
@@ -298,20 +328,19 @@
         scratch_shapes=[pltpu.VMEM((KEYS, 128), BF), pltpu.SemaphoreType.DMA((YS,))],
     )(row)
     slots = lax.all_to_all(slots, "lon", 0, 0, axis_index_groups=along_y)
-    field_left = lax.ppermute(last, "lon", right)
-    field_right = lax.ppermute(first, "lon", left)
+    border = lax.ppermute(border, "lon", borders)
     merid, merid_edges = call(
         merid_own_kernel, (shape(LAT, MROWS, C), shape(2, MROWS, C)), 300_000_000
     )(field)
-    merid = call(
+    merid, field_left, field_right = call(
         merid_edge_kernel,
-        shape(LAT, MROWS, C),
+        (shape(LAT, MROWS, C), shape(ECELLS, C), shape(ECELLS, C)),
         10_000_000,
-        in_specs=[ANY, VMEM, VMEM, VMEM],
-        out_specs=ANY,
-        input_output_aliases={0: 0},
+        in_specs=[SMEM, ANY, VMEM, VMEM, VMEM],
+        out_specs=[ANY, VMEM, VMEM],
+        input_output_aliases={1: 0},
         scratch_shapes=[pltpu.VMEM((2, MROWS, C), BF), pltpu.SemaphoreType.DMA((2,))],
-    )(merid, merid_edges, field_left, field_right)
+    )(z, merid, merid_edges, row, border)
     slots, merid = lax.optimization_barrier((slots, merid))
     merid = lax.all_to_all(merid, "lat", 0, 0)
     zonal = call(

time: 96.8 us -> 98.1 us (1.013)
  waiting for transfers between devices: 15.7 us -> 17 us
    ppermute x2 -> x1, starting transfers between devices: 9.49 us -> 7.52 us  [per_device(): border = lax.ppermute(border, 'lon', borders)]
    all_to_all x1, starting transfers between devices: 8.79 us -> 10.6 us  [per_device(): merid = lax.all_to_all(merid, 'lat', 0, 0)]
    ppermute x2 -> x1, waiting for transfers between devices: 4.41 us -> 5.59 us  [per_device(): border = lax.ppermute(border, 'lon', borders)]
  transfers between devices with their start and end apart: 7 -> 6, of which waited for: 4 -> 4; matrix products, arithmetic and copies ran while one was open for 0% -> 0% of each run, Pallas kernels for 10% -> 10%
where the time goes in v7:
time: 98.1 us; the launch traced here: 97.5 us
  starting transfers between devices  34.4 us (35%)
  blocking collectives  30.2 us (31%)
  waiting for transfers between devices  17 us (17%)
  Pallas kernels  15.7 us (16%)
    all_to_all x1, blocking collectives, per_device(): row = lax.all_to_all(row, 'lon', 0, 0, axis_index_groups=along_z)  18.7 us
    all_to_all x1, blocking collectives, per_device(): merid = lax.all_to_all(merid, 'lat', 0, 0)  11.5 us
    all_to_all x1, starting transfers between devices, per_device(): merid = lax.all_to_all(merid, 'lat', 0, 0)  10.6 us
    ppermute x1, starting transfers between devices, per_device(): border = lax.ppermute(border, 'lon', borders)  7.52 us
    all_to_all x1, starting transfers between devices, per_device(): slots = lax.all_to_all(slots, 'lon', 0, 0, axis_index_groups=along_y)  6.84 us
    all_to_all x1, waiting for transfers between devices, per_device(): zonal = lax.all_to_all(zonal, 'lon', 0, 0, axis_index_groups=along_z)  6.07 us
    ppermute x1, waiting for transfers between devices, per_device(): border = lax.ppermute(border, 'lon', borders)  5.59 us
    ppermute x1, starting transfers between devices, per_device(): far = lax.ppermute(far, 'lat', far_pairs)  4.12 us
  transfers between devices with their start and end apart: 6, of which 4 were waited for; matrix products, arithmetic and copies ran while one was open for 0% of the time, Pallas kernels for 10%

profile of v7, /device:TPU:7, one launch (start us, length us, event | category | flops | bytes accessed | tf_op | source)
XLA Modules:
  0.0 97.5 jit_solution(2677031804935512149)
XLA Ops:
  0.0 1.7 %shard_map.64 = (bf16[4,64,512]{2,1,0:T(8,128)(2,1)S(1)}, bf16[16,512]{1,0:T(8,128)(2,1)S(1)}) custom-call(s32[1]{0:T(128)} %bitcast.1.z_ref, bf16[4,64,512]{2,1,0:T(8,128)(2,1)} %field_ref.1, bf16[512,1152]{1,0:T(8,128)(2,1)} %w_ref.2), custom_call_target="tpu_custom_call" | custom-call | flops 200000000 | bytes 2000000 | tf_op jit(solution)/shard_map/pallas_call | solution.py:310
  1.7 0.0 copy-start.1
  1.7 18.7 %all_to_all.25.in_ref.row_ref.own_ref = bf16[4,64,512]{2,1,0:T(8,128)(2,1)S(1)} all-to-all(bf16[4,64,512]{2,1,0:T(8,128)(2,1)S(1)} %get-tuple-element.28), channel_id=1, replica_groups={{0,1,2,3},{4,5,6,7},{8,9,10,11},{12,13,14,15},{16,17,18,19},{20,21,22,2..., dimensions={0} | all-to-all | bytes 524288 | tf_op jit(solution)/shard_map/all_to_all | solution.py:322
  20.4 0.9 shard_map.65
  21.3 6.8 %all-to-all-start.1 = ((bf16[8,272,128]{2,1,0:T(8,128)(2,1)}), bf16[8,272,128]{2,1,0:T(8,128)(2,1)S(1)}, u32[]{:S(2)}, u32[]{:S(2)}) async-start(bf16[8,272,128]{2,1,0:T(8,128)(2,1)} %shard_map.65), calls=%async_computation.1 | async-start | bytes 1114112 | tf_op jit(solution)/shard_map/all_to_all | solution.py:330
  28.1 7.5 %collective-permute-start = (bf16[16,512]{1,0:T(8,128)(2,1)S(1)}, bf16[16,512]{1,0:T(8,128)(2,1)S(1)}, u32[]{:S(2)}, u32[]{:S(2)}) collective-permute-start(bf16[16,512]{1,0:T(8,128)(2,1)S(1)} %get-tuple-element.31), channel_id=1, source_target_pairs={{3,4},{7,8},{11,12},{15,16},{19,20},{23,24},{27,28},{31,0},{4,3},{... | collective-permute-start | bytes 49160 | tf_op jit(solution)/shard_map/ppermute | solution.py:331
  35.6 0.0 copy-done.1
  35.7 1.2 %shard_map.66 = (bf16[16,24,512]{2,1,0:T(8,128)(2,1)}, bf16[2,24,512]{2,1,0:T(8,128)(2,1)S(1)}) custom-call(bf16[4,64,512]{2,1,0:T(8,128)(2,1)S(1)} %copy-done.1), custom_call_target="tpu_custom_call" | custom-call | flops 300000000 | bytes 2000000 | tf_op jit(solution)/shard_map/pallas_call | solution.py:332
  36.9 5.6 %collective-permute-done.border_ref = bf16[16,512]{1,0:T(8,128)(2,1)S(1)} collective-permute-done((bf16[16,512]{1,0:T(8,128)(2,1)S(1)}, bf16[16,512]{1,0:T(8,128)(2,1)S(1)}, u32[]{:S(2)}, u32[]{:S(2)}) %collective-permute-start) | collective-permute-done | bytes 16416 | tf_op jit(solution)/shard_map/ppermute | solution.py:331
  42.5 0.9 shard_map.67
  43.4 0.0 all-to-all-done.1.all_ref
  43.4 10.6 %all-to-all-start.3 = ((bf16[16,24,512]{2,1,0:T(8,128)(2,1)}), bf16[16,24,512]{2,1,0:T(8,128)(2,1)S(1)}, u32[]{:S(2)}, u32[]{:S(2)}) async-start(bf16[16,24,512]{2,1,0:T(8,128)(2,1)} %get-tuple-element.34), calls=%async_computation.3 | async-start | bytes 786432 | tf_op jit(solution)/shard_map/all_to_all | solution.py:345
  54.1 0.0 copy-start
  54.1 4.0 %shard_map.68 = bf16[4,80,256]{2,1,0:T(8,128)(2,1)} custom-call(s32[1]{0:T(128)} %bitcast.y_ref, bf16[4,64,512]{2,1,0:T(8,128)(2,1)S(1)} %all_to_all.25.in_ref.row_ref.own_ref, bf16[8,272,128]{2,1,0:T(8,128)(2,1)S(1)} %all-to-all-done.1.all_ref), custom_call_target="tpu_custom_call" | custom-call | flops 4000000000 | bytes 2000000 | tf_op jit(solution)/shard_map/pallas_call | solution.py:346
  58.1 3.4 %all-to-all-done.3.in_ref = bf16[16,24,512]{2,1,0:T(8,128)(2,1)S(1)} async-done(((bf16[16,24,512]{2,1,0:T(8,128)(2,1)}), bf16[16,24,512]{2,1,0:T(8,128)(2,1)S(1)}, u32[]{:S(2)}, u32[]{:S(2)}) %all-to-all-start.3) | async-done | bytes 393248 | tf_op jit(solution)/shard_map/all_to_all | solution.py:345
  61.5 3.3 %all-to-all-start.2 = ((bf16[4,80,256]{2,1,0:T(8,128)(2,1)}), bf16[4,80,256]{2,1,0:T(8,128)(2,1)S(1)}, u32[]{:S(2)}, u32[]{:S(2)}) async-start(bf16[4,80,256]{2,1,0:T(8,128)(2,1)} %shard_map.68), calls=%async_computation.2 | async-start | bytes 327680 | tf_op jit(solution)/shard_map/all_to_all | solution.py:349
  64.9 0.0 copy-done
  64.9 0.0 copy-start.2
  64.9 1.9 %shard_map.69 = bf16[16,24,256]{2,1,0:T(8,128)(2,1)S(1)} custom-call(bf16[16,24,512]{2,1,0:T(8,128)(2,1)S(1)} %all-to-all-done.3.in_ref, bf16[512,1152]{1,0:T(8,128)(2,1)S(1)} %copy-done), custom_call_target="tpu_custom_call" | custom-call | flops 1000000000 | bytes 2000000 | tf_op jit(solution)/shard_map/pallas_call | solution.py:350
  66.7 6.1 %all-to-all-done.2.zonal_ref = bf16[4,80,256]{2,1,0:T(8,128)(2,1)S(1)} async-done(((bf16[4,80,256]{2,1,0:T(8,128)(2,1)}), bf16[4,80,256]{2,1,0:T(8,128)(2,1)S(1)}, u32[]{:S(2)}, u32[]{:S(2)}) %all-to-all-start.2) | async-done | bytes 163872 | tf_op jit(solution)/shard_map/all_to_all | solution.py:349
  72.8 11.5 %all_to_all.26.merid_ref = bf16[16,24,256]{2,1,0:T(8,128)(2,1)S(1)} all-to-all(bf16[16,24,256]{2,1,0:T(8,128)(2,1)S(1)} %shard_map.69), channel_id=1, replica_groups=mesh['lat'=16,'lon'=32] {'lat'}, dimensions={0} | all-to-all | bytes 393216 | tf_op jit(solution)/shard_map/all_to_all | solution.py:351
  84.4 0.0 copy-done.2
  84.4 0.0 copy-start.3
  84.4 0.6 shard_map.70
  85.0 4.1 %collective-permute-start.1 = (bf16[3,80,512]{2,1,0:T(8,128)(2,1)S(1)}, bf16[3,80,512]{2,1,0:T(8,128)(2,1)S(1)}, u32[]{:S(2)}, u32[]{:S(2)}) collective-permute-start(bf16[3,80,512]{2,1,0:T(8,128)(2,1)S(1)} %get-tuple-element.39), channel_id=1, source_target_pairs={{32,64},{96,128},{160,192},{224,256},{288,320},{352,384},{416,448}... | collective-permute-start | bytes 737288 | tf_op jit(solution)/shard_map/ppermute | solution.py:359
  89.1 1.9 %collective-permute-start.2 = (bf16[3,80,512]{2,1,0:T(8,128)(2,1)S(1)}, bf16[3,80,512]{2,1,0:T(8,128)(2,1)S(1)}, u32[]{:S(2)}, u32[]{:S(2)}) collective-permute-start(bf16[3,80,512]{2,1,0:T(8,128)(2,1)S(1)} %get-tuple-element.40), channel_id=1, source_target_pairs={{0,32},{64,96},{128,160},{192,224},{256,288},{320,352},{384,416},{... | collective-permute-start | bytes 737288 | tf_op jit(solution)/shard_map/ppermute | solution.py:358
  91.1 0.0 copy-done.3
  91.1 1.6 %shard_map.71 = (f32[256,512]{1,0:T(8,128)S(1)}, bf16[512,1024]{1,0:T(8,128)(2,1)S(1)}, bf16[1024,512]{1,0:T(8,128)(2,1)S(1)}) custom-call(bf16[4,80,512]{2,1,0:T(8,128)(2,1)S(1)} %get-tuple-element.37.mixed_ref, f32[49,512]{1,0:T(8,128)S(1)} %reshape.15.conv_ref, bf16[512,1024]{1,0:T(8,128)(2,1)} %w_in_hbm.1, bf16[1024,512]{1,0:T(8,128)(2,1)} %w_back_hbm.1), custom_call_target="tpu_custom_call" | custom-call | flops 1000000000 | bytes 2000000 | tf_op jit(solution)/shard_map/pallas_call | solution.py:361
  92.7 2.0 %collective-permute-done.1.far_ref = bf16[3,80,512]{2,1,0:T(8,128)(2,1)S(1)} collective-permute-done((bf16[3,80,512]{2,1,0:T(8,128)(2,1)S(1)}, bf16[3,80,512]{2,1,0:T(8,128)(2,1)S(1)}, u32[]{:S(2)}, u32[]{:S(2)}) %collective-permute-start.1) | collective-permute-done | bytes 245792 | tf_op jit(solution)/shard_map/ppermute | solution.py:359
  94.6 0.0 collective-permute-done.2.near_ref
  94.6 2.9 %shard_map.72 = bf16[4,64,512]{2,1,0:T(8,128)(2,1)} custom-call(s32[1]{0:T(128)} %bitcast.2.odd_ref, bf16[4,80,512]{2,1,0:T(8,128)(2,1)S(1)} %get-tuple-element.37.mixed_ref, f32[256,512]{1,0:T(8,128)S(1)} %get-tuple-element.38.own_ref, bf16[3,80,512]{2,1,0:T(8,128)(2,1)S(1)} %collective-permute-done.1.far_ref, ...), custom_call_target="tpu_custom_call" | custom-call | flops 2000000000 | bytes 2000000 | tf_op jit(solution)/shard_map/pallas_call | solution.py:368
  (1 shorter events, 0.0 us)
Async XLA Ops:
  1.7 34.0 %copy-start.1 = (bf16[4,64,512]{2,1,0:T(8,128)(2,1)S(1)}, bf16[4,64,512]{2,1,0:T(8,128)(2,1)}, u32[]{:S(2)}) copy-start(bf16[4,64,512]{2,1,0:T(8,128)(2,1)} %field_ref.1) | copy-start | bytes 786436
  21.3 22.2 %all-to-all-start.1 = ((bf16[8,272,128]{2,1,0:T(8,128)(2,1)}), bf16[8,272,128]{2,1,0:T(8,128)(2,1)S(1)}, u32[]{:S(2)}, u32[]{:S(2)}) async-start(bf16[8,272,128]{2,1,0:T(8,128)(2,1)} %shard_map.65), calls=%async_computation.1 | async-start | bytes 1114112 | tf_op jit(solution)/shard_map/all_to_all | solution.py:330
  28.1 14.4 %collective-permute-start = (bf16[16,512]{1,0:T(8,128)(2,1)S(1)}, bf16[16,512]{1,0:T(8,128)(2,1)S(1)}, u32[]{:S(2)}, u32[]{:S(2)}) collective-permute-start(bf16[16,512]{1,0:T(8,128)(2,1)S(1)} %get-tuple-element.31), channel_id=1, source_target_pairs={{3,4},{7,8},{11,12},{15,16},{19,20},{23,24},{27,28},{31,0},{4,3},{... | collective-permute-start | bytes 49160 | tf_op jit(solution)/shard_map/ppermute | solution.py:331
  43.4 18.1 %all-to-all-start.3 = ((bf16[16,24,512]{2,1,0:T(8,128)(2,1)}), bf16[16,24,512]{2,1,0:T(8,128)(2,1)S(1)}, u32[]{:S(2)}, u32[]{:S(2)}) async-start(bf16[16,24,512]{2,1,0:T(8,128)(2,1)} %get-tuple-element.34), calls=%async_computation.3 | async-start | bytes 786432 | tf_op jit(solution)/shard_map/all_to_all | solution.py:345
  54.1 10.8 %copy-start = (bf16[512,1152]{1,0:T(8,128)(2,1)S(1)}, bf16[512,1152]{1,0:T(8,128)(2,1)}, u32[]{:S(2)}) copy-start(bf16[512,1152]{1,0:T(8,128)(2,1)} %w_ref.2) | copy-start | bytes 3538948
  61.5 11.3 %all-to-all-start.2 = ((bf16[4,80,256]{2,1,0:T(8,128)(2,1)}), bf16[4,80,256]{2,1,0:T(8,128)(2,1)S(1)}, u32[]{:S(2)}, u32[]{:S(2)}) async-start(bf16[4,80,256]{2,1,0:T(8,128)(2,1)} %shard_map.68), calls=%async_computation.2 | async-start | bytes 327680 | tf_op jit(solution)/shard_map/all_to_all | solution.py:349
  64.9 19.5 %copy-start.2 = (bf16[512,512]{1,0:T(8,128)(2,1)S(1)}, bf16[512,512]{1,0:T(8,128)(2,1)}, u32[]{:S(2)}) copy-start(bf16[512,512]{1,0:T(8,128)(2,1)} %w_ref.3) | copy-start | bytes 1572868
  84.4 6.7 %copy-start.3 = (f32[7,7,512]{2,1,0:T(8,128)S(1)}, f32[7,7,512]{2,1,0:T(8,128)}, u32[]{:S(2)}) copy-start(f32[7,7,512]{2,1,0:T(8,128)} %param.9) | copy-start | bytes 301060
  85.0 9.6 %collective-permute-start.1 = (bf16[3,80,512]{2,1,0:T(8,128)(2,1)S(1)}, bf16[3,80,512]{2,1,0:T(8,128)(2,1)S(1)}, u32[]{:S(2)}, u32[]{:S(2)}) collective-permute-start(bf16[3,80,512]{2,1,0:T(8,128)(2,1)S(1)} %get-tuple-element.39), channel_id=1, source_target_pairs={{32,64},{96,128},{160,192},{224,256},{288,320},{352,384},{416,448}... | collective-permute-start | bytes 737288 | tf_op jit(solution)/shard_map/ppermute | solution.py:359
  89.1 5.5 %collective-permute-start.2 = (bf16[3,80,512]{2,1,0:T(8,128)(2,1)S(1)}, bf16[3,80,512]{2,1,0:T(8,128)(2,1)S(1)}, u32[]{:S(2)}, u32[]{:S(2)}) collective-permute-start(bf16[3,80,512]{2,1,0:T(8,128)(2,1)S(1)} %get-tuple-element.40), channel_id=1, source_target_pairs={{0,32},{64,96},{128,160},{192,224},{256,288},{320,352},{384,416},{... | collective-permute-start | bytes 737288 | tf_op jit(solution)/shard_map/ppermute | solution.py:358

commit v8 on v6

--- a/solution.py
+++ b/solution.py
@@ -18,6 +18,9 @@
 WIDE = W + 2 * E
 MC = WIDE // LAT
 EDGES = (1, LAT - 2)
+HALO = 3
+TALL = R + 2 * HALO
+BROWS = 56
 MROWS = 24
 YS = 8
 ZS = 4
@@ -72,7 +75,29 @@
     return pltpu.with_memory_space_constraint(array, pltpu.HBM)
 
 
-def zonal_project_kernel(field_hbm, w_hbm, out_ref, first_ref, last_ref, field_ref, wq_ref, wkv_ref, sems):
+def by_partner(odd, far, near):
+    far, near = far.astype(F32), near.astype(F32)
+    return jnp.where(odd, near, far), jnp.where(odd, far, near)
+
+
+def for_partner(odd_ref, values, far_ref, near_ref):
+    odd = odd_ref[0] == 1
+    head, tail = values[0:HALO], values[R - HALO : R]
+
+    @pl.when(odd)
+    def after_is_far():
+        far_ref[...] = tail
+        near_ref[...] = head
+
+    @pl.when(jnp.logical_not(odd))
+    def before_is_far():
+        far_ref[...] = head
+        near_ref[...] = tail
+
+
+def zonal_project_kernel(
+    odd_ref, field_hbm, w_hbm, out_ref, first_ref, last_ref, far_ref, near_ref, field_ref, wq_ref, wkv_ref, sems
+):
     loads = [
         pltpu.make_async_copy(field_hbm, field_ref, sems.at[0]),
         pltpu.make_async_copy(w_hbm.at[:, 512:640], wkv_ref, sems.at[1]),
@@ -84,6 +109,7 @@
     field = field_ref[...].astype(F32)
     first_ref[...] = field[:, 0:E].reshape(R * E, C).astype(BF)
     last_ref[...] = field[:, W - E : W].reshape(R * E, C).astype(BF)
+    for_partner(odd_ref, field_ref[...], far_ref, near_ref)
     normed = layer_norm(field.reshape(CELLS, C)).astype(BF)
     loads[1].wait()
     out_ref[:, :, 256:384] = mm(normed, wkv_ref[...]).astype(BF).reshape(R, W, 128)
@@ -174,6 +200,13 @@
     key = iota((count, count), 1)
     key = (key - ((key * 2731) >> 16) * MROWS) >> 2
     bias = jnp.where(row == key, 0.0, -1e30)
+    dims = (LAT, BROWS, 1)
+    j = iota(dims, 1)
+    q = (j * 205) >> 10
+    tall = iota(dims, 0) * R - HALO + q
+    token = (tall >> 2) * MROWS + (j - q * MC) * R + (tall & 3)
+    token = jnp.where(j < TALL * MC, token, -1)
+    spread = one_hot(token == iota((LAT, BROWS, count), 2)).reshape(LAT * BROWS, count)
     low = iota((count, 128), 1) < HD
     scale = 1.0 / math.sqrt(HD)
     for pair in range(2):
@@ -185,34 +218,16 @@
             weight = jnp.exp(score - jnp.max(score, axis=-1, keepdims=True))
             mass = jnp.sum(weight, axis=-1, keepdims=True)
             outs.append(mm(weight.astype(BF), v) / mass)
-        both = jnp.where(low, outs[0], outs[1]).reshape(LAT, MROWS, 128)
-        out_ref[:, :, lanes] = both.astype(BF)
-
-
-def mix_kernel(odd_ref, zonal_ref, merid_ref, left_ref, right_ref, field_ref, w_ref, mixed_ref, far_ref, near_ref):
-    rows = R * WIDE
-    merid = merid_ref[...].astype(F32).reshape(LAT * MROWS, 256).astype(BF)
-    dims = (R, WIDE, LAT * MROWS)
-    r, w, t = iota(dims, 0), iota(dims, 1), iota(dims, 2)
-    m = (t * 2731) >> 16
-    i = t - m * MROWS
-    cell = one_hot((m * MC + (i >> 2) == w) & ((i & 3) == r) & (i < R * MC))
-    merid = mm(cell.reshape(rows, LAT * MROWS), merid).astype(BF)
-    attended = mm(zonal_ref[...].reshape(rows, 256), w_ref[0:256]) + mm(merid, w_ref[256:512])
-    wide = widened(left_ref[...], field_ref[...], right_ref[...])
-    mixed = (wide + attended.reshape(R, WIDE, C)).astype(BF)
-    mixed_ref[...] = mixed
-    odd = odd_ref[0] == 1
-
-    @pl.when(odd)
-    def after_is_far():
-        far_ref[...] = mixed[1:4]
-        near_ref[...] = mixed[0:3]
-
-    @pl.when(jnp.logical_not(odd))
-    def before_is_far():
-        far_ref[...] = mixed[0:3]
-        near_ref[...] = mixed[1:4]
+        both = jnp.where(low, outs[0], outs[1]).astype(BF)
+        out_ref[:, :, lanes] = mm(spread, both).reshape(LAT, BROWS, 128).astype(BF)
+
+
+def zonal_halo_kernel(odd_ref, zonal_ref, left_ref, right_ref, far_ref, near_ref):
+    parts = [zonal_ref[...].astype(F32)]
+    for ref in (left_ref, right_ref):
+        edge = ref[...].astype(F32).reshape(R, E, C)
+        parts += [edge[:, :, 0:256], edge[:, :, 256:512]]
+    for_partner(odd_ref, jnp.concatenate(parts, axis=1).astype(BF), far_ref, near_ref)
 
 
 def conv_part(rows, conv_ref, lanes, r):
@@ -228,41 +243,46 @@
     return total
 
 
-def own_conv_kernel(
-    mixed_ref, conv_ref, w_in_hbm, w_back_hbm, out_ref, w_in_ref, w_back_ref, sems
+def block_kernel(
+    odd_ref, zonal_ref, far_z_ref, near_z_ref, merid_ref, left_ref, right_ref, field_ref, far_f_ref, near_f_ref,
+    w_out_ref, conv_ref, w_in_hbm, w_back_hbm, out_ref, mixed_ref, conv_out, w_in_ref, w_back_ref, sems,
 ):
     pairs = ((w_in_hbm, w_in_ref), (w_back_hbm, w_back_ref))
     loads = [pltpu.make_async_copy(a, b, sems.at[i]) for i, (a, b) in enumerate(pairs)]
     for load in loads:
         load.start()
+    odd = odd_ref[0] == 1
+    rows = TALL * WIDE
+    dims = (TALL, WIDE, 1)
+    q, w = iota(dims, 0), iota(dims, 1)
+    m = (w * 205) >> 10
+    token = m * BROWS + q * MC + w - m * MC
+    pick = one_hot(token == iota((TALL, WIDE, LAT * BROWS), 2)).reshape(rows, LAT * BROWS)
+    merid = mm(pick, merid_ref[...].reshape(LAT * BROWS, 256)).astype(BF)
+    halos = by_partner(odd, far_z_ref[...], near_z_ref[...])
+    zonal = [halos[0][:, 0:WIDE], zonal_ref[...].astype(F32), halos[1][:, 0:WIDE]]
+    zonal = jnp.concatenate(zonal, axis=0).astype(BF)
+    attended = mm(zonal.reshape(rows, 256), w_out_ref[0:256]) + mm(merid, w_out_ref[256:512])
+    wide = []
+    for halo, rest in zip(halos, by_partner(odd, far_f_ref[...], near_f_ref[...])):
+        corner = [halo[:, i : i + E] for i in range(WIDE, WIDE + 4 * E, E)]
+        corner = [jnp.concatenate(corner[n : n + 2], axis=2) for n in (0, 2)]
+        wide.append(jnp.concatenate([corner[0], rest, corner[1]], axis=1))
+    wide.insert(1, widened(left_ref[...], field_ref[...], right_ref[...]))
+    wide = jnp.concatenate(wide, axis=0)
+    mixed_ref[...] = (wide + attended.reshape(TALL, WIDE, C)).astype(BF).astype(F32)
     for lane in range(0, C, 128):
         lanes = slice(lane, lane + 128)
-        rows = {3 + i: mixed_ref[i, :, lanes].astype(F32) for i in range(R)}
+        window = {i: mixed_ref[i, :, lanes] for i in range(TALL)}
         for r in range(R):
-            out_ref[r * W : (r + 1) * W, lanes] = conv_part(rows, conv_ref, lanes, r)
-    for load in loads:
-        load.wait()
-
-
-def block_kernel(
-    odd_ref, mixed_ref, own_ref, far_ref, near_ref, conv_ref, w_in_ref, w_back_ref, out_ref, conv_out
-):
-    odd = odd_ref[0] == 1
-    for lane in range(0, C, 128):
-        lanes = slice(lane, lane + 128)
-        rows = {}
-        for i in range(3):
-            far, near = far_ref[i, :, lanes].astype(F32), near_ref[i, :, lanes].astype(F32)
-            rows[i] = jnp.where(odd, near, far)
-            rows[7 + i] = jnp.where(odd, far, near)
-        for r in range(R):
-            here = (slice(r * W, (r + 1) * W), lanes)
-            conv_out[here] = own_ref[here] + conv_part(rows, conv_ref, lanes, r)
+            conv_out[r * W : (r + 1) * W, lanes] = conv_part(window, conv_ref, lanes, r)
     normed = layer_norm(conv_out[...]).astype(BF)
+    loads[0].wait()
     hidden = mm(normed, w_in_ref[...])
     hidden = 0.5 * hidden * (1.0 + lax.erf(hidden * math.sqrt(0.5)))
+    loads[1].wait()
     back = mm(hidden.astype(BF), w_back_ref[...])
-    own = mixed_ref[...].astype(F32)[:, E : E + W].reshape(CELLS, C)
+    own = mixed_ref[HALO : HALO + R, E : E + W, :].reshape(CELLS, C)
     out_ref[...] = (own + back).astype(BF).reshape(R, W, C)
 
 
@@ -277,18 +297,18 @@
     y = (lax.axis_index("lon").astype(jnp.int32) >> 2).reshape(1)
     odd = (lax.axis_index("lat").astype(jnp.int32) & 1).reshape(1)
     field, y, odd = lax.optimization_barrier((field, y, odd))
-    row, first, last = call(
+    row, first, last, far_f, near_f = call(
         zonal_project_kernel,
-        (shape(R, W, 384), shape(R * E, C), shape(R * E, C)),
+        (shape(R, W, 384), shape(R * E, C), shape(R * E, C), shape(HALO, W, C), shape(HALO, W, C)),
         200_000_000,
-        in_specs=[ANY, ANY],
+        in_specs=[SMEM, ANY, ANY],
         scratch_shapes=[
             pltpu.VMEM((R, W, C), BF),
             pltpu.VMEM((C, 256), BF),
             pltpu.VMEM((C, 128), BF),
             pltpu.SemaphoreType.DMA((3,)),
         ],
-    )(in_hbm(field), in_hbm(w_qkv))
+    )(odd, in_hbm(field), in_hbm(w_qkv))
     row = lax.all_to_all(row, "lon", 0, 0, axis_index_groups=along_z)
     slots = call(
         spread_kernel,
@@ -312,37 +332,41 @@
         input_output_aliases={0: 0},
         scratch_shapes=[pltpu.VMEM((2, MROWS, C), BF), pltpu.SemaphoreType.DMA((2,))],
     )(merid, merid_edges, field_left, field_right)
-    slots, merid = lax.optimization_barrier((slots, merid))
+    near_f = lax.ppermute(near_f, "lat", near_pairs)
+    far_f = lax.ppermute(far_f, "lat", far_pairs)
+    slots, merid, far_f, near_f = lax.optimization_barrier((slots, merid, far_f, near_f))
     merid = lax.all_to_all(merid, "lat", 0, 0)
     zonal = call(
         zonal_kernel, shape(ZS, WIDE, 256), 4_000_000_000, vmem=24, in_specs=[SMEM, VMEM, VMEM]
     )(y, row, slots)
     zonal = lax.all_to_all(zonal, "lon", 0, 0, axis_index_groups=along_z)
-    merid = call(merid_kernel, shape(LAT, MROWS, 256), 1_000_000_000)(merid, w_qkv)
+    merid = call(merid_kernel, shape(LAT, BROWS, 256), 1_000_000_000)(merid, w_qkv)
     merid = lax.all_to_all(merid, "lat", 0, 0)
-    mixed, far, near = call(
-        mix_kernel,
-        (shape(R, WIDE, C), shape(3, WIDE, C), shape(3, WIDE, C)),
-        800_000_000,
-        in_specs=[SMEM] + [VMEM] * 6,
-    )(odd, zonal, merid, field_left, field_right, field, w_out)
-    near = lax.ppermute(near, "lat", near_pairs)
-    far = lax.ppermute(far, "lat", far_pairs)
-    conv_w = conv_w.reshape(49, C)
-    own, w_in, w_back = call(
-        own_conv_kernel,
-        (jax.ShapeDtypeStruct((CELLS, C), F32), shape(*w_in.shape), shape(*w_back.shape)),
-        1_000_000_000,
-        in_specs=[VMEM, VMEM, ANY, ANY],
-        scratch_shapes=[pltpu.SemaphoreType.DMA((2,))],
-    )(mixed, conv_w, in_hbm(w_in), in_hbm(w_back))
+    far_z, near_z = call(
+        zonal_halo_kernel,
+        (shape(HALO, WIDE + 4 * E, 256), shape(HALO, WIDE + 4 * E, 256)),
+        10_000_000,
+        in_specs=[SMEM] + [VMEM] * 3,
+    )(odd, zonal, field_left, field_right)
+    near_z = lax.ppermute(near_z, "lat", near_pairs)
+    far_z = lax.ppermute(far_z, "lat", far_pairs)
     return call(
         block_kernel,
         shape(R, W, C),
-        2_000_000_000,
-        in_specs=[SMEM] + [VMEM] * 7,
-        scratch_shapes=[pltpu.VMEM((CELLS, C), F32)],
-    )(odd, mixed, own, far, near, conv_w, w_in, w_back)
+        4_000_000_000,
+        vmem=24,
+        in_specs=[SMEM] + [VMEM] * 11 + [ANY, ANY],
+        scratch_shapes=[
+            pltpu.VMEM((TALL, WIDE, C), F32),
+            pltpu.VMEM((CELLS, C), F32),
+            pltpu.VMEM(w_in.shape, BF),
+            pltpu.VMEM(w_back.shape, BF),
+            pltpu.SemaphoreType.DMA((2,)),
+        ],
+    )(
+        odd, zonal, far_z, near_z, merid, field_left, field_right, field, far_f, near_f,
+        w_out, conv_w.reshape(49, C), in_hbm(w_in), in_hbm(w_back),
+    )
 
 
 def solution(mesh):

time: 96.8 us -> 101 us (1.043)
  the two profiles are of different devices: /device:TPU:7 before, /device:TPU:89 now
where the time goes in v8:
time: 101 us; the launch traced here: 100 us
  starting transfers between devices  52 us (51%)
  Pallas kernels  19.2 us (19%)
  blocking collectives  17.4 us (17%)
  waiting for transfers between devices  11.4 us (11%)
    all_to_all x1, blocking collectives, per_device(): row = lax.all_to_all(row, 'lon', 0, 0, axis_index_groups=along_z)  17.4 us
    all_to_all x2, starting transfers between devices, per_device(): merid = lax.all_to_all(merid, 'lat', 0, 0)  13.6 us
    all_to_all x1, starting transfers between devices, per_device(): zonal = lax.all_to_all(zonal, 'lon', 0, 0, axis_index_groups=along_z)  8.76 us
    pallas_call x1, Pallas kernels, per_device(): call(block_kernel, shape(R, W, C), 4000000000, vmem=24, in_specs=[SMEM] +...  6.79 us
    all_to_all x1, starting transfers between devices, per_device(): slots = lax.all_to_all(slots, 'lon', 0, 0, axis_index_groups=along_y)  6.76 us
    ppermute x1, starting transfers between devices, per_device(): far_f = lax.ppermute(far_f, 'lat', far_pairs)  5.9 us
    ppermute x1, starting transfers between devices, per_device(): field_right = lax.ppermute(first, 'lon', left)  5.88 us
    all_to_all x2, waiting for transfers between devices, per_device(): merid = lax.all_to_all(merid, 'lat', 0, 0)  5.02 us
  transfers between devices with their start and end apart: 10, of which 4 were waited for; matrix products, arithmetic and copies ran while one was open for 0% of the time, Pallas kernels for 10%

profile of v8, /device:TPU:89, one launch (start us, length us, event | category | flops | bytes accessed | tf_op | source)
XLA Modules:
  0.0 100.4 jit_solution(2529250827422690592)
XLA Ops:
  0.0 1.7 %shard_map.64 = (bf16[4,64,384]{2,1,0:T(8,128)(2,1)S(1)}, bf16[32,512]{1,0:T(8,128)(2,1)S(1)}, bf16[32,512]{1,0:T(8,128)(2,1)S(1)}, bf16[3,64,512]{2,1,0:T(8,128)(2,1)S(1)}, bf16[3,64,512]{2,1,0:T(8,128)(2,1)S(1)}) custom-call(s32[1]{0:T(128)} %bitcast.1.odd_ref, bf16[4,64,512]{2,1,0:T(8,128)(2,1)} %field_ref.1, bf16[512,1152]{1,0:T(8,128)(2,1)} %w_ref.1), custom_call_target="tpu_custom_call" | custom-call | flops 200000000 | bytes 2000000 | tf_op jit(solution)/shard_map/pallas_call | solution.py:300
  1.7 0.0 copy-start.1
  1.7 17.4 %all_to_all.25.in_ref.own_ref = bf16[4,64,384]{2,1,0:T(8,128)(2,1)S(1)} all-to-all(bf16[4,64,384]{2,1,0:T(8,128)(2,1)S(1)} %get-tuple-element.24), channel_id=1, replica_groups={{0,1,2,3},{4,5,6,7},{8,9,10,11},{12,13,14,15},{16,17,18,19},{20,21,22,2..., dimensions={0} | all-to-all | bytes 393216 | tf_op jit(solution)/shard_map/all_to_all | solution.py:312
  19.1 0.9 shard_map.65
  20.0 6.8 %all-to-all-start.1 = ((bf16[8,272,128]{2,1,0:T(8,128)(2,1)}), bf16[8,272,128]{2,1,0:T(8,128)(2,1)S(1)}, u32[]{:S(2)}, u32[]{:S(2)}) async-start(bf16[8,272,128]{2,1,0:T(8,128)(2,1)} %shard_map.65), calls=%async_computation.1 | async-start | bytes 1114112 | tf_op jit(solution)/shard_map/all_to_all | solution.py:320
  26.8 5.9 %collective-permute-start.2 = (bf16[3,64,512]{2,1,0:T(8,128)(2,1)S(1)}, bf16[3,64,512]{2,1,0:T(8,128)(2,1)S(1)}, u32[]{:S(2)}, u32[]{:S(2)}) collective-permute-start(bf16[3,64,512]{2,1,0:T(8,128)(2,1)S(1)} %get-tuple-element.29), channel_id=1, source_target_pairs={{32,64},{96,128},{160,192},{224,256},{288,320},{352,384},{416,448}... | collective-permute-start | bytes 589832 | tf_op jit(solution)/shard_map/ppermute | solution.py:336
  32.7 1.9 %collective-permute-start.3 = (bf16[3,64,512]{2,1,0:T(8,128)(2,1)S(1)}, bf16[3,64,512]{2,1,0:T(8,128)(2,1)S(1)}, u32[]{:S(2)}, u32[]{:S(2)}) collective-permute-start(bf16[3,64,512]{2,1,0:T(8,128)(2,1)S(1)} %get-tuple-element.30), channel_id=1, source_target_pairs={{0,32},{64,96},{128,160},{192,224},{256,288},{320,352},{384,416},{... | collective-permute-start | bytes 589832 | tf_op jit(solution)/shard_map/ppermute | solution.py:335
  34.6 2.4 %collective-permute-start = (bf16[32,512]{1,0:T(8,128)(2,1)S(1)}, bf16[32,512]{1,0:T(8,128)(2,1)S(1)}, u32[]{:S(2)}, u32[]{:S(2)}) collective-permute-start(bf16[32,512]{1,0:T(8,128)(2,1)S(1)} %get-tuple-element.27), channel_id=1, source_target_pairs={{0,1},{1,2},{2,3},{3,4},{4,5},{5,6},{6,7},{7,8},{8,9},{9,10},{10,1... | collective-permute-start | bytes 98312 | tf_op jit(solution)/shard_map/ppermute | solution.py:321
  37.1 5.9 %collective-permute-start.1 = (bf16[32,512]{1,0:T(8,128)(2,1)S(1)}, bf16[32,512]{1,0:T(8,128)(2,1)S(1)}, u32[]{:S(2)}, u32[]{:S(2)}) collective-permute-start(bf16[32,512]{1,0:T(8,128)(2,1)S(1)} %get-tuple-element.28), channel_id=1, source_target_pairs={{1,0},{2,1},{3,2},{4,3},{5,4},{6,5},{7,6},{8,7},{9,8},{10,9},{11,1... | collective-permute-start | bytes 98312 | tf_op jit(solution)/shard_map/ppermute | solution.py:322
  42.9 0.0 copy-done.1
  43.0 1.3 %shard_map.66 = (bf16[16,24,512]{2,1,0:T(8,128)(2,1)}, bf16[2,24,512]{2,1,0:T(8,128)(2,1)S(1)}) custom-call(bf16[4,64,512]{2,1,0:T(8,128)(2,1)S(1)} %copy-done.1), custom_call_target="tpu_custom_call" | custom-call | flops 300000000 | bytes 2000000 | tf_op jit(solution)/shard_map/pallas_call | solution.py:323
  44.2 0.0 collective-permute-done.left_ref
  44.2 0.0 collective-permute-done.1.right_ref
  44.2 0.9 shard_map.67
  45.2 0.0 collective-permute-done.2.far_f_ref
  45.2 0.0 collective-permute-done.3.near_f_ref
  45.2 0.0 all-to-all-done.1.all_ref
  45.2 6.5 %all-to-all-start.3 = ((bf16[16,24,512]{2,1,0:T(8,128)(2,1)}), bf16[16,24,512]{2,1,0:T(8,128)(2,1)S(1)}, u32[]{:S(2)}, u32[]{:S(2)}) async-start(bf16[16,24,512]{2,1,0:T(8,128)(2,1)} %shard_map.67), calls=%async_computation.3 | async-start | bytes 786432 | tf_op jit(solution)/shard_map/all_to_all | solution.py:338
  51.7 0.0 copy-start
  51.7 4.0 %shard_map.68 = bf16[4,80,256]{2,1,0:T(8,128)(2,1)} custom-call(s32[1]{0:T(128)} %bitcast.y_ref, bf16[4,64,384]{2,1,0:T(8,128)(2,1)S(1)} %all_to_all.25.in_ref.own_ref, bf16[8,272,128]{2,1,0:T(8,128)(2,1)S(1)} %all-to-all-done.1.all_ref), custom_call_target="tpu_custom_call" | custom-call | flops 4000000000 | bytes 2000000 | tf_op jit(solution)/shard_map/pallas_call | solution.py:339
  55.7 3.8 %all-to-all-done.3.in_ref = bf16[16,24,512]{2,1,0:T(8,128)(2,1)S(1)} async-done(((bf16[16,24,512]{2,1,0:T(8,128)(2,1)}), bf16[16,24,512]{2,1,0:T(8,128)(2,1)S(1)}, u32[]{:S(2)}, u32[]{:S(2)}) %all-to-all-start.3) | async-done | bytes 393248 | tf_op jit(solution)/shard_map/all_to_all | solution.py:338
  59.5 8.8 %all-to-all-start.2 = ((bf16[4,80,256]{2,1,0:T(8,128)(2,1)}), bf16[4,80,256]{2,1,0:T(8,128)(2,1)S(1)}, u32[]{:S(2)}, u32[]{:S(2)}) async-start(bf16[4,80,256]{2,1,0:T(8,128)(2,1)} %shard_map.68), calls=%async_computation.2 | async-start | bytes 327680 | tf_op jit(solution)/shard_map/all_to_all | solution.py:342
  68.3 0.0 copy-done
  68.3 3.5 %shard_map.70 = bf16[16,56,256]{2,1,0:T(8,128)(2,1)} custom-call(bf16[16,24,512]{2,1,0:T(8,128)(2,1)S(1)} %all-to-all-done.3.in_ref, bf16[512,1152]{1,0:T(8,128)(2,1)S(1)} %copy-done), custom_call_target="tpu_custom_call" | custom-call | flops 1000000000 | bytes 2000000 | tf_op jit(solution)/shard_map/pallas_call | solution.py:343
  71.8 0.0 copy-start.3
  71.8 0.0 copy-start.2
  71.8 3.9 %all-to-all-done.2.zonal_ref = bf16[4,80,256]{2,1,0:T(8,128)(2,1)S(1)} async-done(((bf16[4,80,256]{2,1,0:T(8,128)(2,1)}), bf16[4,80,256]{2,1,0:T(8,128)(2,1)S(1)}, u32[]{:S(2)}, u32[]{:S(2)}) %all-to-all-start.2) | async-done | bytes 163872 | tf_op jit(solution)/shard_map/all_to_all | solution.py:342
  75.7 7.2 %all-to-all-start.4 = ((bf16[16,56,256]{2,1,0:T(8,128)(2,1)}), bf16[16,56,256]{2,1,0:T(8,128)(2,1)S(1)}, u32[]{:S(2)}, u32[]{:S(2)}) async-start(bf16[16,56,256]{2,1,0:T(8,128)(2,1)} %shard_map.70), calls=%async_computation.4 | async-start | bytes 917504 | tf_op jit(solution)/shard_map/all_to_all | solution.py:344
  82.9 3.4 %collective-permute-start.4 = (bf16[3,112,256]{2,1,0:T(8,128)(2,1)S(1)}, bf16[3,112,256]{2,1,0:T(8,128)(2,1)S(1)}, u32[]{:S(2)}, u32[]{:S(2)}) collective-permute-start(bf16[3,112,256]{2,1,0:T(8,128)(2,1)S(1)} %get-tuple-element.32), channel_id=1, source_target_pairs={{32,64},{96,128},{160,192},{224,256},{288,320},{352,384},{416,448}... | collective-permute-start | bytes 516104 | tf_op jit(solution)/shard_map/ppermute | solution.py:352
  86.2 3.4 %collective-permute-start.5 = (bf16[3,112,256]{2,1,0:T(8,128)(2,1)S(1)}, bf16[3,112,256]{2,1,0:T(8,128)(2,1)S(1)}, u32[]{:S(2)}, u32[]{:S(2)}) collective-permute-start(bf16[3,112,256]{2,1,0:T(8,128)(2,1)S(1)} %get-tuple-element.33), channel_id=1, source_target_pairs={{0,32},{64,96},{128,160},{192,224},{256,288},{320,352},{384,416},{... | collective-permute-start | bytes 516104 | tf_op jit(solution)/shard_map/ppermute | solution.py:351
  89.7 0.0 copy-done.3
  89.7 2.5 %collective-permute-done.4.far_z_ref = bf16[3,112,256]{2,1,0:T(8,128)(2,1)S(1)} collective-permute-done((bf16[3,112,256]{2,1,0:T(8,128)(2,1)S(1)}, bf16[3,112,256]{2,1,0:T(8,128)(2,1)S(1)}, u32[]{:S(2)}, u32[]{:S(2)}) %collective-permute-start.4) | collective-permute-done | bytes 172064 | tf_op jit(solution)/shard_map/ppermute | solution.py:352
  92.2 0.0 collective-permute-done.5.near_z_ref
  92.2 1.2 %all-to-all-done.4.merid_ref = bf16[16,56,256]{2,1,0:T(8,128)(2,1)S(1)} async-done(((bf16[16,56,256]{2,1,0:T(8,128)(2,1)}), bf16[16,56,256]{2,1,0:T(8,128)(2,1)S(1)}, u32[]{:S(2)}, u32[]{:S(2)}) %all-to-all-start.4) | async-done | bytes 458784 | tf_op jit(solution)/shard_map/all_to_all | solution.py:344
  93.4 0.0 copy-done.2
  93.4 6.8 %shard_map.71 = bf16[4,64,512]{2,1,0:T(8,128)(2,1)} custom-call(s32[1]{0:T(128)} %bitcast.1.odd_ref, bf16[4,80,256]{2,1,0:T(8,128)(2,1)S(1)} %all-to-all-done.2.zonal_ref, bf16[3,112,256]{2,1,0:T(8,128)(2,1)S(1)} %collective-permute-done.4.far_z_ref, bf16[3,112,256]{2,1,0:T(8,128)(2,1)S(1)} %collective-permute-done.5.near_z_ref, ...), custom_call_target="tpu_custom_call" | custom-call | flops 4000000000 | bytes 2000000 | tf_op jit(solution)/shard_map/pallas_call | solution.py:353
  (2 shorter events, 0.0 us)
Async XLA Ops:
  1.7 41.2 %copy-start.1 = (bf16[4,64,512]{2,1,0:T(8,128)(2,1)S(1)}, bf16[4,64,512]{2,1,0:T(8,128)(2,1)}, u32[]{:S(2)}) copy-start(bf16[4,64,512]{2,1,0:T(8,128)(2,1)} %field_ref.1) | copy-start | bytes 786436
  20.0 25.1 %all-to-all-start.1 = ((bf16[8,272,128]{2,1,0:T(8,128)(2,1)}), bf16[8,272,128]{2,1,0:T(8,128)(2,1)S(1)}, u32[]{:S(2)}, u32[]{:S(2)}) async-start(bf16[8,272,128]{2,1,0:T(8,128)(2,1)} %shard_map.65), calls=%async_computation.1 | async-start | bytes 1114112 | tf_op jit(solution)/shard_map/all_to_all | solution.py:320
  26.8 18.4 %collective-permute-start.2 = (bf16[3,64,512]{2,1,0:T(8,128)(2,1)S(1)}, bf16[3,64,512]{2,1,0:T(8,128)(2,1)S(1)}, u32[]{:S(2)}, u32[]{:S(2)}) collective-permute-start(bf16[3,64,512]{2,1,0:T(8,128)(2,1)S(1)} %get-tuple-element.29), channel_id=1, source_target_pairs={{32,64},{96,128},{160,192},{224,256},{288,320},{352,384},{416,448}... | collective-permute-start | bytes 589832 | tf_op jit(solution)/shard_map/ppermute | solution.py:336
  32.7 12.5 %collective-permute-start.3 = (bf16[3,64,512]{2,1,0:T(8,128)(2,1)S(1)}, bf16[3,64,512]{2,1,0:T(8,128)(2,1)S(1)}, u32[]{:S(2)}, u32[]{:S(2)}) collective-permute-start(bf16[3,64,512]{2,1,0:T(8,128)(2,1)S(1)} %get-tuple-element.30), channel_id=1, source_target_pairs={{0,32},{64,96},{128,160},{192,224},{256,288},{320,352},{384,416},{... | collective-permute-start | bytes 589832 | tf_op jit(solution)/shard_map/ppermute | solution.py:335
  34.6 9.6 %collective-permute-start = (bf16[32,512]{1,0:T(8,128)(2,1)S(1)}, bf16[32,512]{1,0:T(8,128)(2,1)S(1)}, u32[]{:S(2)}, u32[]{:S(2)}) collective-permute-start(bf16[32,512]{1,0:T(8,128)(2,1)S(1)} %get-tuple-element.27), channel_id=1, source_target_pairs={{0,1},{1,2},{2,3},{3,4},{4,5},{5,6},{6,7},{7,8},{8,9},{9,10},{10,1... | collective-permute-start | bytes 98312 | tf_op jit(solution)/shard_map/ppermute | solution.py:321
  37.1 7.2 %collective-permute-start.1 = (bf16[32,512]{1,0:T(8,128)(2,1)S(1)}, bf16[32,512]{1,0:T(8,128)(2,1)S(1)}, u32[]{:S(2)}, u32[]{:S(2)}) collective-permute-start(bf16[32,512]{1,0:T(8,128)(2,1)S(1)} %get-tuple-element.28), channel_id=1, source_target_pairs={{1,0},{2,1},{3,2},{4,3},{5,4},{6,5},{7,6},{8,7},{9,8},{10,9},{11,1... | collective-permute-start | bytes 98312 | tf_op jit(solution)/shard_map/ppermute | solution.py:322
  45.2 14.3 %all-to-all-start.3 = ((bf16[16,24,512]{2,1,0:T(8,128)(2,1)}), bf16[16,24,512]{2,1,0:T(8,128)(2,1)S(1)}, u32[]{:S(2)}, u32[]{:S(2)}) async-start(bf16[16,24,512]{2,1,0:T(8,128)(2,1)} %shard_map.67), calls=%async_computation.3 | async-start | bytes 786432 | tf_op jit(solution)/shard_map/all_to_all | solution.py:338
  51.7 16.6 %copy-start = (bf16[512,1152]{1,0:T(8,128)(2,1)S(1)}, bf16[512,1152]{1,0:T(8,128)(2,1)}, u32[]{:S(2)}) copy-start(bf16[512,1152]{1,0:T(8,128)(2,1)} %w_ref.1) | copy-start | bytes 3538948
  59.5 16.2 %all-to-all-start.2 = ((bf16[4,80,256]{2,1,0:T(8,128)(2,1)}), bf16[4,80,256]{2,1,0:T(8,128)(2,1)S(1)}, u32[]{:S(2)}, u32[]{:S(2)}) async-start(bf16[4,80,256]{2,1,0:T(8,128)(2,1)} %shard_map.68), calls=%async_computation.2 | async-start | bytes 327680 | tf_op jit(solution)/shard_map/all_to_all | solution.py:342
  71.8 17.9 %copy-start.3 = (f32[7,7,512]{2,1,0:T(8,128)S(1)}, f32[7,7,512]{2,1,0:T(8,128)}, u32[]{:S(2)}) copy-start(f32[7,7,512]{2,1,0:T(8,128)} %param.9) | copy-start | bytes 301060
  71.8 21.6 %copy-start.2 = (bf16[512,512]{1,0:T(8,128)(2,1)S(1)}, bf16[512,512]{1,0:T(8,128)(2,1)}, u32[]{:S(2)}) copy-start(bf16[512,512]{1,0:T(8,128)(2,1)} %w_out_ref.1) | copy-start | bytes 1572868
  75.7 17.7 %all-to-all-start.4 = ((bf16[16,56,256]{2,1,0:T(8,128)(2,1)}), bf16[16,56,256]{2,1,0:T(8,128)(2,1)S(1)}, u32[]{:S(2)}, u32[]{:S(2)}) async-start(bf16[16,56,256]{2,1,0:T(8,128)(2,1)} %shard_map.70), calls=%async_computation.4 | async-start | bytes 917504 | tf_op jit(solution)/shard_map/all_to_all | solution.py:344
  82.9 9.3 %collective-permute-start.4 = (bf16[3,112,256]{2,1,0:T(8,128)(2,1)S(1)}, bf16[3,112,256]{2,1,0:T(8,128)(2,1)S(1)}, u32[]{:S(2)}, u32[]{:S(2)}) collective-permute-start(bf16[3,112,256]{2,1,0:T(8,128)(2,1)S(1)} %get-tuple-element.32), channel_id=1, source_target_pairs={{32,64},{96,128},{160,192},{224,256},{288,320},{352,384},{416,448}... | collective-permute-start | bytes 516104 | tf_op jit(solution)/shard_map/ppermute | solution.py:352
  86.2 6.0 %collective-permute-start.5 = (bf16[3,112,256]{2,1,0:T(8,128)(2,1)S(1)}, bf16[3,112,256]{2,1,0:T(8,128)(2,1)S(1)}, u32[]{:S(2)}, u32[]{:S(2)}) collective-permute-start(bf16[3,112,256]{2,1,0:T(8,128)(2,1)S(1)} %get-tuple-element.33), channel_id=1, source_target_pairs={{0,32},{64,96},{128,160},{192,224},{256,288},{320,352},{384,416},{... | collective-permute-start | bytes 516104 | tf_op jit(solution)/shard_map/ppermute | solution.py:351

commit v9 on v6

--- a/solution.py
+++ b/solution.py
@@ -15,8 +15,9 @@
 W = 64
 CELLS = R * W
 E = 8
-WIDE = W + 2 * E
-MC = WIDE // LAT
+WIDE = W + E
+MWIDE = W + 2 * E
+MC = MWIDE // LAT
 EDGES = (1, LAT - 2)
 MROWS = 24
 YS = 8
@@ -111,13 +112,13 @@
     kv_one = jnp.where(ones, jnp.ones_like(kv), kv)
     behind = all_ref[lax.rem(y + YS - 1, YS), SPAN:KEYS, :].astype(F32)
     ahead = all_ref[lax.rem(y + 1, YS), SPAN:KEYS, :].astype(F32)
-    count = SPAN + 2 * E
+    count = SPAN + E
     low = iota((count, 128), 1) < HD
     for pair in range(2):
         lanes = slice(pair * 128, pair * 128 + 128)
-        rows = slice(pair * E, pair * E + E)
+        before, after = slice(pair * E + E // 2, pair * E + E), slice(pair * E, pair * E + E // 2)
         q = own_ref[:, :, lanes].astype(F32).reshape(SPAN, 128)
-        q = jnp.concatenate([behind[rows], q, ahead[rows]], axis=0) * (1.0 / math.sqrt(HD))
+        q = jnp.concatenate([behind[before], q, ahead[after]], axis=0) * (1.0 / math.sqrt(HD))
         outs = []
         for head in range(2):
             placed = q if head == 0 else pltpu.roll(q, HD, 1)
@@ -135,7 +136,7 @@
 
 def widened(left, own, right):
     left, right = (a.astype(F32).reshape(R, E, a.shape[-1]) for a in (left, right))
-    return jnp.concatenate([left, own.astype(F32), right], axis=1)
+    return jnp.concatenate([left[:, E // 2 :], own.astype(F32), right[:, 0 : E // 2]], axis=1)
 
 
 def merid_own_kernel(field_ref, out_ref, edge_ref):
@@ -193,7 +194,7 @@
     rows = R * WIDE
     merid = merid_ref[...].astype(F32).reshape(LAT * MROWS, 256).astype(BF)
     dims = (R, WIDE, LAT * MROWS)
-    r, w, t = iota(dims, 0), iota(dims, 1), iota(dims, 2)
+    r, w, t = iota(dims, 0), iota(dims, 1) + E // 2, iota(dims, 2)
     m = (t * 2731) >> 16
     i = t - m * MROWS
     cell = one_hot((m * MC + (i >> 2) == w) & ((i & 3) == r) & (i < R * MC))
@@ -223,7 +224,7 @@
             if r + a in rows:
                 term = rows[r + a] * conv_ref[a * 7 + b, lanes][None, :]
                 column = term if column is None else column + term
-        moved = column[b + 5 : b + 5 + W]
+        moved = column[b + 1 : b + 1 + W]
         total = moved if total is None else total + moved
     return total
 
@@ -262,7 +263,7 @@
     hidden = mm(normed, w_in_ref[...])
     hidden = 0.5 * hidden * (1.0 + lax.erf(hidden * math.sqrt(0.5)))
     back = mm(hidden.astype(BF), w_back_ref[...])
-    own = mixed_ref[...].astype(F32)[:, E : E + W].reshape(CELLS, C)
+    own = mixed_ref[...].astype(F32)[:, E // 2 : E // 2 + W].reshape(CELLS, C)
     out_ref[...] = (own + back).astype(BF).reshape(R, W, C)
 
 

time: 96.8 us -> 96.2 us (level)
  no operation moved by 1% of the time
where the time goes in v9:
time: 96.2 us; the launch traced here: 95.1 us
  starting transfers between devices  34.5 us (36%)
  blocking collectives  29.6 us (31%)
  Pallas kernels  15.6 us (16%)
  waiting for transfers between devices  15.2 us (16%)
    all_to_all x1, blocking collectives, per_device(): row = lax.all_to_all(row, 'lon', 0, 0, axis_index_groups=along_z)  17.9 us
    all_to_all x1, blocking collectives, per_device(): merid = lax.all_to_all(merid, 'lat', 0, 0)  11.6 us
    all_to_all x1, starting transfers between devices, per_device(): merid = lax.all_to_all(merid, 'lat', 0, 0)  8.79 us
    ppermute x1, starting transfers between devices, per_device(): field_right = lax.ppermute(first, 'lon', left)  7.58 us
    all_to_all x1, starting transfers between devices, per_device(): slots = lax.all_to_all(slots, 'lon', 0, 0, axis_index_groups=along_y)  6.83 us
    all_to_all x1, waiting for transfers between devices, per_device(): zonal = lax.all_to_all(zonal, 'lon', 0, 0, axis_index_groups=along_z)  5.7 us
    ppermute x1, waiting for transfers between devices, per_device(): field_left = lax.ppermute(last, 'lon', right)  4.41 us
    ppermute x1, starting transfers between devices, per_device(): far = lax.ppermute(far, 'lat', far_pairs)  4.12 us
  transfers between devices with their start and end apart: 7, of which 4 were waited for; matrix products, arithmetic and copies ran while one was open for 0% of the time, Pallas kernels for 10%

profile of v9, /device:TPU:7, one launch (start us, length us, event | category | flops | bytes accessed | tf_op | source)
XLA Modules:
  0.0 95.1 jit_solution(967287040628281842)
XLA Ops:
  0.0 1.7 %shard_map.64 = (bf16[4,64,384]{2,1,0:T(8,128)(2,1)S(1)}, bf16[32,512]{1,0:T(8,128)(2,1)S(1)}, bf16[32,512]{1,0:T(8,128)(2,1)S(1)}) custom-call(bf16[4,64,512]{2,1,0:T(8,128)(2,1)} %field_ref.1, bf16[512,1152]{1,0:T(8,128)(2,1)} %w_ref.2), custom_call_target="tpu_custom_call" | custom-call | flops 200000000 | bytes 2000000 | tf_op jit(solution)/shard_map/pallas_call | solution.py:281
  1.7 0.0 copy-start.1
  1.7 17.9 %all_to_all.25.in_ref.own_ref = bf16[4,64,384]{2,1,0:T(8,128)(2,1)S(1)} all-to-all(bf16[4,64,384]{2,1,0:T(8,128)(2,1)S(1)} %get-tuple-element.24), channel_id=1, replica_groups={{0,1,2,3},{4,5,6,7},{8,9,10,11},{12,13,14,15},{16,17,18,19},{20,21,22,2..., dimensions={0} | all-to-all | bytes 393216 | tf_op jit(solution)/shard_map/all_to_all | solution.py:293
  19.6 0.9 shard_map.65
  20.5 6.8 %all-to-all-start.1 = ((bf16[8,272,128]{2,1,0:T(8,128)(2,1)}), bf16[8,272,128]{2,1,0:T(8,128)(2,1)S(1)}, u32[]{:S(2)}, u32[]{:S(2)}) async-start(bf16[8,272,128]{2,1,0:T(8,128)(2,1)} %shard_map.65), calls=%async_computation.1 | async-start | bytes 1114112 | tf_op jit(solution)/shard_map/all_to_all | solution.py:301
  27.3 1.9 %collective-permute-start = (bf16[32,512]{1,0:T(8,128)(2,1)S(1)}, bf16[32,512]{1,0:T(8,128)(2,1)S(1)}, u32[]{:S(2)}, u32[]{:S(2)}) collective-permute-start(bf16[32,512]{1,0:T(8,128)(2,1)S(1)} %get-tuple-element.27), channel_id=1, source_target_pairs={{0,1},{1,2},{2,3},{3,4},{4,5},{5,6},{6,7},{7,8},{8,9},{9,10},{10,1... | collective-permute-start | bytes 98312 | tf_op jit(solution)/shard_map/ppermute | solution.py:302
  29.2 7.6 %collective-permute-start.1 = (bf16[32,512]{1,0:T(8,128)(2,1)S(1)}, bf16[32,512]{1,0:T(8,128)(2,1)S(1)}, u32[]{:S(2)}, u32[]{:S(2)}) collective-permute-start(bf16[32,512]{1,0:T(8,128)(2,1)S(1)} %get-tuple-element.28), channel_id=1, source_target_pairs={{1,0},{2,1},{3,2},{4,3},{5,4},{6,5},{7,6},{8,7},{9,8},{10,9},{11,1... | collective-permute-start | bytes 98312 | tf_op jit(solution)/shard_map/ppermute | solution.py:303
  36.8 0.0 copy-done.1
  36.8 1.2 %shard_map.66 = (bf16[16,24,512]{2,1,0:T(8,128)(2,1)}, bf16[2,24,512]{2,1,0:T(8,128)(2,1)S(1)}) custom-call(bf16[4,64,512]{2,1,0:T(8,128)(2,1)S(1)} %copy-done.1), custom_call_target="tpu_custom_call" | custom-call | flops 300000000 | bytes 2000000 | tf_op jit(solution)/shard_map/pallas_call | solution.py:304
  38.1 4.4 %collective-permute-done.left_ref = bf16[32,512]{1,0:T(8,128)(2,1)S(1)} collective-permute-done((bf16[32,512]{1,0:T(8,128)(2,1)S(1)}, bf16[32,512]{1,0:T(8,128)(2,1)S(1)}, u32[]{:S(2)}, u32[]{:S(2)}) %collective-permute-start) | collective-permute-done | bytes 32800 | tf_op jit(solution)/shard_map/ppermute | solution.py:302
  42.5 0.0 collective-permute-done.1.right_ref
  42.5 0.9 shard_map.67
  43.4 0.0 all-to-all-done.1.all_ref
  43.4 8.8 %all-to-all-start.3 = ((bf16[16,24,512]{2,1,0:T(8,128)(2,1)}), bf16[16,24,512]{2,1,0:T(8,128)(2,1)S(1)}, u32[]{:S(2)}, u32[]{:S(2)}) async-start(bf16[16,24,512]{2,1,0:T(8,128)(2,1)} %shard_map.67), calls=%async_computation.3 | async-start | bytes 786432 | tf_op jit(solution)/shard_map/all_to_all | solution.py:317
  52.2 0.0 copy-start
  52.2 4.0 %shard_map.68 = bf16[4,72,256]{2,1,0:T(8,128)(2,1)} custom-call(s32[1]{0:T(128)} %bitcast.y_ref, bf16[4,64,384]{2,1,0:T(8,128)(2,1)S(1)} %all_to_all.25.in_ref.own_ref, bf16[8,272,128]{2,1,0:T(8,128)(2,1)S(1)} %all-to-all-done.1.all_ref), custom_call_target="tpu_custom_call" | custom-call | flops 4000000000 | bytes 2000000 | tf_op jit(solution)/shard_map/pallas_call | solution.py:318
  56.2 3.4 %all-to-all-done.3.in_ref = bf16[16,24,512]{2,1,0:T(8,128)(2,1)S(1)} async-done(((bf16[16,24,512]{2,1,0:T(8,128)(2,1)}), bf16[16,24,512]{2,1,0:T(8,128)(2,1)S(1)}, u32[]{:S(2)}, u32[]{:S(2)}) %all-to-all-start.3) | async-done | bytes 393248 | tf_op jit(solution)/shard_map/all_to_all | solution.py:317
  59.7 3.3 %all-to-all-start.2 = ((bf16[4,72,256]{2,1,0:T(8,128)(2,1)}), bf16[4,72,256]{2,1,0:T(8,128)(2,1)S(1)}, u32[]{:S(2)}, u32[]{:S(2)}) async-start(bf16[4,72,256]{2,1,0:T(8,128)(2,1)} %shard_map.68), calls=%async_computation.2 | async-start | bytes 294912 | tf_op jit(solution)/shard_map/all_to_all | solution.py:321
  63.0 0.0 copy-done
  63.0 0.0 copy-start.2
  63.0 1.9 %shard_map.69 = bf16[16,24,256]{2,1,0:T(8,128)(2,1)S(1)} custom-call(bf16[16,24,512]{2,1,0:T(8,128)(2,1)S(1)} %all-to-all-done.3.in_ref, bf16[512,1152]{1,0:T(8,128)(2,1)S(1)} %copy-done), custom_call_target="tpu_custom_call" | custom-call | flops 1000000000 | bytes 2000000 | tf_op jit(solution)/shard_map/pallas_call | solution.py:322
  64.9 5.7 %all-to-all-done.2.zonal_ref = bf16[4,72,256]{2,1,0:T(8,128)(2,1)S(1)} async-done(((bf16[4,72,256]{2,1,0:T(8,128)(2,1)}), bf16[4,72,256]{2,1,0:T(8,128)(2,1)S(1)}, u32[]{:S(2)}, u32[]{:S(2)}) %all-to-all-start.2) | async-done | bytes 147488 | tf_op jit(solution)/shard_map/all_to_all | solution.py:321
  70.6 11.6 %all_to_all.26.merid_ref = bf16[16,24,256]{2,1,0:T(8,128)(2,1)S(1)} all-to-all(bf16[16,24,256]{2,1,0:T(8,128)(2,1)S(1)} %shard_map.69), channel_id=1, replica_groups=mesh['lat'=16,'lon'=32] {'lat'}, dimensions={0} | all-to-all | bytes 393216 | tf_op jit(solution)/shard_map/all_to_all | solution.py:323
  82.2 0.0 copy-done.2
  82.2 0.0 copy-start.3
  82.2 0.6 shard_map.70
  82.9 4.1 %collective-permute-start.2 = (bf16[3,72,512]{2,1,0:T(8,128)(2,1)S(1)}, bf16[3,72,512]{2,1,0:T(8,128)(2,1)S(1)}, u32[]{:S(2)}, u32[]{:S(2)}) collective-permute-start(bf16[3,72,512]{2,1,0:T(8,128)(2,1)S(1)} %get-tuple-element.33), channel_id=1, source_target_pairs={{32,64},{96,128},{160,192},{224,256},{288,320},{352,384},{416,448}... | collective-permute-start | bytes 663560 | tf_op jit(solution)/shard_map/ppermute | solution.py:331
  87.0 1.9 %collective-permute-start.3 = (bf16[3,72,512]{2,1,0:T(8,128)(2,1)S(1)}, bf16[3,72,512]{2,1,0:T(8,128)(2,1)S(1)}, u32[]{:S(2)}, u32[]{:S(2)}) collective-permute-start(bf16[3,72,512]{2,1,0:T(8,128)(2,1)S(1)} %get-tuple-element.34), channel_id=1, source_target_pairs={{0,32},{64,96},{128,160},{192,224},{256,288},{320,352},{384,416},{... | collective-permute-start | bytes 663560 | tf_op jit(solution)/shard_map/ppermute | solution.py:330
  88.9 0.0 copy-done.3
  88.9 1.6 %shard_map.71 = (f32[256,512]{1,0:T(8,128)S(1)}, bf16[512,1024]{1,0:T(8,128)(2,1)S(1)}, bf16[1024,512]{1,0:T(8,128)(2,1)S(1)}) custom-call(bf16[4,72,512]{2,1,0:T(8,128)(2,1)S(1)} %get-tuple-element.31.mixed_ref, f32[49,512]{1,0:T(8,128)S(1)} %reshape.11.conv_ref, bf16[512,1024]{1,0:T(8,128)(2,1)} %w_in_hbm.1, bf16[1024,512]{1,0:T(8,128)(2,1)} %w_back_hbm.1), custom_call_target="tpu_custom_call" | custom-call | flops 1000000000 | bytes 2000000 | tf_op jit(solution)/shard_map/pallas_call | solution.py:333
  90.5 1.7 %collective-permute-done.2.far_ref = bf16[3,72,512]{2,1,0:T(8,128)(2,1)S(1)} collective-permute-done((bf16[3,72,512]{2,1,0:T(8,128)(2,1)S(1)}, bf16[3,72,512]{2,1,0:T(8,128)(2,1)S(1)}, u32[]{:S(2)}, u32[]{:S(2)}) %collective-permute-start.2) | collective-permute-done | bytes 221216 | tf_op jit(solution)/shard_map/ppermute | solution.py:331
  92.2 0.0 collective-permute-done.3.near_ref
  92.2 2.9 %shard_map.72 = bf16[4,64,512]{2,1,0:T(8,128)(2,1)} custom-call(s32[1]{0:T(128)} %bitcast.1.odd_ref, bf16[4,72,512]{2,1,0:T(8,128)(2,1)S(1)} %get-tuple-element.31.mixed_ref, f32[256,512]{1,0:T(8,128)S(1)} %get-tuple-element.32.own_ref, bf16[3,72,512]{2,1,0:T(8,128)(2,1)S(1)} %collective-permute-done.2.far_ref, ...), custom_call_target="tpu_custom_call" | custom-call | flops 2000000000 | bytes 2000000 | tf_op jit(solution)/shard_map/pallas_call | solution.py:340
  (1 shorter events, 0.0 us)
Async XLA Ops:
  1.7 35.2 %copy-start.1 = (bf16[4,64,512]{2,1,0:T(8,128)(2,1)S(1)}, bf16[4,64,512]{2,1,0:T(8,128)(2,1)}, u32[]{:S(2)}) copy-start(bf16[4,64,512]{2,1,0:T(8,128)(2,1)} %field_ref.1) | copy-start | bytes 786436
  20.5 22.9 %all-to-all-start.1 = ((bf16[8,272,128]{2,1,0:T(8,128)(2,1)}), bf16[8,272,128]{2,1,0:T(8,128)(2,1)S(1)}, u32[]{:S(2)}, u32[]{:S(2)}) async-start(bf16[8,272,128]{2,1,0:T(8,128)(2,1)} %shard_map.65), calls=%async_computation.1 | async-start | bytes 1114112 | tf_op jit(solution)/shard_map/all_to_all | solution.py:301
  27.3 15.2 %collective-permute-start = (bf16[32,512]{1,0:T(8,128)(2,1)S(1)}, bf16[32,512]{1,0:T(8,128)(2,1)S(1)}, u32[]{:S(2)}, u32[]{:S(2)}) collective-permute-start(bf16[32,512]{1,0:T(8,128)(2,1)S(1)} %get-tuple-element.27), channel_id=1, source_target_pairs={{0,1},{1,2},{2,3},{3,4},{4,5},{5,6},{6,7},{7,8},{8,9},{9,10},{10,1... | collective-permute-start | bytes 98312 | tf_op jit(solution)/shard_map/ppermute | solution.py:302
  29.2 13.2 %collective-permute-start.1 = (bf16[32,512]{1,0:T(8,128)(2,1)S(1)}, bf16[32,512]{1,0:T(8,128)(2,1)S(1)}, u32[]{:S(2)}, u32[]{:S(2)}) collective-permute-start(bf16[32,512]{1,0:T(8,128)(2,1)S(1)} %get-tuple-element.28), channel_id=1, source_target_pairs={{1,0},{2,1},{3,2},{4,3},{5,4},{6,5},{7,6},{8,7},{9,8},{10,9},{11,1... | collective-permute-start | bytes 98312 | tf_op jit(solution)/shard_map/ppermute | solution.py:303
  43.4 16.2 %all-to-all-start.3 = ((bf16[16,24,512]{2,1,0:T(8,128)(2,1)}), bf16[16,24,512]{2,1,0:T(8,128)(2,1)S(1)}, u32[]{:S(2)}, u32[]{:S(2)}) async-start(bf16[16,24,512]{2,1,0:T(8,128)(2,1)} %shard_map.67), calls=%async_computation.3 | async-start | bytes 786432 | tf_op jit(solution)/shard_map/all_to_all | solution.py:317
  52.2 10.8 %copy-start = (bf16[512,1152]{1,0:T(8,128)(2,1)S(1)}, bf16[512,1152]{1,0:T(8,128)(2,1)}, u32[]{:S(2)}) copy-start(bf16[512,1152]{1,0:T(8,128)(2,1)} %w_ref.2) | copy-start | bytes 3538948
  59.7 10.9 %all-to-all-start.2 = ((bf16[4,72,256]{2,1,0:T(8,128)(2,1)}), bf16[4,72,256]{2,1,0:T(8,128)(2,1)S(1)}, u32[]{:S(2)}, u32[]{:S(2)}) async-start(bf16[4,72,256]{2,1,0:T(8,128)(2,1)} %shard_map.68), calls=%async_computation.2 | async-start | bytes 294912 | tf_op jit(solution)/shard_map/all_to_all | solution.py:321
  63.0 19.2 %copy-start.2 = (bf16[512,512]{1,0:T(8,128)(2,1)S(1)}, bf16[512,512]{1,0:T(8,128)(2,1)}, u32[]{:S(2)}) copy-start(bf16[512,512]{1,0:T(8,128)(2,1)} %w_ref.3) | copy-start | bytes 1572868
  82.2 6.7 %copy-start.3 = (f32[7,7,512]{2,1,0:T(8,128)S(1)}, f32[7,7,512]{2,1,0:T(8,128)}, u32[]{:S(2)}) copy-start(f32[7,7,512]{2,1,0:T(8,128)} %param.9) | copy-start | bytes 301060
  82.9 9.4 %collective-permute-start.2 = (bf16[3,72,512]{2,1,0:T(8,128)(2,1)S(1)}, bf16[3,72,512]{2,1,0:T(8,128)(2,1)S(1)}, u32[]{:S(2)}, u32[]{:S(2)}) collective-permute-start(bf16[3,72,512]{2,1,0:T(8,128)(2,1)S(1)} %get-tuple-element.33), channel_id=1, source_target_pairs={{32,64},{96,128},{160,192},{224,256},{288,320},{352,384},{416,448}... | collective-permute-start | bytes 663560 | tf_op jit(solution)/shard_map/ppermute | solution.py:331
  87.0 5.2 %collective-permute-start.3 = (bf16[3,72,512]{2,1,0:T(8,128)(2,1)S(1)}, bf16[3,72,512]{2,1,0:T(8,128)(2,1)S(1)}, u32[]{:S(2)}, u32[]{:S(2)}) collective-permute-start(bf16[3,72,512]{2,1,0:T(8,128)(2,1)S(1)} %get-tuple-element.34), channel_id=1, source_target_pairs={{0,32},{64,96},{128,160},{192,224},{256,288},{320,352},{384,416},{... | collective-permute-start | bytes 663560 | tf_op jit(solution)/shard_map/ppermute | solution.py:330

commit v10 on v9

--- a/solution.py
+++ b/solution.py
@@ -19,7 +19,9 @@
 MWIDE = W + 2 * E
 MC = MWIDE // LAT
 EDGES = (1, LAT - 2)
-MROWS = 24
+MCELLS = 16
+MLANES = 640
+BROWS = 40
 YS = 8
 ZS = 4
 SPAN = ZS * W
@@ -139,13 +141,25 @@
     return jnp.concatenate([left[:, E // 2 :], own.astype(F32), right[:, 0 : E // 2]], axis=1)
 
 
+def merid_slots(normed, first, row_step, width):
+    dims = first.shape[:-2] + (MCELLS, normed.shape[0])
+    i, u = iota(dims, len(dims) - 2), iota(dims, len(dims) - 1)
+    c = first + (i >> 2)
+    main = one_hot(((i & 3) * row_step + c == u) & (c >= 0) & (c < width))
+    c = first + MC - 1
+    last = one_hot(((i & 3) * row_step + c == u) & (c >= 0) & (c < width))
+    shape_2d, shape_out = (-1, normed.shape[0]), dims[:-1] + (C,)
+    main = mm(main.reshape(shape_2d), normed).reshape(shape_out)
+    last = mm(last.reshape(shape_2d), normed).reshape(shape_out)
+    block = iota(dims[:-1] + (128,), len(dims) - 2) >> 2
+    tail = sum(jnp.where(block == b, last[..., b * 128 : b * 128 + 128], 0.0) for b in range(4))
+    return jnp.concatenate([main, tail], axis=-1)
+
+
 def merid_own_kernel(field_ref, out_ref, edge_ref):
     normed = layer_norm(field_ref[...].astype(F32).reshape(CELLS, C)).astype(BF)
-    dims = (LAT, MROWS, CELLS)
-    m, i, u = iota(dims, 0), iota(dims, 1), iota(dims, 2)
-    c = m * MC + (i >> 2) - E
-    hit = ((i & 3) * W + c == u) & (c >= 0) & (c < W) & (i < R * MC)
-    slots = mm(one_hot(hit).reshape(LAT * MROWS, CELLS), normed).reshape(LAT, MROWS, C).astype(BF)
+    first = iota((LAT, MCELLS, CELLS), 0) * MC - E
+    slots = merid_slots(normed, first, W, W).astype(BF)
     out_ref[...] = slots
     edge_ref[0] = slots[EDGES[0]]
     edge_ref[1] = slots[EDGES[1]]
@@ -155,10 +169,8 @@
     copies = []
     for n, (m, ref) in enumerate(zip(EDGES, (left_ref, right_ref))):
         normed = layer_norm(ref[...].astype(F32)).astype(BF)
-        i, u = iota((MROWS, R * E), 0), iota((MROWS, R * E), 1)
-        c = m * MC + (i >> 2) - n * (W + E)
-        hit = ((i & 3) * E + c == u) & (c >= 0) & (c < E) & (i < R * MC)
-        done_ref[n] = (edge_ref[n].astype(F32) + mm(one_hot(hit), normed)).astype(BF)
+        first = jnp.full((MCELLS, R * E), m * MC - n * (W + E), jnp.int32)
+        done_ref[n] = (edge_ref[n].astype(F32) + merid_slots(normed, first, E, E)).astype(BF)
         copies.append(pltpu.make_async_copy(done_ref.at[n], out_hbm.at[m], sems.at[n]))
         copies[n].start()
     for copy in copies:
@@ -166,17 +178,25 @@
 
 
 def merid_kernel(in_ref, w_ref, out_ref):
-    count = LAT * MROWS
-    normed = in_ref[...].astype(F32).reshape(count, C).astype(BF)
+    last = in_ref[:, :, C:MLANES].reshape(CELLS, 128)
+    t, u = iota((LAT * R, CELLS), 0), iota((LAT * R, CELLS), 1)
+    place = ((t >> 2) << 4) + (t & 3)
+    last = [mm(one_hot(u == place + b * R), last) for b in range(4)]
+    last = jnp.concatenate(last, axis=1).astype(BF)
+    normed = jnp.concatenate([in_ref[:, :, 0:C].reshape(CELLS, C), last], axis=0)
+    count = CELLS + LAT * R
     queries = mm(normed, w_ref[:, 256:512]).astype(BF)
     keys = mm(normed, w_ref[:, 640:896]).astype(BF)
     values = mm(normed, w_ref[:, 896:1152]).astype(BF)
-    row = iota((LAT, MROWS, count), 1).reshape(count, count) >> 2
-    key = iota((count, count), 1)
-    key = (key - ((key * 2731) >> 16) * MROWS) >> 2
+    t, s = iota((count, count), 0), iota((count, count), 1)
+    row = jnp.where(t < CELLS, (t >> 2) & 3, 4)
+    key = jnp.where(s < CELLS, (s >> 2) & 3, 4)
     bias = jnp.where(row == key, 0.0, -1e30)
     low = iota((count, 128), 1) < HD
     scale = 1.0 / math.sqrt(HD)
+    parts, tail = [], None
+    t, u = iota((LAT * 2 * R, LAT * R), 0), iota((LAT * 2 * R, LAT * R), 1)
+    same = u == ((t >> 3) << 2) + (t & 3)
     for pair in range(2):
         lanes = slice(pair * 128, pair * 128 + 128)
         q, k, v = queries[:, lanes], keys[:, lanes], values[:, lanes]
@@ -186,20 +206,31 @@
             weight = jnp.exp(score - jnp.max(score, axis=-1, keepdims=True))
             mass = jnp.sum(weight, axis=-1, keepdims=True)
             outs.append(mm(weight.astype(BF), v) / mass)
-        both = jnp.where(low, outs[0], outs[1]).reshape(LAT, MROWS, 128)
-        out_ref[:, :, lanes] = both.astype(BF)
+        both = jnp.where(low, outs[0], outs[1])
+        parts.append(both[0:CELLS].reshape(LAT, MCELLS, 128))
+        placed = mm(one_hot(same & (((t >> 2) & 1) == pair)), both[CELLS:].astype(BF))
+        tail = placed if tail is None else tail + placed
+    parts.append(tail.reshape(LAT, 2 * R, 128))
+    out_ref[...] = jnp.concatenate(parts, axis=1).astype(BF)
 
 
 def mix_kernel(odd_ref, zonal_ref, merid_ref, left_ref, right_ref, field_ref, w_ref, mixed_ref, far_ref, near_ref):
     rows = R * WIDE
-    merid = merid_ref[...].astype(F32).reshape(LAT * MROWS, 256).astype(BF)
-    dims = (R, WIDE, LAT * MROWS)
-    r, w, t = iota(dims, 0), iota(dims, 1) + E // 2, iota(dims, 2)
-    m = (t * 2731) >> 16
-    i = t - m * MROWS
-    cell = one_hot((m * MC + (i >> 2) == w) & ((i & 3) == r) & (i < R * MC))
-    merid = mm(cell.reshape(rows, LAT * MROWS), merid).astype(BF)
-    attended = mm(zonal_ref[...].reshape(rows, 256), w_ref[0:256]) + mm(merid, w_ref[256:512])
+    x = merid_ref[...].astype(F32)
+    pairs = [x[:, p * MCELLS : (p + 1) * MCELLS].reshape(CELLS, 128).astype(BF) for p in range(2)]
+    last = x[:, 2 * MCELLS :].reshape(LAT * 2 * R, 128).astype(BF)
+    dims = (R, WIDE, 1)
+    r, w = iota(dims, 0), iota(dims, 1) + E // 2
+    m = (w * 205) >> 10
+    cc = w - m * MC
+    place = jnp.where(cc < MC - 1, m * MCELLS + cc * R + r, -1)
+    place = one_hot(place == iota((R, WIDE, CELLS), 2)).reshape(rows, CELLS)
+    attended = mm(zonal_ref[...].reshape(rows, 256), w_ref[0:256])
+    for p in range(2):
+        place_last = jnp.where(cc == MC - 1, m * 2 * R + p * R + r, -1)
+        place_last = one_hot(place_last == iota((R, WIDE, LAT * 2 * R), 2)).reshape(rows, LAT * 2 * R)
+        merid = mm(place, pairs[p]) + mm(place_last, last)
+        attended = attended + mm(merid.astype(BF), w_ref[256 + p * 128 : 384 + p * 128])
     wide = widened(left_ref[...], field_ref[...], right_ref[...])
     mixed = (wide + attended.reshape(R, WIDE, C)).astype(BF)
     mixed_ref[...] = mixed
@@ -302,16 +333,16 @@
     field_left = lax.ppermute(last, "lon", right)
     field_right = lax.ppermute(first, "lon", left)
     merid, merid_edges = call(
-        merid_own_kernel, (shape(LAT, MROWS, C), shape(2, MROWS, C)), 300_000_000
+        merid_own_kernel, (shape(LAT, MCELLS, MLANES), shape(2, MCELLS, MLANES)), 300_000_000
     )(field)
     merid = call(
         merid_edge_kernel,
-        shape(LAT, MROWS, C),
+        shape(LAT, MCELLS, MLANES),
         10_000_000,
         in_specs=[ANY, VMEM, VMEM, VMEM],
         out_specs=ANY,
         input_output_aliases={0: 0},
-        scratch_shapes=[pltpu.VMEM((2, MROWS, C), BF), pltpu.SemaphoreType.DMA((2,))],
+        scratch_shapes=[pltpu.VMEM((2, MCELLS, MLANES), BF), pltpu.SemaphoreType.DMA((2,))],
     )(merid, merid_edges, field_left, field_right)
     slots, merid = lax.optimization_barrier((slots, merid))
     merid = lax.all_to_all(merid, "lat", 0, 0)
@@ -319,7 +350,7 @@
         zonal_kernel, shape(ZS, WIDE, 256), 4_000_000_000, vmem=24, in_specs=[SMEM, VMEM, VMEM]
     )(y, row, slots)
     zonal = lax.all_to_all(zonal, "lon", 0, 0, axis_index_groups=along_z)
-    merid = call(merid_kernel, shape(LAT, MROWS, 256), 1_000_000_000)(merid, w_qkv)
+    merid = call(merid_kernel, shape(LAT, BROWS, 128), 1_000_000_000)(merid, w_qkv)
     merid = lax.all_to_all(merid, "lat", 0, 0)
     mixed, far, near = call(
         mix_kernel,

time: 96.2 us -> 95.5 us (level)
  no operation moved by 1% of the time
where the time goes in v10:
time: 95.5 us; the launch traced here: 94.2 us
  starting transfers between devices  34.4 us (36%)
  blocking collectives  29.2 us (31%)
  Pallas kernels  15.9 us (17%)
  waiting for transfers between devices  14.4 us (15%)
    all_to_all x1, blocking collectives, per_device(): row = lax.all_to_all(row, 'lon', 0, 0, axis_index_groups=along_z)  17.9 us
    all_to_all x1, blocking collectives, per_device(): merid = lax.all_to_all(merid, 'lat', 0, 0)  11.3 us
    all_to_all x1, starting transfers between devices, per_device(): merid = lax.all_to_all(merid, 'lat', 0, 0)  8.78 us
    ppermute x1, starting transfers between devices, per_device(): field_right = lax.ppermute(first, 'lon', left)  7.58 us
    all_to_all x1, starting transfers between devices, per_device(): slots = lax.all_to_all(slots, 'lon', 0, 0, axis_index_groups=along_y)  6.83 us
    all_to_all x1, waiting for transfers between devices, per_device(): zonal = lax.all_to_all(zonal, 'lon', 0, 0, axis_index_groups=along_z)  5.59 us
    ppermute x1, waiting for transfers between devices, per_device(): field_left = lax.ppermute(last, 'lon', right)  4.4 us
    ppermute x1, starting transfers between devices, per_device(): far = lax.ppermute(far, 'lat', far_pairs)  4.09 us
  transfers between devices with their start and end apart: 7, of which 4 were waited for; matrix products, arithmetic and copies ran while one was open for 0% of the time, Pallas kernels for 10%

profile of v10, /device:TPU:7, one launch (start us, length us, event | category | flops | bytes accessed | tf_op | source)
XLA Modules:
  0.0 94.2 jit_solution(17341797619334230085)
XLA Ops:
  0.0 1.7 %shard_map.64 = (bf16[4,64,384]{2,1,0:T(8,128)(2,1)S(1)}, bf16[32,512]{1,0:T(8,128)(2,1)S(1)}, bf16[32,512]{1,0:T(8,128)(2,1)S(1)}) custom-call(bf16[4,64,512]{2,1,0:T(8,128)(2,1)} %field_ref.1, bf16[512,1152]{1,0:T(8,128)(2,1)} %w_ref.2), custom_call_target="tpu_custom_call" | custom-call | flops 200000000 | bytes 2000000 | tf_op jit(solution)/shard_map/pallas_call | solution.py:312
  1.7 0.0 copy-start.1
  1.7 17.9 %all_to_all.25.in_ref.own_ref = bf16[4,64,384]{2,1,0:T(8,128)(2,1)S(1)} all-to-all(bf16[4,64,384]{2,1,0:T(8,128)(2,1)S(1)} %get-tuple-element.24), channel_id=1, replica_groups={{0,1,2,3},{4,5,6,7},{8,9,10,11},{12,13,14,15},{16,17,18,19},{20,21,22,2..., dimensions={0} | all-to-all | bytes 393216 | tf_op jit(solution)/shard_map/all_to_all | solution.py:324
  19.6 0.9 shard_map.65
  20.5 6.8 %all-to-all-start.1 = ((bf16[8,272,128]{2,1,0:T(8,128)(2,1)}), bf16[8,272,128]{2,1,0:T(8,128)(2,1)S(1)}, u32[]{:S(2)}, u32[]{:S(2)}) async-start(bf16[8,272,128]{2,1,0:T(8,128)(2,1)} %shard_map.65), calls=%async_computation.1 | async-start | bytes 1114112 | tf_op jit(solution)/shard_map/all_to_all | solution.py:332
  27.3 1.9 %collective-permute-start = (bf16[32,512]{1,0:T(8,128)(2,1)S(1)}, bf16[32,512]{1,0:T(8,128)(2,1)S(1)}, u32[]{:S(2)}, u32[]{:S(2)}) collective-permute-start(bf16[32,512]{1,0:T(8,128)(2,1)S(1)} %get-tuple-element.27), channel_id=1, source_target_pairs={{0,1},{1,2},{2,3},{3,4},{4,5},{5,6},{6,7},{7,8},{8,9},{9,10},{10,1... | collective-permute-start | bytes 98312 | tf_op jit(solution)/shard_map/ppermute | solution.py:333
  29.2 7.6 %collective-permute-start.1 = (bf16[32,512]{1,0:T(8,128)(2,1)S(1)}, bf16[32,512]{1,0:T(8,128)(2,1)S(1)}, u32[]{:S(2)}, u32[]{:S(2)}) collective-permute-start(bf16[32,512]{1,0:T(8,128)(2,1)S(1)} %get-tuple-element.28), channel_id=1, source_target_pairs={{1,0},{2,1},{3,2},{4,3},{5,4},{6,5},{7,6},{8,7},{9,8},{10,9},{11,1... | collective-permute-start | bytes 98312 | tf_op jit(solution)/shard_map/ppermute | solution.py:334
  36.8 0.0 copy-done.1
  36.8 1.2 %shard_map.66 = (bf16[16,16,640]{2,1,0:T(8,128)(2,1)}, bf16[2,16,640]{2,1,0:T(8,128)(2,1)S(1)}) custom-call(bf16[4,64,512]{2,1,0:T(8,128)(2,1)S(1)} %copy-done.1), custom_call_target="tpu_custom_call" | custom-call | flops 300000000 | bytes 2000000 | tf_op jit(solution)/shard_map/pallas_call | solution.py:335
  38.1 4.4 %collective-permute-done.left_ref = bf16[32,512]{1,0:T(8,128)(2,1)S(1)} collective-permute-done((bf16[32,512]{1,0:T(8,128)(2,1)S(1)}, bf16[32,512]{1,0:T(8,128)(2,1)S(1)}, u32[]{:S(2)}, u32[]{:S(2)}) %collective-permute-start) | collective-permute-done | bytes 32800 | tf_op jit(solution)/shard_map/ppermute | solution.py:333
  42.5 0.0 collective-permute-done.1.right_ref
  42.5 0.9 %shard_map.67 = bf16[16,16,640]{2,1,0:T(8,128)(2,1)} custom-call(bf16[16,16,640]{2,1,0:T(8,128)(2,1)} %get-tuple-element.25.slots_hbm, bf16[2,16,640]{2,1,0:T(8,128)(2,1)S(1)} %get-tuple-element.26.edge_ref, bf16[32,512]{1,0:T(8,128)(2,1)S(1)} %collective-permute-done.left_ref, ...), custom_call_target="tpu_custom_call", output_to_operand_aliasing={{}: (0, {})} | custom-call | flops 10000000 | bytes 2000000 | tf_op jit(solution)/shard_map/pallas_call | solution.py:338
  43.4 0.0 all-to-all-done.1.all_ref
  43.4 8.8 %all-to-all-start.3 = ((bf16[16,16,640]{2,1,0:T(8,128)(2,1)}), bf16[16,16,640]{2,1,0:T(8,128)(2,1)S(1)}, u32[]{:S(2)}, u32[]{:S(2)}) async-start(bf16[16,16,640]{2,1,0:T(8,128)(2,1)} %shard_map.67), calls=%async_computation.3 | async-start | bytes 655360 | tf_op jit(solution)/shard_map/all_to_all | solution.py:348
  52.2 0.0 copy-start
  52.2 4.0 %shard_map.68 = bf16[4,72,256]{2,1,0:T(8,128)(2,1)} custom-call(s32[1]{0:T(128)} %bitcast.y_ref, bf16[4,64,384]{2,1,0:T(8,128)(2,1)S(1)} %all_to_all.25.in_ref.own_ref, bf16[8,272,128]{2,1,0:T(8,128)(2,1)S(1)} %all-to-all-done.1.all_ref), custom_call_target="tpu_custom_call" | custom-call | flops 4000000000 | bytes 2000000 | tf_op jit(solution)/shard_map/pallas_call | solution.py:349
  56.2 2.7 %all-to-all-done.3.in_ref = bf16[16,16,640]{2,1,0:T(8,128)(2,1)S(1)} async-done(((bf16[16,16,640]{2,1,0:T(8,128)(2,1)}), bf16[16,16,640]{2,1,0:T(8,128)(2,1)S(1)}, u32[]{:S(2)}, u32[]{:S(2)}) %all-to-all-start.3) | async-done | bytes 327712 | tf_op jit(solution)/shard_map/all_to_all | solution.py:348
  59.0 3.3 %all-to-all-start.2 = ((bf16[4,72,256]{2,1,0:T(8,128)(2,1)}), bf16[4,72,256]{2,1,0:T(8,128)(2,1)S(1)}, u32[]{:S(2)}, u32[]{:S(2)}) async-start(bf16[4,72,256]{2,1,0:T(8,128)(2,1)} %shard_map.68), calls=%async_computation.2 | async-start | bytes 294912 | tf_op jit(solution)/shard_map/all_to_all | solution.py:352
  62.3 0.0 copy-done
  62.3 0.0 copy-start.2
  62.3 2.0 %shard_map.69 = bf16[16,40,128]{2,1,0:T(8,128)(2,1)S(1)} custom-call(bf16[16,16,640]{2,1,0:T(8,128)(2,1)S(1)} %all-to-all-done.3.in_ref, bf16[512,1152]{1,0:T(8,128)(2,1)S(1)} %copy-done), custom_call_target="tpu_custom_call" | custom-call | flops 1000000000 | bytes 2000000 | tf_op jit(solution)/shard_map/pallas_call | solution.py:353
  64.3 5.6 %all-to-all-done.2.zonal_ref = bf16[4,72,256]{2,1,0:T(8,128)(2,1)S(1)} async-done(((bf16[4,72,256]{2,1,0:T(8,128)(2,1)}), bf16[4,72,256]{2,1,0:T(8,128)(2,1)S(1)}, u32[]{:S(2)}, u32[]{:S(2)}) %all-to-all-start.2) | async-done | bytes 147488 | tf_op jit(solution)/shard_map/all_to_all | solution.py:352
  69.9 11.3 %all_to_all.26.merid_ref = bf16[16,40,128]{2,1,0:T(8,128)(2,1)S(1)} all-to-all(bf16[16,40,128]{2,1,0:T(8,128)(2,1)S(1)} %shard_map.69), channel_id=1, replica_groups=mesh['lat'=16,'lon'=32] {'lat'}, dimensions={0} | all-to-all | bytes 327680 | tf_op jit(solution)/shard_map/all_to_all | solution.py:354
  81.2 0.0 copy-done.2
  81.2 0.0 copy-start.3
  81.2 0.8 shard_map.70
  81.9 4.1 %collective-permute-start.2 = (bf16[3,72,512]{2,1,0:T(8,128)(2,1)S(1)}, bf16[3,72,512]{2,1,0:T(8,128)(2,1)S(1)}, u32[]{:S(2)}, u32[]{:S(2)}) collective-permute-start(bf16[3,72,512]{2,1,0:T(8,128)(2,1)S(1)} %get-tuple-element.33), channel_id=1, source_target_pairs={{32,64},{96,128},{160,192},{224,256},{288,320},{352,384},{416,448}... | collective-permute-start | bytes 663560 | tf_op jit(solution)/shard_map/ppermute | solution.py:362
  86.1 1.9 %collective-permute-start.3 = (bf16[3,72,512]{2,1,0:T(8,128)(2,1)S(1)}, bf16[3,72,512]{2,1,0:T(8,128)(2,1)S(1)}, u32[]{:S(2)}, u32[]{:S(2)}) collective-permute-start(bf16[3,72,512]{2,1,0:T(8,128)(2,1)S(1)} %get-tuple-element.34), channel_id=1, source_target_pairs={{0,32},{64,96},{128,160},{192,224},{256,288},{320,352},{384,416},{... | collective-permute-start | bytes 663560 | tf_op jit(solution)/shard_map/ppermute | solution.py:361
  88.0 0.0 copy-done.3
  88.0 1.6 %shard_map.71 = (f32[256,512]{1,0:T(8,128)S(1)}, bf16[512,1024]{1,0:T(8,128)(2,1)S(1)}, bf16[1024,512]{1,0:T(8,128)(2,1)S(1)}) custom-call(bf16[4,72,512]{2,1,0:T(8,128)(2,1)S(1)} %get-tuple-element.31.mixed_ref, f32[49,512]{1,0:T(8,128)S(1)} %reshape.11.conv_ref, bf16[512,1024]{1,0:T(8,128)(2,1)} %w_in_hbm.1, bf16[1024,512]{1,0:T(8,128)(2,1)} %w_back_hbm.1), custom_call_target="tpu_custom_call" | custom-call | flops 1000000000 | bytes 2000000 | tf_op jit(solution)/shard_map/pallas_call | solution.py:364
  89.6 1.7 %collective-permute-done.2.far_ref = bf16[3,72,512]{2,1,0:T(8,128)(2,1)S(1)} collective-permute-done((bf16[3,72,512]{2,1,0:T(8,128)(2,1)S(1)}, bf16[3,72,512]{2,1,0:T(8,128)(2,1)S(1)}, u32[]{:S(2)}, u32[]{:S(2)}) %collective-permute-start.2) | collective-permute-done | bytes 221216 | tf_op jit(solution)/shard_map/ppermute | solution.py:362
  91.3 0.0 collective-permute-done.3.near_ref
  91.3 2.9 %shard_map.72 = bf16[4,64,512]{2,1,0:T(8,128)(2,1)} custom-call(s32[1]{0:T(128)} %bitcast.1.odd_ref, bf16[4,72,512]{2,1,0:T(8,128)(2,1)S(1)} %get-tuple-element.31.mixed_ref, f32[256,512]{1,0:T(8,128)S(1)} %get-tuple-element.32.own_ref, bf16[3,72,512]{2,1,0:T(8,128)(2,1)S(1)} %collective-permute-done.2.far_ref, ...), custom_call_target="tpu_custom_call" | custom-call | flops 2000000000 | bytes 2000000 | tf_op jit(solution)/shard_map/pallas_call | solution.py:371
  (1 shorter events, 0.0 us)
Async XLA Ops:
  1.7 35.2 %copy-start.1 = (bf16[4,64,512]{2,1,0:T(8,128)(2,1)S(1)}, bf16[4,64,512]{2,1,0:T(8,128)(2,1)}, u32[]{:S(2)}) copy-start(bf16[4,64,512]{2,1,0:T(8,128)(2,1)} %field_ref.1) | copy-start | bytes 786436
  20.5 22.9 %all-to-all-start.1 = ((bf16[8,272,128]{2,1,0:T(8,128)(2,1)}), bf16[8,272,128]{2,1,0:T(8,128)(2,1)S(1)}, u32[]{:S(2)}, u32[]{:S(2)}) async-start(bf16[8,272,128]{2,1,0:T(8,128)(2,1)} %shard_map.65), calls=%async_computation.1 | async-start | bytes 1114112 | tf_op jit(solution)/shard_map/all_to_all | solution.py:332
  27.3 15.2 %collective-permute-start = (bf16[32,512]{1,0:T(8,128)(2,1)S(1)}, bf16[32,512]{1,0:T(8,128)(2,1)S(1)}, u32[]{:S(2)}, u32[]{:S(2)}) collective-permute-start(bf16[32,512]{1,0:T(8,128)(2,1)S(1)} %get-tuple-element.27), channel_id=1, source_target_pairs={{0,1},{1,2},{2,3},{3,4},{4,5},{5,6},{6,7},{7,8},{8,9},{9,10},{10,1... | collective-permute-start | bytes 98312 | tf_op jit(solution)/shard_map/ppermute | solution.py:333
  29.2 13.2 %collective-permute-start.1 = (bf16[32,512]{1,0:T(8,128)(2,1)S(1)}, bf16[32,512]{1,0:T(8,128)(2,1)S(1)}, u32[]{:S(2)}, u32[]{:S(2)}) collective-permute-start(bf16[32,512]{1,0:T(8,128)(2,1)S(1)} %get-tuple-element.28), channel_id=1, source_target_pairs={{1,0},{2,1},{3,2},{4,3},{5,4},{6,5},{7,6},{8,7},{9,8},{10,9},{11,1... | collective-permute-start | bytes 98312 | tf_op jit(solution)/shard_map/ppermute | solution.py:334
  43.4 15.5 %all-to-all-start.3 = ((bf16[16,16,640]{2,1,0:T(8,128)(2,1)}), bf16[16,16,640]{2,1,0:T(8,128)(2,1)S(1)}, u32[]{:S(2)}, u32[]{:S(2)}) async-start(bf16[16,16,640]{2,1,0:T(8,128)(2,1)} %shard_map.67), calls=%async_computation.3 | async-start | bytes 655360 | tf_op jit(solution)/shard_map/all_to_all | solution.py:348
  52.2 10.1 %copy-start = (bf16[512,1152]{1,0:T(8,128)(2,1)S(1)}, bf16[512,1152]{1,0:T(8,128)(2,1)}, u32[]{:S(2)}) copy-start(bf16[512,1152]{1,0:T(8,128)(2,1)} %w_ref.2) | copy-start | bytes 3538948
  59.0 10.9 %all-to-all-start.2 = ((bf16[4,72,256]{2,1,0:T(8,128)(2,1)}), bf16[4,72,256]{2,1,0:T(8,128)(2,1)S(1)}, u32[]{:S(2)}, u32[]{:S(2)}) async-start(bf16[4,72,256]{2,1,0:T(8,128)(2,1)} %shard_map.68), calls=%async_computation.2 | async-start | bytes 294912 | tf_op jit(solution)/shard_map/all_to_all | solution.py:352
  62.3 18.9 %copy-start.2 = (bf16[512,512]{1,0:T(8,128)(2,1)S(1)}, bf16[512,512]{1,0:T(8,128)(2,1)}, u32[]{:S(2)}) copy-start(bf16[512,512]{1,0:T(8,128)(2,1)} %w_ref.3) | copy-start | bytes 1572868
  81.2 6.8 %copy-start.3 = (f32[7,7,512]{2,1,0:T(8,128)S(1)}, f32[7,7,512]{2,1,0:T(8,128)}, u32[]{:S(2)}) copy-start(f32[7,7,512]{2,1,0:T(8,128)} %param.9) | copy-start | bytes 301060
  81.9 9.4 %collective-permute-start.2 = (bf16[3,72,512]{2,1,0:T(8,128)(2,1)S(1)}, bf16[3,72,512]{2,1,0:T(8,128)(2,1)S(1)}, u32[]{:S(2)}, u32[]{:S(2)}) collective-permute-start(bf16[3,72,512]{2,1,0:T(8,128)(2,1)S(1)} %get-tuple-element.33), channel_id=1, source_target_pairs={{32,64},{96,128},{160,192},{224,256},{288,320},{352,384},{416,448}... | collective-permute-start | bytes 663560 | tf_op jit(solution)/shard_map/ppermute | solution.py:362
  86.1 5.3 %collective-permute-start.3 = (bf16[3,72,512]{2,1,0:T(8,128)(2,1)S(1)}, bf16[3,72,512]{2,1,0:T(8,128)(2,1)S(1)}, u32[]{:S(2)}, u32[]{:S(2)}) collective-permute-start(bf16[3,72,512]{2,1,0:T(8,128)(2,1)S(1)} %get-tuple-element.34), channel_id=1, source_target_pairs={{0,32},{64,96},{128,160},{192,224},{256,288},{320,352},{384,416},{... | collective-permute-start | bytes 663560 | tf_op jit(solution)/shard_map/ppermute | solution.py:361

commit v11 on v10

--- a/solution.py
+++ b/solution.py
@@ -107,7 +107,8 @@
         copy.wait()
 
 
-def zonal_kernel(y_ref, own_ref, all_ref, out_ref):
+def zonal_kernel(y_ref, z_ref, own_ref, all_ref, *outs_ref):
+    *outs_ref, heads_ref = outs_ref
     y = y_ref[0]
     kv = all_ref[:, 0:SPAN, :].reshape(YS * SPAN, 128)
     ones = iota((YS * SPAN, 128), 1) < HD
@@ -131,9 +132,10 @@
         even, odd = outs
         blended = jnp.where(low, pltpu.roll(even, HD, 1), odd)
         mass = jnp.where(low, even, pltpu.roll(odd, HD, 1))
-        heads = blended / mass
-        for z in range(ZS):
-            out_ref[z, :, lanes] = heads[z * W : z * W + WIDE].astype(BF)
+        heads_ref[:, lanes] = blended / mass
+    for k, out_ref in enumerate(outs_ref):
+        start = pl.multiple_of((z_ref[0] ^ k) * W, W)
+        out_ref[...] = heads_ref[pl.ds(start, WIDE), :].astype(BF)
 
 
 def widened(left, own, right):
@@ -214,7 +216,12 @@
     out_ref[...] = jnp.concatenate(parts, axis=1).astype(BF)
 
 
-def mix_kernel(odd_ref, zonal_ref, merid_ref, left_ref, right_ref, field_ref, w_ref, mixed_ref, far_ref, near_ref):
+def mix_kernel(
+    odd_ref, z_ref, z0_ref, z1_ref, z2_ref, z3_ref, merid_ref, left_ref, right_ref, field_ref, w_ref,
+    mixed_ref, far_ref, near_ref, zonal_ref,
+):
+    for k, ref in enumerate((z0_ref, z1_ref, z2_ref, z3_ref)):
+        zonal_ref[z_ref[0] ^ k] = ref[...]
     rows = R * WIDE
     x = merid_ref[...].astype(F32)
     pairs = [x[:, p * MCELLS : (p + 1) * MCELLS].reshape(CELLS, 128).astype(BF) for p in range(2)]
@@ -306,9 +313,10 @@
     near_pairs, far_pairs = (pairs + [(j, i) for i, j in pairs] for pairs in (near_pairs, far_pairs))
     along_y = [[y * ZS + z for y in range(YS)] for z in range(ZS)]
     along_z = [[y * ZS + z for z in range(ZS)] for y in range(YS)]
-    y = (lax.axis_index("lon").astype(jnp.int32) >> 2).reshape(1)
+    lon = lax.axis_index("lon").astype(jnp.int32)
+    y, z = (lon >> 2).reshape(1), (lon & 3).reshape(1)
     odd = (lax.axis_index("lat").astype(jnp.int32) & 1).reshape(1)
-    field, y, odd = lax.optimization_barrier((field, y, odd))
+    field, y, z, odd = lax.optimization_barrier((field, y, z, odd))
     row, first, last = call(
         zonal_project_kernel,
         (shape(R, W, 384), shape(R * E, C), shape(R * E, C)),
@@ -347,17 +355,26 @@
     slots, merid = lax.optimization_barrier((slots, merid))
     merid = lax.all_to_all(merid, "lat", 0, 0)
     zonal = call(
-        zonal_kernel, shape(ZS, WIDE, 256), 4_000_000_000, vmem=24, in_specs=[SMEM, VMEM, VMEM]
-    )(y, row, slots)
-    zonal = lax.all_to_all(zonal, "lon", 0, 0, axis_index_groups=along_z)
+        zonal_kernel,
+        (shape(WIDE, 256),) * ZS,
+        4_000_000_000,
+        vmem=24,
+        in_specs=[SMEM, SMEM, VMEM, VMEM],
+        scratch_shapes=[pltpu.VMEM((SPAN + E, 256), F32)],
+    )(y, z, row, slots)
+    zonal = list(zonal)
+    for k in range(1, ZS):
+        zonal[k] = lax.ppermute(zonal[k], "lon", [(i, i ^ k) for i in range(LON)])
     merid = call(merid_kernel, shape(LAT, BROWS, 128), 1_000_000_000)(merid, w_qkv)
+    merid, zonal[2] = lax.optimization_barrier((merid, zonal[2]))
     merid = lax.all_to_all(merid, "lat", 0, 0)
     mixed, far, near = call(
         mix_kernel,
         (shape(R, WIDE, C), shape(3, WIDE, C), shape(3, WIDE, C)),
         800_000_000,
-        in_specs=[SMEM] + [VMEM] * 6,
-    )(odd, zonal, merid, field_left, field_right, field, w_out)
+        in_specs=[SMEM, SMEM] + [VMEM] * 9,
+        scratch_shapes=[pltpu.VMEM((R, WIDE, 256), BF)],
+    )(odd, z, *zonal, merid, field_left, field_right, field, w_out)
     near = lax.ppermute(near, "lat", near_pairs)
     far = lax.ppermute(far, "lat", far_pairs)
     conv_w = conv_w.reshape(49, C)

time: 95.5 us -> 95.8 us (level)
  starting transfers between devices: 34.4 us -> 47.9 us
  blocking collectives: 29.2 us -> 17.9 us
  waiting for transfers between devices: 14.4 us -> 13 us
    all_to_all x1 -> x0, blocking collectives: 11.3 us -> none  [per_device(): merid = lax.all_to_all(merid, 'lat', 0, 0)]
    ppermute x0 -> x3, starting transfers between devices: none -> 9.34 us  [per_device(): zonal[k] = lax.ppermute(zonal[k], 'lon', [(i, i ^ k) for i in range(LON)])]
    ppermute x0 -> x3, waiting for transfers between devices: none -> 7.5 us  [per_device(): zonal[k] = lax.ppermute(zonal[k], 'lon', [(i, i ^ k) for i in range(LON)])]
    all_to_all x1 -> x2, starting transfers between devices: 8.78 us -> 15.6 us  [per_device(): merid = lax.all_to_all(merid, 'lat', 0, 0)]
    all_to_all x1 -> x0, waiting for transfers between devices: 5.59 us -> none  [per_device(): zonal = lax.all_to_all(zonal, 'lon', 0, 0, axis_index_groups=along_z)]
    all_to_all x1 -> x0, starting transfers between devices: 3.34 us -> none  [per_device(): zonal = lax.all_to_all(zonal, 'lon', 0, 0, axis_index_groups=along_z)]
    all_to_all x1 -> x2, waiting for transfers between devices: 2.72 us -> 0.01 us  [per_device(): merid = lax.all_to_all(merid, 'lat', 0, 0)]
  transfers between devices with their start and end apart: 7 -> 10, of which waited for: 4 -> 4; matrix products, arithmetic and copies ran while one was open for 0% -> 0% of each run, Pallas kernels for 10% -> 10%
where the time goes in v11:
time: 95.8 us; the launch traced here: 94.9 us
  starting transfers between devices  47.9 us (50%)
  blocking collectives  17.9 us (19%)
  Pallas kernels  16 us (17%)
  waiting for transfers between devices  13 us (14%)
    all_to_all x1, blocking collectives, per_device(): row = lax.all_to_all(row, 'lon', 0, 0, axis_index_groups=along_z)  17.9 us
    all_to_all x2, starting transfers between devices, per_device(): merid = lax.all_to_all(merid, 'lat', 0, 0)  15.6 us
    ppermute x3, starting transfers between devices, per_device(): zonal[k] = lax.ppermute(zonal[k], 'lon', [(i, i ^ k) for i in range(LON)])  9.34 us
    ppermute x1, starting transfers between devices, per_device(): field_right = lax.ppermute(first, 'lon', left)  7.58 us
    ppermute x3, waiting for transfers between devices, per_device(): zonal[k] = lax.ppermute(zonal[k], 'lon', [(i, i ^ k) for i in range(LON)])  7.5 us
    all_to_all x1, starting transfers between devices, per_device(): slots = lax.all_to_all(slots, 'lon', 0, 0, axis_index_groups=along_y)  6.83 us
    ppermute x1, starting transfers between devices, per_device(): far = lax.ppermute(far, 'lat', far_pairs)  4.74 us
    ppermute x1, waiting for transfers between devices, per_device(): field_left = lax.ppermute(last, 'lon', right)  4.39 us
  transfers between devices with their start and end apart: 10, of which 4 were waited for; matrix products, arithmetic and copies ran while one was open for 0% of the time, Pallas kernels for 10%

profile of v11, /device:TPU:7, one launch (start us, length us, event | category | flops | bytes accessed | tf_op | source)
XLA Modules:
  0.0 94.9 jit_solution(14710099009205976159)
XLA Ops:
  0.0 1.7 %shard_map.64 = (bf16[4,64,384]{2,1,0:T(8,128)(2,1)S(1)}, bf16[32,512]{1,0:T(8,128)(2,1)S(1)}, bf16[32,512]{1,0:T(8,128)(2,1)S(1)}) custom-call(bf16[4,64,512]{2,1,0:T(8,128)(2,1)} %field_ref.1, bf16[512,1152]{1,0:T(8,128)(2,1)} %w_ref.2), custom_call_target="tpu_custom_call" | custom-call | flops 200000000 | bytes 2000000 | tf_op jit(solution)/shard_map/pallas_call | solution.py:320
  1.7 0.0 copy-start.1
  1.7 17.9 %all_to_all.20.in_ref.own_ref = bf16[4,64,384]{2,1,0:T(8,128)(2,1)S(1)} all-to-all(bf16[4,64,384]{2,1,0:T(8,128)(2,1)S(1)} %get-tuple-element.32), channel_id=1, replica_groups={{0,1,2,3},{4,5,6,7},{8,9,10,11},{12,13,14,15},{16,17,18,19},{20,21,22,2..., dimensions={0} | all-to-all | bytes 393216 | tf_op jit(solution)/shard_map/all_to_all | solution.py:332
  19.6 0.9 shard_map.65
  20.5 6.8 %all-to-all-start.1 = ((bf16[8,272,128]{2,1,0:T(8,128)(2,1)}), bf16[8,272,128]{2,1,0:T(8,128)(2,1)S(1)}, u32[]{:S(2)}, u32[]{:S(2)}) async-start(bf16[8,272,128]{2,1,0:T(8,128)(2,1)} %shard_map.65), calls=%async_computation.1 | async-start | bytes 1114112 | tf_op jit(solution)/shard_map/all_to_all | solution.py:340
  27.3 1.9 %collective-permute-start = (bf16[32,512]{1,0:T(8,128)(2,1)S(1)}, bf16[32,512]{1,0:T(8,128)(2,1)S(1)}, u32[]{:S(2)}, u32[]{:S(2)}) collective-permute-start(bf16[32,512]{1,0:T(8,128)(2,1)S(1)} %get-tuple-element.35), channel_id=1, source_target_pairs={{0,1},{1,2},{2,3},{3,4},{4,5},{5,6},{6,7},{7,8},{8,9},{9,10},{10,1... | collective-permute-start | bytes 98312 | tf_op jit(solution)/shard_map/ppermute | solution.py:341
  29.2 7.6 %collective-permute-start.1 = (bf16[32,512]{1,0:T(8,128)(2,1)S(1)}, bf16[32,512]{1,0:T(8,128)(2,1)S(1)}, u32[]{:S(2)}, u32[]{:S(2)}) collective-permute-start(bf16[32,512]{1,0:T(8,128)(2,1)S(1)} %get-tuple-element.36), channel_id=1, source_target_pairs={{1,0},{2,1},{3,2},{4,3},{5,4},{6,5},{7,6},{8,7},{9,8},{10,9},{11,1... | collective-permute-start | bytes 98312 | tf_op jit(solution)/shard_map/ppermute | solution.py:342
  36.8 0.0 copy-done.1
  36.8 1.2 %shard_map.66 = (bf16[16,16,640]{2,1,0:T(8,128)(2,1)}, bf16[2,16,640]{2,1,0:T(8,128)(2,1)S(1)}) custom-call(bf16[4,64,512]{2,1,0:T(8,128)(2,1)S(1)} %copy-done.1), custom_call_target="tpu_custom_call" | custom-call | flops 300000000 | bytes 2000000 | tf_op jit(solution)/shard_map/pallas_call | solution.py:343
  38.1 4.4 %collective-permute-done.left_ref = bf16[32,512]{1,0:T(8,128)(2,1)S(1)} collective-permute-done((bf16[32,512]{1,0:T(8,128)(2,1)S(1)}, bf16[32,512]{1,0:T(8,128)(2,1)S(1)}, u32[]{:S(2)}, u32[]{:S(2)}) %collective-permute-start) | collective-permute-done | bytes 32800 | tf_op jit(solution)/shard_map/ppermute | solution.py:341
  42.5 0.0 collective-permute-done.1.right_ref
  42.5 0.9 shard_map.67
  43.4 0.0 all-to-all-done.1.all_ref
  43.4 8.8 %all-to-all-start.2 = ((bf16[16,16,640]{2,1,0:T(8,128)(2,1)}), bf16[16,16,640]{2,1,0:T(8,128)(2,1)S(1)}, u32[]{:S(2)}, u32[]{:S(2)}) async-start(bf16[16,16,640]{2,1,0:T(8,128)(2,1)} %shard_map.67), calls=%async_computation.2 | async-start | bytes 655360 | tf_op jit(solution)/shard_map/all_to_all | solution.py:356
  52.2 0.0 copy-start
  52.2 3.4 %shard_map.68 = (bf16[72,256]{1,0:T(8,128)(2,1)S(1)}, bf16[72,256]{1,0:T(8,128)(2,1)S(1)}, bf16[72,256]{1,0:T(8,128)(2,1)S(1)}, bf16[72,256]{1,0:T(8,128)(2,1)S(1)}) custom-call(s32[1]{0:T(128)} %bitcast.y_ref, s32[1]{0:T(128)} %bitcast.1.z_ref, bf16[4,64,384]{2,1,0:T(8,128)(2,1)S(1)} %all_to_all.20.in_ref.own_ref, ...), custom_call_target="tpu_custom_call" | custom-call | flops 4000000000 | bytes 2000000 | tf_op jit(solution)/shard_map/pallas_call | solution.py:357
  55.6 0.0 copy-start.2
  55.6 3.6 %collective-permute-start.3 = (bf16[72,256]{1,0:T(8,128)(2,1)S(1)}, bf16[72,256]{1,0:T(8,128)(2,1)S(1)}, u32[]{:S(2)}, u32[]{:S(2)}) collective-permute-start(bf16[72,256]{1,0:T(8,128)(2,1)S(1)} %get-tuple-element.41), channel_id=1, source_target_pairs={{0,2},{1,3},{2,0},{3,1},{4,6},{5,7},{6,4},{7,5},{8,10},{9,11},{10,... | collective-permute-start | bytes 110600 | tf_op jit(solution)/shard_map/ppermute | solution.py:367
  59.2 0.0 all-to-all-done.2.in_ref
  59.2 0.0 copy-done
  59.2 2.6 %shard_map.69 = bf16[16,40,128]{2,1,0:T(8,128)(2,1)} custom-call(bf16[16,16,640]{2,1,0:T(8,128)(2,1)S(1)} %all-to-all-done.2.in_ref, bf16[512,1152]{1,0:T(8,128)(2,1)S(1)} %copy-done), custom_call_target="tpu_custom_call" | custom-call | flops 1000000000 | bytes 2000000 | tf_op jit(solution)/shard_map/pallas_call | solution.py:368
  61.9 2.6 %collective-permute-done.3.z2_ref = bf16[72,256]{1,0:T(8,128)(2,1)S(1)} collective-permute-done((bf16[72,256]{1,0:T(8,128)(2,1)S(1)}, bf16[72,256]{1,0:T(8,128)(2,1)S(1)}, u32[]{:S(2)}, u32[]{:S(2)}) %collective-permute-start.3) | collective-permute-done | bytes 36896 | tf_op jit(solution)/shard_map/ppermute | solution.py:367
  64.5 6.8 %all-to-all-start.3 = ((bf16[16,40,128]{2,1,0:T(8,128)(2,1)}), bf16[16,40,128]{2,1,0:T(8,128)(2,1)S(1)}, u32[]{:S(2)}, u32[]{:S(2)}) async-start(bf16[16,40,128]{2,1,0:T(8,128)(2,1)} %shard_map.69), calls=%async_computation.3 | async-start | bytes 327680 | tf_op jit(solution)/shard_map/all_to_all | solution.py:370
  71.2 3.8 %collective-permute-start.2 = (bf16[72,256]{1,0:T(8,128)(2,1)S(1)}, bf16[72,256]{1,0:T(8,128)(2,1)S(1)}, u32[]{:S(2)}, u32[]{:S(2)}) collective-permute-start(bf16[72,256]{1,0:T(8,128)(2,1)S(1)} %get-tuple-element.39), channel_id=1, source_target_pairs={{0,1},{1,0},{2,3},{3,2},{4,5},{5,4},{6,7},{7,6},{8,9},{9,8},{10,11... | collective-permute-start | bytes 110600 | tf_op jit(solution)/shard_map/ppermute | solution.py:367
  75.1 1.9 %collective-permute-start.4 = (bf16[72,256]{1,0:T(8,128)(2,1)S(1)}, bf16[72,256]{1,0:T(8,128)(2,1)S(1)}, u32[]{:S(2)}, u32[]{:S(2)}) collective-permute-start(bf16[72,256]{1,0:T(8,128)(2,1)S(1)} %get-tuple-element.43), channel_id=1, source_target_pairs={{0,3},{1,2},{2,1},{3,0},{4,7},{5,6},{6,5},{7,4},{8,11},{9,10},{10,... | collective-permute-start | bytes 110600 | tf_op jit(solution)/shard_map/ppermute | solution.py:367
  77.0 0.0 collective-permute-done.2.z1_ref
  77.0 4.9 %collective-permute-done.4.z3_ref = bf16[72,256]{1,0:T(8,128)(2,1)S(1)} collective-permute-done((bf16[72,256]{1,0:T(8,128)(2,1)S(1)}, bf16[72,256]{1,0:T(8,128)(2,1)S(1)}, u32[]{:S(2)}, u32[]{:S(2)}) %collective-permute-start.4) | collective-permute-done | bytes 36896 | tf_op jit(solution)/shard_map/ppermute | solution.py:367
  81.9 0.0 all-to-all-done.3.merid_ref
  81.9 0.0 copy-done.2
  81.9 0.0 copy-start.3
  81.9 0.8 shard_map.70
  82.7 4.7 %collective-permute-start.5 = (bf16[3,72,512]{2,1,0:T(8,128)(2,1)S(1)}, bf16[3,72,512]{2,1,0:T(8,128)(2,1)S(1)}, u32[]{:S(2)}, u32[]{:S(2)}) collective-permute-start(bf16[3,72,512]{2,1,0:T(8,128)(2,1)S(1)} %get-tuple-element.47), channel_id=1, source_target_pairs={{32,64},{96,128},{160,192},{224,256},{288,320},{352,384},{416,448}... | collective-permute-start | bytes 663560 | tf_op jit(solution)/shard_map/ppermute | solution.py:379
  87.5 1.9 %collective-permute-start.6 = (bf16[3,72,512]{2,1,0:T(8,128)(2,1)S(1)}, bf16[3,72,512]{2,1,0:T(8,128)(2,1)S(1)}, u32[]{:S(2)}, u32[]{:S(2)}) collective-permute-start(bf16[3,72,512]{2,1,0:T(8,128)(2,1)S(1)} %get-tuple-element.48), channel_id=1, source_target_pairs={{0,32},{64,96},{128,160},{192,224},{256,288},{320,352},{384,416},{... | collective-permute-start | bytes 663560 | tf_op jit(solution)/shard_map/ppermute | solution.py:378
  89.4 0.0 copy-done.3
  89.4 1.6 %shard_map.71 = (f32[256,512]{1,0:T(8,128)S(1)}, bf16[512,1024]{1,0:T(8,128)(2,1)S(1)}, bf16[1024,512]{1,0:T(8,128)(2,1)S(1)}) custom-call(bf16[4,72,512]{2,1,0:T(8,128)(2,1)S(1)} %get-tuple-element.45.mixed_ref, f32[49,512]{1,0:T(8,128)S(1)} %reshape.15.conv_ref, bf16[512,1024]{1,0:T(8,128)(2,1)} %w_in_hbm.1, bf16[1024,512]{1,0:T(8,128)(2,1)} %w_back_hbm.1), custom_call_target="tpu_custom_call" | custom-call | flops 1000000000 | bytes 2000000 | tf_op jit(solution)/shard_map/pallas_call | solution.py:381
  91.0 1.1 %collective-permute-done.5.far_ref = bf16[3,72,512]{2,1,0:T(8,128)(2,1)S(1)} collective-permute-done((bf16[3,72,512]{2,1,0:T(8,128)(2,1)S(1)}, bf16[3,72,512]{2,1,0:T(8,128)(2,1)S(1)}, u32[]{:S(2)}, u32[]{:S(2)}) %collective-permute-start.5) | collective-permute-done | bytes 221216 | tf_op jit(solution)/shard_map/ppermute | solution.py:379
  92.1 0.0 collective-permute-done.6.near_ref
  92.1 2.9 %shard_map.72 = bf16[4,64,512]{2,1,0:T(8,128)(2,1)} custom-call(s32[1]{0:T(128)} %bitcast.2.odd_ref, bf16[4,72,512]{2,1,0:T(8,128)(2,1)S(1)} %get-tuple-element.45.mixed_ref, f32[256,512]{1,0:T(8,128)S(1)} %get-tuple-element.46.own_ref, bf16[3,72,512]{2,1,0:T(8,128)(2,1)S(1)} %collective-permute-done.5.far_ref, ...), custom_call_target="tpu_custom_call" | custom-call | flops 2000000000 | bytes 2000000 | tf_op jit(solution)/shard_map/pallas_call | solution.py:388
  (1 shorter events, 0.0 us)
Async XLA Ops:
  1.7 35.2 %copy-start.1 = (bf16[4,64,512]{2,1,0:T(8,128)(2,1)S(1)}, bf16[4,64,512]{2,1,0:T(8,128)(2,1)}, u32[]{:S(2)}) copy-start(bf16[4,64,512]{2,1,0:T(8,128)(2,1)} %field_ref.1) | copy-start | bytes 786436
  20.5 22.9 %all-to-all-start.1 = ((bf16[8,272,128]{2,1,0:T(8,128)(2,1)}), bf16[8,272,128]{2,1,0:T(8,128)(2,1)S(1)}, u32[]{:S(2)}, u32[]{:S(2)}) async-start(bf16[8,272,128]{2,1,0:T(8,128)(2,1)} %shard_map.65), calls=%async_computation.1 | async-start | bytes 1114112 | tf_op jit(solution)/shard_map/all_to_all | solution.py:340
  27.3 15.2 %collective-permute-start = (bf16[32,512]{1,0:T(8,128)(2,1)S(1)}, bf16[32,512]{1,0:T(8,128)(2,1)S(1)}, u32[]{:S(2)}, u32[]{:S(2)}) collective-permute-start(bf16[32,512]{1,0:T(8,128)(2,1)S(1)} %get-tuple-element.35), channel_id=1, source_target_pairs={{0,1},{1,2},{2,3},{3,4},{4,5},{5,6},{6,7},{7,8},{8,9},{9,10},{10,1... | collective-permute-start | bytes 98312 | tf_op jit(solution)/shard_map/ppermute | solution.py:341
  29.2 13.2 %collective-permute-start.1 = (bf16[32,512]{1,0:T(8,128)(2,1)S(1)}, bf16[32,512]{1,0:T(8,128)(2,1)S(1)}, u32[]{:S(2)}, u32[]{:S(2)}) collective-permute-start(bf16[32,512]{1,0:T(8,128)(2,1)S(1)} %get-tuple-element.36), channel_id=1, source_target_pairs={{1,0},{2,1},{3,2},{4,3},{5,4},{6,5},{7,6},{8,7},{9,8},{10,9},{11,1... | collective-permute-start | bytes 98312 | tf_op jit(solution)/shard_map/ppermute | solution.py:342
  43.4 15.8 %all-to-all-start.2 = ((bf16[16,16,640]{2,1,0:T(8,128)(2,1)}), bf16[16,16,640]{2,1,0:T(8,128)(2,1)S(1)}, u32[]{:S(2)}, u32[]{:S(2)}) async-start(bf16[16,16,640]{2,1,0:T(8,128)(2,1)} %shard_map.67), calls=%async_computation.2 | async-start | bytes 655360 | tf_op jit(solution)/shard_map/all_to_all | solution.py:356
  52.2 7.0 %copy-start = (bf16[512,1152]{1,0:T(8,128)(2,1)S(1)}, bf16[512,1152]{1,0:T(8,128)(2,1)}, u32[]{:S(2)}) copy-start(bf16[512,1152]{1,0:T(8,128)(2,1)} %w_ref.2) | copy-start | bytes 3538948
  55.6 26.3 %copy-start.2 = (bf16[512,512]{1,0:T(8,128)(2,1)S(1)}, bf16[512,512]{1,0:T(8,128)(2,1)}, u32[]{:S(2)}) copy-start(bf16[512,512]{1,0:T(8,128)(2,1)} %w_ref.3) | copy-start | bytes 1572868
  55.6 8.8 %collective-permute-start.3 = (bf16[72,256]{1,0:T(8,128)(2,1)S(1)}, bf16[72,256]{1,0:T(8,128)(2,1)S(1)}, u32[]{:S(2)}, u32[]{:S(2)}) collective-permute-start(bf16[72,256]{1,0:T(8,128)(2,1)S(1)} %get-tuple-element.41), channel_id=1, source_target_pairs={{0,2},{1,3},{2,0},{3,1},{4,6},{5,7},{6,4},{7,5},{8,10},{9,11},{10,... | collective-permute-start | bytes 110600 | tf_op jit(solution)/shard_map/ppermute | solution.py:367
  64.5 17.5 %all-to-all-start.3 = ((bf16[16,40,128]{2,1,0:T(8,128)(2,1)}), bf16[16,40,128]{2,1,0:T(8,128)(2,1)S(1)}, u32[]{:S(2)}, u32[]{:S(2)}) async-start(bf16[16,40,128]{2,1,0:T(8,128)(2,1)} %shard_map.69), calls=%async_computation.3 | async-start | bytes 327680 | tf_op jit(solution)/shard_map/all_to_all | solution.py:370
  71.2 5.8 %collective-permute-start.2 = (bf16[72,256]{1,0:T(8,128)(2,1)S(1)}, bf16[72,256]{1,0:T(8,128)(2,1)S(1)}, u32[]{:S(2)}, u32[]{:S(2)}) collective-permute-start(bf16[72,256]{1,0:T(8,128)(2,1)S(1)} %get-tuple-element.39), channel_id=1, source_target_pairs={{0,1},{1,0},{2,3},{3,2},{4,5},{5,4},{6,7},{7,6},{8,9},{9,8},{10,11... | collective-permute-start | bytes 110600 | tf_op jit(solution)/shard_map/ppermute | solution.py:367
  75.1 6.9 %collective-permute-start.4 = (bf16[72,256]{1,0:T(8,128)(2,1)S(1)}, bf16[72,256]{1,0:T(8,128)(2,1)S(1)}, u32[]{:S(2)}, u32[]{:S(2)}) collective-permute-start(bf16[72,256]{1,0:T(8,128)(2,1)S(1)} %get-tuple-element.43), channel_id=1, source_target_pairs={{0,3},{1,2},{2,1},{3,0},{4,7},{5,6},{6,5},{7,4},{8,11},{9,10},{10,... | collective-permute-start | bytes 110600 | tf_op jit(solution)/shard_map/ppermute | solution.py:367
  81.9 7.5 %copy-start.3 = (f32[7,7,512]{2,1,0:T(8,128)S(1)}, f32[7,7,512]{2,1,0:T(8,128)}, u32[]{:S(2)}) copy-start(f32[7,7,512]{2,1,0:T(8,128)} %param.9) | copy-start | bytes 301060
  82.7 9.4 %collective-permute-start.5 = (bf16[3,72,512]{2,1,0:T(8,128)(2,1)S(1)}, bf16[3,72,512]{2,1,0:T(8,128)(2,1)S(1)}, u32[]{:S(2)}, u32[]{:S(2)}) collective-permute-start(bf16[3,72,512]{2,1,0:T(8,128)(2,1)S(1)} %get-tuple-element.47), channel_id=1, source_target_pairs={{32,64},{96,128},{160,192},{224,256},{288,320},{352,384},{416,448}... | collective-permute-start | bytes 663560 | tf_op jit(solution)/shard_map/ppermute | solution.py:379
  87.5 4.6 %collective-permute-start.6 = (bf16[3,72,512]{2,1,0:T(8,128)(2,1)S(1)}, bf16[3,72,512]{2,1,0:T(8,128)(2,1)S(1)}, u32[]{:S(2)}, u32[]{:S(2)}) collective-permute-start(bf16[3,72,512]{2,1,0:T(8,128)(2,1)S(1)} %get-tuple-element.48), channel_id=1, source_target_pairs={{0,32},{64,96},{128,160},{192,224},{256,288},{320,352},{384,416},{... | collective-permute-start | bytes 663560 | tf_op jit(solution)/shard_map/ppermute | solution.py:378

commit v12 on v11

--- a/solution.py
+++ b/solution.py
@@ -366,7 +366,7 @@
     for k in range(1, ZS):
         zonal[k] = lax.ppermute(zonal[k], "lon", [(i, i ^ k) for i in range(LON)])
     merid = call(merid_kernel, shape(LAT, BROWS, 128), 1_000_000_000)(merid, w_qkv)
-    merid, zonal[2] = lax.optimization_barrier((merid, zonal[2]))
+    merid, *zonal = lax.optimization_barrier((merid, *zonal))
     merid = lax.all_to_all(merid, "lat", 0, 0)
     mixed, far, near = call(
         mix_kernel,

time: 95.8 us -> 97.2 us (1.015)
  blocking collectives: 17.9 us -> 30.5 us
  waiting for transfers between devices: 13 us -> 7.21 us
  starting transfers between devices: 47.9 us -> 42.6 us
    all_to_all x0 -> x1, blocking collectives: none -> 12.6 us  [per_device(): merid = lax.all_to_all(merid, 'lat', 0, 0)]
    all_to_all x2 -> x1, starting transfers between devices: 15.6 us -> 8.77 us  [per_device(): merid = lax.all_to_all(merid, 'lat', 0, 0)]
    ppermute x3, waiting for transfers between devices: 7.5 us -> 1.07 us  [per_device(): zonal[k] = lax.ppermute(zonal[k], 'lon', [(i, i ^ k) for i in range(LON)])]
    ppermute x3, starting transfers between devices: 9.34 us -> 11.5 us  [per_device(): zonal[k] = lax.ppermute(zonal[k], 'lon', [(i, i ^ k) for i in range(LON)])]
  transfers between devices with their start and end apart: 10 -> 9, of which waited for: 4 -> 3; matrix products, arithmetic and copies ran while one was open for 0% -> 0% of each run, Pallas kernels for 10% -> 9%
where the time goes in v12:
time: 97.2 us; the launch traced here: 95.8 us
  starting transfers between devices  42.6 us (44%)
  blocking collectives  30.5 us (31%)
  Pallas kernels  15.3 us (16%)
  waiting for transfers between devices  7.21 us (7%)
    all_to_all x1, blocking collectives, per_device(): row = lax.all_to_all(row, 'lon', 0, 0, axis_index_groups=along_z)  17.9 us
    all_to_all x1, blocking collectives, per_device(): merid = lax.all_to_all(merid, 'lat', 0, 0)  12.6 us
    ppermute x3, starting transfers between devices, per_device(): zonal[k] = lax.ppermute(zonal[k], 'lon', [(i, i ^ k) for i in range(LON)])  11.5 us
    all_to_all x1, starting transfers between devices, per_device(): merid = lax.all_to_all(merid, 'lat', 0, 0)  8.77 us
    ppermute x1, starting transfers between devices, per_device(): field_right = lax.ppermute(first, 'lon', left)  7.58 us
    all_to_all x1, starting transfers between devices, per_device(): slots = lax.all_to_all(slots, 'lon', 0, 0, axis_index_groups=along_y)  6.83 us
    ppermute x1, waiting for transfers between devices, per_device(): field_left = lax.ppermute(last, 'lon', right)  4.4 us
    ppermute x1, starting transfers between devices, per_device(): far = lax.ppermute(far, 'lat', far_pairs)  4.09 us
  transfers between devices with their start and end apart: 9, of which 3 were waited for; matrix products, arithmetic and copies ran while one was open for 0% of the time, Pallas kernels for 9%

profile of v12, /device:TPU:7, one launch (start us, length us, event | category | flops | bytes accessed | tf_op | source)
XLA Modules:
  0.0 95.8 jit_solution(15646206512468158595)
XLA Ops:
  0.0 1.7 %shard_map.64 = (bf16[4,64,384]{2,1,0:T(8,128)(2,1)S(1)}, bf16[32,512]{1,0:T(8,128)(2,1)S(1)}, bf16[32,512]{1,0:T(8,128)(2,1)S(1)}) custom-call(bf16[4,64,512]{2,1,0:T(8,128)(2,1)} %field_ref.1, bf16[512,1152]{1,0:T(8,128)(2,1)} %w_ref.2), custom_call_target="tpu_custom_call" | custom-call | flops 200000000 | bytes 2000000 | tf_op jit(solution)/shard_map/pallas_call | solution.py:320
  1.7 0.0 copy-start.1
  1.7 17.9 %all_to_all.20.in_ref.own_ref = bf16[4,64,384]{2,1,0:T(8,128)(2,1)S(1)} all-to-all(bf16[4,64,384]{2,1,0:T(8,128)(2,1)S(1)} %get-tuple-element.34), channel_id=1, replica_groups={{0,1,2,3},{4,5,6,7},{8,9,10,11},{12,13,14,15},{16,17,18,19},{20,21,22,2..., dimensions={0} | all-to-all | bytes 393216 | tf_op jit(solution)/shard_map/all_to_all | solution.py:332
  19.6 0.9 shard_map.65
  20.5 6.8 %all-to-all-start.1 = ((bf16[8,272,128]{2,1,0:T(8,128)(2,1)}), bf16[8,272,128]{2,1,0:T(8,128)(2,1)S(1)}, u32[]{:S(2)}, u32[]{:S(2)}) async-start(bf16[8,272,128]{2,1,0:T(8,128)(2,1)} %shard_map.65), calls=%async_computation.1 | async-start | bytes 1114112 | tf_op jit(solution)/shard_map/all_to_all | solution.py:340
  27.3 1.9 %collective-permute-start = (bf16[32,512]{1,0:T(8,128)(2,1)S(1)}, bf16[32,512]{1,0:T(8,128)(2,1)S(1)}, u32[]{:S(2)}, u32[]{:S(2)}) collective-permute-start(bf16[32,512]{1,0:T(8,128)(2,1)S(1)} %get-tuple-element.37), channel_id=1, source_target_pairs={{0,1},{1,2},{2,3},{3,4},{4,5},{5,6},{6,7},{7,8},{8,9},{9,10},{10,1... | collective-permute-start | bytes 98312 | tf_op jit(solution)/shard_map/ppermute | solution.py:341
  29.2 7.6 %collective-permute-start.1 = (bf16[32,512]{1,0:T(8,128)(2,1)S(1)}, bf16[32,512]{1,0:T(8,128)(2,1)S(1)}, u32[]{:S(2)}, u32[]{:S(2)}) collective-permute-start(bf16[32,512]{1,0:T(8,128)(2,1)S(1)} %get-tuple-element.38), channel_id=1, source_target_pairs={{1,0},{2,1},{3,2},{4,3},{5,4},{6,5},{7,6},{8,7},{9,8},{10,9},{11,1... | collective-permute-start | bytes 98312 | tf_op jit(solution)/shard_map/ppermute | solution.py:342
  36.8 0.0 copy-done.1
  36.8 1.2 %shard_map.66 = (bf16[16,16,640]{2,1,0:T(8,128)(2,1)}, bf16[2,16,640]{2,1,0:T(8,128)(2,1)S(1)}) custom-call(bf16[4,64,512]{2,1,0:T(8,128)(2,1)S(1)} %copy-done.1), custom_call_target="tpu_custom_call" | custom-call | flops 300000000 | bytes 2000000 | tf_op jit(solution)/shard_map/pallas_call | solution.py:343
  38.1 4.4 %collective-permute-done.left_ref = bf16[32,512]{1,0:T(8,128)(2,1)S(1)} collective-permute-done((bf16[32,512]{1,0:T(8,128)(2,1)S(1)}, bf16[32,512]{1,0:T(8,128)(2,1)S(1)}, u32[]{:S(2)}, u32[]{:S(2)}) %collective-permute-start) | collective-permute-done | bytes 32800 | tf_op jit(solution)/shard_map/ppermute | solution.py:341
  42.5 0.0 collective-permute-done.1.right_ref
  42.5 1.0 shard_map.67
  43.4 0.0 all-to-all-done.1.all_ref
  43.5 8.8 %all-to-all-start.2 = ((bf16[16,16,640]{2,1,0:T(8,128)(2,1)}), bf16[16,16,640]{2,1,0:T(8,128)(2,1)S(1)}, u32[]{:S(2)}, u32[]{:S(2)}) async-start(bf16[16,16,640]{2,1,0:T(8,128)(2,1)} %shard_map.67), calls=%async_computation.2 | async-start | bytes 655360 | tf_op jit(solution)/shard_map/all_to_all | solution.py:356
  52.2 0.0 copy-start
  52.2 3.4 %shard_map.69 = (bf16[72,256]{1,0:T(8,128)(2,1)S(1)}, bf16[72,256]{1,0:T(8,128)(2,1)S(1)}, bf16[72,256]{1,0:T(8,128)(2,1)S(1)}, bf16[72,256]{1,0:T(8,128)(2,1)S(1)}) custom-call(s32[1]{0:T(128)} %bitcast.y_ref, s32[1]{0:T(128)} %bitcast.1.z_ref, bf16[4,64,384]{2,1,0:T(8,128)(2,1)S(1)} %all_to_all.20.in_ref.own_ref, ...), custom_call_target="tpu_custom_call" | custom-call | flops 4000000000 | bytes 2000000 | tf_op jit(solution)/shard_map/pallas_call | solution.py:357
  55.6 3.8 %collective-permute-start.2 = (bf16[72,256]{1,0:T(8,128)(2,1)S(1)}, bf16[72,256]{1,0:T(8,128)(2,1)S(1)}, u32[]{:S(2)}, u32[]{:S(2)}) collective-permute-start(bf16[72,256]{1,0:T(8,128)(2,1)S(1)} %get-tuple-element.43), channel_id=1, source_target_pairs={{0,1},{1,0},{2,3},{3,2},{4,5},{5,4},{6,7},{7,6},{8,9},{9,8},{10,11... | collective-permute-start | bytes 110600 | tf_op jit(solution)/shard_map/ppermute | solution.py:367
  59.4 3.8 %collective-permute-start.3 = (bf16[72,256]{1,0:T(8,128)(2,1)S(1)}, bf16[72,256]{1,0:T(8,128)(2,1)S(1)}, u32[]{:S(2)}, u32[]{:S(2)}) collective-permute-start(bf16[72,256]{1,0:T(8,128)(2,1)S(1)} %get-tuple-element.44), channel_id=1, source_target_pairs={{0,2},{1,3},{2,0},{3,1},{4,6},{5,7},{6,4},{7,5},{8,10},{9,11},{10,... | collective-permute-start | bytes 110600 | tf_op jit(solution)/shard_map/ppermute | solution.py:367
  63.2 0.0 copy-start.2
  63.2 3.9 %collective-permute-start.4 = (bf16[72,256]{1,0:T(8,128)(2,1)S(1)}, bf16[72,256]{1,0:T(8,128)(2,1)S(1)}, u32[]{:S(2)}, u32[]{:S(2)}) collective-permute-start(bf16[72,256]{1,0:T(8,128)(2,1)S(1)} %get-tuple-element.45), channel_id=1, source_target_pairs={{0,3},{1,2},{2,1},{3,0},{4,7},{5,6},{6,5},{7,4},{8,11},{9,10},{10,... | collective-permute-start | bytes 110600 | tf_op jit(solution)/shard_map/ppermute | solution.py:367
  67.2 0.0 all-to-all-done.2.in_ref
  67.2 0.0 copy-done
  67.2 2.0 %shard_map.68 = bf16[16,40,128]{2,1,0:T(8,128)(2,1)S(1)} custom-call(bf16[16,16,640]{2,1,0:T(8,128)(2,1)S(1)} %all-to-all-done.2.in_ref, bf16[512,1152]{1,0:T(8,128)(2,1)S(1)} %copy-done), custom_call_target="tpu_custom_call" | custom-call | flops 1000000000 | bytes 2000000 | tf_op jit(solution)/shard_map/pallas_call | solution.py:368
  69.1 0.0 collective-permute-done.2.z1_ref
  69.2 0.0 collective-permute-done.3.z2_ref
  69.2 1.1 %collective-permute-done.4.z3_ref = bf16[72,256]{1,0:T(8,128)(2,1)S(1)} collective-permute-done((bf16[72,256]{1,0:T(8,128)(2,1)S(1)}, bf16[72,256]{1,0:T(8,128)(2,1)S(1)}, u32[]{:S(2)}, u32[]{:S(2)}) %collective-permute-start.4) | collective-permute-done | bytes 36896 | tf_op jit(solution)/shard_map/ppermute | solution.py:367
  70.2 12.6 %all_to_all.21.merid_ref = bf16[16,40,128]{2,1,0:T(8,128)(2,1)S(1)} all-to-all(bf16[16,40,128]{2,1,0:T(8,128)(2,1)S(1)} %shard_map.68), channel_id=1, replica_groups=mesh['lat'=16,'lon'=32] {'lat'}, dimensions={0} | all-to-all | bytes 327680 | tf_op jit(solution)/shard_map/all_to_all | solution.py:370
  82.8 0.0 copy-done.2
  82.8 0.0 copy-start.3
  82.8 0.8 shard_map.70
  83.6 4.1 %collective-permute-start.5 = (bf16[3,72,512]{2,1,0:T(8,128)(2,1)S(1)}, bf16[3,72,512]{2,1,0:T(8,128)(2,1)S(1)}, u32[]{:S(2)}, u32[]{:S(2)}) collective-permute-start(bf16[3,72,512]{2,1,0:T(8,128)(2,1)S(1)} %get-tuple-element.53), channel_id=1, source_target_pairs={{32,64},{96,128},{160,192},{224,256},{288,320},{352,384},{416,448}... | collective-permute-start | bytes 663560 | tf_op jit(solution)/shard_map/ppermute | solution.py:379
  87.7 1.9 %collective-permute-start.6 = (bf16[3,72,512]{2,1,0:T(8,128)(2,1)S(1)}, bf16[3,72,512]{2,1,0:T(8,128)(2,1)S(1)}, u32[]{:S(2)}, u32[]{:S(2)}) collective-permute-start(bf16[3,72,512]{2,1,0:T(8,128)(2,1)S(1)} %get-tuple-element.54), channel_id=1, source_target_pairs={{0,32},{64,96},{128,160},{192,224},{256,288},{320,352},{384,416},{... | collective-permute-start | bytes 663560 | tf_op jit(solution)/shard_map/ppermute | solution.py:378
  89.6 0.0 copy-done.3
  89.6 1.6 %shard_map.71 = (f32[256,512]{1,0:T(8,128)S(1)}, bf16[512,1024]{1,0:T(8,128)(2,1)S(1)}, bf16[1024,512]{1,0:T(8,128)(2,1)S(1)}) custom-call(bf16[4,72,512]{2,1,0:T(8,128)(2,1)S(1)} %get-tuple-element.51.mixed_ref, f32[49,512]{1,0:T(8,128)S(1)} %reshape.15.conv_ref, bf16[512,1024]{1,0:T(8,128)(2,1)} %w_in_hbm.1, bf16[1024,512]{1,0:T(8,128)(2,1)} %w_back_hbm.1), custom_call_target="tpu_custom_call" | custom-call | flops 1000000000 | bytes 2000000 | tf_op jit(solution)/shard_map/pallas_call | solution.py:381
  91.2 1.7 %collective-permute-done.5.far_ref = bf16[3,72,512]{2,1,0:T(8,128)(2,1)S(1)} collective-permute-done((bf16[3,72,512]{2,1,0:T(8,128)(2,1)S(1)}, bf16[3,72,512]{2,1,0:T(8,128)(2,1)S(1)}, u32[]{:S(2)}, u32[]{:S(2)}) %collective-permute-start.5) | collective-permute-done | bytes 221216 | tf_op jit(solution)/shard_map/ppermute | solution.py:379
  92.9 0.0 collective-permute-done.6.near_ref
  92.9 2.9 %shard_map.72 = bf16[4,64,512]{2,1,0:T(8,128)(2,1)} custom-call(s32[1]{0:T(128)} %bitcast.2.odd_ref, bf16[4,72,512]{2,1,0:T(8,128)(2,1)S(1)} %get-tuple-element.51.mixed_ref, f32[256,512]{1,0:T(8,128)S(1)} %get-tuple-element.52.own_ref, bf16[3,72,512]{2,1,0:T(8,128)(2,1)S(1)} %collective-permute-done.5.far_ref, ...), custom_call_target="tpu_custom_call" | custom-call | flops 2000000000 | bytes 2000000 | tf_op jit(solution)/shard_map/pallas_call | solution.py:388
  (1 shorter events, 0.0 us)
Async XLA Ops:
  1.7 35.2 %copy-start.1 = (bf16[4,64,512]{2,1,0:T(8,128)(2,1)S(1)}, bf16[4,64,512]{2,1,0:T(8,128)(2,1)}, u32[]{:S(2)}) copy-start(bf16[4,64,512]{2,1,0:T(8,128)(2,1)} %field_ref.1) | copy-start | bytes 786436
  20.5 22.9 %all-to-all-start.1 = ((bf16[8,272,128]{2,1,0:T(8,128)(2,1)}), bf16[8,272,128]{2,1,0:T(8,128)(2,1)S(1)}, u32[]{:S(2)}, u32[]{:S(2)}) async-start(bf16[8,272,128]{2,1,0:T(8,128)(2,1)} %shard_map.65), calls=%async_computation.1 | async-start | bytes 1114112 | tf_op jit(solution)/shard_map/all_to_all | solution.py:340
  27.3 15.2 %collective-permute-start = (bf16[32,512]{1,0:T(8,128)(2,1)S(1)}, bf16[32,512]{1,0:T(8,128)(2,1)S(1)}, u32[]{:S(2)}, u32[]{:S(2)}) collective-permute-start(bf16[32,512]{1,0:T(8,128)(2,1)S(1)} %get-tuple-element.37), channel_id=1, source_target_pairs={{0,1},{1,2},{2,3},{3,4},{4,5},{5,6},{6,7},{7,8},{8,9},{9,10},{10,1... | collective-permute-start | bytes 98312 | tf_op jit(solution)/shard_map/ppermute | solution.py:341
  29.2 13.2 %collective-permute-start.1 = (bf16[32,512]{1,0:T(8,128)(2,1)S(1)}, bf16[32,512]{1,0:T(8,128)(2,1)S(1)}, u32[]{:S(2)}, u32[]{:S(2)}) collective-permute-start(bf16[32,512]{1,0:T(8,128)(2,1)S(1)} %get-tuple-element.38), channel_id=1, source_target_pairs={{1,0},{2,1},{3,2},{4,3},{5,4},{6,5},{7,6},{8,7},{9,8},{10,9},{11,1... | collective-permute-start | bytes 98312 | tf_op jit(solution)/shard_map/ppermute | solution.py:342
  43.5 23.7 %all-to-all-start.2 = ((bf16[16,16,640]{2,1,0:T(8,128)(2,1)}), bf16[16,16,640]{2,1,0:T(8,128)(2,1)S(1)}, u32[]{:S(2)}, u32[]{:S(2)}) async-start(bf16[16,16,640]{2,1,0:T(8,128)(2,1)} %shard_map.67), calls=%async_computation.2 | async-start | bytes 655360 | tf_op jit(solution)/shard_map/all_to_all | solution.py:356
  52.2 14.9 %copy-start = (bf16[512,1152]{1,0:T(8,128)(2,1)S(1)}, bf16[512,1152]{1,0:T(8,128)(2,1)}, u32[]{:S(2)}) copy-start(bf16[512,1152]{1,0:T(8,128)(2,1)} %w_ref.2) | copy-start | bytes 3538948
  55.6 13.5 %collective-permute-start.2 = (bf16[72,256]{1,0:T(8,128)(2,1)S(1)}, bf16[72,256]{1,0:T(8,128)(2,1)S(1)}, u32[]{:S(2)}, u32[]{:S(2)}) collective-permute-start(bf16[72,256]{1,0:T(8,128)(2,1)S(1)} %get-tuple-element.43), channel_id=1, source_target_pairs={{0,1},{1,0},{2,3},{3,2},{4,5},{5,4},{6,7},{7,6},{8,9},{9,8},{10,11... | collective-permute-start | bytes 110600 | tf_op jit(solution)/shard_map/ppermute | solution.py:367
  59.4 9.7 %collective-permute-start.3 = (bf16[72,256]{1,0:T(8,128)(2,1)S(1)}, bf16[72,256]{1,0:T(8,128)(2,1)S(1)}, u32[]{:S(2)}, u32[]{:S(2)}) collective-permute-start(bf16[72,256]{1,0:T(8,128)(2,1)S(1)} %get-tuple-element.44), channel_id=1, source_target_pairs={{0,2},{1,3},{2,0},{3,1},{4,6},{5,7},{6,4},{7,5},{8,10},{9,11},{10,... | collective-permute-start | bytes 110600 | tf_op jit(solution)/shard_map/ppermute | solution.py:367
  63.2 19.6 %copy-start.2 = (bf16[512,512]{1,0:T(8,128)(2,1)S(1)}, bf16[512,512]{1,0:T(8,128)(2,1)}, u32[]{:S(2)}) copy-start(bf16[512,512]{1,0:T(8,128)(2,1)} %w_ref.3) | copy-start | bytes 1572868
  63.2 7.0 %collective-permute-start.4 = (bf16[72,256]{1,0:T(8,128)(2,1)S(1)}, bf16[72,256]{1,0:T(8,128)(2,1)S(1)}, u32[]{:S(2)}, u32[]{:S(2)}) collective-permute-start(bf16[72,256]{1,0:T(8,128)(2,1)S(1)} %get-tuple-element.45), channel_id=1, source_target_pairs={{0,3},{1,2},{2,1},{3,0},{4,7},{5,6},{6,5},{7,4},{8,11},{9,10},{10,... | collective-permute-start | bytes 110600 | tf_op jit(solution)/shard_map/ppermute | solution.py:367
  82.8 6.8 %copy-start.3 = (f32[7,7,512]{2,1,0:T(8,128)S(1)}, f32[7,7,512]{2,1,0:T(8,128)}, u32[]{:S(2)}) copy-start(f32[7,7,512]{2,1,0:T(8,128)} %param.9) | copy-start | bytes 301060
  83.6 9.4 %collective-permute-start.5 = (bf16[3,72,512]{2,1,0:T(8,128)(2,1)S(1)}, bf16[3,72,512]{2,1,0:T(8,128)(2,1)S(1)}, u32[]{:S(2)}, u32[]{:S(2)}) collective-permute-start(bf16[3,72,512]{2,1,0:T(8,128)(2,1)S(1)} %get-tuple-element.53), channel_id=1, source_target_pairs={{32,64},{96,128},{160,192},{224,256},{288,320},{352,384},{416,448}... | collective-permute-start | bytes 663560 | tf_op jit(solution)/shard_map/ppermute | solution.py:379
  87.7 5.3 %collective-permute-start.6 = (bf16[3,72,512]{2,1,0:T(8,128)(2,1)S(1)}, bf16[3,72,512]{2,1,0:T(8,128)(2,1)S(1)}, u32[]{:S(2)}, u32[]{:S(2)}) collective-permute-start(bf16[3,72,512]{2,1,0:T(8,128)(2,1)S(1)} %get-tuple-element.54), channel_id=1, source_target_pairs={{0,32},{64,96},{128,160},{192,224},{256,288},{320,352},{384,416},{... | collective-permute-start | bytes 663560 | tf_op jit(solution)/shard_map/ppermute | solution.py:378

commit v13 on v10

--- a/solution.py
+++ b/solution.py
@@ -75,7 +75,9 @@
     return pltpu.with_memory_space_constraint(array, pltpu.HBM)
 
 
-def zonal_project_kernel(field_hbm, w_hbm, out_ref, first_ref, last_ref, field_ref, wq_ref, wkv_ref, sems):
+def zonal_project_kernel(
+    side_ref, field_hbm, w_hbm, out_ref, outer_ref, inner_ref, field_ref, wq_ref, wkv_ref, sems
+):
     loads = [
         pltpu.make_async_copy(field_hbm, field_ref, sems.at[0]),
         pltpu.make_async_copy(w_hbm.at[:, 512:640], wkv_ref, sems.at[1]),
@@ -85,8 +87,11 @@
         load.start()
     loads[0].wait()
     field = field_ref[...].astype(F32)
-    first_ref[...] = field[:, 0:E].reshape(R * E, C).astype(BF)
-    last_ref[...] = field[:, W - E : W].reshape(R * E, C).astype(BF)
+    side = side_ref[0] == 1
+    first = field[:, 0:E].reshape(R * E, C)
+    last = field[:, W - E : W].reshape(R * E, C)
+    outer_ref[...] = jnp.where(side, last, first).astype(BF)
+    inner_ref[...] = jnp.where(side, first, last).astype(BF)
     normed = layer_norm(field.reshape(CELLS, C)).astype(BF)
     loads[1].wait()
     out_ref[:, :, 256:384] = mm(normed, wkv_ref[...]).astype(BF).reshape(R, W, 128)
@@ -165,10 +170,16 @@
     edge_ref[1] = slots[EDGES[1]]
 
 
-def merid_edge_kernel(slots_hbm, edge_ref, left_ref, right_ref, out_hbm, done_ref, sems):
+def merid_edge_kernel(
+    side_ref, slots_hbm, edge_ref, outer_ref, inner_ref, out_hbm, left_ref, right_ref, done_ref, sems
+):
+    side = side_ref[0] == 1
+    outer, inner = outer_ref[...].astype(F32), inner_ref[...].astype(F32)
+    halos = (jnp.where(side, inner, outer), jnp.where(side, outer, inner))
     copies = []
-    for n, (m, ref) in enumerate(zip(EDGES, (left_ref, right_ref))):
-        normed = layer_norm(ref[...].astype(F32)).astype(BF)
+    for n, (m, ref, halo) in enumerate(zip(EDGES, (left_ref, right_ref), halos)):
+        ref[...] = halo.astype(BF)
+        normed = layer_norm(halo).astype(BF)
         first = jnp.full((MCELLS, R * E), m * MC - n * (W + E), jnp.int32)
         done_ref[n] = (edge_ref[n].astype(F32) + merid_slots(normed, first, E, E)).astype(BF)
         copies.append(pltpu.make_async_copy(done_ref.at[n], out_hbm.at[m], sems.at[n]))
@@ -299,28 +310,30 @@
 
 
 def per_device(field, w_qkv, w_out, conv_w, w_in, w_back):
-    right = [(i, (i + 1) % LON) for i in range(LON)]
-    left = [(j, i) for i, j in right]
+    inner_pairs = [(i, i + 1) for i in range(0, LON, 2)]
+    outer_pairs = [(i, (i + 1) % LON) for i in range(1, LON, 2)]
+    inner_pairs, outer_pairs = (pairs + [(j, i) for i, j in pairs] for pairs in (inner_pairs, outer_pairs))
     near_pairs = [(i, i + 1) for i in range(0, LAT, 2)]
     far_pairs = [(i, i + 1) for i in range(1, LAT - 1, 2)]
     near_pairs, far_pairs = (pairs + [(j, i) for i, j in pairs] for pairs in (near_pairs, far_pairs))
     along_y = [[y * ZS + z for y in range(YS)] for z in range(ZS)]
     along_z = [[y * ZS + z for z in range(ZS)] for y in range(YS)]
-    y = (lax.axis_index("lon").astype(jnp.int32) >> 2).reshape(1)
+    lon = lax.axis_index("lon").astype(jnp.int32)
+    y, side = (lon >> 2).reshape(1), (lon & 1).reshape(1)
     odd = (lax.axis_index("lat").astype(jnp.int32) & 1).reshape(1)
-    field, y, odd = lax.optimization_barrier((field, y, odd))
-    row, first, last = call(
+    field, y, side, odd = lax.optimization_barrier((field, y, side, odd))
+    row, outer, inner = call(
         zonal_project_kernel,
         (shape(R, W, 384), shape(R * E, C), shape(R * E, C)),
         200_000_000,
-        in_specs=[ANY, ANY],
+        in_specs=[SMEM, ANY, ANY],
         scratch_shapes=[
             pltpu.VMEM((R, W, C), BF),
             pltpu.VMEM((C, 256), BF),
             pltpu.VMEM((C, 128), BF),
             pltpu.SemaphoreType.DMA((3,)),
         ],
-    )(in_hbm(field), in_hbm(w_qkv))
+    )(side, in_hbm(field), in_hbm(w_qkv))
     row = lax.all_to_all(row, "lon", 0, 0, axis_index_groups=along_z)
     slots = call(
         spread_kernel,
@@ -330,20 +343,20 @@
         scratch_shapes=[pltpu.VMEM((KEYS, 128), BF), pltpu.SemaphoreType.DMA((YS,))],
     )(row)
     slots = lax.all_to_all(slots, "lon", 0, 0, axis_index_groups=along_y)
-    field_left = lax.ppermute(last, "lon", right)
-    field_right = lax.ppermute(first, "lon", left)
+    inner = lax.ppermute(inner, "lon", inner_pairs)
+    outer = lax.ppermute(outer, "lon", outer_pairs)
     merid, merid_edges = call(
         merid_own_kernel, (shape(LAT, MCELLS, MLANES), shape(2, MCELLS, MLANES)), 300_000_000
     )(field)
-    merid = call(
+    merid, field_left, field_right = call(
         merid_edge_kernel,
-        shape(LAT, MCELLS, MLANES),
+        (shape(LAT, MCELLS, MLANES), shape(R * E, C), shape(R * E, C)),
         10_000_000,
-        in_specs=[ANY, VMEM, VMEM, VMEM],
-        out_specs=ANY,
-        input_output_aliases={0: 0},
+        in_specs=[SMEM, ANY, VMEM, VMEM, VMEM],
+        out_specs=[ANY, VMEM, VMEM],
+        input_output_aliases={1: 0},
         scratch_shapes=[pltpu.VMEM((2, MCELLS, MLANES), BF), pltpu.SemaphoreType.DMA((2,))],
-    )(merid, merid_edges, field_left, field_right)
+    )(side, merid, merid_edges, outer, inner)
     slots, merid = lax.optimization_barrier((slots, merid))
     merid = lax.all_to_all(merid, "lat", 0, 0)
     zonal = call(

time: 95.5 us -> 94.8 us (level)
  no operation moved by 1% of the time
where the time goes in v13:
time: 94.8 us; the launch traced here: 94.2 us
  starting transfers between devices  33.8 us (36%)
  blocking collectives  29.2 us (31%)
  Pallas kernels  15.9 us (17%)
  waiting for transfers between devices  15.1 us (16%)
    all_to_all x1, blocking collectives, per_device(): row = lax.all_to_all(row, 'lon', 0, 0, axis_index_groups=along_z)  17.9 us
    all_to_all x1, blocking collectives, per_device(): merid = lax.all_to_all(merid, 'lat', 0, 0)  11.3 us
    all_to_all x1, starting transfers between devices, per_device(): merid = lax.all_to_all(merid, 'lat', 0, 0)  8.76 us
    ppermute x1, starting transfers between devices, per_device(): outer = lax.ppermute(outer, 'lon', outer_pairs)  6.95 us
    all_to_all x1, starting transfers between devices, per_device(): slots = lax.all_to_all(slots, 'lon', 0, 0, axis_index_groups=along_y)  6.83 us
    all_to_all x1, waiting for transfers between devices, per_device(): zonal = lax.all_to_all(zonal, 'lon', 0, 0, axis_index_groups=along_z)  5.59 us
    ppermute x1, waiting for transfers between devices, per_device(): outer = lax.ppermute(outer, 'lon', outer_pairs)  5.01 us
    ppermute x1, starting transfers between devices, per_device(): far = lax.ppermute(far, 'lat', far_pairs)  4.09 us
  transfers between devices with their start and end apart: 7, of which 4 were waited for; matrix products, arithmetic and copies ran while one was open for 0% of the time, Pallas kernels for 10%

profile of v13, /device:TPU:7, one launch (start us, length us, event | category | flops | bytes accessed | tf_op | source)
XLA Modules:
  0.0 94.2 jit_solution(4548606625864844356)
XLA Ops:
  0.0 1.7 %shard_map.64 = (bf16[4,64,384]{2,1,0:T(8,128)(2,1)S(1)}, bf16[32,512]{1,0:T(8,128)(2,1)S(1)}, bf16[32,512]{1,0:T(8,128)(2,1)S(1)}) custom-call(s32[1]{0:T(128)} %bitcast.1.side_ref, bf16[4,64,512]{2,1,0:T(8,128)(2,1)} %field_ref.1, bf16[512,1152]{1,0:T(8,128)(2,1)} %w_ref.2), custom_call_target="tpu_custom_call" | custom-call | flops 200000000 | bytes 2000000 | tf_op jit(solution)/shard_map/pallas_call | solution.py:325
  1.7 0.0 copy-start.1
  1.7 17.9 %all_to_all.25.in_ref.own_ref = bf16[4,64,384]{2,1,0:T(8,128)(2,1)S(1)} all-to-all(bf16[4,64,384]{2,1,0:T(8,128)(2,1)S(1)} %get-tuple-element.29), channel_id=1, replica_groups={{0,1,2,3},{4,5,6,7},{8,9,10,11},{12,13,14,15},{16,17,18,19},{20,21,22,2..., dimensions={0} | all-to-all | bytes 393216 | tf_op jit(solution)/shard_map/all_to_all | solution.py:337
  19.6 0.9 shard_map.65
  20.5 6.8 %all-to-all-start.1 = ((bf16[8,272,128]{2,1,0:T(8,128)(2,1)}), bf16[8,272,128]{2,1,0:T(8,128)(2,1)S(1)}, u32[]{:S(2)}, u32[]{:S(2)}) async-start(bf16[8,272,128]{2,1,0:T(8,128)(2,1)} %shard_map.65), calls=%async_computation.1 | async-start | bytes 1114112 | tf_op jit(solution)/shard_map/all_to_all | solution.py:345
  27.3 7.0 %collective-permute-start = (bf16[32,512]{1,0:T(8,128)(2,1)S(1)}, bf16[32,512]{1,0:T(8,128)(2,1)S(1)}, u32[]{:S(2)}, u32[]{:S(2)}) collective-permute-start(bf16[32,512]{1,0:T(8,128)(2,1)S(1)} %get-tuple-element.32), channel_id=1, source_target_pairs={{1,2},{3,4},{5,6},{7,8},{9,10},{11,12},{13,14},{15,16},{17,18},{19... | collective-permute-start | bytes 98312 | tf_op jit(solution)/shard_map/ppermute | solution.py:347
  34.3 1.9 %collective-permute-start.1 = (bf16[32,512]{1,0:T(8,128)(2,1)S(1)}, bf16[32,512]{1,0:T(8,128)(2,1)S(1)}, u32[]{:S(2)}, u32[]{:S(2)}) collective-permute-start(bf16[32,512]{1,0:T(8,128)(2,1)S(1)} %get-tuple-element.33), channel_id=1, source_target_pairs={{0,1},{2,3},{4,5},{6,7},{8,9},{10,11},{12,13},{14,15},{16,17},{18,... | collective-permute-start | bytes 98312 | tf_op jit(solution)/shard_map/ppermute | solution.py:346
  36.2 0.0 copy-done.1
  36.2 1.2 %shard_map.66 = (bf16[16,16,640]{2,1,0:T(8,128)(2,1)}, bf16[2,16,640]{2,1,0:T(8,128)(2,1)S(1)}) custom-call(bf16[4,64,512]{2,1,0:T(8,128)(2,1)S(1)} %copy-done.1), custom_call_target="tpu_custom_call" | custom-call | flops 300000000 | bytes 2000000 | tf_op jit(solution)/shard_map/pallas_call | solution.py:348
  37.5 5.0 %collective-permute-done.outer_ref = bf16[32,512]{1,0:T(8,128)(2,1)S(1)} collective-permute-done((bf16[32,512]{1,0:T(8,128)(2,1)S(1)}, bf16[32,512]{1,0:T(8,128)(2,1)S(1)}, u32[]{:S(2)}, u32[]{:S(2)}) %collective-permute-start) | collective-permute-done | bytes 32800 | tf_op jit(solution)/shard_map/ppermute | solution.py:347
  42.5 0.0 collective-permute-done.1.inner_ref
  42.5 0.9 %shard_map.67 = (bf16[16,16,640]{2,1,0:T(8,128)(2,1)}, bf16[32,512]{1,0:T(8,128)(2,1)S(1)}, bf16[32,512]{1,0:T(8,128)(2,1)S(1)}) custom-call(s32[1]{0:T(128)} %bitcast.1.side_ref, bf16[16,16,640]{2,1,0:T(8,128)(2,1)} %get-tuple-element.30.slots_hbm, bf16[2,16,640]{2,1,0:T(8,128)(2,1)S(1)} %get-tuple-element.31.edge_ref, ...), custom_call_target="tpu_custom_call", output_to_operand_aliasing={{0}: (1, {})} | custom-call | flops 10000000 | bytes 2000000 | tf_op jit(solution)/shard_map/pallas_call | solution.py:351
  43.4 0.0 all-to-all-done.1.all_ref
  43.4 8.8 %all-to-all-start.3 = ((bf16[16,16,640]{2,1,0:T(8,128)(2,1)}), bf16[16,16,640]{2,1,0:T(8,128)(2,1)S(1)}, u32[]{:S(2)}, u32[]{:S(2)}) async-start(bf16[16,16,640]{2,1,0:T(8,128)(2,1)} %get-tuple-element.36), calls=%async_computation.3 | async-start | bytes 655360 | tf_op jit(solution)/shard_map/all_to_all | solution.py:361
  52.2 0.0 copy-start
  52.2 4.0 %shard_map.68 = bf16[4,72,256]{2,1,0:T(8,128)(2,1)} custom-call(s32[1]{0:T(128)} %bitcast.y_ref, bf16[4,64,384]{2,1,0:T(8,128)(2,1)S(1)} %all_to_all.25.in_ref.own_ref, bf16[8,272,128]{2,1,0:T(8,128)(2,1)S(1)} %all-to-all-done.1.all_ref), custom_call_target="tpu_custom_call" | custom-call | flops 4000000000 | bytes 2000000 | tf_op jit(solution)/shard_map/pallas_call | solution.py:362
  56.2 2.7 %all-to-all-done.3.in_ref = bf16[16,16,640]{2,1,0:T(8,128)(2,1)S(1)} async-done(((bf16[16,16,640]{2,1,0:T(8,128)(2,1)}), bf16[16,16,640]{2,1,0:T(8,128)(2,1)S(1)}, u32[]{:S(2)}, u32[]{:S(2)}) %all-to-all-start.3) | async-done | bytes 327712 | tf_op jit(solution)/shard_map/all_to_all | solution.py:361
  58.9 3.3 %all-to-all-start.2 = ((bf16[4,72,256]{2,1,0:T(8,128)(2,1)}), bf16[4,72,256]{2,1,0:T(8,128)(2,1)S(1)}, u32[]{:S(2)}, u32[]{:S(2)}) async-start(bf16[4,72,256]{2,1,0:T(8,128)(2,1)} %shard_map.68), calls=%async_computation.2 | async-start | bytes 294912 | tf_op jit(solution)/shard_map/all_to_all | solution.py:365
  62.3 0.0 copy-done
  62.3 0.0 copy-start.2
  62.3 2.0 %shard_map.69 = bf16[16,40,128]{2,1,0:T(8,128)(2,1)S(1)} custom-call(bf16[16,16,640]{2,1,0:T(8,128)(2,1)S(1)} %all-to-all-done.3.in_ref, bf16[512,1152]{1,0:T(8,128)(2,1)S(1)} %copy-done), custom_call_target="tpu_custom_call" | custom-call | flops 1000000000 | bytes 2000000 | tf_op jit(solution)/shard_map/pallas_call | solution.py:366
  64.3 5.6 %all-to-all-done.2.zonal_ref = bf16[4,72,256]{2,1,0:T(8,128)(2,1)S(1)} async-done(((bf16[4,72,256]{2,1,0:T(8,128)(2,1)}), bf16[4,72,256]{2,1,0:T(8,128)(2,1)S(1)}, u32[]{:S(2)}, u32[]{:S(2)}) %all-to-all-start.2) | async-done | bytes 147488 | tf_op jit(solution)/shard_map/all_to_all | solution.py:365
  69.9 11.3 %all_to_all.26.merid_ref = bf16[16,40,128]{2,1,0:T(8,128)(2,1)S(1)} all-to-all(bf16[16,40,128]{2,1,0:T(8,128)(2,1)S(1)} %shard_map.69), channel_id=1, replica_groups=mesh['lat'=16,'lon'=32] {'lat'}, dimensions={0} | all-to-all | bytes 327680 | tf_op jit(solution)/shard_map/all_to_all | solution.py:367
  81.2 0.0 copy-done.2
  81.2 0.0 copy-start.3
  81.2 0.8 shard_map.70
  81.9 4.1 %collective-permute-start.2 = (bf16[3,72,512]{2,1,0:T(8,128)(2,1)S(1)}, bf16[3,72,512]{2,1,0:T(8,128)(2,1)S(1)}, u32[]{:S(2)}, u32[]{:S(2)}) collective-permute-start(bf16[3,72,512]{2,1,0:T(8,128)(2,1)S(1)} %get-tuple-element.41), channel_id=1, source_target_pairs={{32,64},{96,128},{160,192},{224,256},{288,320},{352,384},{416,448}... | collective-permute-start | bytes 663560 | tf_op jit(solution)/shard_map/ppermute | solution.py:375
  86.0 1.9 %collective-permute-start.3 = (bf16[3,72,512]{2,1,0:T(8,128)(2,1)S(1)}, bf16[3,72,512]{2,1,0:T(8,128)(2,1)S(1)}, u32[]{:S(2)}, u32[]{:S(2)}) collective-permute-start(bf16[3,72,512]{2,1,0:T(8,128)(2,1)S(1)} %get-tuple-element.42), channel_id=1, source_target_pairs={{0,32},{64,96},{128,160},{192,224},{256,288},{320,352},{384,416},{... | collective-permute-start | bytes 663560 | tf_op jit(solution)/shard_map/ppermute | solution.py:374
  88.0 0.0 copy-done.3
  88.0 1.6 %shard_map.71 = (f32[256,512]{1,0:T(8,128)S(1)}, bf16[512,1024]{1,0:T(8,128)(2,1)S(1)}, bf16[1024,512]{1,0:T(8,128)(2,1)S(1)}) custom-call(bf16[4,72,512]{2,1,0:T(8,128)(2,1)S(1)} %get-tuple-element.39.mixed_ref, f32[49,512]{1,0:T(8,128)S(1)} %reshape.15.conv_ref, bf16[512,1024]{1,0:T(8,128)(2,1)} %w_in_hbm.1, bf16[1024,512]{1,0:T(8,128)(2,1)} %w_back_hbm.1), custom_call_target="tpu_custom_call" | custom-call | flops 1000000000 | bytes 2000000 | tf_op jit(solution)/shard_map/pallas_call | solution.py:377
  89.6 1.7 %collective-permute-done.2.far_ref = bf16[3,72,512]{2,1,0:T(8,128)(2,1)S(1)} collective-permute-done((bf16[3,72,512]{2,1,0:T(8,128)(2,1)S(1)}, bf16[3,72,512]{2,1,0:T(8,128)(2,1)S(1)}, u32[]{:S(2)}, u32[]{:S(2)}) %collective-permute-start.2) | collective-permute-done | bytes 221216 | tf_op jit(solution)/shard_map/ppermute | solution.py:375
  91.3 0.0 collective-permute-done.3.near_ref
  91.3 2.9 %shard_map.72 = bf16[4,64,512]{2,1,0:T(8,128)(2,1)} custom-call(s32[1]{0:T(128)} %bitcast.2.odd_ref, bf16[4,72,512]{2,1,0:T(8,128)(2,1)S(1)} %get-tuple-element.39.mixed_ref, f32[256,512]{1,0:T(8,128)S(1)} %get-tuple-element.40.own_ref, bf16[3,72,512]{2,1,0:T(8,128)(2,1)S(1)} %collective-permute-done.2.far_ref, ...), custom_call_target="tpu_custom_call" | custom-call | flops 2000000000 | bytes 2000000 | tf_op jit(solution)/shard_map/pallas_call | solution.py:384
  (1 shorter events, 0.0 us)
Async XLA Ops:
  1.7 34.5 %copy-start.1 = (bf16[4,64,512]{2,1,0:T(8,128)(2,1)S(1)}, bf16[4,64,512]{2,1,0:T(8,128)(2,1)}, u32[]{:S(2)}) copy-start(bf16[4,64,512]{2,1,0:T(8,128)(2,1)} %field_ref.1) | copy-start | bytes 786436
  20.5 22.9 %all-to-all-start.1 = ((bf16[8,272,128]{2,1,0:T(8,128)(2,1)}), bf16[8,272,128]{2,1,0:T(8,128)(2,1)S(1)}, u32[]{:S(2)}, u32[]{:S(2)}) async-start(bf16[8,272,128]{2,1,0:T(8,128)(2,1)} %shard_map.65), calls=%async_computation.1 | async-start | bytes 1114112 | tf_op jit(solution)/shard_map/all_to_all | solution.py:345
  27.3 15.2 %collective-permute-start = (bf16[32,512]{1,0:T(8,128)(2,1)S(1)}, bf16[32,512]{1,0:T(8,128)(2,1)S(1)}, u32[]{:S(2)}, u32[]{:S(2)}) collective-permute-start(bf16[32,512]{1,0:T(8,128)(2,1)S(1)} %get-tuple-element.32), channel_id=1, source_target_pairs={{1,2},{3,4},{5,6},{7,8},{9,10},{11,12},{13,14},{15,16},{17,18},{19... | collective-permute-start | bytes 98312 | tf_op jit(solution)/shard_map/ppermute | solution.py:347
  34.3 8.2 %collective-permute-start.1 = (bf16[32,512]{1,0:T(8,128)(2,1)S(1)}, bf16[32,512]{1,0:T(8,128)(2,1)S(1)}, u32[]{:S(2)}, u32[]{:S(2)}) collective-permute-start(bf16[32,512]{1,0:T(8,128)(2,1)S(1)} %get-tuple-element.33), channel_id=1, source_target_pairs={{0,1},{2,3},{4,5},{6,7},{8,9},{10,11},{12,13},{14,15},{16,17},{18,... | collective-permute-start | bytes 98312 | tf_op jit(solution)/shard_map/ppermute | solution.py:346
  43.4 15.5 %all-to-all-start.3 = ((bf16[16,16,640]{2,1,0:T(8,128)(2,1)}), bf16[16,16,640]{2,1,0:T(8,128)(2,1)S(1)}, u32[]{:S(2)}, u32[]{:S(2)}) async-start(bf16[16,16,640]{2,1,0:T(8,128)(2,1)} %get-tuple-element.36), calls=%async_computation.3 | async-start | bytes 655360 | tf_op jit(solution)/shard_map/all_to_all | solution.py:361
  52.2 10.1 %copy-start = (bf16[512,1152]{1,0:T(8,128)(2,1)S(1)}, bf16[512,1152]{1,0:T(8,128)(2,1)}, u32[]{:S(2)}) copy-start(bf16[512,1152]{1,0:T(8,128)(2,1)} %w_ref.2) | copy-start | bytes 3538948
  58.9 10.9 %all-to-all-start.2 = ((bf16[4,72,256]{2,1,0:T(8,128)(2,1)}), bf16[4,72,256]{2,1,0:T(8,128)(2,1)S(1)}, u32[]{:S(2)}, u32[]{:S(2)}) async-start(bf16[4,72,256]{2,1,0:T(8,128)(2,1)} %shard_map.68), calls=%async_computation.2 | async-start | bytes 294912 | tf_op jit(solution)/shard_map/all_to_all | solution.py:365
  62.3 18.9 %copy-start.2 = (bf16[512,512]{1,0:T(8,128)(2,1)S(1)}, bf16[512,512]{1,0:T(8,128)(2,1)}, u32[]{:S(2)}) copy-start(bf16[512,512]{1,0:T(8,128)(2,1)} %w_ref.3) | copy-start | bytes 1572868
  81.2 6.8 %copy-start.3 = (f32[7,7,512]{2,1,0:T(8,128)S(1)}, f32[7,7,512]{2,1,0:T(8,128)}, u32[]{:S(2)}) copy-start(f32[7,7,512]{2,1,0:T(8,128)} %param.9) | copy-start | bytes 301060
  81.9 9.4 %collective-permute-start.2 = (bf16[3,72,512]{2,1,0:T(8,128)(2,1)S(1)}, bf16[3,72,512]{2,1,0:T(8,128)(2,1)S(1)}, u32[]{:S(2)}, u32[]{:S(2)}) collective-permute-start(bf16[3,72,512]{2,1,0:T(8,128)(2,1)S(1)} %get-tuple-element.41), channel_id=1, source_target_pairs={{32,64},{96,128},{160,192},{224,256},{288,320},{352,384},{416,448}... | collective-permute-start | bytes 663560 | tf_op jit(solution)/shard_map/ppermute | solution.py:375
  86.0 5.3 %collective-permute-start.3 = (bf16[3,72,512]{2,1,0:T(8,128)(2,1)S(1)}, bf16[3,72,512]{2,1,0:T(8,128)(2,1)S(1)}, u32[]{:S(2)}, u32[]{:S(2)}) collective-permute-start(bf16[3,72,512]{2,1,0:T(8,128)(2,1)S(1)} %get-tuple-element.42), channel_id=1, source_target_pairs={{0,32},{64,96},{128,160},{192,224},{256,288},{320,352},{384,416},{... | collective-permute-start | bytes 663560 | tf_op jit(solution)/shard_map/ppermute | solution.py:374

commit v14 on v13

--- a/solution.py
+++ b/solution.py
@@ -335,6 +335,8 @@
         ],
     )(side, in_hbm(field), in_hbm(w_qkv))
     row = lax.all_to_all(row, "lon", 0, 0, axis_index_groups=along_z)
+    outer = lax.ppermute(outer, "lon", outer_pairs)
+    row, outer = lax.optimization_barrier((row, outer))
     slots = call(
         spread_kernel,
         shape(YS, KEYS, 128),
@@ -344,7 +346,6 @@
     )(row)
     slots = lax.all_to_all(slots, "lon", 0, 0, axis_index_groups=along_y)
     inner = lax.ppermute(inner, "lon", inner_pairs)
-    outer = lax.ppermute(outer, "lon", outer_pairs)
     merid, merid_edges = call(
         merid_own_kernel, (shape(LAT, MCELLS, MLANES), shape(2, MCELLS, MLANES)), 300_000_000
     )(field)

time: 94.8 us -> 98 us (1.034)
  blocking collectives: 29.2 us -> 11.7 us
  starting transfers between devices: 33.8 us -> 49.2 us
  waiting for transfers between devices: 15.1 us -> 19.7 us
    all_to_all x1 -> x0, blocking collectives: 17.9 us -> none  [per_device(): row = lax.all_to_all(row, 'lon', 0, 0, axis_index_groups=along_z)]
    all_to_all x0 -> x1, starting transfers between devices: none -> 10.2 us  [per_device(): row = lax.all_to_all(row, 'lon', 0, 0, axis_index_groups=along_z)]
    all_to_all x1, waiting for transfers between devices: 0.01 us -> 7.98 us  [per_device(): slots = lax.all_to_all(slots, 'lon', 0, 0, axis_index_groups=along_y)]
    ppermute x1, waiting for transfers between devices: 5.01 us -> 1.64 us  [per_device(): outer = lax.ppermute(outer, 'lon', outer_pairs)]
    ppermute x1, starting transfers between devices: 1.92 us -> 5.25 us  [per_device(): inner = lax.ppermute(inner, 'lon', inner_pairs)]
    ppermute x1, starting transfers between devices: 6.95 us -> 8.37 us  [per_device(): outer = lax.ppermute(outer, 'lon', outer_pairs)]
    all_to_all x1, starting transfers between devices: 3.34 us -> 4.57 us  [per_device(): zonal = lax.all_to_all(zonal, 'lon', 0, 0, axis_index_groups=along_z)]
  transfers between devices with their start and end apart: 7 -> 8, of which waited for: 4 -> 6; matrix products, arithmetic and copies ran while one was open for 0% -> 0% of each run, Pallas kernels for 10% -> 10%
where the time goes in v14:
time: 98 us; the launch traced here: 97.3 us
  starting transfers between devices  49.2 us (50%)
  waiting for transfers between devices  19.7 us (20%)
  Pallas kernels  16.6 us (17%)
  blocking collectives  11.7 us (12%)
    all_to_all x1, blocking collectives, per_device(): merid = lax.all_to_all(merid, 'lat', 0, 0)  11.7 us
    all_to_all x1, starting transfers between devices, per_device(): row = lax.all_to_all(row, 'lon', 0, 0, axis_index_groups=along_z)  10.2 us
    all_to_all x1, starting transfers between devices, per_device(): merid = lax.all_to_all(merid, 'lat', 0, 0)  8.76 us
    ppermute x1, starting transfers between devices, per_device(): outer = lax.ppermute(outer, 'lon', outer_pairs)  8.37 us
    all_to_all x1, waiting for transfers between devices, per_device(): slots = lax.all_to_all(slots, 'lon', 0, 0, axis_index_groups=along_y)  7.98 us
    all_to_all x1, starting transfers between devices, per_device(): slots = lax.all_to_all(slots, 'lon', 0, 0, axis_index_groups=along_y)  6.1 us
    all_to_all x1, waiting for transfers between devices, per_device(): zonal = lax.all_to_all(zonal, 'lon', 0, 0, axis_index_groups=along_z)  5.42 us
    ppermute x1, starting transfers between devices, per_device(): inner = lax.ppermute(inner, 'lon', inner_pairs)  5.25 us
  transfers between devices with their start and end apart: 8, of which 6 were waited for; matrix products, arithmetic and copies ran while one was open for 0% of the time, Pallas kernels for 10%

profile of v14, /device:TPU:7, one launch (start us, length us, event | category | flops | bytes accessed | tf_op | source)
XLA Modules:
  0.0 97.3 jit_solution(4901422994375391385)
XLA Ops:
  0.0 2.3 %shard_map.64 = (bf16[4,64,384]{2,1,0:T(8,128)(2,1)}, bf16[32,512]{1,0:T(8,128)(2,1)S(1)}, bf16[32,512]{1,0:T(8,128)(2,1)S(1)}) custom-call(s32[1]{0:T(128)} %bitcast.1.side_ref, bf16[4,64,512]{2,1,0:T(8,128)(2,1)} %field_ref.1, bf16[512,1152]{1,0:T(8,128)(2,1)} %w_ref.2), custom_call_target="tpu_custom_call" | custom-call | flops 200000000 | bytes 2000000 | tf_op jit(solution)/shard_map/pallas_call | solution.py:325
  2.3 0.0 copy-start.1
  2.3 10.2 %all-to-all-start = ((bf16[4,64,384]{2,1,0:T(8,128)(2,1)}), bf16[4,64,384]{2,1,0:T(8,128)(2,1)S(1)}, u32[]{:S(2)}, u32[]{:S(2)}) async-start(bf16[4,64,384]{2,1,0:T(8,128)(2,1)} %get-tuple-element.31), calls=%async_computation | async-start | bytes 393216 | tf_op jit(solution)/shard_map/all_to_all | solution.py:337
  12.5 8.4 %collective-permute-start = (bf16[32,512]{1,0:T(8,128)(2,1)S(1)}, bf16[32,512]{1,0:T(8,128)(2,1)S(1)}, u32[]{:S(2)}, u32[]{:S(2)}) collective-permute-start(bf16[32,512]{1,0:T(8,128)(2,1)S(1)} %get-tuple-element.32), channel_id=1, source_target_pairs={{1,2},{3,4},{5,6},{7,8},{9,10},{11,12},{13,14},{15,16},{17,18},{19... | collective-permute-start | bytes 98312 | tf_op jit(solution)/shard_map/ppermute | solution.py:338
  20.9 1.6 %collective-permute-done.outer_ref = bf16[32,512]{1,0:T(8,128)(2,1)S(1)} collective-permute-done((bf16[32,512]{1,0:T(8,128)(2,1)S(1)}, bf16[32,512]{1,0:T(8,128)(2,1)S(1)}, u32[]{:S(2)}, u32[]{:S(2)}) %collective-permute-start) | collective-permute-done | bytes 32800 | tf_op jit(solution)/shard_map/ppermute | solution.py:338
  22.5 0.0 all-to-all-done.in_ref.own_ref
  22.5 0.9 shard_map.65
  23.5 6.1 %all-to-all-start.1 = ((bf16[8,272,128]{2,1,0:T(8,128)(2,1)}), bf16[8,272,128]{2,1,0:T(8,128)(2,1)S(1)}, u32[]{:S(2)}, u32[]{:S(2)}) async-start(bf16[8,272,128]{2,1,0:T(8,128)(2,1)} %shard_map.65), calls=%async_computation.1 | async-start | bytes 1114112 | tf_op jit(solution)/shard_map/all_to_all | solution.py:347
  29.6 5.2 %collective-permute-start.1 = (bf16[32,512]{1,0:T(8,128)(2,1)S(1)}, bf16[32,512]{1,0:T(8,128)(2,1)S(1)}, u32[]{:S(2)}, u32[]{:S(2)}) collective-permute-start(bf16[32,512]{1,0:T(8,128)(2,1)S(1)} %get-tuple-element.37), channel_id=1, source_target_pairs={{0,1},{2,3},{4,5},{6,7},{8,9},{10,11},{12,13},{14,15},{16,17},{18,... | collective-permute-start | bytes 98312 | tf_op jit(solution)/shard_map/ppermute | solution.py:348
  34.8 0.0 copy-done.1
  34.8 1.2 %shard_map.66 = (bf16[16,16,640]{2,1,0:T(8,128)(2,1)}, bf16[2,16,640]{2,1,0:T(8,128)(2,1)S(1)}) custom-call(bf16[4,64,512]{2,1,0:T(8,128)(2,1)S(1)} %copy-done.1), custom_call_target="tpu_custom_call" | custom-call | flops 300000000 | bytes 2000000 | tf_op jit(solution)/shard_map/pallas_call | solution.py:349
  36.1 0.2 collective-permute-done.1.inner_ref
  36.2 0.9 shard_map.67
  37.2 8.0 %all-to-all-done.1.all_ref = bf16[8,272,128]{2,1,0:T(8,128)(2,1)S(1)} async-done(((bf16[8,272,128]{2,1,0:T(8,128)(2,1)}), bf16[8,272,128]{2,1,0:T(8,128)(2,1)S(1)}, u32[]{:S(2)}, u32[]{:S(2)}) %all-to-all-start.1) | async-done | bytes 557088 | tf_op jit(solution)/shard_map/all_to_all | solution.py:347
  45.2 8.8 %all-to-all-start.3 = ((bf16[16,16,640]{2,1,0:T(8,128)(2,1)}), bf16[16,16,640]{2,1,0:T(8,128)(2,1)S(1)}, u32[]{:S(2)}, u32[]{:S(2)}) async-start(bf16[16,16,640]{2,1,0:T(8,128)(2,1)} %get-tuple-element.40), calls=%async_computation.3 | async-start | bytes 655360 | tf_op jit(solution)/shard_map/all_to_all | solution.py:362
  53.9 0.0 copy-start
  53.9 4.0 %shard_map.68 = bf16[4,72,256]{2,1,0:T(8,128)(2,1)} custom-call(s32[1]{0:T(128)} %bitcast.y_ref, bf16[4,64,384]{2,1,0:T(8,128)(2,1)S(1)} %all-to-all-done.in_ref.own_ref, bf16[8,272,128]{2,1,0:T(8,128)(2,1)S(1)} %all-to-all-done.1.all_ref), custom_call_target="tpu_custom_call" | custom-call | flops 4000000000 | bytes 2000000 | tf_op jit(solution)/shard_map/pallas_call | solution.py:363
  58.0 2.7 %all-to-all-done.3.in_ref = bf16[16,16,640]{2,1,0:T(8,128)(2,1)S(1)} async-done(((bf16[16,16,640]{2,1,0:T(8,128)(2,1)}), bf16[16,16,640]{2,1,0:T(8,128)(2,1)S(1)}, u32[]{:S(2)}, u32[]{:S(2)}) %all-to-all-start.3) | async-done | bytes 327712 | tf_op jit(solution)/shard_map/all_to_all | solution.py:362
  60.7 4.6 %all-to-all-start.2 = ((bf16[4,72,256]{2,1,0:T(8,128)(2,1)}), bf16[4,72,256]{2,1,0:T(8,128)(2,1)S(1)}, u32[]{:S(2)}, u32[]{:S(2)}) async-start(bf16[4,72,256]{2,1,0:T(8,128)(2,1)} %shard_map.68), calls=%async_computation.2 | async-start | bytes 294912 | tf_op jit(solution)/shard_map/all_to_all | solution.py:366
  65.2 0.0 copy-done
  65.2 0.0 copy-start.2
  65.3 2.0 %shard_map.69 = bf16[16,40,128]{2,1,0:T(8,128)(2,1)S(1)} custom-call(bf16[16,16,640]{2,1,0:T(8,128)(2,1)S(1)} %all-to-all-done.3.in_ref, bf16[512,1152]{1,0:T(8,128)(2,1)S(1)} %copy-done), custom_call_target="tpu_custom_call" | custom-call | flops 1000000000 | bytes 2000000 | tf_op jit(solution)/shard_map/pallas_call | solution.py:367
  67.2 5.4 %all-to-all-done.2.zonal_ref = bf16[4,72,256]{2,1,0:T(8,128)(2,1)S(1)} async-done(((bf16[4,72,256]{2,1,0:T(8,128)(2,1)}), bf16[4,72,256]{2,1,0:T(8,128)(2,1)S(1)}, u32[]{:S(2)}, u32[]{:S(2)}) %all-to-all-start.2) | async-done | bytes 147488 | tf_op jit(solution)/shard_map/all_to_all | solution.py:366
  72.6 11.7 %all_to_all.25.merid_ref = bf16[16,40,128]{2,1,0:T(8,128)(2,1)S(1)} all-to-all(bf16[16,40,128]{2,1,0:T(8,128)(2,1)S(1)} %shard_map.69), channel_id=1, replica_groups=mesh['lat'=16,'lon'=32] {'lat'}, dimensions={0} | all-to-all | bytes 327680 | tf_op jit(solution)/shard_map/all_to_all | solution.py:368
  84.3 0.0 copy-done.2
  84.3 0.0 copy-start.3
  84.3 0.8 shard_map.70
  85.1 4.1 %collective-permute-start.2 = (bf16[3,72,512]{2,1,0:T(8,128)(2,1)S(1)}, bf16[3,72,512]{2,1,0:T(8,128)(2,1)S(1)}, u32[]{:S(2)}, u32[]{:S(2)}) collective-permute-start(bf16[3,72,512]{2,1,0:T(8,128)(2,1)S(1)} %get-tuple-element.45), channel_id=1, source_target_pairs={{32,64},{96,128},{160,192},{224,256},{288,320},{352,384},{416,448}... | collective-permute-start | bytes 663560 | tf_op jit(solution)/shard_map/ppermute | solution.py:376
  89.2 1.9 %collective-permute-start.3 = (bf16[3,72,512]{2,1,0:T(8,128)(2,1)S(1)}, bf16[3,72,512]{2,1,0:T(8,128)(2,1)S(1)}, u32[]{:S(2)}, u32[]{:S(2)}) collective-permute-start(bf16[3,72,512]{2,1,0:T(8,128)(2,1)S(1)} %get-tuple-element.46), channel_id=1, source_target_pairs={{0,32},{64,96},{128,160},{192,224},{256,288},{320,352},{384,416},{... | collective-permute-start | bytes 663560 | tf_op jit(solution)/shard_map/ppermute | solution.py:375
  91.1 0.0 copy-done.3
  91.2 1.6 %shard_map.71 = (f32[256,512]{1,0:T(8,128)S(1)}, bf16[512,1024]{1,0:T(8,128)(2,1)S(1)}, bf16[1024,512]{1,0:T(8,128)(2,1)S(1)}) custom-call(bf16[4,72,512]{2,1,0:T(8,128)(2,1)S(1)} %get-tuple-element.43.mixed_ref, f32[49,512]{1,0:T(8,128)S(1)} %reshape.15.conv_ref, bf16[512,1024]{1,0:T(8,128)(2,1)} %w_in_hbm.1, bf16[1024,512]{1,0:T(8,128)(2,1)} %w_back_hbm.1), custom_call_target="tpu_custom_call" | custom-call | flops 1000000000 | bytes 2000000 | tf_op jit(solution)/shard_map/pallas_call | solution.py:378
  92.7 1.7 %collective-permute-done.2.far_ref = bf16[3,72,512]{2,1,0:T(8,128)(2,1)S(1)} collective-permute-done((bf16[3,72,512]{2,1,0:T(8,128)(2,1)S(1)}, bf16[3,72,512]{2,1,0:T(8,128)(2,1)S(1)}, u32[]{:S(2)}, u32[]{:S(2)}) %collective-permute-start.2) | collective-permute-done | bytes 221216 | tf_op jit(solution)/shard_map/ppermute | solution.py:376
  94.4 0.0 collective-permute-done.3.near_ref
  94.5 2.9 %shard_map.72 = bf16[4,64,512]{2,1,0:T(8,128)(2,1)} custom-call(s32[1]{0:T(128)} %bitcast.2.odd_ref, bf16[4,72,512]{2,1,0:T(8,128)(2,1)S(1)} %get-tuple-element.43.mixed_ref, f32[256,512]{1,0:T(8,128)S(1)} %get-tuple-element.44.own_ref, bf16[3,72,512]{2,1,0:T(8,128)(2,1)S(1)} %collective-permute-done.2.far_ref, ...), custom_call_target="tpu_custom_call" | custom-call | flops 2000000000 | bytes 2000000 | tf_op jit(solution)/shard_map/pallas_call | solution.py:385
  (1 shorter events, 0.0 us)
Async XLA Ops:
  2.3 32.5 %copy-start.1 = (bf16[4,64,512]{2,1,0:T(8,128)(2,1)S(1)}, bf16[4,64,512]{2,1,0:T(8,128)(2,1)}, u32[]{:S(2)}) copy-start(bf16[4,64,512]{2,1,0:T(8,128)(2,1)} %field_ref.1) | copy-start | bytes 786436
  2.3 20.2 %all-to-all-start = ((bf16[4,64,384]{2,1,0:T(8,128)(2,1)}), bf16[4,64,384]{2,1,0:T(8,128)(2,1)S(1)}, u32[]{:S(2)}, u32[]{:S(2)}) async-start(bf16[4,64,384]{2,1,0:T(8,128)(2,1)} %get-tuple-element.31), calls=%async_computation | async-start | bytes 393216 | tf_op jit(solution)/shard_map/all_to_all | solution.py:337
  12.5 10.0 %collective-permute-start = (bf16[32,512]{1,0:T(8,128)(2,1)S(1)}, bf16[32,512]{1,0:T(8,128)(2,1)S(1)}, u32[]{:S(2)}, u32[]{:S(2)}) collective-permute-start(bf16[32,512]{1,0:T(8,128)(2,1)S(1)} %get-tuple-element.32), channel_id=1, source_target_pairs={{1,2},{3,4},{5,6},{7,8},{9,10},{11,12},{13,14},{15,16},{17,18},{19... | collective-permute-start | bytes 98312 | tf_op jit(solution)/shard_map/ppermute | solution.py:338
  23.5 21.7 %all-to-all-start.1 = ((bf16[8,272,128]{2,1,0:T(8,128)(2,1)}), bf16[8,272,128]{2,1,0:T(8,128)(2,1)S(1)}, u32[]{:S(2)}, u32[]{:S(2)}) async-start(bf16[8,272,128]{2,1,0:T(8,128)(2,1)} %shard_map.65), calls=%async_computation.1 | async-start | bytes 1114112 | tf_op jit(solution)/shard_map/all_to_all | solution.py:347
  29.6 6.7 %collective-permute-start.1 = (bf16[32,512]{1,0:T(8,128)(2,1)S(1)}, bf16[32,512]{1,0:T(8,128)(2,1)S(1)}, u32[]{:S(2)}, u32[]{:S(2)}) collective-permute-start(bf16[32,512]{1,0:T(8,128)(2,1)S(1)} %get-tuple-element.37), channel_id=1, source_target_pairs={{0,1},{2,3},{4,5},{6,7},{8,9},{10,11},{12,13},{14,15},{16,17},{18,... | collective-permute-start | bytes 98312 | tf_op jit(solution)/shard_map/ppermute | solution.py:348
  45.2 15.5 %all-to-all-start.3 = ((bf16[16,16,640]{2,1,0:T(8,128)(2,1)}), bf16[16,16,640]{2,1,0:T(8,128)(2,1)S(1)}, u32[]{:S(2)}, u32[]{:S(2)}) async-start(bf16[16,16,640]{2,1,0:T(8,128)(2,1)} %get-tuple-element.40), calls=%async_computation.3 | async-start | bytes 655360 | tf_op jit(solution)/shard_map/all_to_all | solution.py:362
  53.9 11.3 %copy-start = (bf16[512,1152]{1,0:T(8,128)(2,1)S(1)}, bf16[512,1152]{1,0:T(8,128)(2,1)}, u32[]{:S(2)}) copy-start(bf16[512,1152]{1,0:T(8,128)(2,1)} %w_ref.2) | copy-start | bytes 3538948
  60.7 12.0 %all-to-all-start.2 = ((bf16[4,72,256]{2,1,0:T(8,128)(2,1)}), bf16[4,72,256]{2,1,0:T(8,128)(2,1)S(1)}, u32[]{:S(2)}, u32[]{:S(2)}) async-start(bf16[4,72,256]{2,1,0:T(8,128)(2,1)} %shard_map.68), calls=%async_computation.2 | async-start | bytes 294912 | tf_op jit(solution)/shard_map/all_to_all | solution.py:366
  65.2 19.1 %copy-start.2 = (bf16[512,512]{1,0:T(8,128)(2,1)S(1)}, bf16[512,512]{1,0:T(8,128)(2,1)}, u32[]{:S(2)}) copy-start(bf16[512,512]{1,0:T(8,128)(2,1)} %w_ref.3) | copy-start | bytes 1572868
  84.3 6.8 %copy-start.3 = (f32[7,7,512]{2,1,0:T(8,128)S(1)}, f32[7,7,512]{2,1,0:T(8,128)}, u32[]{:S(2)}) copy-start(f32[7,7,512]{2,1,0:T(8,128)} %param.9) | copy-start | bytes 301060
  85.1 9.4 %collective-permute-start.2 = (bf16[3,72,512]{2,1,0:T(8,128)(2,1)S(1)}, bf16[3,72,512]{2,1,0:T(8,128)(2,1)S(1)}, u32[]{:S(2)}, u32[]{:S(2)}) collective-permute-start(bf16[3,72,512]{2,1,0:T(8,128)(2,1)S(1)} %get-tuple-element.45), channel_id=1, source_target_pairs={{32,64},{96,128},{160,192},{224,256},{288,320},{352,384},{416,448}... | collective-permute-start | bytes 663560 | tf_op jit(solution)/shard_map/ppermute | solution.py:376
  89.2 5.3 %collective-permute-start.3 = (bf16[3,72,512]{2,1,0:T(8,128)(2,1)S(1)}, bf16[3,72,512]{2,1,0:T(8,128)(2,1)S(1)}, u32[]{:S(2)}, u32[]{:S(2)}) collective-permute-start(bf16[3,72,512]{2,1,0:T(8,128)(2,1)S(1)} %get-tuple-element.46), channel_id=1, source_target_pairs={{0,32},{64,96},{128,160},{192,224},{256,288},{320,352},{384,416},{... | collective-permute-start | bytes 663560 | tf_op jit(solution)/shard_map/ppermute | solution.py:375

commit v15 on v13

--- a/solution.py
+++ b/solution.py
@@ -291,22 +291,24 @@
     odd_ref, mixed_ref, own_ref, far_ref, near_ref, conv_ref, w_in_ref, w_back_ref, out_ref, conv_out
 ):
     odd = odd_ref[0] == 1
-    for lane in range(0, C, 128):
-        lanes = slice(lane, lane + 128)
-        rows = {}
-        for i in range(3):
-            far, near = far_ref[i, :, lanes].astype(F32), near_ref[i, :, lanes].astype(F32)
-            rows[i] = jnp.where(odd, near, far)
-            rows[7 + i] = jnp.where(odd, far, near)
-        for r in range(R):
-            here = (slice(r * W, (r + 1) * W), lanes)
-            conv_out[here] = own_ref[here] + conv_part(rows, conv_ref, lanes, r)
-    normed = layer_norm(conv_out[...]).astype(BF)
-    hidden = mm(normed, w_in_ref[...])
-    hidden = 0.5 * hidden * (1.0 + lax.erf(hidden * math.sqrt(0.5)))
-    back = mm(hidden.astype(BF), w_back_ref[...])
-    own = mixed_ref[...].astype(F32)[:, E // 2 : E // 2 + W].reshape(CELLS, C)
-    out_ref[...] = (own + back).astype(BF).reshape(R, W, C)
+    for half in range(0, R, 2):
+        cells = slice(half * W, (half + 2) * W)
+        for lane in range(0, C, 128):
+            lanes = slice(lane, lane + 128)
+            rows = {}
+            for i in range(3):
+                far, near = far_ref[i, :, lanes].astype(F32), near_ref[i, :, lanes].astype(F32)
+                rows[i] = jnp.where(odd, near, far)
+                rows[7 + i] = jnp.where(odd, far, near)
+            for r in range(half, half + 2):
+                here = (slice(r * W, (r + 1) * W), lanes)
+                conv_out[here] = own_ref[here] + conv_part(rows, conv_ref, lanes, r)
+        normed = layer_norm(conv_out[cells]).astype(BF)
+        hidden = mm(normed, w_in_ref[...])
+        hidden = 0.5 * hidden * (1.0 + lax.erf(hidden * math.sqrt(0.5)))
+        back = mm(hidden.astype(BF), w_back_ref[...])
+        own = mixed_ref[half : half + 2].astype(F32)[:, E // 2 : E // 2 + W].reshape(2 * W, C)
+        out_ref[half : half + 2] = (own + back).astype(BF).reshape(2, W, C)
 
 
 def per_device(field, w_qkv, w_out, conv_w, w_in, w_back):

time: 94.8 us -> 94.9 us (level)
  no operation moved by 1% of the time
where the time goes in v15:
time: 94.9 us; the launch traced here: 94.3 us
  starting transfers between devices  33.8 us (36%)
  blocking collectives  29.2 us (31%)
  Pallas kernels  16 us (17%)
  waiting for transfers between devices  15.1 us (16%)
    all_to_all x1, blocking collectives, per_device(): row = lax.all_to_all(row, 'lon', 0, 0, axis_index_groups=along_z)  17.9 us
    all_to_all x1, blocking collectives, per_device(): merid = lax.all_to_all(merid, 'lat', 0, 0)  11.3 us
    all_to_all x1, starting transfers between devices, per_device(): merid = lax.all_to_all(merid, 'lat', 0, 0)  8.76 us
    ppermute x1, starting transfers between devices, per_device(): outer = lax.ppermute(outer, 'lon', outer_pairs)  6.95 us
    all_to_all x1, starting transfers between devices, per_device(): slots = lax.all_to_all(slots, 'lon', 0, 0, axis_index_groups=along_y)  6.83 us
    all_to_all x1, waiting for transfers between devices, per_device(): zonal = lax.all_to_all(zonal, 'lon', 0, 0, axis_index_groups=along_z)  5.59 us
    ppermute x1, waiting for transfers between devices, per_device(): outer = lax.ppermute(outer, 'lon', outer_pairs)  5.01 us
    ppermute x1, starting transfers between devices, per_device(): far = lax.ppermute(far, 'lat', far_pairs)  4.09 us
  transfers between devices with their start and end apart: 7, of which 4 were waited for; matrix products, arithmetic and copies ran while one was open for 0% of the time, Pallas kernels for 10%

profile of v15, /device:TPU:7, one launch (start us, length us, event | category | flops | bytes accessed | tf_op | source)
XLA Modules:
  0.0 94.3 jit_solution(16872878652453865464)
XLA Ops:
  0.0 1.7 %shard_map.64 = (bf16[4,64,384]{2,1,0:T(8,128)(2,1)S(1)}, bf16[32,512]{1,0:T(8,128)(2,1)S(1)}, bf16[32,512]{1,0:T(8,128)(2,1)S(1)}) custom-call(s32[1]{0:T(128)} %bitcast.1.side_ref, bf16[4,64,512]{2,1,0:T(8,128)(2,1)} %field_ref.1, bf16[512,1152]{1,0:T(8,128)(2,1)} %w_ref.2), custom_call_target="tpu_custom_call" | custom-call | flops 200000000 | bytes 2000000 | tf_op jit(solution)/shard_map/pallas_call | solution.py:327
  1.7 0.0 copy-start.1
  1.7 17.9 %all_to_all.25.in_ref.own_ref = bf16[4,64,384]{2,1,0:T(8,128)(2,1)S(1)} all-to-all(bf16[4,64,384]{2,1,0:T(8,128)(2,1)S(1)} %get-tuple-element.29), channel_id=1, replica_groups={{0,1,2,3},{4,5,6,7},{8,9,10,11},{12,13,14,15},{16,17,18,19},{20,21,22,2..., dimensions={0} | all-to-all | bytes 393216 | tf_op jit(solution)/shard_map/all_to_all | solution.py:339
  19.6 0.9 shard_map.65
  20.5 6.8 %all-to-all-start.1 = ((bf16[8,272,128]{2,1,0:T(8,128)(2,1)}), bf16[8,272,128]{2,1,0:T(8,128)(2,1)S(1)}, u32[]{:S(2)}, u32[]{:S(2)}) async-start(bf16[8,272,128]{2,1,0:T(8,128)(2,1)} %shard_map.65), calls=%async_computation.1 | async-start | bytes 1114112 | tf_op jit(solution)/shard_map/all_to_all | solution.py:347
  27.3 7.0 %collective-permute-start = (bf16[32,512]{1,0:T(8,128)(2,1)S(1)}, bf16[32,512]{1,0:T(8,128)(2,1)S(1)}, u32[]{:S(2)}, u32[]{:S(2)}) collective-permute-start(bf16[32,512]{1,0:T(8,128)(2,1)S(1)} %get-tuple-element.32), channel_id=1, source_target_pairs={{1,2},{3,4},{5,6},{7,8},{9,10},{11,12},{13,14},{15,16},{17,18},{19... | collective-permute-start | bytes 98312 | tf_op jit(solution)/shard_map/ppermute | solution.py:349
  34.3 1.9 %collective-permute-start.1 = (bf16[32,512]{1,0:T(8,128)(2,1)S(1)}, bf16[32,512]{1,0:T(8,128)(2,1)S(1)}, u32[]{:S(2)}, u32[]{:S(2)}) collective-permute-start(bf16[32,512]{1,0:T(8,128)(2,1)S(1)} %get-tuple-element.33), channel_id=1, source_target_pairs={{0,1},{2,3},{4,5},{6,7},{8,9},{10,11},{12,13},{14,15},{16,17},{18,... | collective-permute-start | bytes 98312 | tf_op jit(solution)/shard_map/ppermute | solution.py:348
  36.2 0.0 copy-done.1
  36.2 1.2 %shard_map.66 = (bf16[16,16,640]{2,1,0:T(8,128)(2,1)}, bf16[2,16,640]{2,1,0:T(8,128)(2,1)S(1)}) custom-call(bf16[4,64,512]{2,1,0:T(8,128)(2,1)S(1)} %copy-done.1), custom_call_target="tpu_custom_call" | custom-call | flops 300000000 | bytes 2000000 | tf_op jit(solution)/shard_map/pallas_call | solution.py:350
  37.5 5.0 %collective-permute-done.outer_ref = bf16[32,512]{1,0:T(8,128)(2,1)S(1)} collective-permute-done((bf16[32,512]{1,0:T(8,128)(2,1)S(1)}, bf16[32,512]{1,0:T(8,128)(2,1)S(1)}, u32[]{:S(2)}, u32[]{:S(2)}) %collective-permute-start) | collective-permute-done | bytes 32800 | tf_op jit(solution)/shard_map/ppermute | solution.py:349
  42.5 0.0 collective-permute-done.1.inner_ref
  42.5 0.9 %shard_map.67 = (bf16[16,16,640]{2,1,0:T(8,128)(2,1)}, bf16[32,512]{1,0:T(8,128)(2,1)S(1)}, bf16[32,512]{1,0:T(8,128)(2,1)S(1)}) custom-call(s32[1]{0:T(128)} %bitcast.1.side_ref, bf16[16,16,640]{2,1,0:T(8,128)(2,1)} %get-tuple-element.30.slots_hbm, bf16[2,16,640]{2,1,0:T(8,128)(2,1)S(1)} %get-tuple-element.31.edge_ref, ...), custom_call_target="tpu_custom_call", output_to_operand_aliasing={{0}: (1, {})} | custom-call | flops 10000000 | bytes 2000000 | tf_op jit(solution)/shard_map/pallas_call | solution.py:353
  43.4 0.0 all-to-all-done.1.all_ref
  43.4 8.8 %all-to-all-start.3 = ((bf16[16,16,640]{2,1,0:T(8,128)(2,1)}), bf16[16,16,640]{2,1,0:T(8,128)(2,1)S(1)}, u32[]{:S(2)}, u32[]{:S(2)}) async-start(bf16[16,16,640]{2,1,0:T(8,128)(2,1)} %get-tuple-element.36), calls=%async_computation.3 | async-start | bytes 655360 | tf_op jit(solution)/shard_map/all_to_all | solution.py:363
  52.2 0.0 copy-start
  52.2 4.0 %shard_map.68 = bf16[4,72,256]{2,1,0:T(8,128)(2,1)} custom-call(s32[1]{0:T(128)} %bitcast.y_ref, bf16[4,64,384]{2,1,0:T(8,128)(2,1)S(1)} %all_to_all.25.in_ref.own_ref, bf16[8,272,128]{2,1,0:T(8,128)(2,1)S(1)} %all-to-all-done.1.all_ref), custom_call_target="tpu_custom_call" | custom-call | flops 4000000000 | bytes 2000000 | tf_op jit(solution)/shard_map/pallas_call | solution.py:364
  56.2 2.7 %all-to-all-done.3.in_ref = bf16[16,16,640]{2,1,0:T(8,128)(2,1)S(1)} async-done(((bf16[16,16,640]{2,1,0:T(8,128)(2,1)}), bf16[16,16,640]{2,1,0:T(8,128)(2,1)S(1)}, u32[]{:S(2)}, u32[]{:S(2)}) %all-to-all-start.3) | async-done | bytes 327712 | tf_op jit(solution)/shard_map/all_to_all | solution.py:363
  58.9 3.3 %all-to-all-start.2 = ((bf16[4,72,256]{2,1,0:T(8,128)(2,1)}), bf16[4,72,256]{2,1,0:T(8,128)(2,1)S(1)}, u32[]{:S(2)}, u32[]{:S(2)}) async-start(bf16[4,72,256]{2,1,0:T(8,128)(2,1)} %shard_map.68), calls=%async_computation.2 | async-start | bytes 294912 | tf_op jit(solution)/shard_map/all_to_all | solution.py:367
  62.3 0.0 copy-done
  62.3 0.0 copy-start.2
  62.3 2.0 %shard_map.69 = bf16[16,40,128]{2,1,0:T(8,128)(2,1)S(1)} custom-call(bf16[16,16,640]{2,1,0:T(8,128)(2,1)S(1)} %all-to-all-done.3.in_ref, bf16[512,1152]{1,0:T(8,128)(2,1)S(1)} %copy-done), custom_call_target="tpu_custom_call" | custom-call | flops 1000000000 | bytes 2000000 | tf_op jit(solution)/shard_map/pallas_call | solution.py:368
  64.3 5.6 %all-to-all-done.2.zonal_ref = bf16[4,72,256]{2,1,0:T(8,128)(2,1)S(1)} async-done(((bf16[4,72,256]{2,1,0:T(8,128)(2,1)}), bf16[4,72,256]{2,1,0:T(8,128)(2,1)S(1)}, u32[]{:S(2)}, u32[]{:S(2)}) %all-to-all-start.2) | async-done | bytes 147488 | tf_op jit(solution)/shard_map/all_to_all | solution.py:367
  69.9 11.3 %all_to_all.26.merid_ref = bf16[16,40,128]{2,1,0:T(8,128)(2,1)S(1)} all-to-all(bf16[16,40,128]{2,1,0:T(8,128)(2,1)S(1)} %shard_map.69), channel_id=1, replica_groups=mesh['lat'=16,'lon'=32] {'lat'}, dimensions={0} | all-to-all | bytes 327680 | tf_op jit(solution)/shard_map/all_to_all | solution.py:369
  81.2 0.0 copy-done.2
  81.2 0.0 copy-start.3
  81.2 0.8 shard_map.70
  81.9 4.1 %collective-permute-start.2 = (bf16[3,72,512]{2,1,0:T(8,128)(2,1)S(1)}, bf16[3,72,512]{2,1,0:T(8,128)(2,1)S(1)}, u32[]{:S(2)}, u32[]{:S(2)}) collective-permute-start(bf16[3,72,512]{2,1,0:T(8,128)(2,1)S(1)} %get-tuple-element.41), channel_id=1, source_target_pairs={{32,64},{96,128},{160,192},{224,256},{288,320},{352,384},{416,448}... | collective-permute-start | bytes 663560 | tf_op jit(solution)/shard_map/ppermute | solution.py:377
  86.0 1.9 %collective-permute-start.3 = (bf16[3,72,512]{2,1,0:T(8,128)(2,1)S(1)}, bf16[3,72,512]{2,1,0:T(8,128)(2,1)S(1)}, u32[]{:S(2)}, u32[]{:S(2)}) collective-permute-start(bf16[3,72,512]{2,1,0:T(8,128)(2,1)S(1)} %get-tuple-element.42), channel_id=1, source_target_pairs={{0,32},{64,96},{128,160},{192,224},{256,288},{320,352},{384,416},{... | collective-permute-start | bytes 663560 | tf_op jit(solution)/shard_map/ppermute | solution.py:376
  88.0 0.0 copy-done.3
  88.0 1.6 %shard_map.71 = (f32[256,512]{1,0:T(8,128)S(1)}, bf16[512,1024]{1,0:T(8,128)(2,1)S(1)}, bf16[1024,512]{1,0:T(8,128)(2,1)S(1)}) custom-call(bf16[4,72,512]{2,1,0:T(8,128)(2,1)S(1)} %get-tuple-element.39.mixed_ref, f32[49,512]{1,0:T(8,128)S(1)} %reshape.15.conv_ref, bf16[512,1024]{1,0:T(8,128)(2,1)} %w_in_hbm.1, bf16[1024,512]{1,0:T(8,128)(2,1)} %w_back_hbm.1), custom_call_target="tpu_custom_call" | custom-call | flops 1000000000 | bytes 2000000 | tf_op jit(solution)/shard_map/pallas_call | solution.py:379
  89.6 1.7 %collective-permute-done.2.far_ref = bf16[3,72,512]{2,1,0:T(8,128)(2,1)S(1)} collective-permute-done((bf16[3,72,512]{2,1,0:T(8,128)(2,1)S(1)}, bf16[3,72,512]{2,1,0:T(8,128)(2,1)S(1)}, u32[]{:S(2)}, u32[]{:S(2)}) %collective-permute-start.2) | collective-permute-done | bytes 221216 | tf_op jit(solution)/shard_map/ppermute | solution.py:377
  91.3 0.0 collective-permute-done.3.near_ref
  91.3 3.0 %shard_map.72 = bf16[4,64,512]{2,1,0:T(8,128)(2,1)} custom-call(s32[1]{0:T(128)} %bitcast.2.odd_ref, bf16[4,72,512]{2,1,0:T(8,128)(2,1)S(1)} %get-tuple-element.39.mixed_ref, f32[256,512]{1,0:T(8,128)S(1)} %get-tuple-element.40.own_ref, bf16[3,72,512]{2,1,0:T(8,128)(2,1)S(1)} %collective-permute-done.2.far_ref, ...), custom_call_target="tpu_custom_call" | custom-call | flops 2000000000 | bytes 2000000 | tf_op jit(solution)/shard_map/pallas_call | solution.py:386
  (1 shorter events, 0.0 us)
Async XLA Ops:
  1.7 34.5 %copy-start.1 = (bf16[4,64,512]{2,1,0:T(8,128)(2,1)S(1)}, bf16[4,64,512]{2,1,0:T(8,128)(2,1)}, u32[]{:S(2)}) copy-start(bf16[4,64,512]{2,1,0:T(8,128)(2,1)} %field_ref.1) | copy-start | bytes 786436
  20.5 22.9 %all-to-all-start.1 = ((bf16[8,272,128]{2,1,0:T(8,128)(2,1)}), bf16[8,272,128]{2,1,0:T(8,128)(2,1)S(1)}, u32[]{:S(2)}, u32[]{:S(2)}) async-start(bf16[8,272,128]{2,1,0:T(8,128)(2,1)} %shard_map.65), calls=%async_computation.1 | async-start | bytes 1114112 | tf_op jit(solution)/shard_map/all_to_all | solution.py:347
  27.3 15.2 %collective-permute-start = (bf16[32,512]{1,0:T(8,128)(2,1)S(1)}, bf16[32,512]{1,0:T(8,128)(2,1)S(1)}, u32[]{:S(2)}, u32[]{:S(2)}) collective-permute-start(bf16[32,512]{1,0:T(8,128)(2,1)S(1)} %get-tuple-element.32), channel_id=1, source_target_pairs={{1,2},{3,4},{5,6},{7,8},{9,10},{11,12},{13,14},{15,16},{17,18},{19... | collective-permute-start | bytes 98312 | tf_op jit(solution)/shard_map/ppermute | solution.py:349
  34.3 8.2 %collective-permute-start.1 = (bf16[32,512]{1,0:T(8,128)(2,1)S(1)}, bf16[32,512]{1,0:T(8,128)(2,1)S(1)}, u32[]{:S(2)}, u32[]{:S(2)}) collective-permute-start(bf16[32,512]{1,0:T(8,128)(2,1)S(1)} %get-tuple-element.33), channel_id=1, source_target_pairs={{0,1},{2,3},{4,5},{6,7},{8,9},{10,11},{12,13},{14,15},{16,17},{18,... | collective-permute-start | bytes 98312 | tf_op jit(solution)/shard_map/ppermute | solution.py:348
  43.4 15.5 %all-to-all-start.3 = ((bf16[16,16,640]{2,1,0:T(8,128)(2,1)}), bf16[16,16,640]{2,1,0:T(8,128)(2,1)S(1)}, u32[]{:S(2)}, u32[]{:S(2)}) async-start(bf16[16,16,640]{2,1,0:T(8,128)(2,1)} %get-tuple-element.36), calls=%async_computation.3 | async-start | bytes 655360 | tf_op jit(solution)/shard_map/all_to_all | solution.py:363
  52.2 10.1 %copy-start = (bf16[512,1152]{1,0:T(8,128)(2,1)S(1)}, bf16[512,1152]{1,0:T(8,128)(2,1)}, u32[]{:S(2)}) copy-start(bf16[512,1152]{1,0:T(8,128)(2,1)} %w_ref.2) | copy-start | bytes 3538948
  58.9 10.9 %all-to-all-start.2 = ((bf16[4,72,256]{2,1,0:T(8,128)(2,1)}), bf16[4,72,256]{2,1,0:T(8,128)(2,1)S(1)}, u32[]{:S(2)}, u32[]{:S(2)}) async-start(bf16[4,72,256]{2,1,0:T(8,128)(2,1)} %shard_map.68), calls=%async_computation.2 | async-start | bytes 294912 | tf_op jit(solution)/shard_map/all_to_all | solution.py:367
  62.3 18.9 %copy-start.2 = (bf16[512,512]{1,0:T(8,128)(2,1)S(1)}, bf16[512,512]{1,0:T(8,128)(2,1)}, u32[]{:S(2)}) copy-start(bf16[512,512]{1,0:T(8,128)(2,1)} %w_ref.3) | copy-start | bytes 1572868
  81.2 6.8 %copy-start.3 = (f32[7,7,512]{2,1,0:T(8,128)S(1)}, f32[7,7,512]{2,1,0:T(8,128)}, u32[]{:S(2)}) copy-start(f32[7,7,512]{2,1,0:T(8,128)} %param.9) | copy-start | bytes 301060
  81.9 9.4 %collective-permute-start.2 = (bf16[3,72,512]{2,1,0:T(8,128)(2,1)S(1)}, bf16[3,72,512]{2,1,0:T(8,128)(2,1)S(1)}, u32[]{:S(2)}, u32[]{:S(2)}) collective-permute-start(bf16[3,72,512]{2,1,0:T(8,128)(2,1)S(1)} %get-tuple-element.41), channel_id=1, source_target_pairs={{32,64},{96,128},{160,192},{224,256},{288,320},{352,384},{416,448}... | collective-permute-start | bytes 663560 | tf_op jit(solution)/shard_map/ppermute | solution.py:377
  86.0 5.3 %collective-permute-start.3 = (bf16[3,72,512]{2,1,0:T(8,128)(2,1)S(1)}, bf16[3,72,512]{2,1,0:T(8,128)(2,1)S(1)}, u32[]{:S(2)}, u32[]{:S(2)}) collective-permute-start(bf16[3,72,512]{2,1,0:T(8,128)(2,1)S(1)} %get-tuple-element.42), channel_id=1, source_target_pairs={{0,32},{64,96},{128,160},{192,224},{256,288},{320,352},{384,416},{... | collective-permute-start | bytes 663560 | tf_op jit(solution)/shard_map/ppermute | solution.py:376

commit v16 on v13

--- a/solution.py
+++ b/solution.py
@@ -14,6 +14,7 @@
 R = 4
 W = 64
 CELLS = R * W
+ECELLS = 16
 E = 8
 WIDE = W + E
 MWIDE = W + 2 * E
@@ -88,8 +89,10 @@
     loads[0].wait()
     field = field_ref[...].astype(F32)
     side = side_ref[0] == 1
-    first = field[:, 0:E].reshape(R * E, C)
-    last = field[:, W - E : W].reshape(R * E, C)
+    i, u = iota((2 * ECELLS, CELLS), 0), iota((2 * ECELLS, CELLS), 1)
+    select = one_hot(u == ((i >> 2) & 3) * W + (i & 3) + jnp.where(i < ECELLS, 0, W - 4))
+    edges = mm(select, field_ref[...].reshape(CELLS, C))
+    first, last = edges[0:ECELLS], edges[ECELLS:]
     outer_ref[...] = jnp.where(side, last, first).astype(BF)
     inner_ref[...] = jnp.where(side, first, last).astype(BF)
     normed = layer_norm(field.reshape(CELLS, C)).astype(BF)
@@ -176,6 +179,10 @@
     side = side_ref[0] == 1
     outer, inner = outer_ref[...].astype(F32), inner_ref[...].astype(F32)
     halos = (jnp.where(side, inner, outer), jnp.where(side, outer, inner))
+    i, u = iota((R * E, ECELLS), 0), iota((R * E, ECELLS), 1)
+    cell = ((i >> 3) << 2) + (i & 3)
+    fits = [one_hot((u == cell) & (((i >> 2) & 1) == 1 - n)) for n in range(2)]
+    halos = [mm(fit, halo.astype(BF)) for fit, halo in zip(fits, halos)]
     copies = []
     for n, (m, ref, halo) in enumerate(zip(EDGES, (left_ref, right_ref), halos)):
         ref[...] = halo.astype(BF)
@@ -324,7 +331,7 @@
     field, y, side, odd = lax.optimization_barrier((field, y, side, odd))
     row, outer, inner = call(
         zonal_project_kernel,
-        (shape(R, W, 384), shape(R * E, C), shape(R * E, C)),
+        (shape(R, W, 384), shape(ECELLS, C), shape(ECELLS, C)),
         200_000_000,
         in_specs=[SMEM, ANY, ANY],
         scratch_shapes=[

time: 94.8 us -> 94.8 us (level)
    ppermute x1, waiting for transfers between devices: 5.01 us -> 3.65 us  [per_device(): outer = lax.ppermute(outer, 'lon', outer_pairs)]
  transfers between devices with their start and end apart: 7 -> 7, of which waited for: 4 -> 5; matrix products, arithmetic and copies ran while one was open for 0% -> 0% of each run, Pallas kernels for 10% -> 10%
where the time goes in v16:
time: 94.8 us; the launch traced here: 94.2 us
  starting transfers between devices  34.4 us (36%)
  blocking collectives  29.2 us (31%)
  Pallas kernels  16.1 us (17%)
  waiting for transfers between devices  14.3 us (15%)
    all_to_all x1, blocking collectives, per_device(): row = lax.all_to_all(row, 'lon', 0, 0, axis_index_groups=along_z)  17.9 us
    all_to_all x1, blocking collectives, per_device(): merid = lax.all_to_all(merid, 'lat', 0, 0)  11.3 us
    all_to_all x1, starting transfers between devices, per_device(): merid = lax.all_to_all(merid, 'lat', 0, 0)  9.36 us
    ppermute x1, starting transfers between devices, per_device(): outer = lax.ppermute(outer, 'lon', outer_pairs)  6.95 us
    all_to_all x1, starting transfers between devices, per_device(): slots = lax.all_to_all(slots, 'lon', 0, 0, axis_index_groups=along_y)  6.84 us
    all_to_all x1, waiting for transfers between devices, per_device(): zonal = lax.all_to_all(zonal, 'lon', 0, 0, axis_index_groups=along_z)  5.59 us
    ppermute x1, starting transfers between devices, per_device(): far = lax.ppermute(far, 'lat', far_pairs)  4.09 us
    pallas_call x1, Pallas kernels, per_device(): call(zonal_kernel, shape(ZS, WIDE, 256), 4000000000, vmem=24, in_specs=[S...  4.02 us
  transfers between devices with their start and end apart: 7, of which 5 were waited for; matrix products, arithmetic and copies ran while one was open for 0% of the time, Pallas kernels for 10%

profile of v16, /device:TPU:7, one launch (start us, length us, event | category | flops | bytes accessed | tf_op | source)
XLA Modules:
  0.0 94.2 jit_solution(1081567890824756978)
XLA Ops:
  0.0 1.7 %shard_map.64 = (bf16[4,64,384]{2,1,0:T(8,128)(2,1)S(1)}, bf16[16,512]{1,0:T(8,128)(2,1)S(1)}, bf16[16,512]{1,0:T(8,128)(2,1)S(1)}) custom-call(s32[1]{0:T(128)} %bitcast.1.side_ref, bf16[4,64,512]{2,1,0:T(8,128)(2,1)} %field_ref.1, bf16[512,1152]{1,0:T(8,128)(2,1)} %w_ref.2), custom_call_target="tpu_custom_call" | custom-call | flops 200000000 | bytes 2000000 | tf_op jit(solution)/shard_map/pallas_call | solution.py:332
  1.7 0.0 copy-start.1
  1.7 17.9 %all_to_all.25.in_ref.own_ref = bf16[4,64,384]{2,1,0:T(8,128)(2,1)S(1)} all-to-all(bf16[4,64,384]{2,1,0:T(8,128)(2,1)S(1)} %get-tuple-element.29), channel_id=1, replica_groups={{0,1,2,3},{4,5,6,7},{8,9,10,11},{12,13,14,15},{16,17,18,19},{20,21,22,2..., dimensions={0} | all-to-all | bytes 393216 | tf_op jit(solution)/shard_map/all_to_all | solution.py:344
  19.6 0.9 shard_map.65
  20.5 6.8 %all-to-all-start.1 = ((bf16[8,272,128]{2,1,0:T(8,128)(2,1)}), bf16[8,272,128]{2,1,0:T(8,128)(2,1)S(1)}, u32[]{:S(2)}, u32[]{:S(2)}) async-start(bf16[8,272,128]{2,1,0:T(8,128)(2,1)} %shard_map.65), calls=%async_computation.1 | async-start | bytes 1114112 | tf_op jit(solution)/shard_map/all_to_all | solution.py:352
  27.3 7.0 %collective-permute-start = (bf16[16,512]{1,0:T(8,128)(2,1)S(1)}, bf16[16,512]{1,0:T(8,128)(2,1)S(1)}, u32[]{:S(2)}, u32[]{:S(2)}) collective-permute-start(bf16[16,512]{1,0:T(8,128)(2,1)S(1)} %get-tuple-element.32), channel_id=1, source_target_pairs={{1,2},{3,4},{5,6},{7,8},{9,10},{11,12},{13,14},{15,16},{17,18},{19... | collective-permute-start | bytes 49160 | tf_op jit(solution)/shard_map/ppermute | solution.py:354
  34.3 1.9 %collective-permute-start.1 = (bf16[16,512]{1,0:T(8,128)(2,1)S(1)}, bf16[16,512]{1,0:T(8,128)(2,1)S(1)}, u32[]{:S(2)}, u32[]{:S(2)}) collective-permute-start(bf16[16,512]{1,0:T(8,128)(2,1)S(1)} %get-tuple-element.33), channel_id=1, source_target_pairs={{0,1},{2,3},{4,5},{6,7},{8,9},{10,11},{12,13},{14,15},{16,17},{18,... | collective-permute-start | bytes 49160 | tf_op jit(solution)/shard_map/ppermute | solution.py:353
  36.2 0.0 copy-done.1
  36.2 1.2 %shard_map.66 = (bf16[16,16,640]{2,1,0:T(8,128)(2,1)}, bf16[2,16,640]{2,1,0:T(8,128)(2,1)S(1)}) custom-call(bf16[4,64,512]{2,1,0:T(8,128)(2,1)S(1)} %copy-done.1), custom_call_target="tpu_custom_call" | custom-call | flops 300000000 | bytes 2000000 | tf_op jit(solution)/shard_map/pallas_call | solution.py:355
  37.5 3.7 %collective-permute-done.outer_ref = bf16[16,512]{1,0:T(8,128)(2,1)S(1)} collective-permute-done((bf16[16,512]{1,0:T(8,128)(2,1)S(1)}, bf16[16,512]{1,0:T(8,128)(2,1)S(1)}, u32[]{:S(2)}, u32[]{:S(2)}) %collective-permute-start) | collective-permute-done | bytes 16416 | tf_op jit(solution)/shard_map/ppermute | solution.py:354
  41.1 0.0 collective-permute-done.1.inner_ref
  41.1 1.1 %shard_map.67 = (bf16[16,16,640]{2,1,0:T(8,128)(2,1)}, bf16[32,512]{1,0:T(8,128)(2,1)S(1)}, bf16[32,512]{1,0:T(8,128)(2,1)S(1)}) custom-call(s32[1]{0:T(128)} %bitcast.1.side_ref, bf16[16,16,640]{2,1,0:T(8,128)(2,1)} %get-tuple-element.30.slots_hbm, bf16[2,16,640]{2,1,0:T(8,128)(2,1)S(1)} %get-tuple-element.31.edge_ref, ...), custom_call_target="tpu_custom_call", output_to_operand_aliasing={{0}: (1, {})} | custom-call | flops 10000000 | bytes 2000000 | tf_op jit(solution)/shard_map/pallas_call | solution.py:358
  42.2 0.6 all-to-all-done.1.all_ref
  42.8 9.4 %all-to-all-start.3 = ((bf16[16,16,640]{2,1,0:T(8,128)(2,1)}), bf16[16,16,640]{2,1,0:T(8,128)(2,1)S(1)}, u32[]{:S(2)}, u32[]{:S(2)}) async-start(bf16[16,16,640]{2,1,0:T(8,128)(2,1)} %get-tuple-element.36), calls=%async_computation.3 | async-start | bytes 655360 | tf_op jit(solution)/shard_map/all_to_all | solution.py:368
  52.2 0.0 copy-start
  52.2 4.0 %shard_map.68 = bf16[4,72,256]{2,1,0:T(8,128)(2,1)} custom-call(s32[1]{0:T(128)} %bitcast.y_ref, bf16[4,64,384]{2,1,0:T(8,128)(2,1)S(1)} %all_to_all.25.in_ref.own_ref, bf16[8,272,128]{2,1,0:T(8,128)(2,1)S(1)} %all-to-all-done.1.all_ref), custom_call_target="tpu_custom_call" | custom-call | flops 4000000000 | bytes 2000000 | tf_op jit(solution)/shard_map/pallas_call | solution.py:369
  56.2 2.7 %all-to-all-done.3.in_ref = bf16[16,16,640]{2,1,0:T(8,128)(2,1)S(1)} async-done(((bf16[16,16,640]{2,1,0:T(8,128)(2,1)}), bf16[16,16,640]{2,1,0:T(8,128)(2,1)S(1)}, u32[]{:S(2)}, u32[]{:S(2)}) %all-to-all-start.3) | async-done | bytes 327712 | tf_op jit(solution)/shard_map/all_to_all | solution.py:368
  58.9 3.3 %all-to-all-start.2 = ((bf16[4,72,256]{2,1,0:T(8,128)(2,1)}), bf16[4,72,256]{2,1,0:T(8,128)(2,1)S(1)}, u32[]{:S(2)}, u32[]{:S(2)}) async-start(bf16[4,72,256]{2,1,0:T(8,128)(2,1)} %shard_map.68), calls=%async_computation.2 | async-start | bytes 294912 | tf_op jit(solution)/shard_map/all_to_all | solution.py:372
  62.3 0.0 copy-done
  62.3 0.0 copy-start.2
  62.3 2.0 %shard_map.69 = bf16[16,40,128]{2,1,0:T(8,128)(2,1)S(1)} custom-call(bf16[16,16,640]{2,1,0:T(8,128)(2,1)S(1)} %all-to-all-done.3.in_ref, bf16[512,1152]{1,0:T(8,128)(2,1)S(1)} %copy-done), custom_call_target="tpu_custom_call" | custom-call | flops 1000000000 | bytes 2000000 | tf_op jit(solution)/shard_map/pallas_call | solution.py:373
  64.3 5.6 %all-to-all-done.2.zonal_ref = bf16[4,72,256]{2,1,0:T(8,128)(2,1)S(1)} async-done(((bf16[4,72,256]{2,1,0:T(8,128)(2,1)}), bf16[4,72,256]{2,1,0:T(8,128)(2,1)S(1)}, u32[]{:S(2)}, u32[]{:S(2)}) %all-to-all-start.2) | async-done | bytes 147488 | tf_op jit(solution)/shard_map/all_to_all | solution.py:372
  69.9 11.3 %all_to_all.26.merid_ref = bf16[16,40,128]{2,1,0:T(8,128)(2,1)S(1)} all-to-all(bf16[16,40,128]{2,1,0:T(8,128)(2,1)S(1)} %shard_map.69), channel_id=1, replica_groups=mesh['lat'=16,'lon'=32] {'lat'}, dimensions={0} | all-to-all | bytes 327680 | tf_op jit(solution)/shard_map/all_to_all | solution.py:374
  81.2 0.0 copy-done.2
  81.2 0.0 copy-start.3
  81.2 0.8 shard_map.70
  81.9 4.1 %collective-permute-start.2 = (bf16[3,72,512]{2,1,0:T(8,128)(2,1)S(1)}, bf16[3,72,512]{2,1,0:T(8,128)(2,1)S(1)}, u32[]{:S(2)}, u32[]{:S(2)}) collective-permute-start(bf16[3,72,512]{2,1,0:T(8,128)(2,1)S(1)} %get-tuple-element.41), channel_id=1, source_target_pairs={{32,64},{96,128},{160,192},{224,256},{288,320},{352,384},{416,448}... | collective-permute-start | bytes 663560 | tf_op jit(solution)/shard_map/ppermute | solution.py:382
  86.0 1.9 %collective-permute-start.3 = (bf16[3,72,512]{2,1,0:T(8,128)(2,1)S(1)}, bf16[3,72,512]{2,1,0:T(8,128)(2,1)S(1)}, u32[]{:S(2)}, u32[]{:S(2)}) collective-permute-start(bf16[3,72,512]{2,1,0:T(8,128)(2,1)S(1)} %get-tuple-element.42), channel_id=1, source_target_pairs={{0,32},{64,96},{128,160},{192,224},{256,288},{320,352},{384,416},{... | collective-permute-start | bytes 663560 | tf_op jit(solution)/shard_map/ppermute | solution.py:381
  88.0 0.0 copy-done.3
  88.0 1.6 %shard_map.71 = (f32[256,512]{1,0:T(8,128)S(1)}, bf16[512,1024]{1,0:T(8,128)(2,1)S(1)}, bf16[1024,512]{1,0:T(8,128)(2,1)S(1)}) custom-call(bf16[4,72,512]{2,1,0:T(8,128)(2,1)S(1)} %get-tuple-element.39.mixed_ref, f32[49,512]{1,0:T(8,128)S(1)} %reshape.15.conv_ref, bf16[512,1024]{1,0:T(8,128)(2,1)} %w_in_hbm.1, bf16[1024,512]{1,0:T(8,128)(2,1)} %w_back_hbm.1), custom_call_target="tpu_custom_call" | custom-call | flops 1000000000 | bytes 2000000 | tf_op jit(solution)/shard_map/pallas_call | solution.py:384
  89.6 1.7 %collective-permute-done.2.far_ref = bf16[3,72,512]{2,1,0:T(8,128)(2,1)S(1)} collective-permute-done((bf16[3,72,512]{2,1,0:T(8,128)(2,1)S(1)}, bf16[3,72,512]{2,1,0:T(8,128)(2,1)S(1)}, u32[]{:S(2)}, u32[]{:S(2)}) %collective-permute-start.2) | collective-permute-done | bytes 221216 | tf_op jit(solution)/shard_map/ppermute | solution.py:382
  91.3 0.0 collective-permute-done.3.near_ref
  91.3 2.9 %shard_map.72 = bf16[4,64,512]{2,1,0:T(8,128)(2,1)} custom-call(s32[1]{0:T(128)} %bitcast.2.odd_ref, bf16[4,72,512]{2,1,0:T(8,128)(2,1)S(1)} %get-tuple-element.39.mixed_ref, f32[256,512]{1,0:T(8,128)S(1)} %get-tuple-element.40.own_ref, bf16[3,72,512]{2,1,0:T(8,128)(2,1)S(1)} %collective-permute-done.2.far_ref, ...), custom_call_target="tpu_custom_call" | custom-call | flops 2000000000 | bytes 2000000 | tf_op jit(solution)/shard_map/pallas_call | solution.py:391
  (1 shorter events, 0.0 us)
Async XLA Ops:
  1.7 34.5 %copy-start.1 = (bf16[4,64,512]{2,1,0:T(8,128)(2,1)S(1)}, bf16[4,64,512]{2,1,0:T(8,128)(2,1)}, u32[]{:S(2)}) copy-start(bf16[4,64,512]{2,1,0:T(8,128)(2,1)} %field_ref.1) | copy-start | bytes 786436
  20.5 22.4 %all-to-all-start.1 = ((bf16[8,272,128]{2,1,0:T(8,128)(2,1)}), bf16[8,272,128]{2,1,0:T(8,128)(2,1)S(1)}, u32[]{:S(2)}, u32[]{:S(2)}) async-start(bf16[8,272,128]{2,1,0:T(8,128)(2,1)} %shard_map.65), calls=%async_computation.1 | async-start | bytes 1114112 | tf_op jit(solution)/shard_map/all_to_all | solution.py:352
  27.3 13.8 %collective-permute-start = (bf16[16,512]{1,0:T(8,128)(2,1)S(1)}, bf16[16,512]{1,0:T(8,128)(2,1)S(1)}, u32[]{:S(2)}, u32[]{:S(2)}) collective-permute-start(bf16[16,512]{1,0:T(8,128)(2,1)S(1)} %get-tuple-element.32), channel_id=1, source_target_pairs={{1,2},{3,4},{5,6},{7,8},{9,10},{11,12},{13,14},{15,16},{17,18},{19... | collective-permute-start | bytes 49160 | tf_op jit(solution)/shard_map/ppermute | solution.py:354
  34.3 6.8 %collective-permute-start.1 = (bf16[16,512]{1,0:T(8,128)(2,1)S(1)}, bf16[16,512]{1,0:T(8,128)(2,1)S(1)}, u32[]{:S(2)}, u32[]{:S(2)}) collective-permute-start(bf16[16,512]{1,0:T(8,128)(2,1)S(1)} %get-tuple-element.33), channel_id=1, source_target_pairs={{0,1},{2,3},{4,5},{6,7},{8,9},{10,11},{12,13},{14,15},{16,17},{18,... | collective-permute-start | bytes 49160 | tf_op jit(solution)/shard_map/ppermute | solution.py:353
  42.8 16.1 %all-to-all-start.3 = ((bf16[16,16,640]{2,1,0:T(8,128)(2,1)}), bf16[16,16,640]{2,1,0:T(8,128)(2,1)S(1)}, u32[]{:S(2)}, u32[]{:S(2)}) async-start(bf16[16,16,640]{2,1,0:T(8,128)(2,1)} %get-tuple-element.36), calls=%async_computation.3 | async-start | bytes 655360 | tf_op jit(solution)/shard_map/all_to_all | solution.py:368
  52.2 10.1 %copy-start = (bf16[512,1152]{1,0:T(8,128)(2,1)S(1)}, bf16[512,1152]{1,0:T(8,128)(2,1)}, u32[]{:S(2)}) copy-start(bf16[512,1152]{1,0:T(8,128)(2,1)} %w_ref.2) | copy-start | bytes 3538948
  58.9 10.9 %all-to-all-start.2 = ((bf16[4,72,256]{2,1,0:T(8,128)(2,1)}), bf16[4,72,256]{2,1,0:T(8,128)(2,1)S(1)}, u32[]{:S(2)}, u32[]{:S(2)}) async-start(bf16[4,72,256]{2,1,0:T(8,128)(2,1)} %shard_map.68), calls=%async_computation.2 | async-start | bytes 294912 | tf_op jit(solution)/shard_map/all_to_all | solution.py:372
  62.3 18.9 %copy-start.2 = (bf16[512,512]{1,0:T(8,128)(2,1)S(1)}, bf16[512,512]{1,0:T(8,128)(2,1)}, u32[]{:S(2)}) copy-start(bf16[512,512]{1,0:T(8,128)(2,1)} %w_ref.3) | copy-start | bytes 1572868
  81.2 6.8 %copy-start.3 = (f32[7,7,512]{2,1,0:T(8,128)S(1)}, f32[7,7,512]{2,1,0:T(8,128)}, u32[]{:S(2)}) copy-start(f32[7,7,512]{2,1,0:T(8,128)} %param.9) | copy-start | bytes 301060
  81.9 9.4 %collective-permute-start.2 = (bf16[3,72,512]{2,1,0:T(8,128)(2,1)S(1)}, bf16[3,72,512]{2,1,0:T(8,128)(2,1)S(1)}, u32[]{:S(2)}, u32[]{:S(2)}) collective-permute-start(bf16[3,72,512]{2,1,0:T(8,128)(2,1)S(1)} %get-tuple-element.41), channel_id=1, source_target_pairs={{32,64},{96,128},{160,192},{224,256},{288,320},{352,384},{416,448}... | collective-permute-start | bytes 663560 | tf_op jit(solution)/shard_map/ppermute | solution.py:382
  86.0 5.3 %collective-permute-start.3 = (bf16[3,72,512]{2,1,0:T(8,128)(2,1)S(1)}, bf16[3,72,512]{2,1,0:T(8,128)(2,1)S(1)}, u32[]{:S(2)}, u32[]{:S(2)}) collective-permute-start(bf16[3,72,512]{2,1,0:T(8,128)(2,1)S(1)} %get-tuple-element.42), channel_id=1, source_target_pairs={{0,32},{64,96},{128,160},{192,224},{256,288},{320,352},{384,416},{... | collective-permute-start | bytes 663560 | tf_op jit(solution)/shard_map/ppermute | solution.py:381

commit v17 on v16

--- a/solution.py
+++ b/solution.py
@@ -179,18 +179,18 @@
     side = side_ref[0] == 1
     outer, inner = outer_ref[...].astype(F32), inner_ref[...].astype(F32)
     halos = (jnp.where(side, inner, outer), jnp.where(side, outer, inner))
+    copies = []
+    for n, (m, halo) in enumerate(zip(EDGES, halos)):
+        normed = layer_norm(halo).astype(BF)
+        first = jnp.full((MCELLS, ECELLS), m * MC - (E // 2 if n == 0 else W + E), jnp.int32)
+        done_ref[n] = (edge_ref[n].astype(F32) + merid_slots(normed, first, 4, 4)).astype(BF)
+        copies.append(pltpu.make_async_copy(done_ref.at[n], out_hbm.at[m], sems.at[n]))
+        copies[n].start()
     i, u = iota((R * E, ECELLS), 0), iota((R * E, ECELLS), 1)
     cell = ((i >> 3) << 2) + (i & 3)
-    fits = [one_hot((u == cell) & (((i >> 2) & 1) == 1 - n)) for n in range(2)]
-    halos = [mm(fit, halo.astype(BF)) for fit, halo in zip(fits, halos)]
-    copies = []
-    for n, (m, ref, halo) in enumerate(zip(EDGES, (left_ref, right_ref), halos)):
-        ref[...] = halo.astype(BF)
-        normed = layer_norm(halo).astype(BF)
-        first = jnp.full((MCELLS, R * E), m * MC - n * (W + E), jnp.int32)
-        done_ref[n] = (edge_ref[n].astype(F32) + merid_slots(normed, first, E, E)).astype(BF)
-        copies.append(pltpu.make_async_copy(done_ref.at[n], out_hbm.at[m], sems.at[n]))
-        copies[n].start()
+    for n, (ref, halo) in enumerate(zip((left_ref, right_ref), halos)):
+        fit = one_hot((u == cell) & (((i >> 2) & 1) == 1 - n))
+        ref[...] = mm(fit, halo.astype(BF)).astype(BF)
     for copy in copies:
         copy.wait()
 

time: 94.8 us -> 94.8 us (level)
  no operation moved by 1% of the time
where the time goes in v17:
time: 94.8 us; the launch traced here: 94.2 us
  starting transfers between devices  34.4 us (36%)
  blocking collectives  29.2 us (31%)
  Pallas kernels  15.9 us (17%)
  waiting for transfers between devices  14.5 us (15%)
    all_to_all x1, blocking collectives, per_device(): row = lax.all_to_all(row, 'lon', 0, 0, axis_index_groups=along_z)  17.9 us
    all_to_all x1, blocking collectives, per_device(): merid = lax.all_to_all(merid, 'lat', 0, 0)  11.3 us
    all_to_all x1, starting transfers between devices, per_device(): merid = lax.all_to_all(merid, 'lat', 0, 0)  9.36 us
    ppermute x1, starting transfers between devices, per_device(): outer = lax.ppermute(outer, 'lon', outer_pairs)  6.95 us
    all_to_all x1, starting transfers between devices, per_device(): slots = lax.all_to_all(slots, 'lon', 0, 0, axis_index_groups=along_y)  6.84 us
    all_to_all x1, waiting for transfers between devices, per_device(): zonal = lax.all_to_all(zonal, 'lon', 0, 0, axis_index_groups=along_z)  5.59 us
    ppermute x1, starting transfers between devices, per_device(): far = lax.ppermute(far, 'lat', far_pairs)  4.09 us
    pallas_call x1, Pallas kernels, per_device(): call(zonal_kernel, shape(ZS, WIDE, 256), 4000000000, vmem=24, in_specs=[S...  4.02 us
  transfers between devices with their start and end apart: 7, of which 5 were waited for; matrix products, arithmetic and copies ran while one was open for 0% of the time, Pallas kernels for 10%

profile of v17, /device:TPU:7, one launch (start us, length us, event | category | flops | bytes accessed | tf_op | source)
XLA Modules:
  0.0 94.2 jit_solution(16206974569033851716)
XLA Ops:
  0.0 1.7 %shard_map.64 = (bf16[4,64,384]{2,1,0:T(8,128)(2,1)S(1)}, bf16[16,512]{1,0:T(8,128)(2,1)S(1)}, bf16[16,512]{1,0:T(8,128)(2,1)S(1)}) custom-call(s32[1]{0:T(128)} %bitcast.1.side_ref, bf16[4,64,512]{2,1,0:T(8,128)(2,1)} %field_ref.1, bf16[512,1152]{1,0:T(8,128)(2,1)} %w_ref.2), custom_call_target="tpu_custom_call" | custom-call | flops 200000000 | bytes 2000000 | tf_op jit(solution)/shard_map/pallas_call | solution.py:332
  1.7 0.0 copy-start.1
  1.7 17.9 %all_to_all.25.in_ref.own_ref = bf16[4,64,384]{2,1,0:T(8,128)(2,1)S(1)} all-to-all(bf16[4,64,384]{2,1,0:T(8,128)(2,1)S(1)} %get-tuple-element.29), channel_id=1, replica_groups={{0,1,2,3},{4,5,6,7},{8,9,10,11},{12,13,14,15},{16,17,18,19},{20,21,22,2..., dimensions={0} | all-to-all | bytes 393216 | tf_op jit(solution)/shard_map/all_to_all | solution.py:344
  19.6 0.9 shard_map.65
  20.5 6.8 %all-to-all-start.1 = ((bf16[8,272,128]{2,1,0:T(8,128)(2,1)}), bf16[8,272,128]{2,1,0:T(8,128)(2,1)S(1)}, u32[]{:S(2)}, u32[]{:S(2)}) async-start(bf16[8,272,128]{2,1,0:T(8,128)(2,1)} %shard_map.65), calls=%async_computation.1 | async-start | bytes 1114112 | tf_op jit(solution)/shard_map/all_to_all | solution.py:352
  27.3 7.0 %collective-permute-start = (bf16[16,512]{1,0:T(8,128)(2,1)S(1)}, bf16[16,512]{1,0:T(8,128)(2,1)S(1)}, u32[]{:S(2)}, u32[]{:S(2)}) collective-permute-start(bf16[16,512]{1,0:T(8,128)(2,1)S(1)} %get-tuple-element.32), channel_id=1, source_target_pairs={{1,2},{3,4},{5,6},{7,8},{9,10},{11,12},{13,14},{15,16},{17,18},{19... | collective-permute-start | bytes 49160 | tf_op jit(solution)/shard_map/ppermute | solution.py:354
  34.3 1.9 %collective-permute-start.1 = (bf16[16,512]{1,0:T(8,128)(2,1)S(1)}, bf16[16,512]{1,0:T(8,128)(2,1)S(1)}, u32[]{:S(2)}, u32[]{:S(2)}) collective-permute-start(bf16[16,512]{1,0:T(8,128)(2,1)S(1)} %get-tuple-element.33), channel_id=1, source_target_pairs={{0,1},{2,3},{4,5},{6,7},{8,9},{10,11},{12,13},{14,15},{16,17},{18,... | collective-permute-start | bytes 49160 | tf_op jit(solution)/shard_map/ppermute | solution.py:353
  36.2 0.0 copy-done.1
  36.2 1.2 %shard_map.66 = (bf16[16,16,640]{2,1,0:T(8,128)(2,1)}, bf16[2,16,640]{2,1,0:T(8,128)(2,1)S(1)}) custom-call(bf16[4,64,512]{2,1,0:T(8,128)(2,1)S(1)} %copy-done.1), custom_call_target="tpu_custom_call" | custom-call | flops 300000000 | bytes 2000000 | tf_op jit(solution)/shard_map/pallas_call | solution.py:355
  37.5 3.7 %collective-permute-done.outer_ref = bf16[16,512]{1,0:T(8,128)(2,1)S(1)} collective-permute-done((bf16[16,512]{1,0:T(8,128)(2,1)S(1)}, bf16[16,512]{1,0:T(8,128)(2,1)S(1)}, u32[]{:S(2)}, u32[]{:S(2)}) %collective-permute-start) | collective-permute-done | bytes 16416 | tf_op jit(solution)/shard_map/ppermute | solution.py:354
  41.1 0.0 collective-permute-done.1.inner_ref
  41.1 0.9 %shard_map.67 = (bf16[16,16,640]{2,1,0:T(8,128)(2,1)}, bf16[32,512]{1,0:T(8,128)(2,1)S(1)}, bf16[32,512]{1,0:T(8,128)(2,1)S(1)}) custom-call(s32[1]{0:T(128)} %bitcast.1.side_ref, bf16[16,16,640]{2,1,0:T(8,128)(2,1)} %get-tuple-element.30.slots_hbm, bf16[2,16,640]{2,1,0:T(8,128)(2,1)S(1)} %get-tuple-element.31.edge_ref, ...), custom_call_target="tpu_custom_call", output_to_operand_aliasing={{0}: (1, {})} | custom-call | flops 10000000 | bytes 2000000 | tf_op jit(solution)/shard_map/pallas_call | solution.py:358
  42.1 0.8 all-to-all-done.1.all_ref
  42.8 9.4 %all-to-all-start.3 = ((bf16[16,16,640]{2,1,0:T(8,128)(2,1)}), bf16[16,16,640]{2,1,0:T(8,128)(2,1)S(1)}, u32[]{:S(2)}, u32[]{:S(2)}) async-start(bf16[16,16,640]{2,1,0:T(8,128)(2,1)} %get-tuple-element.36), calls=%async_computation.3 | async-start | bytes 655360 | tf_op jit(solution)/shard_map/all_to_all | solution.py:368
  52.2 0.0 copy-start
  52.2 4.0 %shard_map.68 = bf16[4,72,256]{2,1,0:T(8,128)(2,1)} custom-call(s32[1]{0:T(128)} %bitcast.y_ref, bf16[4,64,384]{2,1,0:T(8,128)(2,1)S(1)} %all_to_all.25.in_ref.own_ref, bf16[8,272,128]{2,1,0:T(8,128)(2,1)S(1)} %all-to-all-done.1.all_ref), custom_call_target="tpu_custom_call" | custom-call | flops 4000000000 | bytes 2000000 | tf_op jit(solution)/shard_map/pallas_call | solution.py:369
  56.2 2.7 %all-to-all-done.3.in_ref = bf16[16,16,640]{2,1,0:T(8,128)(2,1)S(1)} async-done(((bf16[16,16,640]{2,1,0:T(8,128)(2,1)}), bf16[16,16,640]{2,1,0:T(8,128)(2,1)S(1)}, u32[]{:S(2)}, u32[]{:S(2)}) %all-to-all-start.3) | async-done | bytes 327712 | tf_op jit(solution)/shard_map/all_to_all | solution.py:368
  58.9 3.3 %all-to-all-start.2 = ((bf16[4,72,256]{2,1,0:T(8,128)(2,1)}), bf16[4,72,256]{2,1,0:T(8,128)(2,1)S(1)}, u32[]{:S(2)}, u32[]{:S(2)}) async-start(bf16[4,72,256]{2,1,0:T(8,128)(2,1)} %shard_map.68), calls=%async_computation.2 | async-start | bytes 294912 | tf_op jit(solution)/shard_map/all_to_all | solution.py:372
  62.3 0.0 copy-done
  62.3 0.0 copy-start.2
  62.3 2.0 %shard_map.69 = bf16[16,40,128]{2,1,0:T(8,128)(2,1)S(1)} custom-call(bf16[16,16,640]{2,1,0:T(8,128)(2,1)S(1)} %all-to-all-done.3.in_ref, bf16[512,1152]{1,0:T(8,128)(2,1)S(1)} %copy-done), custom_call_target="tpu_custom_call" | custom-call | flops 1000000000 | bytes 2000000 | tf_op jit(solution)/shard_map/pallas_call | solution.py:373
  64.3 5.6 %all-to-all-done.2.zonal_ref = bf16[4,72,256]{2,1,0:T(8,128)(2,1)S(1)} async-done(((bf16[4,72,256]{2,1,0:T(8,128)(2,1)}), bf16[4,72,256]{2,1,0:T(8,128)(2,1)S(1)}, u32[]{:S(2)}, u32[]{:S(2)}) %all-to-all-start.2) | async-done | bytes 147488 | tf_op jit(solution)/shard_map/all_to_all | solution.py:372
  69.9 11.3 %all_to_all.26.merid_ref = bf16[16,40,128]{2,1,0:T(8,128)(2,1)S(1)} all-to-all(bf16[16,40,128]{2,1,0:T(8,128)(2,1)S(1)} %shard_map.69), channel_id=1, replica_groups=mesh['lat'=16,'lon'=32] {'lat'}, dimensions={0} | all-to-all | bytes 327680 | tf_op jit(solution)/shard_map/all_to_all | solution.py:374
  81.2 0.0 copy-done.2
  81.2 0.0 copy-start.3
  81.2 0.8 shard_map.70
  81.9 4.1 %collective-permute-start.2 = (bf16[3,72,512]{2,1,0:T(8,128)(2,1)S(1)}, bf16[3,72,512]{2,1,0:T(8,128)(2,1)S(1)}, u32[]{:S(2)}, u32[]{:S(2)}) collective-permute-start(bf16[3,72,512]{2,1,0:T(8,128)(2,1)S(1)} %get-tuple-element.41), channel_id=1, source_target_pairs={{32,64},{96,128},{160,192},{224,256},{288,320},{352,384},{416,448}... | collective-permute-start | bytes 663560 | tf_op jit(solution)/shard_map/ppermute | solution.py:382
  86.0 1.9 %collective-permute-start.3 = (bf16[3,72,512]{2,1,0:T(8,128)(2,1)S(1)}, bf16[3,72,512]{2,1,0:T(8,128)(2,1)S(1)}, u32[]{:S(2)}, u32[]{:S(2)}) collective-permute-start(bf16[3,72,512]{2,1,0:T(8,128)(2,1)S(1)} %get-tuple-element.42), channel_id=1, source_target_pairs={{0,32},{64,96},{128,160},{192,224},{256,288},{320,352},{384,416},{... | collective-permute-start | bytes 663560 | tf_op jit(solution)/shard_map/ppermute | solution.py:381
  88.0 0.0 copy-done.3
  88.0 1.6 %shard_map.71 = (f32[256,512]{1,0:T(8,128)S(1)}, bf16[512,1024]{1,0:T(8,128)(2,1)S(1)}, bf16[1024,512]{1,0:T(8,128)(2,1)S(1)}) custom-call(bf16[4,72,512]{2,1,0:T(8,128)(2,1)S(1)} %get-tuple-element.39.mixed_ref, f32[49,512]{1,0:T(8,128)S(1)} %reshape.15.conv_ref, bf16[512,1024]{1,0:T(8,128)(2,1)} %w_in_hbm.1, bf16[1024,512]{1,0:T(8,128)(2,1)} %w_back_hbm.1), custom_call_target="tpu_custom_call" | custom-call | flops 1000000000 | bytes 2000000 | tf_op jit(solution)/shard_map/pallas_call | solution.py:384
  89.6 1.7 %collective-permute-done.2.far_ref = bf16[3,72,512]{2,1,0:T(8,128)(2,1)S(1)} collective-permute-done((bf16[3,72,512]{2,1,0:T(8,128)(2,1)S(1)}, bf16[3,72,512]{2,1,0:T(8,128)(2,1)S(1)}, u32[]{:S(2)}, u32[]{:S(2)}) %collective-permute-start.2) | collective-permute-done | bytes 221216 | tf_op jit(solution)/shard_map/ppermute | solution.py:382
  91.3 0.0 collective-permute-done.3.near_ref
  91.3 2.9 %shard_map.72 = bf16[4,64,512]{2,1,0:T(8,128)(2,1)} custom-call(s32[1]{0:T(128)} %bitcast.2.odd_ref, bf16[4,72,512]{2,1,0:T(8,128)(2,1)S(1)} %get-tuple-element.39.mixed_ref, f32[256,512]{1,0:T(8,128)S(1)} %get-tuple-element.40.own_ref, bf16[3,72,512]{2,1,0:T(8,128)(2,1)S(1)} %collective-permute-done.2.far_ref, ...), custom_call_target="tpu_custom_call" | custom-call | flops 2000000000 | bytes 2000000 | tf_op jit(solution)/shard_map/pallas_call | solution.py:391
  (1 shorter events, 0.0 us)
Async XLA Ops:
  1.7 34.5 %copy-start.1 = (bf16[4,64,512]{2,1,0:T(8,128)(2,1)S(1)}, bf16[4,64,512]{2,1,0:T(8,128)(2,1)}, u32[]{:S(2)}) copy-start(bf16[4,64,512]{2,1,0:T(8,128)(2,1)} %field_ref.1) | copy-start | bytes 786436
  20.5 22.4 %all-to-all-start.1 = ((bf16[8,272,128]{2,1,0:T(8,128)(2,1)}), bf16[8,272,128]{2,1,0:T(8,128)(2,1)S(1)}, u32[]{:S(2)}, u32[]{:S(2)}) async-start(bf16[8,272,128]{2,1,0:T(8,128)(2,1)} %shard_map.65), calls=%async_computation.1 | async-start | bytes 1114112 | tf_op jit(solution)/shard_map/all_to_all | solution.py:352
  27.3 13.8 %collective-permute-start = (bf16[16,512]{1,0:T(8,128)(2,1)S(1)}, bf16[16,512]{1,0:T(8,128)(2,1)S(1)}, u32[]{:S(2)}, u32[]{:S(2)}) collective-permute-start(bf16[16,512]{1,0:T(8,128)(2,1)S(1)} %get-tuple-element.32), channel_id=1, source_target_pairs={{1,2},{3,4},{5,6},{7,8},{9,10},{11,12},{13,14},{15,16},{17,18},{19... | collective-permute-start | bytes 49160 | tf_op jit(solution)/shard_map/ppermute | solution.py:354
  34.3 6.8 %collective-permute-start.1 = (bf16[16,512]{1,0:T(8,128)(2,1)S(1)}, bf16[16,512]{1,0:T(8,128)(2,1)S(1)}, u32[]{:S(2)}, u32[]{:S(2)}) collective-permute-start(bf16[16,512]{1,0:T(8,128)(2,1)S(1)} %get-tuple-element.33), channel_id=1, source_target_pairs={{0,1},{2,3},{4,5},{6,7},{8,9},{10,11},{12,13},{14,15},{16,17},{18,... | collective-permute-start | bytes 49160 | tf_op jit(solution)/shard_map/ppermute | solution.py:353
  42.8 16.1 %all-to-all-start.3 = ((bf16[16,16,640]{2,1,0:T(8,128)(2,1)}), bf16[16,16,640]{2,1,0:T(8,128)(2,1)S(1)}, u32[]{:S(2)}, u32[]{:S(2)}) async-start(bf16[16,16,640]{2,1,0:T(8,128)(2,1)} %get-tuple-element.36), calls=%async_computation.3 | async-start | bytes 655360 | tf_op jit(solution)/shard_map/all_to_all | solution.py:368
  52.2 10.1 %copy-start = (bf16[512,1152]{1,0:T(8,128)(2,1)S(1)}, bf16[512,1152]{1,0:T(8,128)(2,1)}, u32[]{:S(2)}) copy-start(bf16[512,1152]{1,0:T(8,128)(2,1)} %w_ref.2) | copy-start | bytes 3538948
  58.9 10.9 %all-to-all-start.2 = ((bf16[4,72,256]{2,1,0:T(8,128)(2,1)}), bf16[4,72,256]{2,1,0:T(8,128)(2,1)S(1)}, u32[]{:S(2)}, u32[]{:S(2)}) async-start(bf16[4,72,256]{2,1,0:T(8,128)(2,1)} %shard_map.68), calls=%async_computation.2 | async-start | bytes 294912 | tf_op jit(solution)/shard_map/all_to_all | solution.py:372
  62.3 18.9 %copy-start.2 = (bf16[512,512]{1,0:T(8,128)(2,1)S(1)}, bf16[512,512]{1,0:T(8,128)(2,1)}, u32[]{:S(2)}) copy-start(bf16[512,512]{1,0:T(8,128)(2,1)} %w_ref.3) | copy-start | bytes 1572868
  81.2 6.8 %copy-start.3 = (f32[7,7,512]{2,1,0:T(8,128)S(1)}, f32[7,7,512]{2,1,0:T(8,128)}, u32[]{:S(2)}) copy-start(f32[7,7,512]{2,1,0:T(8,128)} %param.9) | copy-start | bytes 301060
  81.9 9.4 %collective-permute-start.2 = (bf16[3,72,512]{2,1,0:T(8,128)(2,1)S(1)}, bf16[3,72,512]{2,1,0:T(8,128)(2,1)S(1)}, u32[]{:S(2)}, u32[]{:S(2)}) collective-permute-start(bf16[3,72,512]{2,1,0:T(8,128)(2,1)S(1)} %get-tuple-element.41), channel_id=1, source_target_pairs={{32,64},{96,128},{160,192},{224,256},{288,320},{352,384},{416,448}... | collective-permute-start | bytes 663560 | tf_op jit(solution)/shard_map/ppermute | solution.py:382
  86.0 5.3 %collective-permute-start.3 = (bf16[3,72,512]{2,1,0:T(8,128)(2,1)S(1)}, bf16[3,72,512]{2,1,0:T(8,128)(2,1)S(1)}, u32[]{:S(2)}, u32[]{:S(2)}) collective-permute-start(bf16[3,72,512]{2,1,0:T(8,128)(2,1)S(1)} %get-tuple-element.42), channel_id=1, source_target_pairs={{0,32},{64,96},{128,160},{192,224},{256,288},{320,352},{384,416},{... | collective-permute-start | bytes 663560 | tf_op jit(solution)/shard_map/ppermute | solution.py:381
